TPU v7x, 32 devices: a whole 2x2x4 slice. The times are simulated.
32 devices in a mesh: dp: 4 (over z), context: 2 (over x), tensor: 4 (over y, core).
Axes of the slice: x: 2, y: 2, z: 4, core: 2. Of those that a mesh axis runs over, the one named last changes fastest.
Arguments:
- stream: bfloat16 [8, 1024, 1536], P('dp', 'context'), may hold values from -6 to 6
- seg_ids: int32 [8, 1024], P('dp', 'context'), may hold values from 0 to 3, as said below
- input_weight: bfloat16 [2, 1536, 2, 3072], P(None, ('dp', 'context'), None, 'tensor'), may hold values from -0.15625 to 0.15625
- step_size_weight: bfloat16 [2, 1536, 48], P(None, ('dp', 'context'), 'tensor'), may hold values from -0.15625 to 0.15625
- coefficient_weight: bfloat16 [2, 1536, 256], P(None, ('dp', 'context', 'tensor')), may hold values from -0.15625 to 0.15625
- pre_gain: bfloat16 [2, 1536], P(None, ('dp', 'context', 'tensor')), may hold values from 0.5 to 1.5
- conv_bc: bfloat16 [2, 4, 256], P(None, None, ('dp', 'context', 'tensor')), may hold values from -2 to 2
- bias_bc: bfloat16 [2, 256], P(None, ('dp', 'context', 'tensor')), may hold values from -2 to 2
- output_weight: bfloat16 [2, 3072, 1536], P(None, 'tensor', ('dp', 'context')), may hold values from -0.109375 to 0.109375
- conv_x: float32 [2, 4, 3072], P(None, None, 'tensor'), may hold values from -2 to 2
- bias_x: float32 [2, 3072], P(None, 'tensor'), may hold values from -2 to 2
- dt_bias: float32 [2, 48], P(None, 'tensor'), may hold values from -1 to 1
- a_log: float32 [2, 48], P(None, 'tensor'), may hold values from -12 to -2, as said below
- skip: float32 [2, 48], P(None, 'tensor'), may hold values from 0.5 to 1.5
- gate_gain: float32 [2, 3072], P(None, 'tensor'), may hold values from 0.5 to 1.5
- cotangent: bfloat16 [8, 1024, 1536], P('dp', 'context'), may hold values from -6 to 6
Outputs:
- layer_out: bfloat16 [8, 1024, 1536], P('dp', 'context')
- grad_stream: bfloat16 [8, 1024, 1536], P('dp', 'context')
- grad_w_in: float32 [2, 1536, 2, 3072], P(None, ('dp', 'context'), None, 'tensor')
- grad_w_dt: float32 [2, 1536, 48], P(None, ('dp', 'context'), 'tensor')
- grad_w_bc: float32 [2, 1536, 256], P(None, ('dp', 'context', 'tensor'))
- grad_pre_gain: float32 [2, 1536], P(None, ('dp', 'context', 'tensor'))
- grad_conv_bc: float32 [2, 4, 256], P(None, None, ('dp', 'context', 'tensor'))
- grad_bias_bc: float32 [2, 256], P(None, ('dp', 'context', 'tensor'))
- grad_w_out: float32 [2, 3072, 1536], P(None, 'tensor', ('dp', 'context'))
- grad_conv_x: float32 [2, 4, 3072], P(None, None, 'tensor')
- grad_bias_x: float32 [2, 3072], P(None, 'tensor')
- grad_dt_bias: float32 [2, 48], P(None, 'tensor')
- grad_a_log: float32 [2, 48], P(None, 'tensor')
- grad_skip: float32 [2, 48], P(None, 'tensor')
- grad_gate_gain: float32 [2, 3072], P(None, 'tensor')
Inputs may be any that keep to these rules, and one draw needn't show every extreme that they name: `seg_ids`: document numbers start at 0 in every sequence and never fall along it; of each 2 sequences on one index of dp, one drawn from the seed is a single document, the others hold four documents each. `a_log`: Per-head rates, some slow over a whole sequence, some fast.
All inputs are finite; a program needn't handle non-finite values.
Results may differ from a plain program's by a relative error of at most 0.015.
The roundings to bfloat16 on the way count: a program that leaves them out, or rounds other values in their place, can miss the bound.
Values may be sent and summed in bfloat16 or wider, within the bound.
No kernel may reach another device: no remote copies, remote signals or barrier semaphores. Data moves between devices by JAX's collectives and lax.ppermute only.
A program may use at most 640 MiB of HBM per device.

v0:
```python
import jax
import jax.numpy as jnp
from jax import lax
from jax.sharding import PartitionSpec as P

E = 3072
SPAN = 256
LAYERS = 2


PRECISION_HIGH = lax.Precision.HIGHEST
eps = 1e-05


def shifted(value, axis, steps):
    count = lax.axis_size(axis)
    leading, last = (max(0, -steps), min(count, count - steps))
    return lax.ppermute(value, axis, [(source, source + steps) for source in range(leading, last)])


def prefix(value, axis, join, neutral):
    count, mine = (lax.axis_size(axis), lax.axis_index(axis))
    pieces = jax.tree.map(lambda part: lax.all_gather(part, axis), value)
    subtotal = jax.tree.map(
        lambda part, zero: jnp.full_like(part, 0) + jnp.asarray(zero, part.dtype), value, neutral
    )

    def prefix_step(position, subtotal):
        longer = join(subtotal, jax.tree.map(lambda part: part[position], pieces))
        return jax.tree.map(lambda new, old: jnp.where(position < mine, new, old), longer, subtotal)

    return lax.fori_loop(0, count - 1, prefix_step, subtotal)


def entering(x, axis, combine, identity):
    devices, index = (lax.axis_size(axis), lax.axis_index(axis))
    everything = jax.tree.map(
        lambda part, kind: lax.all_gather(part.astype(kind), axis),
        x,
        jax.tree.map(lambda a: jnp.bfloat16 if a.dtype == jnp.float32 else a.dtype, x),
    )
    start = jax.tree.map(
        lambda part, zero: jnp.broadcast_to(jnp.asarray(zero, part.dtype), part.shape), x, identity
    )

    def entering_step(k, before):
        at = devices - 1 - k
        reached = at > index
        new = combine(
            before, jax.tree.map(lambda part, own: part[at].astype(own.dtype), everything, x)
        )
        return jax.tree.map(lambda a, b: jnp.where(reached, a, b), new, before)

    return lax.fori_loop(0, devices, entering_step, start)


def prenorm(values, gain_vec):
    return values * lax.rsqrt(jnp.mean(values * values, axis=-1, keepdims=True) + eps) * gain_vec


def conv_local(values, weights, bias_vec, same_doc):
    steps_out = values.shape[1] - 3
    summed = bias_vec + weights[0] * values[:, 0:steps_out] * same_doc[:, :, 0:1]
    for offset in range(1, 4):
        summed = (
            summed
            + weights[offset]
            * values[:, offset : offset + steps_out]
            * same_doc[:, :, offset : offset + 1]
        )
    return jax.nn.silu(summed)


def span_step(state_in, block_in):
    scaled_in, b_proj, c_proj, log_decay, seg_block, before = block_in
    cumulate = jnp.cumsum(log_decay, axis=1)
    positions = seg_block.shape[1]
    causal = jnp.arange(positions)[:, None] >= jnp.arange(positions)[None, :]
    within_doc = (seg_block[:, :, None] == seg_block[:, None, :]) & causal[None]
    spread = cumulate[:, :, None, :] - cumulate[:, None, :, :]
    decays = jnp.where(
        within_doc[..., None], jnp.exp(jnp.where(within_doc[..., None], spread, 0.0)), 0.0
    )
    scores = jnp.einsum("stn,sun->stu", c_proj, b_proj, precision=PRECISION_HIGH)
    within = jnp.einsum(
        "stuh,suhp->sthp", decays * scores[..., None], scaled_in, precision=PRECISION_HIGH
    )
    survive = (seg_block == before[:, None]).astype(jnp.float32)
    growth = jnp.exp(cumulate) * survive[..., None]
    carried = (
        jnp.einsum("stn,shpn->sthp", c_proj, state_in, precision=PRECISION_HIGH) * growth[..., None]
    )
    fresh_state = jnp.einsum(
        "suh,suhp,sun->shpn", decays[:, -1], scaled_in, b_proj, precision=PRECISION_HIGH
    )
    return (state_in * growth[:, -1][:, :, None, None] + fresh_state, within + carried)


def run_spans(scaled_in, b_proj, c_proj, log_decay, seg_block, before):
    batch_count, length = seg_block.shape
    span_count = length // SPAN
    prior_ids = jnp.concatenate([before[:, None], seg_block[:, :-1]], axis=1)[:, ::SPAN]

    def split_blocks(values):
        return jnp.moveaxis(
            values.reshape((batch_count, span_count, SPAN) + values.shape[2:]), 1, 0
        )

    zero_state = jnp.zeros(
        (batch_count, scaled_in.shape[2], scaled_in.shape[3], b_proj.shape[2]), jnp.float32
    )
    end_state, outputs = lax.scan(
        span_step,
        zero_state,
        (
            split_blocks(scaled_in),
            split_blocks(b_proj),
            split_blocks(c_proj),
            split_blocks(log_decay),
            split_blocks(seg_block),
            jnp.moveaxis(prior_ids, 1, 0),
        ),
    )
    return (jnp.moveaxis(outputs, 0, 1).reshape(scaled_in.shape), end_state)


def prepare(x_conv, bc_conv, step_size_raw, bias_dt, log_rate, seg_block, before):
    batch_count, length, channels = x_conv.shape
    head_count = bias_dt.shape[0]
    state_width = bc_conv.shape[2] // 2
    step_size = jax.nn.softplus(step_size_raw + bias_dt)
    log_decay = -jnp.exp(log_rate) * step_size
    x_heads = x_conv.reshape(batch_count, length, head_count, channels // head_count)
    b_proj = bc_conv[:, :, :state_width]
    c_proj = bc_conv[:, :, state_width:]
    y_zero, end_state = run_spans(
        x_heads * step_size[..., None], b_proj, c_proj, log_decay, seg_block, before
    )
    survive = (seg_block == before[:, None]).astype(jnp.float32)
    growth = jnp.exp(jnp.cumsum(log_decay, axis=1)) * survive[..., None]
    return (y_zero, end_state, growth[:, -1], growth, c_proj, x_heads)


def mix_heads(y_zero, c_proj, growth, carried, x_heads, gate_pre, skip_vec):
    y_full = (
        y_zero
        + jnp.einsum("stn,shpn->sthp", c_proj, carried, precision=PRECISION_HIGH)
        * growth[..., None]
        + skip_vec[:, None] * x_heads
    )
    return y_full.reshape(gate_pre.shape) * jax.nn.silu(gate_pre)


def rescale(gated_vals, square_sum, gain_vec):
    return gated_vals * lax.rsqrt(square_sum[..., None] / E + eps) * gain_vec


def chain_join(earlier, later):
    return (earlier[0] * later[0], later[0][..., None, None] * earlier[1] + later[1])


def local(
    stream,
    seg_ids,
    input_weight,
    step_size_weight,
    coefficient_weight,
    pre_gain,
    conv_bc,
    bias_bc,
    output_weight,
    conv_x,
    bias_x,
    dt_bias,
    a_log,
    skip,
    gate_gain,
    cotangent,
):
    batch_seq, local_len, model_width = stream.shape
    token_rows = batch_seq * local_len
    edge_ids = shifted(seg_ids[:, -3:], "context", 1)
    ext_ids = jnp.concatenate([edge_ids, seg_ids], axis=1)
    same_doc = jnp.stack(
        [ext_ids[:, offset : offset + local_len] == seg_ids for offset in range(4)], axis=2
    ).astype(jnp.float32)
    prev_ids = edge_ids[:, -1]

    def fetch(layer_pos):
        head_set = (
            lax.all_gather(input_weight[layer_pos], ("dp", "context"), axis=0, tiled=True),
            lax.all_gather(step_size_weight[layer_pos], ("dp", "context"), axis=0, tiled=True),
            lax.all_gather(output_weight[layer_pos], ("dp", "context"), axis=1, tiled=True),
        )
        shared_set = (
            lax.all_gather(
                coefficient_weight[layer_pos], ("dp", "context", "tensor"), axis=0, tiled=True
            ),
            lax.all_gather(pre_gain[layer_pos], ("dp", "context", "tensor"), axis=0, tiled=True),
            lax.all_gather(conv_bc[layer_pos], ("dp", "context", "tensor"), axis=1, tiled=True),
            lax.all_gather(bias_bc[layer_pos], ("dp", "context", "tensor"), axis=0, tiled=True),
        )
        return (head_set, shared_set)

    def convolve(inner_ext, bc_ext, weight_x, bias_xv, weight_bc, bias_bcv):
        return (
            conv_local(inner_ext, weight_x, bias_xv, same_doc),
            conv_local(bc_ext, weight_bc, bias_bcv, same_doc),
        )

    def prepare_local(x_conv, bc_conv, step_size_raw, bias_dt, log_rate):
        return prepare(x_conv, bc_conv, step_size_raw, bias_dt, log_rate, seg_ids, prev_ids)

    current = stream.astype(jnp.float32)
    kept_list = []
    for layer_pos in range(LAYERS):
        head_set, shared_set = fetch(layer_pos)
        in_full, dt_full, out_full = head_set
        bc_full, gain_full, convbc_full, biasbc_full = shared_set
        normed_f, pull_norm = jax.vjp(prenorm, current, gain_full.astype(jnp.float32))
        normed_low = normed_f.astype(jnp.bfloat16).reshape(-1, model_width)
        normalized_input = normed_low
        projected_rows = jnp.einsum(
            "td,dke->tke", normalized_input, in_full, preferred_element_type=jnp.float32
        )
        gate_pre = projected_rows[:, 0].reshape(batch_seq, local_len, -1)
        inner_vals = projected_rows[:, 1].astype(jnp.bfloat16).reshape(batch_seq, local_len, -1)
        bc_unmixed_rows = (
            jnp.dot(normalized_input, bc_full, preferred_element_type=jnp.float32)
            .astype(jnp.bfloat16)
            .reshape(batch_seq, local_len, -1)
        )
        step_size_raw = jnp.dot(
            normalized_input, dt_full, preferred_element_type=jnp.float32
        ).reshape(batch_seq, local_len, -1)
        inner_rim, bc_rim = shifted((inner_vals[:, -3:], bc_unmixed_rows[:, -3:]), "context", 1)
        inner_ext = jnp.concatenate([inner_rim, inner_vals], axis=1).astype(jnp.float32)
        bc_ext = jnp.concatenate([bc_rim, bc_unmixed_rows], axis=1).astype(jnp.float32)
        convolved, pull_conv = jax.vjp(
            convolve,
            inner_ext,
            bc_ext,
            conv_x[layer_pos],
            bias_x[layer_pos],
            convbc_full.astype(jnp.float32),
            biasbc_full.astype(jnp.float32),
        )
        prepared, pull_prep = jax.vjp(
            prepare_local,
            convolved[0],
            convolved[1],
            step_size_raw,
            dt_bias[layer_pos],
            a_log[layer_pos],
        )
        y_zero, end_state, total_decay, growth, c_proj, x_heads = prepared
        carried = prefix(
            (total_decay, end_state),
            "context",
            chain_join,
            (jnp.ones_like(total_decay), jnp.zeros_like(end_state)),
        )[1]
        gated_vals, pull_mix = jax.vjp(
            mix_heads, y_zero, c_proj, growth, carried, x_heads, gate_pre, skip[layer_pos]
        )
        square_sum = lax.psum(jnp.sum(gated_vals * gated_vals, axis=-1), "tensor")
        scaled_rows, pull_scale = jax.vjp(rescale, gated_vals, square_sum, gate_gain[layer_pos])
        scaled_low = scaled_rows.astype(jnp.bfloat16).reshape(token_rows, -1)
        partial_out = jnp.dot(scaled_low, out_full, preferred_element_type=jnp.float32)
        branch_output = lax.psum(partial_out, "tensor")
        current = current + branch_output.reshape(batch_seq, local_len, model_width)
        kept_list.append(
            (
                normalized_input,
                head_set,
                shared_set,
                pull_norm,
                pull_conv,
                pull_prep,
                pull_mix,
                pull_scale,
                gated_vals,
                carried,
                total_decay,
                scaled_low,
            )
        )
    grad_current = cotangent.astype(jnp.float32)
    collected = []
    for layer_pos in reversed(range(LAYERS)):
        (
            normalized_input,
            head_set,
            shared_set,
            pull_norm,
            pull_conv,
            pull_prep,
            pull_mix,
            pull_scale,
            gated_vals,
            carried,
            total_decay,
            scaled_low,
        ) = kept_list[layer_pos]
        head_set, shared_set = fetch(layer_pos)
        in_full, dt_full, out_full = head_set
        bc_full = shared_set[0]
        grad_low = grad_current.astype(jnp.bfloat16).reshape(-1, model_width)
        grad_out_w = jnp.dot(scaled_low.T, grad_low, preferred_element_type=jnp.float32)
        grad_scaled = jnp.dot(grad_low, out_full.T, preferred_element_type=jnp.float32).reshape(
            gated_vals.shape
        )
        grad_gated, grad_square_part, grad_gate_gain = pull_scale(grad_scaled)
        grad_square = lax.psum(grad_square_part, "tensor")
        grad_gated = grad_gated + 2.0 * gated_vals * grad_square[..., None]
        grad_y_zero, grad_c_mix, grad_growth, grad_carried, grad_x_mix, grad_gate, grad_skip = (
            pull_mix(grad_gated)
        )
        adjoint_next = entering(
            (total_decay, grad_carried),
            "context",
            chain_join,
            (jnp.ones_like(total_decay), jnp.zeros_like(grad_carried)),
        )[1]
        grad_total = jnp.sum(adjoint_next * carried, axis=(2, 3))
        grad_x_conv, grad_bc_conv, grad_dt, grad_dt_bias, grad_a_log = pull_prep(
            (grad_y_zero, adjoint_next, grad_total, grad_growth, grad_c_mix, grad_x_mix)
        )
        grad_inner_ext, grad_bc_ext, grad_conv_x, grad_bias_x, grad_conv_bc, grad_bias_bc = (
            pull_conv((grad_x_conv, grad_bc_conv))
        )
        inner_back, bc_back = shifted((grad_inner_ext[:, :3], grad_bc_ext[:, :3]), "context", -1)
        grad_inner = grad_inner_ext[:, 3:] + jnp.pad(
            inner_back, ((0, 0), (local_len - 3, 0), (0, 0))
        )
        grad_bc = (
            grad_bc_ext[:, 3:] + jnp.pad(bc_back, ((0, 0), (local_len - 3, 0), (0, 0)))
        ).reshape(token_rows, -1)
        grad_proj = jnp.stack(
            [
                grad_gate.astype(jnp.bfloat16).reshape(token_rows, -1),
                grad_inner.astype(jnp.bfloat16).reshape(token_rows, -1),
            ],
            axis=1,
        )
        grad_dt_low = grad_dt.astype(jnp.bfloat16).reshape(token_rows, -1)
        grad_in_w = jnp.einsum(
            "td,tke->dke", normalized_input, grad_proj, preferred_element_type=jnp.float32
        )
        grad_dt_w = jnp.dot(normalized_input.T, grad_dt_low, preferred_element_type=jnp.float32)
        normed_wide = normalized_input.astype(jnp.float32)
        grad_bc_w = jnp.dot(normed_wide.T, grad_bc, precision=PRECISION_HIGH)
        grad_normed = jnp.einsum(
            "tke,dke->td", grad_proj, in_full, preferred_element_type=jnp.float32
        )
        grad_normed = grad_normed + jnp.dot(
            grad_dt_low, dt_full.T, preferred_element_type=jnp.float32
        )
        grad_normed = grad_normed + jnp.dot(
            grad_bc, bc_full.astype(jnp.float32).T, precision=PRECISION_HIGH
        )
        grad_local, grad_pre_gain = pull_norm(
            grad_normed.reshape(batch_seq, local_len, model_width)
        )
        grad_current = grad_current + lax.psum(grad_local, "tensor")
        head_grads = (
            lax.psum_scatter(
                grad_in_w.astype(jnp.bfloat16), ("dp", "context"), scatter_dimension=0, tiled=True
            ).astype(jnp.float32),
            lax.psum_scatter(
                grad_dt_w.astype(jnp.bfloat16), ("dp", "context"), scatter_dimension=0, tiled=True
            ).astype(jnp.float32),
            lax.psum_scatter(
                grad_out_w.astype(jnp.bfloat16), ("dp", "context"), scatter_dimension=1, tiled=True
            ).astype(jnp.float32),
        )
        shared_grads = (
            lax.psum_scatter(
                grad_bc_w, ("dp", "context", "tensor"), scatter_dimension=0, tiled=True
            ),
            lax.psum_scatter(
                grad_pre_gain, ("dp", "context", "tensor"), scatter_dimension=0, tiled=True
            ),
            lax.psum_scatter(
                grad_conv_bc, ("dp", "context", "tensor"), scatter_dimension=1, tiled=True
            ),
            lax.psum_scatter(
                grad_bias_bc, ("dp", "context", "tensor"), scatter_dimension=0, tiled=True
            ),
        )
        small_grads = lax.psum(
            (grad_conv_x, grad_bias_x, grad_dt_bias, grad_a_log, grad_skip, grad_gate_gain),
            ("dp", "context"),
        )
        collected.append((head_grads, shared_grads, small_grads))
    ordered = collected[::-1]
    layer_out = current.astype(jnp.bfloat16)
    grad_result = grad_current.astype(jnp.bfloat16)

    def stacked(group_pos, member_pos):
        return jnp.stack([entry[group_pos][member_pos] for entry in ordered], axis=0)

    return (
        layer_out,
        grad_result,
        stacked(0, 0),
        stacked(0, 1),
        stacked(1, 0),
        stacked(1, 1),
        stacked(1, 2),
        stacked(1, 3),
        stacked(0, 2),
        stacked(2, 0),
        stacked(2, 1),
        stacked(2, 2),
        stacked(2, 3),
        stacked(2, 4),
        stacked(2, 5),
    )


def solution(mesh):
    in_specs = (
        P("dp", "context", None),
        P("dp", "context"),
        P(None, ("dp", "context"), None, "tensor"),
        P(None, ("dp", "context"), "tensor"),
        P(None, ("dp", "context", "tensor"), None),
        P(None, ("dp", "context", "tensor")),
        P(None, None, ("dp", "context", "tensor")),
        P(None, ("dp", "context", "tensor")),
        P(None, "tensor", ("dp", "context")),
        P(None, None, "tensor"),
        P(None, "tensor"),
        P(None, "tensor"),
        P(None, "tensor"),
        P(None, "tensor"),
        P(None, "tensor"),
        P("dp", "context", None),
    )
    out_specs = (
        P("dp", "context", None),
        P("dp", "context", None),
        P(None, ("dp", "context"), None, "tensor"),
        P(None, ("dp", "context"), "tensor"),
        P(None, ("dp", "context", "tensor"), None),
        P(None, ("dp", "context", "tensor")),
        P(None, None, ("dp", "context", "tensor")),
        P(None, ("dp", "context", "tensor")),
        P(None, "tensor", ("dp", "context")),
        P(None, None, "tensor"),
        P(None, "tensor"),
        P(None, "tensor"),
        P(None, "tensor"),
        P(None, "tensor"),
        P(None, "tensor"),
    )
    return jax.shard_map(local, mesh=mesh, in_specs=in_specs, out_specs=out_specs, check_vma=False)
```

profile of v0, /device:TPU:0, one launch (start us, length us, event | category | flops | bytes accessed | tf_op | source)
XLA Modules:
  0.0 2311.2 jit_solution(12409439219178624775)
XLA Ops:
  12.3 43.7 %all-reduce.59 = (bf16[1536]{0:T(1024)(128)(2,1)S(1)}, bf16[256]{0:T(256)(128)(2,1)S(1)}, bf16[1536]{0:T(1024)(128)(2,1)}, bf16[256]{0:T(256)(128)(2,1)}) all-reduce(bf16[1536]{0:T(1024)(128)(2,1)S(1)} %dynamic-update-slice, ...), channel_id=2, replica_groups=mesh['dp'=4,'context'=2,'tensor'=4] {'dp','context','tensor'}, use_global_device_ids=true, to_apply=%add.46 | all-reduce | flops 3584 | bytes 14336
  57.3 45.9 %all-gather.5 = bf16[1,1536,256]{2,1,0:T(8,128)(2,1)S(1)} all-gather(bf16[1,48,256]{2,1,0:T(8,128)(2,1)S(1)} %get-tuple-element.3206), channel_id=7, replica_groups=mesh['dp'=4,'context'=2,'tensor'=4] {'dp','context','tensor'}, dimensions={1}, use_global_device_ids=true | all-gather | bytes 811008 | tf_op jit(solution)/shard_map/all_gather | solution.py:196
  109.2 37.0 %all-gather.4 = bf16[1,4,256]{1,0,2:T(2,128)(2,1)S(1)} all-gather(bf16[1,4,8]{1,0,2:T(2,128)(2,1)S(1)} %copy.938), channel_id=6, replica_groups=mesh['dp'=4,'context'=2,'tensor'=4] {'dp','context','tensor'}, dimensions={2}, use_global_device_ids=true | all-gather | bytes 2112 | tf_op jit(solution)/shard_map/all_gather | solution.py:200
  147.1 32.3 %all-gather.1 = bf16[1,1536,12]{2,0,1:T(2,128)(2,1)S(1)} all-gather(bf16[1,192,12]{2,0,1:T(2,128)(2,1)S(1)} %copy.936), channel_id=3, replica_groups=mesh['dp'=4,'context'=2,'tensor'=4] {'dp','context'}, dimensions={1}, use_global_device_ids=true | all-gather | bytes 41472 | tf_op jit(solution)/shard_map/all_gather | solution.py:192
  253.3 131.1 %while.176 = (s32[]{:T(128)}, f32[2,12,64,128]{3,2,1,0:T(8,128)}, f32[2,2,256,12,64]{2,4,3,1,0:T(8,128)}, pred[2,2,256,256,12]{3,2,4,1,0:T(32,128)(4,1)}, f32[2,...) while((s32[]{:T(128)}, f32[2,12,64,128]{3,2,1,0:T(8,128)}, ...), condition=%wide.region_4.6_spmd.clone, body=%wide.region_1.5_spmd.clone.sunk | while | flops 2633506816 | bytes 115836584 | solution.py:112
  439.7 27.4 %all-gather.33.cloned.1.call-done = bf16[1,768,1536]{1,2,0:T(8,128)(2,1)} async-done(((bf16[1,768,192]{1,2,0:T(8,128)(2,1)}), bf16[1,768,1536]{1,2,0:T(8,128)(2,1)}) %all-gather.33.cloned.1.call-update) | async-done | bytes 2359312 | tf_op jit(solution)/shard_map/all_gather | solution.py:193
  478.6 32.0 %all-gather.10 = bf16[1,1536,12]{2,0,1:T(2,128)(2,1)S(1)} all-gather(bf16[1,192,12]{2,0,1:T(2,128)(2,1)S(1)} %copy.939), channel_id=12, replica_groups=mesh['dp'=4,'context'=2,'tensor'=4] {'dp','context'}, dimensions={1}, use_global_device_ids=true | all-gather | bytes 41472 | tf_op jit(solution)/shard_map/all_gather | solution.py:192
  511.2 40.0 %all-gather.13 = bf16[1,4,256]{1,0,2:T(2,128)(2,1)S(1)} all-gather(bf16[1,4,8]{1,0,2:T(2,128)(2,1)S(1)} %copy.941), channel_id=15, replica_groups=mesh['dp'=4,'context'=2,'tensor'=4] {'dp','context','tensor'}, dimensions={2}, use_global_device_ids=true | all-gather | bytes 2112 | tf_op jit(solution)/shard_map/all_gather | solution.py:200
  554.3 39.5 %all-gather.14 = bf16[1,1536,256]{2,1,0:T(8,128)(2,1)S(1)} all-gather(bf16[1,48,256]{2,1,0:T(8,128)(2,1)S(1)} %copy-done.185), channel_id=16, replica_groups=mesh['dp'=4,'context'=2,'tensor'=4] {'dp','context','tensor'}, dimensions={1}, use_global_device_ids=true | all-gather | bytes 811008 | tf_op jit(solution)/shard_map/all_gather | solution.py:196
  616.9 69.4 %all-gather.35.cloned.1.call-done = bf16[1,1536,2,768]{3,1,2,0:T(8,128)(2,1)} async-done(((bf16[1,192,2,768]{3,1,2,0:T(8,128)(2,1)}), bf16[1,1536,2,768]{3,1,2,0:T(8,128)(2,1)}) %all-gather.35.cloned.1.call-update) | async-done | bytes 4718608 | tf_op jit(solution)/shard_map/all_gather | solution.py:191
  758.2 109.0 %while.177 = (s32[]{:T(128)}, f32[2,12,64,128]{3,2,1,0:T(8,128)S(1)}, f32[2,2,256,12,64]{2,4,3,1,0:T(8,128)}, pred[2,2,256,256,12]{3,2,4,1,0:T(32,128)(4,1)}, f3...) while((s32[]{:T(128)}, ...), condition=%wide.region_14.16_spmd.clone, body=%wide.region_11.15_spmd.clone.sunk | while | flops 2633506816 | bytes 122619496 | solution.py:112
  923.0 24.9 %all-gather.39.cloned.1.call-done = bf16[1,768,1536]{1,2,0:T(8,128)(2,1)} async-done(((bf16[1,768,192]{1,2,0:T(8,128)(2,1)}), bf16[1,768,1536]{1,2,0:T(8,128)(2,1)}) %all-gather.39.cloned.1.call-update) | async-done | bytes 2359312 | tf_op jit(solution)/shard_map/all_gather | solution.py:193
  1001.3 99.0 %while.174 = (s32[]{:T(128)}, f32[2,12,64,128]{3,2,1,0:T(8,128)S(1)}, f32[2,2,256,12,64]{2,4,3,1,0:T(8,128)}, f32[2,2,256,128]{3,2,1,0:T(8,128)}, f32[2,2,256,12...) while((s32[]{:T(128)}, ...), condition=%wide.region_32.34_spmd, body=%wide.region_24.33_spmd.sunk | while | flops 5253378048 | bytes 119971240 | solution.py:112
  1187.5 107.0 %all-reduce.66.cloned.1.call-done = f32[2,512,1536]{2,1,0:T(8,128)} async-done(((f32[2,512,1536]{2,1,0:T(8,128)}), f32[2,512,1536]{2,1,0:T(8,128)}) %all-reduce.66.cloned.1.call-update) | async-done | bytes 6291472 | tf_op jit(solution)/shard_map/psum | solution.py:365
  1367.5 97.1 %while.175 = (s32[]{:T(128)}, f32[2,12,64,128]{3,2,1,0:T(8,128)S(1)}, f32[2,2,256,12,64]{2,4,3,1,0:T(8,128)}, f32[2,2,256,128]{3,2,1,0:T(8,128)}, f32[2,2,256,12...) while((s32[]{:T(128)}, ...), condition=%wide.region_52.54_spmd, body=%wide.region_44.53_spmd.sunk | while | flops 5253378048 | bytes 119938408 | solution.py:112
  1543.1 13.9 multiply_reduce_fusion.10
  1618.7 37.8 %all-reduce.57 = (f32[1,4,768]{2,1,0:T(4,128)S(1)}, f32[1,4,768]{2,1,0:T(4,128)S(1)}, f32[1,768]{1,0:T(1,128)S(1)}, f32[1,768]{1,0:T(1,128)S(1)}, f32[1,12]{1,0:...) all-reduce(f32[1,4,768]{2,1,0:T(4,128)S(1)} %add_bitcast_fusion, ...), channel_id=1, replica_groups=mesh['dp'=4,'context'=2,'tensor'=4] {'dp','context'}, use_global_device_ids=true, to_apply=%region_95.97 | all-reduce | flops 9288 | bytes 74304 | tf_op jit(solution)/shard_map/psum | solution.py:391
  1660.1 37.6 %all-reduce.56 = (f32[1536]{0:T(1024)S(1)}, f32[1536]{0:T(1024)S(1)}, f32[4,256]{1,0:T(4,128)S(1)}, f32[4,256]{1,0:T(4,128)S(1)}, f32[256]{0:T(256)S(1)}, /*index=5*/f32[256]{0:T(256)S(1)}) all-reduce(f32[1536]{0:T(1024)S(1)} %copy-done.225, ...), channel_id=31, replica_groups=mesh['dp'=4,'context'=2,'tensor'=4] {'dp','context','tensor'}, use_global_device_ids=true, to_apply=%region_69.71.clone | all-reduce | flops 5632 | bytes 45056
  1701.4 33.9 %reduce-scatter.19.cloned.1.call-done = f32[48,256]{1,0:T(8,128)} async-done(((f32[1536,256]{1,0:T(8,128)}), f32[48,256]{1,0:T(8,128)}) %reduce-scatter.19.cloned.1.call-update) | async-done | bytes 49168 | tf_op jit(solution)/shard_map/reduce_scatter | solution.py:378
  1736.8 70.5 %reduce-scatter.25.cloned.1.call-done = bf16[768,192]{0,1:T(8,128)(2,1)} async-done(((bf16[768,1536]{0,1:T(8,128)(2,1)}), bf16[768,192]{0,1:T(8,128)(2,1)}) %reduce-scatter.25.cloned.1.call-update) | async-done | bytes 294928 | tf_op jit(solution)/shard_map/reduce_scatter | solution.py:373
  1807.3 72.0 %reduce-scatter.23.cloned.1.call-done = bf16[768,192]{0,1:T(8,128)(2,1)} async-done(((bf16[768,1536]{0,1:T(8,128)(2,1)}), bf16[768,192]{0,1:T(8,128)(2,1)}) %reduce-scatter.23.cloned.1.call-update) | async-done | bytes 294928 | tf_op jit(solution)/shard_map/reduce_scatter | solution.py:373
  1881.5 220.4 %all-reduce.68.cloned.1.call-done = (f32[2,512,1536]{2,1,0:T(8,128)}, f32[2,512,1536]{2,1,0:T(8,128)}) async-done(((f32[2,512,1536]{2,1,0:T(8,128)}, f32[2,512,1536]{2,1,0:T(8,128)}), (f32[2,512,1536]{2,1,0:T(8,128)}, f32[2,512,1536]{2,1,0:T(8,128)})) %all-reduce.68.cloned.1.call-update) | async-done | bytes 12582928 | tf_op jit(solution)/shard_map/psum | solution.py:270
  2115.7 85.4 %reduce-scatter.17.cloned.1.call-done = bf16[192,2,768]{2,0,1:T(8,128)(2,1)} async-done(((bf16[1536,2,768]{2,0,1:T(8,128)(2,1)}), bf16[192,2,768]{2,0,1:T(8,128)(2,1)}) %reduce-scatter.17.cloned.1.call-update) | async-done | bytes 589840 | tf_op jit(solution)/shard_map/reduce_scatter | solution.py:367
  2201.1 98.7 %reduce-scatter.15.cloned.1.call-done = bf16[192,2,768]{2,0,1:T(8,128)(2,1)} async-done(((bf16[1536,2,768]{2,0,1:T(8,128)(2,1)}), bf16[192,2,768]{2,0,1:T(8,128)(2,1)}) %reduce-scatter.15.cloned.1.call-update) | async-done | bytes 589840 | tf_op jit(solution)/shard_map/reduce_scatter | solution.py:367
  (1440 shorter events, 1124.0 us)
Async XLA Ops:
  7.2 188.1 %all-gather.29.cloned.1.call-start = ((), (), s32[]{:S(2)}) async-start(), calls=%async_computation.16 | async-start | bytes 5308416 | tf_op jit(solution)/shard_map/all_gather | solution.py:191
  11.2 407.1 %all-gather.31.cloned.1.call-start = ((), (), s32[]{:S(2)}) async-start(), calls=%async_computation.17 | async-start | bytes 2359296 | tf_op jit(solution)/shard_map/all_gather | solution.py:23
  105.7 85.7 %collective-permute-start.2 = (bf16[2,3,256]{2,1,0:T(4,128)(2,1)S(1)}, bf16[2,3,256]{2,1,0:T(4,128)(2,1)S(1)}, u32[]{:S(2)}, u32[]{:S(2)}) collective-permute-start(bf16[2,3,256]{2,1,0:T(4,128)(2,1)S(1)} %slice.573), channel_id=1, source_target_pairs={{0,4},{1,5},{2,6},{3,7},{8,12},{9,13},{10,14},{11,15},{16,20},{17,... | collective-permute-start | bytes 9224 | tf_op jit(solution)/shard_map/ppermute | solution.py:18
  107.2 82.4 %collective-permute-start = (s32[2,3]{1,0:T(2,128)S(1)}, s32[2,3]{1,0:T(2,128)S(1)}, u32[]{:S(2)}, u32[]{:S(2)}) collective-permute-start(s32[2,3]{1,0:T(2,128)S(1)} %slice.433), channel_id=1, source_target_pairs={{0,4},{1,5},{2,6},{3,7},{8,12},{9,13},{10,14},{11,15},{16,20},{17,... | collective-permute-start | bytes 80 | tf_op jit(solution)/shard_map/ppermute | solution.py:18
  384.4 82.6 %all-gather.33.cloned.1.call-start = ((), (), s32[]{:S(2)}) async-start(), calls=%async_computation.18 | async-start | bytes 2654208 | tf_op jit(solution)/shard_map/all_gather | solution.py:193
  386.9 216.8 %all-reduce.64.cloned.1.call-start = ((), (), s32[]{:S(2)}) async-start(), calls=%async_computation.8 | async-start | bytes 12582912 | tf_op jit(solution)/shard_map/psum | solution.py:270
  476.4 209.9 %all-gather.35.cloned.1.call-start = ((), (), s32[]{:S(2)}) async-start(), calls=%async_computation.19 | async-start | bytes 5308416 | tf_op jit(solution)/shard_map/all_gather | solution.py:191
  478.3 425.3 %all-gather.37.cloned.1.call-start = ((), (), s32[]{:S(2)}) async-start(), calls=%async_computation.20 | async-start | bytes 2359296 | tf_op jit(solution)/shard_map/all_gather | solution.py:23
  612.0 91.0 %collective-permute-start.4 = (bf16[2,3,256]{2,1,0:T(4,128)(2,1)S(1)}, bf16[2,3,256]{2,1,0:T(4,128)(2,1)S(1)}, u32[]{:S(2)}, u32[]{:S(2)}) collective-permute-start(bf16[2,3,256]{2,1,0:T(4,128)(2,1)S(1)} %slice.596), channel_id=1, source_target_pairs={{0,4},{1,5},{2,6},{3,7},{8,12},{9,13},{10,14},{11,15},{16,20},{17,... | collective-permute-start | bytes 9224 | tf_op jit(solution)/shard_map/ppermute | solution.py:18
  699.5 6.5 collective-permute-start.3
  868.1 79.8 %all-gather.39.cloned.1.call-start = ((), (), s32[]{:S(2)}) async-start(), calls=%async_computation.21 | async-start | bytes 2654208 | tf_op jit(solution)/shard_map/all_gather | solution.py:193
  868.9 425.6 %all-reduce.66.cloned.1.call-start = ((), (), s32[]{:S(2)}) async-start(), calls=%async_computation.9 | async-start | bytes 12582912 | tf_op jit(solution)/shard_map/psum | solution.py:365
  1129.4 25.2 %collective-permute-start.6 = (f32[2,3,256]{2,1,0:T(4,128)S(1)}, f32[2,3,256]{2,1,0:T(4,128)S(1)}, u32[]{:S(2)}, u32[]{:S(2)}) collective-permute-start(f32[2,3,256]{2,1,0:T(4,128)S(1)} %pad_add_fusion.7), channel_id=1, source_target_pairs={{4,0},{5,1},{6,2},{7,3},{12,8},{13,9},{14,10},{15,11},{20,16},{21,... | collective-permute-start | bytes 18440 | tf_op jit(solution)/shard_map/ppermute | solution.py:18
  1130.8 23.9 %collective-permute-start.5 = (f32[2,3,768]{2,1,0:T(4,128)S(1)}, f32[2,3,768]{2,1,0:T(4,128)S(1)}, u32[]{:S(2)}, u32[]{:S(2)}) collective-permute-start(f32[2,3,768]{2,1,0:T(4,128)S(1)} %pad_add_fusion.5), channel_id=1, source_target_pairs={{4,0},{5,1},{6,2},{7,3},{12,8},{13,9},{14,10},{15,11},{20,16},{21,... | collective-permute-start | bytes 55304 | tf_op jit(solution)/shard_map/ppermute | solution.py:18
  1174.1 443.3 %reduce-scatter.29.cloned.1.call-start = ((), (), s32[]{:S(2)}) async-start(), calls=%async_computation.23 | async-start | bytes 442368
  1187.5 512.4 %reduce-scatter.27.cloned.1.call-start = ((), (), s32[]{:S(2)}) async-start(), calls=%async_computation.22 | async-start | bytes 442368
  1471.0 230.4 %reduce-scatter.21.cloned.1.call-start = ((), (), s32[]{:S(2)}) async-start(), calls=%async_computation.13 | async-start | bytes 1622016 | tf_op jit(solution)/shard_map/reduce_scatter | solution.py:378
  1478.0 257.3 %reduce-scatter.19.cloned.1.call-start = ((), (), s32[]{:S(2)}) async-start(), calls=%async_computation.12 | async-start | bytes 1622016 | tf_op jit(solution)/shard_map/reduce_scatter | solution.py:378
  1501.5 305.8 %reduce-scatter.25.cloned.1.call-start = ((), (), s32[]{:S(2)}) async-start(), calls=%async_computation.15 | async-start | bytes 2654208 | tf_op jit(solution)/shard_map/reduce_scatter | solution.py:373
  1523.4 356.0 %reduce-scatter.23.cloned.1.call-start = ((), (), s32[]{:S(2)}) async-start(), calls=%async_computation.14 | async-start | bytes 2654208 | tf_op jit(solution)/shard_map/reduce_scatter | solution.py:373
  1563.0 16.4 collective-permute-start.7
  1573.0 528.9 %all-reduce.68.cloned.1.call-start = ((), (), s32[]{:S(2)}) async-start(), calls=%async_computation.24 | async-start | bytes 25165824 | tf_op jit(solution)/shard_map/psum | solution.py:270
  1595.5 605.6 %reduce-scatter.17.cloned.1.call-start = ((), (), s32[]{:S(2)}) async-start(), calls=%async_computation.11 | async-start | bytes 5308416 | tf_op jit(solution)/shard_map/reduce_scatter | solution.py:367
  1606.0 693.8 %reduce-scatter.15.cloned.1.call-start = ((), (), s32[]{:S(2)}) async-start(), calls=%async_computation.10 | async-start | bytes 5308416 | tf_op jit(solution)/shard_map/reduce_scatter | solution.py:367
  (369 other events, 4697.4 us)
Sparse Core Ops, SparseCore 0:
  11.3 87.8 all-gather.28
  384.5 27.5 all-gather.30
  414.9 52.0 all-gather.32
  476.5 127.0 all-reduce.63
  606.3 79.9 all-gather.34
  868.2 25.3 all-gather.36
  895.8 52.0 all-gather.38
  1174.2 120.1 all-reduce.65
  1297.7 61.5 reduce-scatter.28
  1471.2 61.4 reduce-scatter.26
  1537.9 96.1 reduce-scatter.20
  1639.2 96.0 reduce-scatter.18
  1739.4 67.8 reduce-scatter.24
  1811.2 68.0 reduce-scatter.22
  1881.8 220.0 all-reduce.67
  2105.4 95.6 reduce-scatter.16
  2204.6 95.2 reduce-scatter.14
where the time goes:
time: 2320 us; the launch traced here: 2310 us
  waiting for transfers between devices  824 us (36%)
  blocking collectives  410 us (18%)
  matrix products  392 us (17%)
  local copies, waits for them, and re-layouts  366 us (16%)
  other arithmetic  279 us (12%)
    psum x2, waiting for transfers between devices, local(): branch_output = lax.psum(partial_out, 'tensor')  230 us
    reduce_scatter x2, waiting for transfers between devices, local(): lax.psum_scatter(grad_in_w.astype(jnp.bfloat16), ('dp', 'context'), scatt...  184 us
    reduce_scatter x2, waiting for transfers between devices, local(): lax.psum_scatter(grad_out_w.astype(jnp.bfloat16), ('dp', 'context'), scat...  143 us
    dot_general x12, matrix products, span_step(): jnp.einsum('stuh,suhp->sthp', decays * scores[..., None], scaled_in, prec...  126 us
    psum x1, waiting for transfers between devices, local(): grad_current = grad_current + lax.psum(grad_local, 'tensor')  107 us
    another operation x102, local copies, waits for them, and re-layouts  89.9 us
    all_gather x2, blocking collectives, fetch(): lax.all_gather(coefficient_weight[layer_pos], ('dp', 'context', 'tensor')...  85.5 us
    unnamed x2, blocking collectives  81.3 us
  transfers between devices with their start and end apart: 26, of which 12 were waited for; matrix products, arithmetic and copies ran while one was open for 20% of the time, Pallas kernels for 0%

commit v1 on v0

v1 whole, which is shorter than its diff:
```python
import functools

import jax
import jax.numpy as jnp
from jax import lax
from jax.experimental import pallas as pl
from jax.experimental.pallas import tpu as pltpu
from jax.sharding import PartitionSpec as P

CHUNK = 128
LANES = 128
eps = 1e-05
F32 = jnp.float32
BF16 = jnp.bfloat16
HIGH = lax.Precision.HIGHEST
NN = (((1,), (0,)), ((), ()))
NT = (((1,), (1,)), ((), ()))
TN = (((0,), (0,)), ((), ()))
NO_LINK = -1e30
FWD_WIDE = True
BWD_WIDE = True
FSTATE = F32


def mm(a, b, dims=NN):
    return lax.dot_general(a, b, dims, preferred_element_type=F32)


def params(mib=48):
    return pltpu.CompilerParams(
        dimension_semantics=("arbitrary",), vmem_limit_bytes=mib * 1024 * 1024
    )


def flipped(value, axis, bit):
    count = lax.axis_size(axis)
    return lax.ppermute(value, axis, [(i, i ^ (1 << bit)) for i in range(count)])


def bits(axis):
    return (lax.axis_size(axis) - 1).bit_length()


def shifted(value, axis, steps):
    count = lax.axis_size(axis)
    leading, last = (max(0, -steps), min(count, count - steps))
    return lax.ppermute(value, axis, [(source, source + steps) for source in range(leading, last)])


def ring(value, axis):
    count = lax.axis_size(axis)
    return lax.ppermute(value, axis, [(i, (i - 1) % count) for i in range(count)])


def summed_over(value, axes):
    for axis in axes:
        for bit in range(bits(axis)):
            value = value + flipped(value, axis, bit)
    return value


def gather_small(value, axes):
    value = value[None]
    for axis in axes:
        index = lax.axis_index(axis)
        for bit in range(bits(axis)):
            other = flipped(value, axis, bit)
            upper = (index >> bit) & 1
            value = jnp.concatenate(
                [jnp.where(upper == 0, value, other), jnp.where(upper == 0, other, value)], axis=0
            )
    return value


def scatter_rows(value):
    index = lax.axis_index("tensor")
    kind = value.dtype
    for bit in range(bits("tensor")):
        mine = (index >> bit) & 1
        half = value.shape[0] // 2
        sent = lax.dynamic_slice_in_dim(value, (1 - mine) * half, half, 0).astype(kind)
        kept = lax.dynamic_slice_in_dim(value, mine * half, half, 0).astype(F32)
        value = kept + flipped(sent, "tensor", bit).astype(F32)
    return value


def own_rows(value):
    index = lax.axis_index("tensor")
    for bit in range(bits("tensor")):
        half = value.shape[0] // 2
        value = lax.dynamic_slice_in_dim(value, ((index >> bit) & 1) * half, half, 0)
    return value


def gather_rows(value):
    index = lax.axis_index("tensor")
    for bit in reversed(range(bits("tensor"))):
        upper = (index >> bit) & 1
        other = flipped(value, "tensor", bit)
        value = jnp.concatenate(
            [jnp.where(upper == 0, value, other), jnp.where(upper == 0, other, value)], axis=0
        )
    return value


def ring_pieces(piece):
    own = [piece]
    for _ in range(lax.axis_size("dp") - 1):
        own.append(ring(own[-1], "dp"))
    table = []
    for arrived in own:
        row = [arrived]
        for _ in range(lax.axis_size("context") - 1):
            row.append(ring(row[-1], "context"))
        table.append(row)
    return table


def place_kernel(count, widths, index_ref, *refs):
    pieces, outs = refs[:count], refs[count:]
    for i in range(count):
        at = 0
        for out, width in zip(outs, widths):
            out[index_ref[i]] = pieces[i][:, at : at + width]
            at += width


def placed(table, widths):
    dp, context = lax.axis_size("dp"), lax.axis_size("context")
    z, x = lax.axis_index("dp"), lax.axis_index("context")
    pieces, index = [], []
    for k, row in enumerate(table):
        for j, piece in enumerate(row):
            pieces.append(piece)
            index.append(((z + k) % dp) * context + (x + j) % context)
    count, rows = len(pieces), pieces[0].shape[0]
    outs = pl.pallas_call(
        functools.partial(place_kernel, count, widths),
        grid_spec=pltpu.PrefetchScalarGridSpec(
            num_scalar_prefetch=1,
            grid=(1,),
            in_specs=[pl.BlockSpec(piece.shape, lambda i, index: (0, 0)) for piece in pieces],
            out_specs=[
                pl.BlockSpec((count, rows, width), lambda i, index: (0, 0, 0)) for width in widths
            ],
        ),
        out_shape=[jax.ShapeDtypeStruct((count, rows, width), BF16) for width in widths],
        compiler_params=params(),
        cost_estimate=pl.CostEstimate(
            flops=0, transcendentals=0, bytes_accessed=4 * count * rows * sum(widths)
        ),
    )(jnp.stack(index).astype(jnp.int32), *pieces)
    return [out.reshape(count * rows, -1) for out in outs]


def ring_scatter(blocks):
    dp, context = lax.axis_size("dp"), lax.axis_size("context")
    z, x = lax.axis_index("dp"), lax.axis_index("context")

    def block(k, j):
        at = ((z + k) % dp) * context + (x + j) % context
        return lax.dynamic_index_in_dim(blocks, at, 0, keepdims=False)

    def over_context(k):
        total = None
        for j in range(1, context):
            part = block(k, j)
            if total is not None:
                part = (total + part.astype(F32)).astype(BF16)
            total = ring(part, "context").astype(F32)
        part = block(k, 0).astype(F32)
        return part if total is None else part + total

    total = None
    for k in list(range(1, dp)) + [0]:
        part = over_context(k)
        if total is not None:
            part = part + total
        if k:
            total = ring(part.astype(BF16), "dp").astype(F32)
        else:
            return part


def silu_parts(value):
    sig = jax.nn.sigmoid(value)
    return value * sig, sig


def softplus(value):
    return jnp.maximum(value, 0.0) + jnp.log1p(jnp.exp(-jnp.abs(value)))


def split_dot(value, table):
    high = value.astype(BF16)
    low = (value - high.astype(F32)).astype(BF16)
    return mm(high, table) + mm(low, table)


def wide_mm(a, b, dims=NN):
    a_high, b_high = a.astype(BF16), b.astype(BF16)
    a_low = (a - a_high.astype(F32)).astype(BF16)
    b_low = (b - b_high.astype(F32)).astype(BF16)
    return mm(a_high, b_high, dims) + (mm(a_low, b_high, dims) + mm(a_high, b_low, dims))


def fmm(a, b, dims=NN):
    return wide_mm(a, b, dims) if FWD_WIDE else mm(a.astype(BF16), b.astype(BF16), dims)


def bmm(a, b, dims=NN):
    return wide_mm(a, b, dims) if BWD_WIDE else mm(a.astype(BF16), b.astype(BF16), dims)


def iota(axis):
    return lax.broadcasted_iota(jnp.int32, (CHUNK, CHUNK), axis)


def rounded(value):
    return value.astype(BF16).astype(F32)


def head_halves(tile, lower):
    zero = jnp.zeros_like(tile)
    return jnp.concatenate([jnp.where(lower, tile, zero), jnp.where(lower, zero, tile)], axis=0)


def column_of(rows):
    pad = jnp.zeros((CHUNK - rows.shape[0], CHUNK), F32)
    return jnp.concatenate([rows, pad], axis=0).T


def scan_forward_kernel(
    heads, width, p_ref, rim_ref, aux_ref, segr_ref, cw_ref, hp_ref, skip_ref, exp_ref,
    z_ref, y_ref, st_ref, end_ref, gr_ref, vbuf, state, offset,
):
    chunk = pl.program_id(0)

    @pl.when(chunk == 0)
    def _():
        vbuf[0:8] = rim_ref[...].astype(F32)
        state[...] = jnp.zeros_like(state)
        offset[...] = jnp.zeros_like(offset)

    @pl.when(chunk > 0)
    def _():
        vbuf[0:8] = vbuf[CHUNK : CHUNK + 8]

    vbuf[8:, :width] = rounded(p_ref[:, :width])
    vbuf[8:, width:] = rounded(p_ref[:, width + LANES :])
    z = cw_ref[4:5] + cw_ref[3:4] * vbuf[8:]
    for k in range(3):
        z = z + cw_ref[k : k + 1] * vbuf[5 + k : 5 + k + CHUNK] * aux_ref[:, k : k + 1]
    z_ref[...] = z
    act = z * jax.nn.sigmoid(z)
    x = act[:, :width]
    b_val, c_val = act[:, width : width + LANES], act[:, width + LANES :]
    lane = iota(1)
    step = jnp.where(
        lane < heads, softplus(p_ref[:, width : width + LANES] + hp_ref[0:1]), 0.0
    )
    decay = hp_ref[1:2] * step
    cum = lax.dot_general(
        (iota(0) >= iota(1)).astype(F32), decay, NN, precision=HIGH, preferred_element_type=F32
    )
    cum_t = cum.T
    seg_col = aux_ref[:, 5:6]
    link = jnp.where((seg_col == segr_ref[0]) & (iota(0) >= iota(1)), 0.0, NO_LINK)
    scores = fmm(c_val, b_val, NT)
    growth = jnp.exp(cum) * aux_ref[:, 3:4]
    last = cum[CHUNK - 1 : CHUNK]
    weight = jnp.exp(last - cum) * (seg_col == seg_col[CHUNK - 1 : CHUNK]).astype(F32)
    wide = split_dot(jnp.concatenate([step, growth, weight], axis=0), exp_ref[...])
    step_e, growth_e, weight_e = wide[:CHUNK], wide[CHUNK : 2 * CHUNK], wide[2 * CHUNK :]
    xd = x * step_e
    lower = lane < LANES // 2
    pieces = []
    for pair in range(heads // 2):
        mats = []
        for head in (2 * pair, 2 * pair + 1):
            spread = cum[:, head : head + 1] - cum_t[head : head + 1, :]
            mats.append(jnp.exp(spread + link) * scores)
        tile = xd[:, pair * LANES : (pair + 1) * LANES]
        pieces.append(fmm(jnp.concatenate(mats, axis=1), head_halves(tile, lower)))
    held = state[...]
    st_ref[0] = held
    carried = fmm(c_val, held) * growth_e
    y_ref[...] = jnp.concatenate(pieces, axis=1) + carried + skip_ref[...] * x
    new = held * growth_e[CHUNK - 1 : CHUNK] + fmm(b_val, xd * weight_e, TN)
    state[...] = new
    end_ref[...] = new
    gr_ref[...] = jnp.exp(offset[...] + cum) * aux_ref[:, 4:5]
    offset[...] = offset[...] + last


def row_spec(width, at=None, rows=CHUNK):
    if at is None:
        return pl.BlockSpec((rows, width), lambda i: (i, 0))
    return pl.BlockSpec((rows, width), lambda i: (i, at))


def whole(shape):
    return pl.BlockSpec(shape, lambda i: (0,) * len(shape))


def scan_forward(proj, rim, aux, seg_rows, consts):
    length, total = proj.shape
    heads, width = consts["heads"], consts["width"]
    chunks, conv = length // CHUNK, total - LANES
    return pl.pallas_call(
        functools.partial(scan_forward_kernel, heads, width),
        grid=(chunks,),
        in_specs=[
            row_spec(total),
            whole((8, conv)),
            row_spec(8),
            pl.BlockSpec((1, 1, CHUNK), lambda i: (i, 0, 0)),
            whole((8, conv)),
            whole((8, LANES)),
            whole((1, width)),
            whole((LANES, width)),
        ],
        out_specs=[
            row_spec(conv),
            row_spec(width),
            pl.BlockSpec((1, LANES, width), lambda i: (i, 0, 0)),
            whole((LANES, width)),
            row_spec(LANES),
        ],
        out_shape=[
            jax.ShapeDtypeStruct((length, conv), F32),
            jax.ShapeDtypeStruct((length, width), F32),
            jax.ShapeDtypeStruct((chunks, LANES, width), F32),
            jax.ShapeDtypeStruct((LANES, width), F32),
            jax.ShapeDtypeStruct((length, LANES), F32),
        ],
        scratch_shapes=[
            pltpu.VMEM((CHUNK + 8, conv), F32),
            pltpu.VMEM((LANES, width), F32),
            pltpu.VMEM((1, LANES), F32),
        ],
        compiler_params=params(),
        cost_estimate=pl.CostEstimate(
            flops=chunks * 400_000_000, transcendentals=0, bytes_accessed=12_000_000
        ),
    )(proj, rim, aux, seg_rows, consts["cw"], consts["hp"], consts["skip"], consts["exp"])


def mix_forward_kernel(y0_ref, zc_ref, gr_ref, sin_ref, gate_ref, exp_ref, y_ref, sq_ref):
    c_val = zc_ref[...] * jax.nn.sigmoid(zc_ref[...])
    carried = fmm(c_val, sin_ref[...].astype(F32))
    y = y0_ref[...] + carried * split_dot(gr_ref[...], exp_ref[...])
    y_ref[...] = y
    gate = gate_ref[...]
    gated = y * (gate * jax.nn.sigmoid(gate))
    square = jnp.sum(gated * gated, axis=1, keepdims=True)
    sq_ref[...] = jnp.broadcast_to(square, (CHUNK, CHUNK)).T[:8]


def mix_forward(y0, z, growth, carried, gate, consts):
    length, width = y0.shape
    last = z.shape[1] // LANES - 1
    return pl.pallas_call(
        mix_forward_kernel,
        grid=(length // CHUNK,),
        in_specs=[
            row_spec(width),
            row_spec(LANES, last),
            row_spec(LANES),
            whole((LANES, width)),
            row_spec(width),
            whole((LANES, width)),
        ],
        out_specs=[row_spec(width), pl.BlockSpec((8, CHUNK), lambda i: (0, i))],
        out_shape=[
            jax.ShapeDtypeStruct((length, width), F32),
            jax.ShapeDtypeStruct((8, length), F32),
        ],
        compiler_params=params(),
        cost_estimate=pl.CostEstimate(
            flops=1_000_000_000, transcendentals=0, bytes_accessed=6_000_000
        ),
    )(y0, z, growth, carried, gate, consts["exp"])


def project_out_kernel(channels, y_ref, gate_ref, sq_ref, gain_ref, w_ref, out_ref):
    scale = lax.rsqrt(column_of(sq_ref[...])[:, 0:1] / channels + eps)
    gate = gate_ref[...]
    gated = y_ref[...] * (gate * jax.nn.sigmoid(gate))
    scaled = (gated * scale * gain_ref[...]).astype(BF16)
    out_ref[...] = mm(scaled, w_ref[...], NT).astype(out_ref.dtype)


def project_out(y, gate, squares, channels, kind, consts):
    length, width = y.shape
    model = consts["out"].shape[0]
    return pl.pallas_call(
        functools.partial(project_out_kernel, float(channels)),
        grid=(length // CHUNK,),
        in_specs=[
            row_spec(width),
            row_spec(width),
            pl.BlockSpec((8, CHUNK), lambda i: (0, i)),
            whole((1, width)),
            whole((model, width)),
        ],
        out_specs=row_spec(model),
        out_shape=jax.ShapeDtypeStruct((length, model), kind),
        compiler_params=params(),
        cost_estimate=pl.CostEstimate(
            flops=4 * length * width * model, transcendentals=0, bytes_accessed=9_000_000
        ),
    )(y, gate, squares, consts["gain"], consts["out"])


def grad_scaled_kernel(g_ref, w_ref, y_ref, gate_ref, gain_ref, gs_ref, dot_ref):
    grad = mm(g_ref[...], w_ref[...])
    gs_ref[...] = grad
    gate = gate_ref[...]
    gated = y_ref[...] * (gate * jax.nn.sigmoid(gate))
    product = jnp.sum(grad * gain_ref[...] * gated, axis=1, keepdims=True)
    dot_ref[...] = jnp.broadcast_to(product, (CHUNK, CHUNK)).T[:8]


def grad_scaled(grad_low, y, gate, consts):
    length, width = y.shape
    model = consts["out"].shape[0]
    return pl.pallas_call(
        grad_scaled_kernel,
        grid=(length // CHUNK,),
        in_specs=[
            row_spec(model),
            whole((model, width)),
            row_spec(width),
            row_spec(width),
            whole((1, width)),
        ],
        out_specs=[row_spec(width), pl.BlockSpec((8, CHUNK), lambda i: (0, i))],
        out_shape=[
            jax.ShapeDtypeStruct((length, width), F32),
            jax.ShapeDtypeStruct((8, length), F32),
        ],
        compiler_params=params(),
        cost_estimate=pl.CostEstimate(
            flops=4 * length * width * model, transcendentals=0, bytes_accessed=9_000_000
        ),
    )(grad_low, consts["out"], y, gate, consts["gain"])


def mix_backward_kernel(
    channels, gs_ref, y_ref, gate_ref, zx_ref, zc_ref, gr_ref, sq_ref, dot_ref, gain_ref, exp_ref,
    scaled_ref, dgate_ref, dy_ref, acc_ref, dsin_ref,
):
    @pl.when(pl.program_id(0) == 0)
    def _():
        acc_ref[...] = jnp.zeros_like(acc_ref)
        dsin_ref[...] = jnp.zeros_like(dsin_ref)

    stats = column_of(jnp.concatenate([sq_ref[...], dot_ref[...]], axis=0))
    scale = lax.rsqrt(stats[:, 0:1] / channels + eps)
    pull = scale * scale * scale * stats[:, 8:9] / channels
    grad, y, gate = gs_ref[...], y_ref[...], gate_ref[...]
    silu, sig = silu_parts(gate)
    gated = y * silu
    unit = gated * scale
    scaled_ref[...] = (unit * gain_ref[...]).astype(BF16)
    dgated = grad * gain_ref[...] * scale - gated * pull
    dy = dgated * silu
    dy_ref[...] = dy
    dgate_ref[...] = (dgated * y * (sig * (1.0 + gate * (1.0 - sig)))).astype(BF16)
    x = zx_ref[...] * jax.nn.sigmoid(zx_ref[...])
    acc_ref[0:1] += jnp.sum(grad * unit, axis=0, keepdims=True)
    acc_ref[1:2] += jnp.sum(dy * x, axis=0, keepdims=True)
    c_low = (zc_ref[...] * jax.nn.sigmoid(zc_ref[...])).astype(BF16)
    dsin_ref[...] += mm(c_low, (dy * split_dot(gr_ref[...], exp_ref[...])).astype(BF16), TN)


def mix_backward(grad, y, gate, z, growth, squares, dots, channels, consts):
    length, width = y.shape
    last = z.shape[1] // LANES - 1
    stat = pl.BlockSpec((8, CHUNK), lambda i: (0, i))
    return pl.pallas_call(
        functools.partial(mix_backward_kernel, float(channels)),
        grid=(length // CHUNK,),
        in_specs=[
            row_spec(width),
            row_spec(width),
            row_spec(width),
            row_spec(width),
            row_spec(LANES, last),
            row_spec(LANES),
            stat,
            stat,
            whole((1, width)),
            whole((LANES, width)),
        ],
        out_specs=[
            row_spec(width),
            row_spec(width),
            row_spec(width),
            whole((8, width)),
            whole((LANES, width)),
        ],
        out_shape=[
            jax.ShapeDtypeStruct((length, width), BF16),
            jax.ShapeDtypeStruct((length, width), BF16),
            jax.ShapeDtypeStruct((length, width), F32),
            jax.ShapeDtypeStruct((8, width), F32),
            jax.ShapeDtypeStruct((LANES, width), F32),
        ],
        compiler_params=params(),
        cost_estimate=pl.CostEstimate(
            flops=1_000_000_000, transcendentals=0, bytes_accessed=12_000_000
        ),
    )(grad, y, gate, z, z, growth, squares, dots, consts["gain"], consts["exp"])


def scan_backward_kernel(
    heads, width, chunks, dy_ref, z_ref, p_ref, before_ref, rim_ref, aux_ref, segr_ref, cw_ref,
    hp_ref, skip_ref, exp_ref, red_ref, st_ref, sin_ref, grprev_ref, dend_ref,
    dproj_ref, wacc_ref, hacc_ref, tail_ref, drim_ref, vbuf, zbuf, dstate,
):
    step_at = pl.program_id(0)
    chunk = chunks - 1 - step_at

    @pl.when(step_at == 0)
    def _():
        dstate[...] = dend_ref[...].astype(F32)
        zbuf[...] = jnp.zeros_like(zbuf)
        wacc_ref[...] = jnp.zeros_like(wacc_ref)
        hacc_ref[...] = jnp.zeros_like(hacc_ref)

    @pl.when(chunk == 0)
    def _():
        vbuf[0:8] = rim_ref[...].astype(F32)

    @pl.when(chunk > 0)
    def _():
        vbuf[0:8, :width] = rounded(before_ref[:, :width])
        vbuf[0:8, width:] = rounded(before_ref[:, width + LANES :])

    vbuf[8:, :width] = rounded(p_ref[:, :width])
    vbuf[8:, width:] = rounded(p_ref[:, width + LANES :])

    z = z_ref[...]
    act, sig = silu_parts(z)
    slope = sig * (1.0 + z * (1.0 - sig))
    x = act[:, :width]
    b_val, c_val = act[:, width : width + LANES], act[:, width + LANES :]
    lane = iota(1)
    pre = p_ref[:, width : width + LANES] + hp_ref[0:1]
    step = jnp.where(lane < heads, softplus(pre), 0.0)
    decay = hp_ref[1:2] * step
    cum = lax.dot_general(
        (iota(0) >= iota(1)).astype(F32), decay, NN, precision=HIGH, preferred_element_type=F32
    )
    cum_t = cum.T
    seg_col = aux_ref[:, 5:6]
    link = jnp.where((seg_col == segr_ref[0]) & (iota(0) <= iota(1)), 0.0, NO_LINK)
    growth = jnp.exp(cum) * aux_ref[:, 3:4]
    last = cum[CHUNK - 1 : CHUNK]
    weight = jnp.exp(last - cum) * (seg_col == seg_col[CHUNK - 1 : CHUNK]).astype(F32)
    reach = jnp.where(chunk == 0, 1.0, grprev_ref[7:8])
    wide = split_dot(
        jnp.concatenate([step, growth, weight, jnp.broadcast_to(reach, (8, LANES))], axis=0),
        exp_ref[...],
    )
    step_e, growth_e = wide[:CHUNK], wide[CHUNK : 2 * CHUNK]
    weight_e, reach_e = wide[2 * CHUNK : 3 * CHUNK], wide[3 * CHUNK : 3 * CHUNK + 1]
    held = st_ref[0] + sin_ref[...].astype(F32) * reach_e
    after = dstate[...]
    xd = x * step_e
    dy = dy_ref[...]
    scores = bmm(b_val, c_val, NT)
    carried = bmm(c_val, held) * growth_e
    fed = bmm(b_val, after) * weight_e
    dy_grown = dy * growth_e
    lower = lane < LANES // 2
    dscores = jnp.zeros((CHUNK, CHUNK), F32)
    into = jnp.zeros((CHUNK, CHUNK), F32)
    rows, pieces = [], []
    for pair in range(heads // 2):
        at = slice(pair * LANES, (pair + 1) * LANES)
        products = bmm(head_halves(xd[:, at], lower), dy[:, at], NT)
        mats = []
        for side, head in enumerate((2 * pair, 2 * pair + 1)):
            spread = cum_t[head : head + 1, :] - cum[:, head : head + 1]
            reachable = jnp.exp(spread + link)
            product = products[side * CHUNK : (side + 1) * CHUNK]
            mat = reachable * scores
            dscores = dscores + reachable * product
            energy = mat * product
            rows.append(jnp.sum(energy, axis=0, keepdims=True))
            into = jnp.where(lane == head, jnp.sum(energy, axis=1, keepdims=True), into)
            mats.append(mat)
        pieces.append(bmm(jnp.concatenate(mats, axis=1), head_halves(dy[:, at], lower)))
    dxd = jnp.concatenate(pieces, axis=1) + fed
    kept = jnp.sum(after * held, axis=0, keepdims=True) * growth_e[CHUNK - 1 : CHUNK]
    sums = split_dot(
        jnp.concatenate(
            [dy * carried, xd * fed, dxd * x, jnp.broadcast_to(kept, (8, width))], axis=0
        ),
        red_ref[...],
    )
    out_of, fed_sum = sums[:CHUNK], sums[CHUNK : 2 * CHUNK]
    dstep, kept_sum = sums[2 * CHUNK : 3 * CHUNK], sums[3 * CHUNK : 3 * CHUNK + 1]
    rows = column_of(jnp.concatenate(rows, axis=0))
    dcum = rows - into + out_of - fed_sum
    end_term = kept_sum + jnp.sum(fed_sum, axis=0, keepdims=True)
    ddecay = (
        lax.dot_general(
            (iota(0) <= iota(1)).astype(F32), dcum, NN, precision=HIGH, preferred_element_type=F32
        )
        + end_term
    )
    ddecay = jnp.where(lane < heads, ddecay, 0.0)
    dpre = jnp.where(lane < heads, (dstep + hp_ref[1:2] * ddecay) * jax.nn.sigmoid(pre), 0.0)
    hacc_ref[0:1] += jnp.sum(dpre, axis=0, keepdims=True)
    hacc_ref[1:2] += jnp.sum(ddecay * decay, axis=0, keepdims=True)
    dx = dxd * step_e + skip_ref[...] * dy
    db = wide_mm(dscores, c_val) + wide_mm(xd * weight_e, after, NT)
    dc = wide_mm(dscores, b_val, TN) + wide_mm(dy_grown, held, NT)
    dstate[...] = after * growth_e[CHUNK - 1 : CHUNK] + bmm(c_val, dy_grown, TN)

    dz = jnp.concatenate([dx, db, dc], axis=1) * slope
    wacc_ref[3:4] += jnp.sum(dz * vbuf[8:], axis=0, keepdims=True)
    wacc_ref[4:5] += jnp.sum(dz, axis=0, keepdims=True)
    dv = cw_ref[3:4] * dz
    for k in range(3):
        masked = dz * aux_ref[:, k : k + 1]
        wacc_ref[k : k + 1] += jnp.sum(
            masked * vbuf[5 + k : 5 + k + CHUNK], axis=0, keepdims=True
        )
        zbuf[k, 8 : 8 + CHUNK] = masked
        dv = dv + cw_ref[k : k + 1] * zbuf[k, 11 - k : 11 - k + CHUNK]
    dproj_ref[:, :width] = dv[:, :width].astype(BF16)
    dproj_ref[:, width : width + LANES] = dpre.astype(BF16)
    dproj_ref[:, width + LANES :] = dv[:, width:].astype(BF16)

    @pl.when(step_at == 0)
    def _():
        tail_ref[...] = dv[CHUNK - 8 :]

    @pl.when(chunk == 0)
    def _():
        drim = cw_ref[0:1] * zbuf[0, 3:11]
        for k in (1, 2):
            drim = drim + cw_ref[k : k + 1] * zbuf[k, 3 - k : 11 - k]
        drim_ref[...] = drim

    for k in range(3):
        zbuf[k, 8 + CHUNK :] = zbuf[k, 8:16]


def scan_backward(dy, z, proj, rim, aux, seg_rows, states, carried, growth, dend, consts):
    length, total = proj.shape
    heads, width = consts["heads"], consts["width"]
    chunks, conv = length // CHUNK, total - LANES
    eights = CHUNK // 8

    def back(columns):
        return pl.BlockSpec((CHUNK, columns), lambda i: (chunks - 1 - i, 0))

    def previous(columns):
        return pl.BlockSpec(
            (8, columns), lambda i: (jnp.maximum((chunks - 1 - i) * eights - 1, 0), 0)
        )

    return pl.pallas_call(
        functools.partial(scan_backward_kernel, heads, width, chunks),
        grid=(chunks,),
        in_specs=[
            back(width),
            back(conv),
            back(total),
            previous(total),
            whole((8, conv)),
            back(8),
            pl.BlockSpec((1, 1, CHUNK), lambda i: (chunks - 1 - i, 0, 0)),
            whole((8, conv)),
            whole((8, LANES)),
            whole((1, width)),
            whole((LANES, width)),
            whole((width, LANES)),
            pl.BlockSpec((1, LANES, width), lambda i: (chunks - 1 - i, 0, 0)),
            whole((LANES, width)),
            previous(LANES),
            whole((LANES, width)),
        ],
        out_specs=[
            back(total),
            whole((8, conv)),
            whole((8, LANES)),
            whole((8, conv)),
            whole((8, conv)),
        ],
        out_shape=[
            jax.ShapeDtypeStruct((length, total), BF16),
            jax.ShapeDtypeStruct((8, conv), F32),
            jax.ShapeDtypeStruct((8, LANES), F32),
            jax.ShapeDtypeStruct((8, conv), F32),
            jax.ShapeDtypeStruct((8, conv), F32),
        ],
        scratch_shapes=[
            pltpu.VMEM((CHUNK + 8, conv), F32),
            pltpu.VMEM((3, CHUNK + 16, conv), F32),
            pltpu.VMEM((LANES, width), F32),
        ],
        compiler_params=params(),
        cost_estimate=pl.CostEstimate(
            flops=chunks * 1_500_000_000, transcendentals=0, bytes_accessed=16_000_000
        ),
    )(
        dy, z, proj, proj, rim, aux, seg_rows, consts["cw"], consts["hp"], consts["skip"],
        consts["exp"], consts["red"], states, carried, growth, dend,
    )


def local(
    stream,
    seg_ids,
    input_weight,
    step_size_weight,
    coefficient_weight,
    pre_gain,
    conv_bc,
    bias_bc,
    output_weight,
    conv_x,
    bias_x,
    dt_bias,
    a_log,
    skip,
    gate_gain,
    cotangent,
):
    layers, rows_in, _, width = input_weight.shape
    sequences, length, model = stream.shape
    heads = dt_bias.shape[1]
    depth = width // heads
    shared = coefficient_weight.shape[2]
    dp, context, tensor = (lax.axis_size(a) for a in ("dp", "context", "tensor"))
    channels = width * tensor
    rows_bc = rows_in // tensor
    bc_part = shared // tensor
    conv = width + shared
    layer_range, seq_range = range(layers), range(sequences)

    def first_piece(layer):
        tile = jnp.concatenate(
            [
                step_size_weight[layer],
                jnp.zeros((rows_in, LANES - heads - bc_part), BF16),
                coefficient_weight[layer].reshape(rows_in, bc_part),
            ],
            axis=1,
        )
        return jnp.concatenate([input_weight[layer, :, 1], tile], axis=1)

    def second_piece(layer):
        return jnp.concatenate([input_weight[layer, :, 0], output_weight[layer].T], axis=1)

    def full_bc(first):
        part = first[:, width + LANES - bc_part :].reshape(dp * context, rows_bc, shared)
        every = gather_small(part, ("tensor",))
        return jnp.moveaxis(every, 0, 1).reshape(model, shared)

    small = jnp.concatenate(
        [pre_gain, conv_bc.reshape(layers, -1), bias_bc], axis=1
    )
    small = gather_small(small, ("tensor", "context", "dp"))
    own_gain, own_conv = pre_gain.shape[1], conv_bc.shape[2]
    gains = jnp.moveaxis(small[:, :, :own_gain], 0, 1).reshape(layers, model).astype(F32)
    conv_all = small[:, :, own_gain : own_gain + 4 * own_conv].reshape(-1, layers, 4, own_conv)
    conv_all = jnp.moveaxis(conv_all, 0, 2).reshape(layers, 4, shared).astype(F32)
    bias_all = jnp.moveaxis(small[:, :, own_gain + 4 * own_conv :], 0, 1)
    bias_all = bias_all.reshape(layers, shared).astype(F32)

    edge_ids = shifted(seg_ids[:, -3:], "context", 1)
    ext_ids = jnp.concatenate([edge_ids, seg_ids], axis=1)
    prior = ext_ids[:, 2 : 2 + length].reshape(sequences, length // CHUNK, CHUNK)[:, :, 0]
    prior = jnp.repeat(prior, CHUNK, axis=1)
    aux_all = jnp.stack(
        [ext_ids[:, k : k + length] == seg_ids for k in range(3)]
        + [seg_ids == prior, seg_ids == edge_ids[:, 2:3], seg_ids, seg_ids, seg_ids],
        axis=2,
    ).astype(F32)
    seg_rows = seg_ids.astype(F32).reshape(sequences, length // CHUNK, 1, CHUNK)

    spread_table = (jnp.arange(LANES)[:, None] == jnp.arange(width)[None, :] // depth).astype(BF16)

    first, second = [None] * layers, [None] * layers
    gate_on = None
    for layer in layer_range:
        piece = first_piece(layer)
        if gate_on is not None:
            piece, gate_on = lax.optimization_barrier((piece, gate_on))
        table = ring_pieces(piece)
        (first[layer],) = placed(table, [width + LANES])
        gate_on = table[-1][0]
        piece, gate_on = lax.optimization_barrier((second_piece(layer), gate_on))
        table = ring_pieces(piece)
        second[layer] = placed(table, [width, width])
        gate_on = table[-1][0]

    consts = []
    for layer in layer_range:
        cw = jnp.concatenate(
            [
                jnp.concatenate([conv_x[layer], conv_all[layer]], axis=1),
                jnp.concatenate([bias_x[layer], bias_all[layer]])[None],
                jnp.zeros((3, conv), F32),
            ],
            axis=0,
        )
        pad = jnp.zeros((LANES - heads,), F32)
        hp = jnp.stack(
            [
                jnp.concatenate([dt_bias[layer], pad]),
                jnp.concatenate([-jnp.exp(a_log[layer]), pad]),
            ]
            + [jnp.zeros((LANES,), F32)] * 6
        )
        consts.append(
            {
                "heads": heads,
                "width": width,
                "cw": cw,
                "hp": hp,
                "skip": jnp.repeat(skip[layer], depth)[None],
                "gain": gate_gain[layer][None],
                "exp": spread_table,
                "red": spread_table.T,
                "front": jnp.concatenate([first[layer], full_bc(first[layer])], axis=1),
                "gate": second[layer][0],
                "out": second[layer][1],
            }
        )

    def chain(value, total, steps, kind):
        carried = shifted(value.astype(kind), "context", steps)
        for _ in range(context - 2):
            whole_value = value + carried.astype(F32) * total
            carried = shifted(whole_value.astype(kind), "context", steps)
        return carried

    def through(growth):
        return jnp.repeat(growth[length - 1, :heads], depth)[None]

    kept = [[None] * sequences for _ in layer_range]
    streams = [own_rows(stream[s]).astype(F32) for s in seq_range]
    normed = []
    for s in seq_range:
        wide = stream[s].astype(F32)
        scale = lax.rsqrt(jnp.mean(wide * wide, axis=-1, keepdims=True) + eps)
        normed.append((wide * scale * gains[0]).astype(BF16))
    finals = []
    for layer in layer_range:
        const = consts[layer]
        nexts = []
        for s in seq_range:
            proj = mm(normed[s], const["front"])
            gate = mm(normed[s], const["gate"])
            rim = shifted(
                jnp.concatenate(
                    [proj[length - 8 :, :width], proj[length - 8 :, width + LANES :]], axis=1
                ).astype(BF16),
                "context",
                1,
            )
            z, y0, states, end, growth = scan_forward(proj, rim, aux_all[s], seg_rows[s], const)
            carried = chain(end, through(growth), 1, FSTATE)
            y, squares = mix_forward(y0, z, growth, carried, gate, const)
            squares = summed_over(squares, ("tensor",))
            kind = F32 if layer + 1 < layers else BF16
            partial = project_out(y, gate, squares, channels, kind, const)
            current = streams[s] + scatter_rows(partial)
            kept[layer][s] = {
                "normed": normed[s], "proj": proj, "gate": gate, "rim": rim, "z": z, "y": y,
                "states": states, "growth": growth, "carried": carried, "squares": squares,
                "stream": streams[s],
            }
            streams[s] = current
            if layer + 1 < layers:
                scale = lax.rsqrt(jnp.mean(current * current, axis=-1, keepdims=True) + eps)
                nexts.append(gather_rows((current * scale * gains[layer + 1]).astype(BF16)))
            else:
                finals.append(gather_rows(current.astype(BF16)))
        normed = nexts
    layer_out = jnp.stack(finals)

    grad_low = [cotangent[s] for s in seq_range]
    grads = [own_rows(cotangent[s]).astype(F32) for s in seq_range]
    out = [None] * layers
    small_local, small_shared = [], []
    for layer in reversed(layer_range):
        const = consts[layer]
        held = kept[layer]
        nexts, back = [], []
        gain_sum = 0.0
        for s in seq_range:
            k = held[s]
            grad, dots = grad_scaled(grad_low[s], k["y"], k["gate"], const)
            dots = summed_over(dots, ("tensor",))
            scaled, dgate, dy, acc, dsin = mix_backward(
                grad, k["y"], k["gate"], k["z"], k["growth"], k["squares"], dots, channels, const
            )
            dend = chain(dsin, through(k["growth"]), -1, BF16)
            dproj, wacc, hacc, tail, drim = scan_backward(
                dy, k["z"], k["proj"], k["rim"], aux_all[s], seg_rows[s], k["states"],
                k["carried"], k["growth"], dend, const,
            )
            fixed = (tail + shifted(drim, "context", -1)).astype(BF16)
            dproj = lax.dynamic_update_slice(dproj, fixed[:, :width], (length - 8, 0))
            dproj = lax.dynamic_update_slice(dproj, fixed[:, width:], (length - 8, width + LANES))
            partial = mm(dproj, const["front"], NT) + mm(dgate, const["gate"], NT)
            total = scatter_rows(partial.astype(BF16))
            current = k["stream"]
            scale = lax.rsqrt(jnp.mean(current * current, axis=-1, keepdims=True) + eps)
            unit = current * scale
            gain_sum = gain_sum + jnp.sum(total * unit, axis=0)
            pulled = total * gains[layer]
            shift = jnp.mean(pulled * unit, axis=-1, keepdims=True)
            grads[s] = grads[s] + scale * (pulled - unit * shift)
            nexts.append(gather_rows(grads[s].astype(BF16)))
            back.append((scaled, dgate, dproj, acc, wacc, hacc))

        def over_tokens(left, right):
            return sum(mm(a, b, TN) for a, b in zip(left, right))

        normed_all = [k["normed"] for k in held]
        front_grad = over_tokens(normed_all, [b[2] for b in back])
        gate_grad = over_tokens(normed_all, [b[1] for b in back]).astype(BF16)
        out_grad = over_tokens(grad_low, [b[0] for b in back]).astype(BF16)
        second_sum = ring_scatter(
            jnp.concatenate([gate_grad, out_grad], axis=1).reshape(dp * context, rows_in, -1)
        )
        bc_grad = front_grad[:, width + LANES :].reshape(dp * context, tensor, rows_bc * shared)
        bc_grad = scatter_rows_of_tensor(bc_grad)
        bc_grad = bc_grad.reshape(model, bc_part).astype(BF16)
        first_blocks = jnp.concatenate(
            [front_grad[:, : width + LANES - bc_part].astype(BF16), bc_grad], axis=1
        )
        first_sum = ring_scatter(first_blocks.reshape(dp * context, rows_in, -1))
        out[layer] = (
            jnp.stack([second_sum[:, :width], first_sum[:, :width]], axis=1),
            first_sum[:, width : width + heads],
            first_sum[:, width + LANES - bc_part :].reshape(rows_bc, shared),
            second_sum[:, width:].T,
        )
        acc, wacc, hacc = (sum(b[i] for b in back) for i in (3, 4, 5))
        small_local.append(
            jnp.concatenate(
                [
                    wacc[:5, :width].reshape(-1),
                    acc[0],
                    acc[1].reshape(heads, depth).sum(axis=1),
                    hacc[0, :heads],
                    hacc[1, :heads],
                ]
            )
        )
        small_shared.append(jnp.concatenate([wacc[:5, width:].reshape(-1), gain_sum]))
        grad_low = nexts
    grad_stream = jnp.stack(grad_low)

    shared_sum = summed_over(jnp.stack(small_shared[::-1]), ("tensor",))
    local_sum = jnp.stack(small_local[::-1])
    cut = local_sum.shape[1]
    both = summed_over(
        jnp.concatenate([local_sum, shared_sum], axis=1), ("context", "dp")
    )
    local_sum, shared_sum = both[:, :cut], both[:, cut:]
    place = (lax.axis_index("dp") * context + lax.axis_index("context")) * tensor
    place = place + lax.axis_index("tensor")
    taps = shared_sum[:, : 5 * shared].reshape(layers, 5, shared)
    taps = lax.dynamic_slice_in_dim(taps, place * own_conv, own_conv, 2)
    grad_gain = lax.dynamic_slice_in_dim(
        shared_sum[:, 5 * shared :], place * own_gain, own_gain, 1
    )
    taps_x = local_sum[:, : 5 * width].reshape(layers, 5, width)
    heads_at = 6 * width
    return (
        layer_out,
        grad_stream,
        jnp.stack([o[0] for o in out]),
        jnp.stack([o[1] for o in out]),
        jnp.stack([o[2] for o in out]),
        grad_gain,
        taps[:, :4],
        taps[:, 4],
        jnp.stack([o[3] for o in out]),
        taps_x[:, :4],
        taps_x[:, 4],
        local_sum[:, heads_at + heads : heads_at + 2 * heads],
        local_sum[:, heads_at + 2 * heads : heads_at + 3 * heads],
        local_sum[:, heads_at : heads_at + heads],
        local_sum[:, 5 * width : 6 * width],
    )


def scatter_rows_of_tensor(value):
    index = lax.axis_index("tensor")
    blocks, _, n = value.shape
    for bit in range(bits("tensor")):
        mine = (index >> bit) & 1
        value = value.reshape(blocks, -1, 2, n)
        sent = lax.dynamic_index_in_dim(value, 1 - mine, 2, keepdims=False).astype(BF16)
        kept = lax.dynamic_index_in_dim(value, mine, 2, keepdims=False).astype(F32)
        value = kept + flipped(sent, "tensor", bit).astype(F32)
    return value.reshape(blocks, n)


def solution(mesh):
    in_specs = (
        P("dp", "context", None),
        P("dp", "context"),
        P(None, ("dp", "context"), None, "tensor"),
        P(None, ("dp", "context"), "tensor"),
        P(None, ("dp", "context", "tensor"), None),
        P(None, ("dp", "context", "tensor")),
        P(None, None, ("dp", "context", "tensor")),
        P(None, ("dp", "context", "tensor")),
        P(None, "tensor", ("dp", "context")),
        P(None, None, "tensor"),
        P(None, "tensor"),
        P(None, "tensor"),
        P(None, "tensor"),
        P(None, "tensor"),
        P(None, "tensor"),
        P("dp", "context", None),
    )
    out_specs = (
        P("dp", "context", None),
        P("dp", "context", None),
        P(None, ("dp", "context"), None, "tensor"),
        P(None, ("dp", "context"), "tensor"),
        P(None, ("dp", "context", "tensor"), None),
        P(None, ("dp", "context", "tensor")),
        P(None, None, ("dp", "context", "tensor")),
        P(None, ("dp", "context", "tensor")),
        P(None, "tensor", ("dp", "context")),
        P(None, None, "tensor"),
        P(None, "tensor"),
        P(None, "tensor"),
        P(None, "tensor"),
        P(None, "tensor"),
        P(None, "tensor"),
        P("dp", "context", None),
    )
    return jax.shard_map(
        local, mesh=mesh, in_specs=in_specs, out_specs=out_specs[:15], check_vma=False
    )
```

time: 2320 us -> 1090 us (0.47)
  waiting for transfers between devices: 824 us -> 332 us
  blocking collectives: 410 us -> 0 us
  matrix products: 392 us -> 77.1 us
  Pallas kernels: 0 us -> 196 us
  local copies, waits for them, and re-layouts: 366 us -> 193 us
  other arithmetic: 279 us -> 108 us
  starting transfers between devices: 18.1 us -> 166 us
    reduce_scatter x6 -> x0, waiting for transfers between devices: 361 us -> none  [the longest x2 184 us: local(): lax.psum_scatter(grad_in_w.astype(jnp.bfloat16), ('dp', 'context'), scatt...]
    psum x3 -> x0, waiting for transfers between devices: 337 us -> none  [the longest x2 230 us: local(): branch_output = lax.psum(partial_out, 'tensor')]
    dot_general x78 -> x28, matrix products: 392 us -> 77.1 us  [mm(): return lax.dot_general(a, b, dims, preferred_element_type=F32)]
    all_gather x12 -> x0, blocking collectives: 268 us -> none  [the longest x2 85.5 us: fetch(): lax.all_gather(coefficient_weight[layer_pos], ('dp', 'context', 'tensor')...]
    ppermute x0 -> x122, waiting for transfers between devices: none -> 254 us  [the longest x56 151 us: ring(): lax.ppermute(value, axis, [(i, (i - 1) % count) for i in range(count)])]
    pallas_call x0 -> x28, Pallas kernels: none -> 196 us  [the longest x4 73.2 us: scan_backward(): pl.pallas_call(functools.partial(scan_backward_kernel, heads, width, chun...]
    all_gather x6 -> x0, waiting for transfers between devices: 122 us -> none  [the longest x2 69.4 us: fetch(): lax.all_gather(input_weight[layer_pos], ('dp', 'context'), axis=0, tiled=...]
    ppermute x0 -> x122, starting transfers between devices: none -> 120 us  [the longest x56 76.9 us: ring(): lax.ppermute(value, axis, [(i, (i - 1) % count) for i in range(count)])]
  transfers between devices with their start and end apart: 26 -> 139, of which waited for: 12 -> 57; matrix products, arithmetic and copies ran while one was open for 20% -> 29% of each run, Pallas kernels for 0% -> 16%
where the time goes in v1:
time: 1090 us; the launch traced here: 1080 us
  waiting for transfers between devices  332 us (30%)
  Pallas kernels  196 us (18%)
  local copies, waits for them, and re-layouts  193 us (18%)
  starting transfers between devices  166 us (15%)
  other arithmetic  108 us (10%)
  matrix products  77.1 us (7%)
    ppermute x56, waiting for transfers between devices, ring(): lax.ppermute(value, axis, [(i, (i - 1) % count) for i in range(count)])  151 us
    ppermute x66, waiting for transfers between devices, flipped(): return lax.ppermute(value, axis, [(i, i ^ 1 << bit) for i in range(count)])  102 us
    ppermute x17, waiting for transfers between devices, shifted(): lax.ppermute(value, axis, [(source, source + steps) for source in range(l...  78.3 us
    dot_general x28, matrix products, mm(): return lax.dot_general(a, b, dims, preferred_element_type=F32)  77.1 us
    ppermute x56, starting transfers between devices, ring(): lax.ppermute(value, axis, [(i, (i - 1) % count) for i in range(count)])  76.9 us
    pallas_call x4, Pallas kernels, scan_backward(): pl.pallas_call(functools.partial(scan_backward_kernel, heads, width, chun...  73.2 us
    unnamed x568, local copies, waits for them, and re-layouts  47.1 us
    ppermute x17, starting transfers between devices, shifted(): lax.ppermute(value, axis, [(source, source + steps) for source in range(l...  46.3 us
  transfers between devices with their start and end apart: 139, of which 57 were waited for; matrix products, arithmetic and copies ran while one was open for 29% of the time, Pallas kernels for 16%

profile of v1, /device:TPU:0, one launch (start us, length us, event | category | flops | bytes accessed | tf_op | source)
XLA Modules:
  0.0 1077.6 jit_solution(16501985453431775652)
XLA Ops:
  101.3 8.3 collective-permute-done.20.refs_4_
  137.0 38.4 %collective-permute-done.14.rim_ref = bf16[8,1024]{1,0:T(8,128)(2,1)S(1)} collective-permute-done((bf16[8,1024]{1,0:T(8,128)(2,1)S(1)}, bf16[8,1024]{1,0:T(8,128)(2,1)S(1)}, u32[]{:S(2)}, u32[]{:S(2)}) %collective-permute-start.14) | collective-permute-done | bytes 16416 | tf_op jit(solution)/shard_map/ppermute | solution.py:47
  175.5 9.4 shard_map.272
  216.6 10.1 collective-permute-done.31.refs_2_
  266.8 7.4 collective-permute-done.34.refs_5_
  285.1 9.6 shard_map.281
  347.0 9.6 shard_map.277
  364.2 8.8 collective-permute-done.45.refs_5_
  372.9 12.3 %collective-permute-done.47.refs_7_ = bf16[192,1536]{1,0:T(8,128)(2,1)S(1)} collective-permute-done((bf16[192,1536]{1,0:T(8,128)(2,1)S(1)}, bf16[192,1536]{1,0:T(8,128)(2,1)S(1)}, u32[]{:S(2)}, u32[]{:S(2)}) %collective-permute-start.47) | collective-permute-done | bytes 589856 | tf_op jit(solution)/shard_map/ppermute | solution.py:52
  419.1 18.1 %shard_map.289 = (bf16[512,1152]{1,0:T(8,128)(2,1)S(1)}, f32[8,1024]{1,0:T(8,128)S(1)}, f32[8,128]{1,0:T(8,128)S(1)}, f32[8,1024]{1,0:T(8,128)S(1)}, f32[8,1024]{1,0:T(8,128)S(1)}) custom-call(f32[512,768]{1,0:T(8,128)S(1)} %get-tuple-element.131.dy_ref, f32[512,1024]{1,0:T(8,128)} %get-tuple-element.109.zc_ref.zx_ref.z_ref, ...), custom_call_target="tpu_custom_call" | custom-call | flops 6000000000 | bytes 16000000 | tf_op jit(solution)/shard_map/pallas_call | solution.py:669
  457.7 9.5 collective-permute-done.75
  482.0 7.7 collective-permute-done.76
  489.9 15.3 %collective-permute-done.60 = bf16[128,1536]{1,0:T(8,128)(2,1)S(1)} collective-permute-done((bf16[128,1536]{1,0:T(8,128)(2,1)S(1)}, bf16[128,1536]{1,0:T(8,128)(2,1)S(1)}, u32[]{:S(2)}, u32[]{:S(2)}) %collective-permute-start.60) | collective-permute-done | bytes 393248 | tf_op jit(solution)/shard_map/ppermute | solution.py:37
  534.3 9.5 shard_map.284
  548.6 17.9 %shard_map.292 = (bf16[512,1152]{1,0:T(8,128)(2,1)S(1)}, f32[8,1024]{1,0:T(8,128)S(1)}, f32[8,128]{1,0:T(8,128)S(1)}, f32[8,1024]{1,0:T(8,128)S(1)}, f32[8,1024]{1,0:T(8,128)S(1)}) custom-call(f32[512,768]{1,0:T(8,128)S(1)} %get-tuple-element.140.dy_ref, f32[512,1024]{1,0:T(8,128)} %get-tuple-element.99.zc_ref.zx_ref.z_ref, ...), custom_call_target="tpu_custom_call" | custom-call | flops 6000000000 | bytes 16000000 | tf_op jit(solution)/shard_map/pallas_call | solution.py:669
  638.6 18.6 %shard_map.295 = (bf16[512,1152]{1,0:T(8,128)(2,1)S(1)}, f32[8,1024]{1,0:T(8,128)S(1)}, f32[8,128]{1,0:T(8,128)S(1)}, f32[8,1024]{1,0:T(8,128)S(1)}, f32[8,1024]{1,0:T(8,128)}) custom-call(f32[512,768]{1,0:T(8,128)S(1)} %copy-done.112, f32[512,1024]{1,0:T(8,128)} %get-tuple-element.124.zc_ref.zx_ref.z_ref, f32[512,1152]{1,0:T(8,128)} %get-tuple-element.452.p_ref.before_ref, ...), custom_call_target="tpu_custom_call" | custom-call | flops 6000000000 | bytes 16000000 | tf_op jit(solution)/shard_map/pallas_call | solution.py:669
  742.5 13.0 %collective-permute-done.91 = bf16[128,1536]{1,0:T(8,128)(2,1)S(1)} collective-permute-done((bf16[128,1536]{1,0:T(8,128)(2,1)S(1)}, bf16[128,1536]{1,0:T(8,128)(2,1)S(1)}, u32[]{:S(2)}, u32[]{:S(2)}) %collective-permute-start.91) | collective-permute-done | bytes 393248 | tf_op jit(solution)/shard_map/ppermute | solution.py:37
  781.6 7.8 collective-permute-done.132
  795.2 9.1 collective-permute-done.133
  868.8 18.6 %shard_map.298 = (bf16[512,1152]{1,0:T(8,128)(2,1)S(1)}, f32[8,1024]{1,0:T(8,128)S(1)}, f32[8,128]{1,0:T(8,128)S(1)}, f32[8,1024]{1,0:T(8,128)S(1)}, f32[8,1024]{1,0:T(8,128)}) custom-call(f32[512,768]{1,0:T(8,128)S(1)} %copy-done.110, f32[512,1024]{1,0:T(8,128)} %get-tuple-element.118.zc_ref.zx_ref.z_ref, f32[512,1152]{1,0:T(8,128)} %get-tuple-element.446.p_ref.before_ref, ...), custom_call_target="tpu_custom_call" | custom-call | flops 6000000000 | bytes 16000000 | tf_op jit(solution)/shard_map/pallas_call | solution.py:669
  890.7 24.6 %collective-permute-done.97 = f32[8,1024]{1,0:T(8,128)S(1)} collective-permute-done((f32[8,1024]{1,0:T(8,128)}, f32[8,1024]{1,0:T(8,128)S(1)}, u32[]{:S(2)}, u32[]{:S(2)}) %collective-permute-start.97) | collective-permute-done | bytes 32800 | tf_op jit(solution)/shard_map/ppermute | solution.py:47
  1000.6 13.2 %collective-permute-done.138 = f32[2,7460]{1,0:T(2,128)S(1)} collective-permute-done((f32[2,7460]{1,0:T(2,128)S(1)}, f32[2,7460]{1,0:T(2,128)S(1)}, u32[]{:S(2)}, u32[]{:S(2)}) %collective-permute-start.138) | collective-permute-done | bytes 59712 | tf_op jit(solution)/shard_map/ppermute | solution.py:37
  1024.7 7.3 collective-permute-done.100
  1050.5 8.7 collective-permute-done.117
  (1215 shorter events, 759.5 us)
Async XLA Ops:
  8.1 35.9 %collective-permute-start.6 = (bf16[192,896]{1,0:T(8,128)(2,1)S(1)}, bf16[192,896]{1,0:T(8,128)(2,1)S(1)}, u32[]{:S(2)}, u32[]{:S(2)}) collective-permute-start(bf16[192,896]{1,0:T(8,128)(2,1)S(1)} %get-tuple-element.430.refs_0_), channel_id=1, source_target_pairs={{0,24},{8,0},{16,8},{24,16},{1,25},{9,1},{17,9},{25,17},{2,26},{10... | collective-permute-start | bytes 1032200 | tf_op jit(solution)/shard_map/ppermute | solution.py:52
  13.2 57.7 %collective-permute-start.5 = (bf16[192,896]{1,0:T(8,128)(2,1)S(1)}, bf16[192,896]{1,0:T(8,128)(2,1)S(1)}, u32[]{:S(2)}, u32[]{:S(2)}) collective-permute-start(bf16[192,896]{1,0:T(8,128)(2,1)S(1)} %get-tuple-element.430.refs_0_), channel_id=1, source_target_pairs={{0,4},{4,0},{1,5},{5,1},{2,6},{6,2},{3,7},{7,3},{8,12},{12,8},{9,1... | collective-permute-start | bytes 1032200 | tf_op jit(solution)/shard_map/ppermute | solution.py:52
  123.8 67.1 %collective-permute-start.17 = (bf16[192,1536]{1,0:T(8,128)(2,1)S(1)}, bf16[192,1536]{1,0:T(8,128)(2,1)S(1)}, u32[]{:S(2)}, u32[]{:S(2)}) collective-permute-start(bf16[192,1536]{1,0:T(8,128)(2,1)S(1)} %pad_maximum_fusion.22.refs_0_), channel_id=1, source_target_pairs={{0,4},{4,0},{1,5},{5,1},{2,6},{6,2},{3,7},{7,3},{8,12},{12,8},{9,1... | collective-permute-start | bytes 1769480 | tf_op jit(solution)/shard_map/ppermute | solution.py:52
  125.0 65.9 %collective-permute-start.19 = (bf16[192,1536]{1,0:T(8,128)(2,1)}, bf16[192,1536]{1,0:T(8,128)(2,1)S(1)}, u32[]{:S(2)}, u32[]{:S(2)}) collective-permute-start(bf16[192,1536]{1,0:T(8,128)(2,1)} %collective-permute-done.18.refs_2_), channel_id=1, source_target_pairs={{0,4},{4,0},{1,5},{5,1},{2,6},{6,2},{3,7},{7,3},{8,12},{12,8},{9,1... | collective-permute-start | bytes 1769480 | tf_op jit(solution)/shard_map/ppermute | solution.py:52
  127.3 63.6 %collective-permute-start.21 = (bf16[192,1536]{1,0:T(8,128)(2,1)}, bf16[192,1536]{1,0:T(8,128)(2,1)S(1)}, u32[]{:S(2)}, u32[]{:S(2)}) collective-permute-start(bf16[192,1536]{1,0:T(8,128)(2,1)} %collective-permute-done.20.refs_4_), channel_id=1, source_target_pairs={{0,4},{4,0},{1,5},{5,1},{2,6},{6,2},{3,7},{7,3},{8,12},{12,8},{9,1... | collective-permute-start | bytes 1769480 | tf_op jit(solution)/shard_map/ppermute | solution.py:52
  128.5 62.4 %collective-permute-start.23 = (bf16[192,1536]{1,0:T(8,128)(2,1)}, bf16[192,1536]{1,0:T(8,128)(2,1)S(1)}, u32[]{:S(2)}, u32[]{:S(2)}) collective-permute-start(bf16[192,1536]{1,0:T(8,128)(2,1)} %collective-permute-done.22.refs_6_), channel_id=1, source_target_pairs={{0,4},{4,0},{1,5},{5,1},{2,6},{6,2},{3,7},{7,3},{8,12},{12,8},{9,1... | collective-permute-start | bytes 1769480 | tf_op jit(solution)/shard_map/ppermute | solution.py:52
  133.2 42.2 %collective-permute-start.14 = (bf16[8,1024]{1,0:T(8,128)(2,1)S(1)}, bf16[8,1024]{1,0:T(8,128)(2,1)S(1)}, u32[]{:S(2)}, u32[]{:S(2)}) collective-permute-start(bf16[8,1024]{1,0:T(8,128)(2,1)S(1)} %pad_maximum_fusion.33), channel_id=1, source_target_pairs={{0,4},{1,5},{2,6},{3,7},{8,12},{9,13},{10,14},{11,15},{16,20},{17,... | collective-permute-start | bytes 49160 | tf_op jit(solution)/shard_map/ppermute | solution.py:47
  244.7 38.0 %collective-permute-start.27 = (f32[128,1536]{1,0:T(8,128)}, f32[128,1536]{1,0:T(8,128)}, u32[]{:S(2)}, u32[]{:S(2)}) collective-permute-start(f32[128,1536]{1,0:T(8,128)} %constant_dynamic-slice_fusion.13), channel_id=1, source_target_pairs={{0,2},{1,3},{2,0},{3,1},{4,6},{5,7},{6,4},{7,5},{8,10},{9,11},{10,... | collective-permute-start | bytes 2359304 | tf_op jit(solution)/shard_map/ppermute | solution.py:37
  325.2 32.5 %collective-permute-start.41 = (bf16[192,1536]{1,0:T(8,128)(2,1)S(1)}, bf16[192,1536]{1,0:T(8,128)(2,1)S(1)}, u32[]{:S(2)}, u32[]{:S(2)}) collective-permute-start(bf16[192,1536]{1,0:T(8,128)(2,1)S(1)} %pad_maximum_fusion.23.refs_0_), channel_id=1, source_target_pairs={{0,4},{4,0},{1,5},{5,1},{2,6},{6,2},{3,7},{7,3},{8,12},{12,8},{9,1... | collective-permute-start | bytes 1769480 | tf_op jit(solution)/shard_map/ppermute | solution.py:52
  344.2 58.7 %collective-permute-start.58 = (f32[256,1536]{1,0:T(8,128)}, f32[256,1536]{1,0:T(8,128)}, u32[]{:S(2)}, u32[]{:S(2)}) collective-permute-start(f32[256,1536]{1,0:T(8,128)} %constant_dynamic-slice_fusion.11), channel_id=1, source_target_pairs={{0,1},{1,0},{2,3},{3,2},{4,5},{5,4},{6,7},{7,6},{8,9},{9,8},{10,11... | collective-permute-start | bytes 4718600 | tf_op jit(solution)/shard_map/ppermute | solution.py:37
  346.9 38.3 %collective-permute-start.47 = (bf16[192,1536]{1,0:T(8,128)(2,1)S(1)}, bf16[192,1536]{1,0:T(8,128)(2,1)S(1)}, u32[]{:S(2)}, u32[]{:S(2)}) collective-permute-start(bf16[192,1536]{1,0:T(8,128)(2,1)S(1)} %collective-permute-done.46.refs_6_), channel_id=1, source_target_pairs={{0,4},{4,0},{1,5},{5,1},{2,6},{6,2},{3,7},{7,3},{8,12},{12,8},{9,1... | collective-permute-start | bytes 1769480 | tf_op jit(solution)/shard_map/ppermute | solution.py:52
  357.7 33.7 %collective-permute-start.40 = (f32[128,768]{1,0:T(8,128)S(1)}, f32[128,768]{1,0:T(8,128)S(1)}, u32[]{:S(2)}, u32[]{:S(2)}) collective-permute-start(f32[128,768]{1,0:T(8,128)S(1)} %get-tuple-element.111), channel_id=1, source_target_pairs={{0,4},{1,5},{2,6},{3,7},{8,12},{9,13},{10,14},{11,15},{16,20},{17,... | collective-permute-start | bytes 1179656 | tf_op jit(solution)/shard_map/ppermute | solution.py:47
  585.9 116.9 %collective-permute-start.82 = (bf16[256,1536]{1,0:T(8,128)(2,1)}, bf16[256,1536]{1,0:T(8,128)(2,1)}, u32[]{:S(2)}, u32[]{:S(2)}) collective-permute-start(bf16[256,1536]{1,0:T(8,128)(2,1)} %constant_dynamic-slice_fusion.7), channel_id=1, source_target_pairs={{0,1},{1,0},{2,3},{3,2},{4,5},{5,4},{6,7},{7,6},{8,9},{9,8},{10,11... | collective-permute-start | bytes 2359304 | tf_op jit(solution)/shard_map/ppermute | solution.py:37
  611.7 94.3 %collective-permute-start.66 = (bf16[256,1536]{1,0:T(8,128)(2,1)}, bf16[256,1536]{1,0:T(8,128)(2,1)}, u32[]{:S(2)}, u32[]{:S(2)}) collective-permute-start(bf16[256,1536]{1,0:T(8,128)(2,1)} %constant_dynamic-slice_fusion.9), channel_id=1, source_target_pairs={{0,1},{1,0},{2,3},{3,2},{4,5},{5,4},{6,7},{7,6},{8,9},{9,8},{10,11... | collective-permute-start | bytes 2359304 | tf_op jit(solution)/shard_map/ppermute | solution.py:37
  631.9 176.8 %collective-permute-start.118 = (bf16[192,1536]{1,0:T(8,128)(2,1)}, bf16[192,1536]{1,0:T(8,128)(2,1)}, u32[]{:S(2)}, u32[]{:S(2)}) collective-permute-start(bf16[192,1536]{1,0:T(8,128)(2,1)} %get-tuple-element.314), channel_id=1, source_target_pairs={{0,4},{4,0},{1,5},{5,1},{2,6},{6,2},{3,7},{7,3},{8,12},{12,8},{9,1... | collective-permute-start | bytes 1769480 | tf_op jit(solution)/shard_map/ppermute | solution.py:52
  635.3 63.3 %collective-permute-start.121 = (bf16[192,1536]{1,0:T(8,128)(2,1)}, bf16[192,1536]{1,0:T(8,128)(2,1)}, u32[]{:S(2)}, u32[]{:S(2)}) collective-permute-start(bf16[192,1536]{1,0:T(8,128)(2,1)} %get-tuple-element.315), channel_id=1, source_target_pairs={{0,4},{4,0},{1,5},{5,1},{2,6},{6,2},{3,7},{7,3},{8,12},{12,8},{9,1... | collective-permute-start | bytes 1769480 | tf_op jit(solution)/shard_map/ppermute | solution.py:52
  664.2 74.7 %collective-permute-start.120 = (bf16[192,1536]{1,0:T(8,128)(2,1)}, bf16[192,1536]{1,0:T(8,128)(2,1)}, u32[]{:S(2)}, u32[]{:S(2)}) collective-permute-start(bf16[192,1536]{1,0:T(8,128)(2,1)} %get-tuple-element.316), channel_id=1, source_target_pairs={{0,4},{4,0},{1,5},{5,1},{2,6},{6,2},{3,7},{7,3},{8,12},{12,8},{9,1... | collective-permute-start | bytes 1769480 | tf_op jit(solution)/shard_map/ppermute | solution.py:52
  698.6 68.7 %collective-permute-start.119 = (bf16[192,1536]{1,0:T(8,128)(2,1)}, bf16[192,1536]{1,0:T(8,128)(2,1)}, u32[]{:S(2)}, u32[]{:S(2)}) collective-permute-start(bf16[192,1536]{1,0:T(8,128)(2,1)} %get-tuple-element.317), channel_id=1, source_target_pairs={{0,4},{4,0},{1,5},{5,1},{2,6},{6,2},{3,7},{7,3},{8,12},{12,8},{9,1... | collective-permute-start | bytes 1769480 | tf_op jit(solution)/shard_map/ppermute | solution.py:52
  760.9 34.1 %collective-permute-start.127 = (bf16[192,896]{1,0:T(8,128)(2,1)S(1)}, bf16[192,896]{1,0:T(8,128)(2,1)S(1)}, u32[]{:S(2)}, u32[]{:S(2)}) collective-permute-start(bf16[192,896]{1,0:T(8,128)(2,1)S(1)} %get-tuple-element.328), channel_id=1, source_target_pairs={{0,4},{4,0},{1,5},{5,1},{2,6},{6,2},{3,7},{7,3},{8,12},{12,8},{9,1... | collective-permute-start | bytes 1032200 | tf_op jit(solution)/shard_map/ppermute | solution.py:52
  860.1 203.7 %collective-permute-start.102 = (bf16[192,1536]{1,0:T(8,128)(2,1)}, bf16[192,1536]{1,0:T(8,128)(2,1)}, u32[]{:S(2)}, u32[]{:S(2)}) collective-permute-start(bf16[192,1536]{1,0:T(8,128)(2,1)} %get-tuple-element.310), channel_id=1, source_target_pairs={{0,4},{4,0},{1,5},{5,1},{2,6},{6,2},{3,7},{7,3},{8,12},{12,8},{9,1... | collective-permute-start | bytes 1769480 | tf_op jit(solution)/shard_map/ppermute | solution.py:52
  863.4 83.8 %collective-permute-start.105 = (bf16[192,1536]{1,0:T(8,128)(2,1)}, bf16[192,1536]{1,0:T(8,128)(2,1)}, u32[]{:S(2)}, u32[]{:S(2)}) collective-permute-start(bf16[192,1536]{1,0:T(8,128)(2,1)} %get-tuple-element.311), channel_id=1, source_target_pairs={{0,4},{4,0},{1,5},{5,1},{2,6},{6,2},{3,7},{7,3},{8,12},{12,8},{9,1... | collective-permute-start | bytes 1769480 | tf_op jit(solution)/shard_map/ppermute | solution.py:52
  863.4 118.3 %collective-permute-start.104 = (bf16[192,1536]{1,0:T(8,128)(2,1)}, bf16[192,1536]{1,0:T(8,128)(2,1)}, u32[]{:S(2)}, u32[]{:S(2)}) collective-permute-start(bf16[192,1536]{1,0:T(8,128)(2,1)} %get-tuple-element.312), channel_id=1, source_target_pairs={{0,4},{4,0},{1,5},{5,1},{2,6},{6,2},{3,7},{7,3},{8,12},{12,8},{9,1... | collective-permute-start | bytes 1769480 | tf_op jit(solution)/shard_map/ppermute | solution.py:52
  865.5 154.7 %collective-permute-start.103 = (bf16[192,1536]{1,0:T(8,128)(2,1)}, bf16[192,1536]{1,0:T(8,128)(2,1)}, u32[]{:S(2)}, u32[]{:S(2)}) collective-permute-start(bf16[192,1536]{1,0:T(8,128)(2,1)} %get-tuple-element.313), channel_id=1, source_target_pairs={{0,4},{4,0},{1,5},{5,1},{2,6},{6,2},{3,7},{7,3},{8,12},{12,8},{9,1... | collective-permute-start | bytes 1769480 | tf_op jit(solution)/shard_map/ppermute | solution.py:52
  997.2 53.0 %collective-permute-start.111 = (bf16[192,896]{1,0:T(8,128)(2,1)}, bf16[192,896]{1,0:T(8,128)(2,1)}, u32[]{:S(2)}, u32[]{:S(2)}) collective-permute-start(bf16[192,896]{1,0:T(8,128)(2,1)} %get-tuple-element.324), channel_id=1, source_target_pairs={{0,4},{4,0},{1,5},{5,1},{2,6},{6,2},{3,7},{7,3},{8,12},{12,8},{9,1... | collective-permute-start | bytes 1032200 | tf_op jit(solution)/shard_map/ppermute | solution.py:52
  (395 other events, 4653.5 us)

commit v2 on v1

--- a/solution.py
+++ b/solution.py
@@ -17,9 +17,9 @@
 NT = (((1,), (1,)), ((), ()))
 TN = (((0,), (0,)), ((), ()))
 NO_LINK = -1e30
+COST_SCALE = 0.5
 FWD_WIDE = True
 BWD_WIDE = True
-FSTATE = F32
 
 
 def mm(a, b, dims=NN):
@@ -30,6 +30,49 @@
     return pltpu.CompilerParams(
         dimension_semantics=("arbitrary",), vmem_limit_bytes=mib * 1024 * 1024
     )
+
+
+PRECEDING = []
+
+
+def kernel_call(body, cost=2.0, **spec):
+    def call(*inputs):
+        tokens = list(PRECEDING)
+        options = dict(spec)
+        grid_spec = options.pop("grid_spec", None)
+        unread = [pl.BlockSpec(memory_space=pl.ANY)] * len(tokens)
+        prefetched = 0
+        if grid_spec is None:
+            options["in_specs"] = list(options["in_specs"]) + unread
+        else:
+            prefetched = grid_spec.num_scalar_prefetch
+            options["grid_spec"] = pltpu.PrefetchScalarGridSpec(
+                num_scalar_prefetch=prefetched,
+                grid=grid_spec.grid,
+                in_specs=list(grid_spec.in_specs) + unread,
+                out_specs=grid_spec.out_specs,
+                scratch_shapes=grid_spec.scratch_shapes,
+            )
+        first = len(inputs)
+
+        def without_tokens(*refs):
+            body(*refs[:first], *refs[first + len(tokens) :])
+
+        out = pl.pallas_call(
+            without_tokens,
+            cost_estimate=pl.CostEstimate(
+                flops=int(cost * 1.0e9 * COST_SCALE), transcendentals=0, bytes_accessed=1024
+            ),
+            **options,
+        )(*inputs, *tokens)
+        PRECEDING[:] = [min(jax.tree.leaves(out), key=lambda one: one.size * one.dtype.itemsize)]
+        return out
+
+    return call
+
+
+def precede(*tokens):
+    PRECEDING.extend(token for token in tokens if token is not None)
 
 
 def flipped(value, axis, bit):
@@ -72,43 +115,55 @@
     return value
 
 
-def scatter_rows(value):
-    index = lax.axis_index("tensor")
-    kind = value.dtype
-    for bit in range(bits("tensor")):
-        mine = (index >> bit) & 1
-        half = value.shape[0] // 2
-        sent = lax.dynamic_slice_in_dim(value, (1 - mine) * half, half, 0).astype(kind)
-        kept = lax.dynamic_slice_in_dim(value, mine * half, half, 0).astype(F32)
-        value = kept + flipped(sent, "tensor", bit).astype(F32)
-    return value
+def slots():
+    count, places = bits("tensor"), []
+    for m in range(lax.axis_size("tensor")):
+        places.append(sum(((m >> b) & 1) << (count - 1 - b) for b in range(count)))
+    return places
+
+
+def rows_order(first):
+    places = slots()
+    if first:
+        half = len(places) // 2
+        places = places[half:] + places[:half]
+    return jnp.array(places, jnp.int32) ^ lax.axis_index("tensor")
 
 
 def own_rows(value):
-    index = lax.axis_index("tensor")
-    for bit in range(bits("tensor")):
-        half = value.shape[0] // 2
-        value = lax.dynamic_slice_in_dim(value, ((index >> bit) & 1) * half, half, 0)
-    return value
-
-
-def gather_rows(value):
-    index = lax.axis_index("tensor")
+    rows = value.shape[0] // lax.axis_size("tensor")
+    return lax.dynamic_slice_in_dim(value, lax.axis_index("tensor") * rows, rows, 0)
+
+
+def gathered(value):
+    pieces = [value]
     for bit in reversed(range(bits("tensor"))):
-        upper = (index >> bit) & 1
-        other = flipped(value, "tensor", bit)
-        value = jnp.concatenate(
-            [jnp.where(upper == 0, value, other), jnp.where(upper == 0, other, value)], axis=0
-        )
-    return value
+        pieces = pieces + [flipped(piece, "tensor", bit) for piece in pieces]
+    return pieces
+
+
+def relay_kernel(from_ref, to_ref):
+    to_ref[...] = from_ref[...]
+
+
+def relayed(piece, *tokens):
+    precede(*tokens)
+    return kernel_call(
+        relay_kernel,
+        grid=(1,),
+        in_specs=[fixed_block(piece.shape)],
+        out_specs=fixed_block(piece.shape),
+        out_shape=jax.ShapeDtypeStruct(piece.shape, piece.dtype),
+        compiler_params=params(),
+    )(piece)
 
 
 def ring_pieces(piece):
-    own = [piece]
-    for _ in range(lax.axis_size("dp") - 1):
-        own.append(ring(own[-1], "dp"))
-    table = []
-    for arrived in own:
+    table, arrived = [], piece
+    for k in range(lax.axis_size("dp")):
+        if k:
+            source = relayed(arrived, table[k - 2][-1]) if k > 1 else arrived
+            arrived = ring(source, "dp")
         row = [arrived]
         for _ in range(lax.axis_size("context") - 1):
             row.append(ring(row[-1], "context"))
@@ -116,16 +171,24 @@
     return table
 
 
-def place_kernel(count, widths, index_ref, *refs):
+def place_kernel(count, widths, tile_at, index_ref, *refs):
     pieces, outs = refs[:count], refs[count:]
     for i in range(count):
         at = 0
         for out, width in zip(outs, widths):
             out[index_ref[i]] = pieces[i][:, at : at + width]
             at += width
-
-
-def placed(table, widths):
+    if tile_at is not None:
+        first, tiles = outs[0], outs[-1]
+        rows = first.shape[1]
+        whole_rows = jnp.concatenate(
+            [first[i, :, tile_at : tile_at + LANES] for i in range(count)], axis=0
+        )
+        for at in range(0, count * rows, LANES):
+            tiles[:, at : at + LANES] = whole_rows[at : at + LANES].astype(F32).T
+
+
+def placed(table, widths, tile_at=None):
     dp, context = lax.axis_size("dp"), lax.axis_size("context")
     z, x = lax.axis_index("dp"), lax.axis_index("context")
     pieces, index = [], []
@@ -134,52 +197,53 @@
             pieces.append(piece)
             index.append(((z + k) % dp) * context + (x + j) % context)
     count, rows = len(pieces), pieces[0].shape[0]
-    outs = pl.pallas_call(
-        functools.partial(place_kernel, count, widths),
+    out_specs = [
+        pl.BlockSpec((count, rows, width), lambda i, index: (0, 0, 0)) for width in widths
+    ]
+    out_shape = [jax.ShapeDtypeStruct((count, rows, width), BF16) for width in widths]
+    if tile_at is not None:
+        out_specs.append(pl.BlockSpec((LANES, count * rows), lambda i, index: (0, 0)))
+        out_shape.append(jax.ShapeDtypeStruct((LANES, count * rows), F32))
+    outs = kernel_call(
+        functools.partial(place_kernel, count, widths, tile_at),
+        cost=3.5,
         grid_spec=pltpu.PrefetchScalarGridSpec(
             num_scalar_prefetch=1,
             grid=(1,),
             in_specs=[pl.BlockSpec(piece.shape, lambda i, index: (0, 0)) for piece in pieces],
-            out_specs=[
-                pl.BlockSpec((count, rows, width), lambda i, index: (0, 0, 0)) for width in widths
-            ],
+            out_specs=out_specs,
         ),
-        out_shape=[jax.ShapeDtypeStruct((count, rows, width), BF16) for width in widths],
+        out_shape=out_shape,
         compiler_params=params(),
-        cost_estimate=pl.CostEstimate(
-            flops=0, transcendentals=0, bytes_accessed=4 * count * rows * sum(widths)
-        ),
     )(jnp.stack(index).astype(jnp.int32), *pieces)
-    return [out.reshape(count * rows, -1) for out in outs]
-
-
-def ring_scatter(blocks):
-    dp, context = lax.axis_size("dp"), lax.axis_size("context")
-    z, x = lax.axis_index("dp"), lax.axis_index("context")
-
-    def block(k, j):
-        at = ((z + k) % dp) * context + (x + j) % context
-        return lax.dynamic_index_in_dim(blocks, at, 0, keepdims=False)
-
-    def over_context(k):
-        total = None
-        for j in range(1, context):
-            part = block(k, j)
-            if total is not None:
-                part = (total + part.astype(F32)).astype(BF16)
-            total = ring(part, "context").astype(F32)
-        part = block(k, 0).astype(F32)
-        return part if total is None else part + total
-
-    total = None
-    for k in list(range(1, dp)) + [0]:
-        part = over_context(k)
-        if total is not None:
-            part = part + total
-        if k:
-            total = ring(part.astype(BF16), "dp").astype(F32)
-        else:
-            return part
+    return [
+        out.reshape(count * rows, -1) if i < len(widths) else out for i, out in enumerate(outs)
+    ]
+
+
+def after(value, *tokens):
+    tokens = tuple(token for token in tokens if token is not None)
+    return lax.optimization_barrier((value, *tokens))[0] if tokens else value
+
+
+def from_others(value, axis):
+    count = lax.axis_size(axis)
+    return [value] + [
+        lax.ppermute(value, axis, [(i, i ^ step) for i in range(count)])
+        for step in range(1, count)
+    ]
+
+
+def scatter_places(value):
+    index = lax.axis_index("tensor")
+    value = value.reshape(-1, value.shape[0] // lax.axis_size("tensor"), value.shape[1])
+    for bit in range(bits("tensor")):
+        mine = (index >> bit) & 1
+        value = value.reshape(-1, 2, *value.shape[1:])
+        sent = lax.dynamic_index_in_dim(value, 1 - mine, 1, keepdims=False)
+        kept = lax.dynamic_index_in_dim(value, mine, 1, keepdims=False)
+        value = kept + flipped(sent, "tensor", bit)
+    return value[0]
 
 
 def silu_parts(value):
@@ -228,6 +292,431 @@
 def column_of(rows):
     pad = jnp.zeros((CHUNK - rows.shape[0], CHUNK), F32)
     return jnp.concatenate([rows, pad], axis=0).T
+
+
+def row_norm(wide):
+    return lax.rsqrt(jnp.mean(wide * wide, axis=-1, keepdims=True) + eps)
+
+
+def columns(array, at, width):
+    return pl.BlockSpec((array.shape[0], width), lambda i, *_: (0, at))
+
+
+def fixed_block(shape):
+    return pl.BlockSpec(shape, lambda i, *_: (0,) * len(shape))
+
+
+def project_kernel(
+    norm, count, width, order_ref, *refs
+):
+    pieces, rest = refs[:count], refs[count:]
+    if norm:
+        gain_ref, halo_ref, rest = rest[0], rest[1], rest[2:]
+    w_refs, (normed_ref, proj_ref, rim_ref) = rest[:3], rest[3:]
+    step = pl.program_id(0)
+
+    def run(rows):
+        normed_ref[...] = rows
+        for j, w_ref in enumerate(w_refs):
+            size = w_ref.shape[1]
+            proj_ref[:, j * size : (j + 1) * size] = mm(rows, w_ref[...])
+
+    if norm:
+        wide = pieces[0][0].astype(F32)
+        run((wide * row_norm(wide) * gain_ref[...]).astype(BF16))
+
+        @pl.when(step == 0)
+        def _():
+            halo = halo_ref[0].astype(F32)
+            halo = (halo * row_norm(halo) * gain_ref[...]).astype(BF16)
+            row = jnp.concatenate([mm(halo, w_ref[...]) for w_ref in w_refs], axis=1)
+            rim_ref[:, :width] = row[8:, :width].astype(BF16)
+            rim_ref[:, width:] = row[8:, width + LANES :].astype(BF16)
+
+    else:
+        for m in range(count):
+
+            @pl.when(step == m)
+            def _(m=m):
+                run(pieces[m][...])
+
+    if norm:
+        return
+
+    @pl.when(order_ref[step] == pl.num_programs(0) - 1)
+    def _():
+        tail = proj_ref[CHUNK - 16 :].astype(BF16)
+        rim_ref[:, :width] = tail[8:, :width]
+        rim_ref[:, width:] = tail[8:, width + LANES :]
+
+
+def project(source, gain, order, front, width, total):
+    weights, at = front
+    third = total // 3
+    norm = gain is not None
+    if norm:
+        stream, halo, sequence = source
+        model, length = stream.shape[2], stream.shape[1]
+        inputs, count = [stream, gain, halo], 1
+        specs = [
+            pl.BlockSpec((1, CHUNK, model), lambda i, order: (sequence, order[i], 0)),
+            fixed_block((1, model)),
+            pl.BlockSpec((1, 16, model), lambda i, order: (sequence, 0, 0)),
+        ]
+    else:
+        model, count = source[0].shape[1], len(source)
+        length = count * CHUNK
+        inputs = list(source)
+        specs = [fixed_block((CHUNK, model))] * count
+    conv = total - LANES
+    return kernel_call(
+        functools.partial(project_kernel, norm, count, width),
+        cost=6.5,
+        grid_spec=pltpu.PrefetchScalarGridSpec(
+            num_scalar_prefetch=1,
+            grid=(length // CHUNK,),
+            in_specs=specs + [columns(weights, at + j, third) for j in range(3)],
+            out_specs=[
+                pl.BlockSpec((CHUNK, model), lambda i, order: (order[i], 0)),
+                pl.BlockSpec((CHUNK, total), lambda i, order: (order[i], 0)),
+                fixed_block((8, conv)),
+            ],
+        ),
+        out_shape=[
+            jax.ShapeDtypeStruct((length, model), BF16),
+            jax.ShapeDtypeStruct((length, total), F32),
+            jax.ShapeDtypeStruct((8, conv), BF16),
+        ],
+        compiler_params=params(),
+    )(order, *inputs, weights, weights, weights)
+
+
+def plain_kernel(a_ref, w_ref, out_ref):
+    out_ref[...] = mm(a_ref[...], w_ref[...])
+
+
+def plain_product(a, weight, width):
+    weights, at = weight
+    length, model = a.shape
+    return kernel_call(
+        plain_kernel,
+        cost=3.7,
+        grid=(length // CHUNK,),
+        in_specs=[row_spec(model), columns(weights, at, width)],
+        out_specs=row_spec(width),
+        out_shape=jax.ShapeDtypeStruct((length, width), F32),
+        compiler_params=params(),
+    )(a, weights)
+
+
+def norm_forward_kernel(stream_ref, keep_ref, first_ref, second_ref, gain_ref, new_ref, low_ref):
+    total = keep_ref[0].astype(F32) + first_ref[0].astype(F32) + second_ref[...].astype(F32)
+    new = stream_ref[...] + total
+    new_ref[...] = new
+    low_ref[...] = (new * row_norm(new) * gain_ref[...]).astype(BF16)
+
+
+def last_forward_kernel(stream_ref, keep_ref, first_ref, second_ref, low_ref):
+    total = keep_ref[0].astype(F32) + first_ref[0].astype(F32) + second_ref[...].astype(F32)
+    low_ref[...] = (stream_ref[...] + total).astype(BF16)
+
+
+def pass_on_kernel(keep_ref, first_ref, out_ref):
+    total = keep_ref[0].astype(F32) + first_ref[0].astype(F32)
+    out_ref[...] = total.astype(out_ref.dtype)
+
+
+def pass_on(kept, first):
+    _, rows, model = kept.shape
+    spec = pl.BlockSpec((1, rows, model), lambda i: (1, 0, 0))
+    return kernel_call(
+        pass_on_kernel,
+        grid=(1,),
+        in_specs=[spec, spec],
+        out_specs=fixed_block((rows, model)),
+        out_shape=jax.ShapeDtypeStruct((rows, model), kept.dtype),
+        compiler_params=params(),
+    )(kept, first)
+
+
+def term_specs(rows, model):
+    return [
+        fixed_block((rows, model)),
+        fixed_block((1, rows, model)),
+        fixed_block((1, rows, model)),
+        fixed_block((rows, model)),
+    ]
+
+
+def norm_forward(stream, terms, gain):
+    rows, model = stream.shape
+    kept, first, second = terms
+    if gain is None:
+        return stream, kernel_call(
+            last_forward_kernel,
+            grid=(1,),
+            in_specs=term_specs(rows, model),
+            out_specs=fixed_block((rows, model)),
+            out_shape=jax.ShapeDtypeStruct((rows, model), BF16),
+            compiler_params=params(),
+        )(stream, kept, first, second)
+    return kernel_call(
+        norm_forward_kernel,
+        grid=(1,),
+        in_specs=term_specs(rows, model) + [fixed_block((1, model))],
+        out_specs=[fixed_block((rows, model))] * 2,
+        out_shape=[
+            jax.ShapeDtypeStruct((rows, model), F32),
+            jax.ShapeDtypeStruct((rows, model), BF16),
+        ],
+        compiler_params=params(),
+    )(stream, kept, first, second, gain)
+
+
+def norm_backward_kernel(
+    stream_ref, keep_ref, first_ref, second_ref, grad_ref, gain_ref, new_ref, low_ref, dgain_ref
+):
+    total = keep_ref[0].astype(F32) + first_ref[0].astype(F32) + second_ref[...].astype(F32)
+    current = stream_ref[...]
+    scale = row_norm(current)
+    unit = current * scale
+    dgain_ref[...] = jnp.broadcast_to(
+        jnp.sum(total * unit, axis=0, keepdims=True), dgain_ref.shape
+    )
+    pulled = total * gain_ref[...]
+    shift = jnp.mean(pulled * unit, axis=-1, keepdims=True)
+    new = grad_ref[...] + scale * (pulled - unit * shift)
+    new_ref[...] = new
+    low_ref[...] = new.astype(BF16)
+
+
+def norm_backward(stream, terms, grad, gain):
+    rows, model = stream.shape
+    return kernel_call(
+        norm_backward_kernel,
+        grid=(1,),
+        in_specs=term_specs(rows, model) + [fixed_block((rows, model)), fixed_block((1, model))],
+        out_specs=[fixed_block((rows, model))] * 2 + [fixed_block((8, model))],
+        out_shape=[
+            jax.ShapeDtypeStruct((rows, model), F32),
+            jax.ShapeDtypeStruct((rows, model), BF16),
+            jax.ShapeDtypeStruct((8, model), F32),
+        ],
+        compiler_params=params(),
+    )(stream, *terms, grad, gain)
+
+
+def assemble_kernel(count, order_ref, *refs):
+    step = pl.program_id(0)
+    for m in range(count):
+
+        @pl.when(step == m)
+        def _(m=m):
+            refs[-1][0] = refs[m][...]
+
+
+def assembled(groups, order):
+    each, (rows, model) = len(groups[0]), groups[0][0].shape
+    pieces = [piece for group in groups for piece in group]
+    count = len(pieces)
+    return kernel_call(
+        functools.partial(assemble_kernel, count),
+        cost=5.0,
+        grid_spec=pltpu.PrefetchScalarGridSpec(
+            num_scalar_prefetch=1,
+            grid=(count,),
+            in_specs=[fixed_block((rows, model))] * count,
+            out_specs=pl.BlockSpec(
+                (1, rows, model), lambda i, order: (i // each, order[i % each], 0)
+            ),
+        ),
+        out_shape=jax.ShapeDtypeStruct((len(groups), each * rows, model), BF16),
+        compiler_params=params(),
+    )(order, *pieces)
+
+
+def input_grad_kernel(parts, width, order_ref, dproj_ref, dgate_ref, tail_ref, rim_ref, *refs):
+    w_refs, gate_ref, sent_ref, kept_ref, fixed_ref, rows_p, rows_g = refs[:3], *refs[3:]
+    half = parts // 2
+
+    @pl.when(pl.program_id(0) == 0)
+    def _():
+        fixed_ref[...] = dproj_ref[...]
+        tail = (tail_ref[...] + rim_ref[...]).astype(BF16)
+        fixed_ref[parts * CHUNK - 16 :, :width] = tail[:, :width]
+        fixed_ref[parts * CHUNK - 16 :, width + LANES :] = tail[:, width:]
+        for m in range(parts):
+            source = pl.ds(pl.multiple_of(order_ref[m] * CHUNK, CHUNK), CHUNK)
+            rows_p[m * CHUNK : (m + 1) * CHUNK] = fixed_ref[source]
+            rows_g[m * CHUNK : (m + 1) * CHUNK] = dgate_ref[source]
+
+    total = mm(rows_g[...], gate_ref[...], NT)
+    for j, w_ref in enumerate(w_refs):
+        size = w_ref.shape[1]
+        total = total + mm(rows_p[:, j * size : (j + 1) * size], w_ref[...], NT)
+    total = total.astype(BF16)
+    for m in range(half):
+        sent_ref[m] = total[m * CHUNK : (m + 1) * CHUNK]
+        kept_ref[m] = total[(half + m) * CHUNK : (half + m + 1) * CHUNK]
+
+
+def input_grad(dproj, dgate, tail, rim, front, gate, order):
+    length, total = dproj.shape
+    width = dgate.shape[1]
+    (front_w, at), (gate_w, gate_at) = front, gate
+    model, third, parts = front_w.shape[0], total // 3, length // CHUNK
+    cut = model // 4
+    half = pl.BlockSpec((parts // 2, CHUNK, cut), lambda i, order: (0, 0, i))
+
+    def rows(offset, size):
+        return pl.BlockSpec((cut, size), lambda i, order: (i, offset))
+
+    return kernel_call(
+        functools.partial(input_grad_kernel, parts, width),
+        cost=7.6,
+        grid_spec=pltpu.PrefetchScalarGridSpec(
+            num_scalar_prefetch=1,
+            grid=(4,),
+            in_specs=[fixed_block(one.shape) for one in (dproj, dgate, tail, rim)]
+            + [rows(at + j, third) for j in range(3)]
+            + [rows(gate_at, width)],
+            out_specs=[half, half, fixed_block((length, total))],
+            scratch_shapes=[
+                pltpu.VMEM((length, total), BF16),
+                pltpu.VMEM((length, width), BF16),
+            ],
+        ),
+        out_shape=[jax.ShapeDtypeStruct((parts // 2, CHUNK, model), BF16)] * 2
+        + [jax.ShapeDtypeStruct((length, total), BF16)],
+        compiler_params=params(),
+    )(order, dproj, dgate, tail, rim, front_w, front_w, front_w, gate_w)
+
+
+def weight_grad_kernel(segments, sequences, rows, places, order_ref, *refs):
+    lefts, rights = refs[: segments * sequences], refs[segments * sequences :]
+    rights, outs, total = rights[: segments * sequences], rights[segments * sequences : -1], refs[-1]
+    at = 0
+    for g in range(segments):
+        width = rights[g * sequences].shape[1]
+        part = None
+        for s in range(sequences):
+            left = lefts[g * sequences + s]
+            left = left[...] if len(left.shape) == 2 else left[0]
+            one = mm(left, rights[g * sequences + s][...], TN)
+            part = one if part is None else part + one
+        total[:, at : at + width] = part
+        at += width
+    if places is None:
+        outs[0][...] = total[...].astype(BF16)
+        return
+    dp, context = places
+    slot = lax.rem(pl.program_id(0) - order_ref[1] + dp, dp)
+
+    def block(j):
+        start = lax.rem(order_ref[0] + j, context) * rows
+        return total[pl.ds(pl.multiple_of(start, 8), rows)].astype(BF16)
+
+    outs[0][0] = block(0)
+    for j in range(1, context):
+        for k in range(dp):
+
+            @pl.when(slot == k)
+            def _(j=j, k=k):
+                outs[1 + (j - 1) * dp + k][...] = block(j)
+
+
+def weight_grad(pairs, ordered):
+    dp, context = lax.axis_size("dp"), lax.axis_size("context")
+    sequences, length = len(pairs[0][0]), pairs[0][1][0].shape[0]
+    widths = [right[0].shape[1] for _, right in pairs]
+    lefts = [one for left, _ in pairs for one in left]
+    rights = [one for _, right in pairs for one in right]
+    model = lefts[0].shape[-1]
+    total, cut = sum(widths), model // dp
+    rows = cut // context
+    order = jnp.stack([lax.axis_index("context"), lax.axis_index("dp")]).astype(jnp.int32)
+    if ordered:
+        others = (context - 1) * dp
+        out_specs = [
+            pl.BlockSpec(
+                (1, rows, total), lambda i, order: (lax.rem(i - order[1] + dp, dp), 0, 0)
+            )
+        ] + [fixed_block((rows, total))] * others
+        out_shape = [jax.ShapeDtypeStruct((dp, rows, total), BF16)] + [
+            jax.ShapeDtypeStruct((rows, total), BF16)
+        ] * others
+    else:
+        out_specs = [pl.BlockSpec((cut, total), lambda i, order: (i, 0))]
+        out_shape = [jax.ShapeDtypeStruct((model, total), BF16)]
+    left_specs, left_arrays = [], []
+    for left in lefts:
+        if isinstance(left, tuple):
+            left_arrays.append(left[0])
+            left_specs.append(
+                pl.BlockSpec((1, length, cut), lambda i, order, s=left[1]: (s, 0, i))
+            )
+        else:
+            left_arrays.append(left)
+            left_specs.append(pl.BlockSpec((length, cut), lambda i, order: (0, i)))
+    return kernel_call(
+        functools.partial(
+            weight_grad_kernel, len(pairs), sequences, rows, (dp, context) if ordered else None
+        ),
+        cost=10.0,
+        grid_spec=pltpu.PrefetchScalarGridSpec(
+            num_scalar_prefetch=1,
+            grid=(dp,),
+            in_specs=left_specs + [fixed_block(one.shape) for one in rights],
+            out_specs=out_specs,
+            scratch_shapes=[pltpu.VMEM((cut, total), F32)],
+        ),
+        out_shape=out_shape,
+        compiler_params=params(56),
+    )(order, *left_arrays, *rights)
+
+
+def ring_add_kernel(own_ref, *refs):
+    total = own_ref[0].astype(F32)
+    for one in refs[:-1]:
+        total = total + one[...].astype(F32)
+    refs[-1][...] = total.astype(refs[-1].dtype)
+
+
+def ring_add(own, k, terms, kind):
+    _, rows, width = own.shape
+    return kernel_call(
+        ring_add_kernel,
+        cost=1.5,
+        grid=(1,),
+        in_specs=[pl.BlockSpec((1, rows, width), lambda i: (k, 0, 0))]
+        + [fixed_block((rows, width))] * len(terms),
+        out_specs=fixed_block((rows, width)),
+        out_shape=jax.ShapeDtypeStruct((rows, width), kind),
+        compiler_params=params(),
+    )(own, *terms)
+
+
+def ring_steps(blocks):
+    dp, context = lax.axis_size("dp"), lax.axis_size("context")
+    own, others = blocks[0], blocks[1:]
+    places = list(range(1, dp)) + [0]
+    sides = []
+    for k in places:
+        side = None
+        for j in range(1, context):
+            part = others[(j - 1) * dp + k]
+            if side is not None:
+                part = (side.astype(F32) + part.astype(F32)).astype(BF16)
+            side = ring(part, "context")
+        sides.append([] if side is None else [side])
+    passed = []
+    for k, side in zip(places, sides):
+        value = ring_add(own, k, side + passed, BF16 if k else F32)
+        if k:
+            passed = [ring(value, "dp")]
+            yield None
+        else:
+            yield value
 
 
 def scan_forward_kernel(
@@ -307,8 +796,9 @@
     length, total = proj.shape
     heads, width = consts["heads"], consts["width"]
     chunks, conv = length // CHUNK, total - LANES
-    return pl.pallas_call(
+    return kernel_call(
         functools.partial(scan_forward_kernel, heads, width),
+        cost=9.5,
         grid=(chunks,),
         in_specs=[
             row_spec(total),
@@ -340,9 +830,6 @@
             pltpu.VMEM((1, LANES), F32),
         ],
         compiler_params=params(),
-        cost_estimate=pl.CostEstimate(
-            flops=chunks * 400_000_000, transcendentals=0, bytes_accessed=12_000_000
-        ),
     )(proj, rim, aux, seg_rows, consts["cw"], consts["hp"], consts["skip"], consts["exp"])
 
 
@@ -360,8 +847,9 @@
 def mix_forward(y0, z, growth, carried, gate, consts):
     length, width = y0.shape
     last = z.shape[1] // LANES - 1
-    return pl.pallas_call(
+    return kernel_call(
         mix_forward_kernel,
+        cost=3.6,
         grid=(length // CHUNK,),
         in_specs=[
             row_spec(width),
@@ -377,86 +865,130 @@
             jax.ShapeDtypeStruct((8, length), F32),
         ],
         compiler_params=params(),
-        cost_estimate=pl.CostEstimate(
-            flops=1_000_000_000, transcendentals=0, bytes_accessed=6_000_000
+    )(y0, z, growth, carried, gate, consts["exp"])
+
+
+def project_out_kernel(channels, parts, order_ref, y_ref, gate_ref, gain_ref, w_ref, *refs):
+    squares, (sent_ref, kept_ref, rows) = refs[:-3], refs[-3:]
+    half = parts // 2
+
+    @pl.when(pl.program_id(0) == 0)
+    def _():
+        for m in range(parts):
+            source = pl.ds(pl.multiple_of(order_ref[m] * CHUNK, CHUNK), CHUNK)
+            square = sum(one[:, source] for one in squares)
+            scale = lax.rsqrt(column_of(square)[:, 0:1] / channels + eps)
+            gate = gate_ref[source]
+            gated = y_ref[source] * (gate * jax.nn.sigmoid(gate))
+            rows[m * CHUNK : (m + 1) * CHUNK] = (gated * scale * gain_ref[...]).astype(BF16)
+
+    total = mm(rows[...], w_ref[...], NT).astype(sent_ref.dtype)
+    for m in range(half):
+        sent_ref[m] = total[m * CHUNK : (m + 1) * CHUNK]
+        kept_ref[m] = total[(half + m) * CHUNK : (half + m + 1) * CHUNK]
+
+
+def project_out(y, gate, squares, channels, kind, order, consts):
+    length, width = y.shape
+    weights, at = consts["out"]
+    model, parts = weights.shape[0], length // CHUNK
+    cut = model // 4
+    half = pl.BlockSpec((parts // 2, CHUNK, cut), lambda i, order: (0, 0, i))
+    return kernel_call(
+        functools.partial(project_out_kernel, float(channels), parts),
+        cost=5.7,
+        grid_spec=pltpu.PrefetchScalarGridSpec(
+            num_scalar_prefetch=1,
+            grid=(4,),
+            in_specs=[
+                fixed_block((length, width)),
+                fixed_block((length, width)),
+                fixed_block((1, width)),
+                pl.BlockSpec((cut, width), lambda i, order: (i, at)),
+            ]
+            + [fixed_block((8, length))] * len(squares),
+            out_specs=[half, half],
+            scratch_shapes=[pltpu.VMEM((length, width), BF16)],
         ),
-    )(y0, z, growth, carried, gate, consts["exp"])
-
-
-def project_out_kernel(channels, y_ref, gate_ref, sq_ref, gain_ref, w_ref, out_ref):
-    scale = lax.rsqrt(column_of(sq_ref[...])[:, 0:1] / channels + eps)
+        out_shape=[jax.ShapeDtypeStruct((parts // 2, CHUNK, model), kind)] * 2,
+        compiler_params=params(),
+    )(order, y, gate, consts["gain"], weights, *squares)
+
+
+def grad_scaled_kernel(count, order_ref, *refs):
+    pieces, rest = refs[:count], refs[count:]
+    w_ref, y_ref, gate_ref, gain_ref, gs_ref, dot_ref = rest[:6]
     gate = gate_ref[...]
     gated = y_ref[...] * (gate * jax.nn.sigmoid(gate))
-    scaled = (gated * scale * gain_ref[...]).astype(BF16)
-    out_ref[...] = mm(scaled, w_ref[...], NT).astype(out_ref.dtype)
-
-
-def project_out(y, gate, squares, channels, kind, consts):
+
+    def run(rows):
+        grad = mm(rows, w_ref[...])
+        gs_ref[...] = grad
+        product = jnp.sum(grad * gain_ref[...] * gated, axis=1, keepdims=True)
+        dot_ref[...] = jnp.broadcast_to(product, (CHUNK, CHUNK)).T[:8]
+
+    if count == 1:
+        run(pieces[0][0])
+    else:
+        for m in range(count):
+
+            @pl.when(pl.program_id(0) == m)
+            def _(m=m):
+                rest[6][...] = pieces[m][...]
+                run(pieces[m][...])
+
+
+def grad_scaled(source, y, gate, order, consts):
     length, width = y.shape
-    model = consts["out"].shape[0]
-    return pl.pallas_call(
-        functools.partial(project_out_kernel, float(channels)),
-        grid=(length // CHUNK,),
-        in_specs=[
-            row_spec(width),
-            row_spec(width),
-            pl.BlockSpec((8, CHUNK), lambda i: (0, i)),
-            whole((1, width)),
-            whole((model, width)),
-        ],
-        out_specs=row_spec(model),
-        out_shape=jax.ShapeDtypeStruct((length, model), kind),
+    weights, at = consts["out"]
+    model = weights.shape[0]
+    row = pl.BlockSpec((CHUNK, width), lambda i, order: (order[i], 0))
+    out_specs = [row, pl.BlockSpec((8, CHUNK), lambda i, order: (0, order[i]))]
+    out_shape = [
+        jax.ShapeDtypeStruct((length, width), F32),
+        jax.ShapeDtypeStruct((8, length), F32),
+    ]
+    if len(source) == 2:
+        stream, sequence = source
+        inputs, count = [stream], 1
+        specs = [pl.BlockSpec((1, CHUNK, model), lambda i, order: (sequence, order[i], 0))]
+    else:
+        inputs, count = list(source), len(source)
+        specs = [fixed_block((CHUNK, model))] * count
+        out_specs.append(pl.BlockSpec((CHUNK, model), lambda i, order: (order[i], 0)))
+        out_shape.append(jax.ShapeDtypeStruct((length, model), BF16))
+    out = kernel_call(
+        functools.partial(grad_scaled_kernel, count),
+        cost=5.5,
+        grid_spec=pltpu.PrefetchScalarGridSpec(
+            num_scalar_prefetch=1,
+            grid=(length // CHUNK,),
+            in_specs=specs + [columns(weights, at, width), row, row, fixed_block((1, width))],
+            out_specs=out_specs,
+        ),
+        out_shape=out_shape,
         compiler_params=params(),
-        cost_estimate=pl.CostEstimate(
-            flops=4 * length * width * model, transcendentals=0, bytes_accessed=9_000_000
-        ),
-    )(y, gate, squares, consts["gain"], consts["out"])
-
-
-def grad_scaled_kernel(g_ref, w_ref, y_ref, gate_ref, gain_ref, gs_ref, dot_ref):
-    grad = mm(g_ref[...], w_ref[...])
-    gs_ref[...] = grad
-    gate = gate_ref[...]
-    gated = y_ref[...] * (gate * jax.nn.sigmoid(gate))
-    product = jnp.sum(grad * gain_ref[...] * gated, axis=1, keepdims=True)
-    dot_ref[...] = jnp.broadcast_to(product, (CHUNK, CHUNK)).T[:8]
-
-
-def grad_scaled(grad_low, y, gate, consts):
-    length, width = y.shape
-    model = consts["out"].shape[0]
-    return pl.pallas_call(
-        grad_scaled_kernel,
-        grid=(length // CHUNK,),
-        in_specs=[
-            row_spec(model),
-            whole((model, width)),
-            row_spec(width),
-            row_spec(width),
-            whole((1, width)),
-        ],
-        out_specs=[row_spec(width), pl.BlockSpec((8, CHUNK), lambda i: (0, i))],
-        out_shape=[
-            jax.ShapeDtypeStruct((length, width), F32),
-            jax.ShapeDtypeStruct((8, length), F32),
-        ],
-        compiler_params=params(),
-        cost_estimate=pl.CostEstimate(
-            flops=4 * length * width * model, transcendentals=0, bytes_accessed=9_000_000
-        ),
-    )(grad_low, consts["out"], y, gate, consts["gain"])
+    )(order, *inputs, weights, y, gate, consts["gain"])
+    return out if count > 1 else (*out, source)
 
 
 def mix_backward_kernel(
-    channels, gs_ref, y_ref, gate_ref, zx_ref, zc_ref, gr_ref, sq_ref, dot_ref, gain_ref, exp_ref,
-    scaled_ref, dgate_ref, dy_ref, acc_ref, dsin_ref,
+    channels, shares, gs_ref, y_ref, gate_ref, zx_ref, zc_ref, gr_ref, gain_ref, exp_ref, *refs
 ):
-    @pl.when(pl.program_id(0) == 0)
+    squares, dots, refs = refs[:shares], refs[shares : 2 * shares], refs[2 * shares :]
+    scaled_ref, dgate_ref, dy_ref, acc_ref, dsin_ref, dsin = refs
+    at = pl.program_id(0)
+
+    @pl.when(at == 0)
     def _():
         acc_ref[...] = jnp.zeros_like(acc_ref)
-        dsin_ref[...] = jnp.zeros_like(dsin_ref)
-
-    stats = column_of(jnp.concatenate([sq_ref[...], dot_ref[...]], axis=0))
+        dsin[...] = jnp.zeros_like(dsin)
+
+    stats = column_of(
+        jnp.concatenate(
+            [sum(one[...] for one in squares), sum(one[...] for one in dots)], axis=0
+        )
+    )
     scale = lax.rsqrt(stats[:, 0:1] / channels + eps)
     pull = scale * scale * scale * stats[:, 8:9] / channels
     grad, y, gate = gs_ref[...], y_ref[...], gate_ref[...]
@@ -472,15 +1004,20 @@
     acc_ref[0:1] += jnp.sum(grad * unit, axis=0, keepdims=True)
     acc_ref[1:2] += jnp.sum(dy * x, axis=0, keepdims=True)
     c_low = (zc_ref[...] * jax.nn.sigmoid(zc_ref[...])).astype(BF16)
-    dsin_ref[...] += mm(c_low, (dy * split_dot(gr_ref[...], exp_ref[...])).astype(BF16), TN)
+    dsin[...] += mm(c_low, (dy * split_dot(gr_ref[...], exp_ref[...])).astype(BF16), TN)
+
+    @pl.when(at == pl.num_programs(0) - 1)
+    def _():
+        dsin_ref[...] = dsin[...].astype(BF16)
 
 
 def mix_backward(grad, y, gate, z, growth, squares, dots, channels, consts):
     length, width = y.shape
     last = z.shape[1] // LANES - 1
     stat = pl.BlockSpec((8, CHUNK), lambda i: (0, i))
-    return pl.pallas_call(
-        functools.partial(mix_backward_kernel, float(channels)),
+    return kernel_call(
+        functools.partial(mix_backward_kernel, float(channels), len(squares)),
+        cost=5.0,
         grid=(length // CHUNK,),
         in_specs=[
             row_spec(width),
@@ -489,11 +1026,10 @@
             row_spec(width),
             row_spec(LANES, last),
             row_spec(LANES),
-            stat,
-            stat,
             whole((1, width)),
             whole((LANES, width)),
-        ],
+        ]
+        + [stat] * (2 * len(squares)),
         out_specs=[
             row_spec(width),
             row_spec(width),
@@ -506,13 +1042,11 @@
             jax.ShapeDtypeStruct((length, width), BF16),
             jax.ShapeDtypeStruct((length, width), F32),
             jax.ShapeDtypeStruct((8, width), F32),
-            jax.ShapeDtypeStruct((LANES, width), F32),
+            jax.ShapeDtypeStruct((LANES, width), BF16),
         ],
+        scratch_shapes=[pltpu.VMEM((LANES, width), F32)],
         compiler_params=params(),
-        cost_estimate=pl.CostEstimate(
-            flops=1_000_000_000, transcendentals=0, bytes_accessed=12_000_000
-        ),
-    )(grad, y, gate, z, z, growth, squares, dots, consts["gain"], consts["exp"])
+    )(grad, y, gate, z, z, growth, consts["gain"], consts["exp"], *squares, *dots)
 
 
 def scan_backward_kernel(
@@ -639,14 +1173,15 @@
 
     @pl.when(step_at == 0)
     def _():
-        tail_ref[...] = dv[CHUNK - 8 :]
+        tail_ref[...] = dv[CHUNK - 16 :]
 
     @pl.when(chunk == 0)
     def _():
         drim = cw_ref[0:1] * zbuf[0, 3:11]
         for k in (1, 2):
             drim = drim + cw_ref[k : k + 1] * zbuf[k, 3 - k : 11 - k]
-        drim_ref[...] = drim
+        drim_ref[0:8] = jnp.zeros_like(drim)
+        drim_ref[8:] = drim
 
     for k in range(3):
         zbuf[k, 8 + CHUNK :] = zbuf[k, 8:16]
@@ -666,8 +1201,9 @@
             (8, columns), lambda i: (jnp.maximum((chunks - 1 - i) * eights - 1, 0), 0)
         )
 
-    return pl.pallas_call(
+    return kernel_call(
         functools.partial(scan_backward_kernel, heads, width, chunks),
+        cost=18.0,
         grid=(chunks,),
         in_specs=[
             back(width),
@@ -691,15 +1227,15 @@
             back(total),
             whole((8, conv)),
             whole((8, LANES)),
-            whole((8, conv)),
-            whole((8, conv)),
+            whole((16, conv)),
+            whole((16, conv)),
         ],
         out_shape=[
             jax.ShapeDtypeStruct((length, total), BF16),
             jax.ShapeDtypeStruct((8, conv), F32),
             jax.ShapeDtypeStruct((8, LANES), F32),
-            jax.ShapeDtypeStruct((8, conv), F32),
-            jax.ShapeDtypeStruct((8, conv), F32),
+            jax.ShapeDtypeStruct((16, conv), F32),
+            jax.ShapeDtypeStruct((16, conv), F32),
         ],
         scratch_shapes=[
             pltpu.VMEM((CHUNK + 8, conv), F32),
@@ -707,9 +1243,6 @@
             pltpu.VMEM((LANES, width), F32),
         ],
         compiler_params=params(),
-        cost_estimate=pl.CostEstimate(
-            flops=chunks * 1_500_000_000, transcendentals=0, bytes_accessed=16_000_000
-        ),
     )(
         dy, z, proj, proj, rim, aux, seg_rows, consts["cw"], consts["hp"], consts["skip"],
         consts["exp"], consts["red"], states, carried, growth, dend,
@@ -734,6 +1267,7 @@
     gate_gain,
     cotangent,
 ):
+    PRECEDING.clear()
     layers, rows_in, _, width = input_weight.shape
     sequences, length, model = stream.shape
     heads = dt_bias.shape[1]
@@ -742,39 +1276,38 @@
     dp, context, tensor = (lax.axis_size(a) for a in ("dp", "context", "tensor"))
     channels = width * tensor
     rows_bc = rows_in // tensor
-    bc_part = shared // tensor
-    conv = width + shared
+    conv, total = width + shared, width + LANES + shared
     layer_range, seq_range = range(layers), range(sequences)
+
+    own_gain, own_conv = pre_gain.shape[1], conv_bc.shape[2]
+    small = jnp.concatenate([pre_gain, conv_bc.reshape(layers, -1), bias_bc], axis=1)
+    small = jnp.pad(small, ((0, 0), (0, shared - small.shape[1])))[:, None]
+    bc_rows = gather_small(jnp.concatenate([coefficient_weight, small], axis=1), ("tensor",))
+    small, bc_rows = bc_rows[:, :, rows_bc], bc_rows[:, :, :rows_bc]
+    taps = small[:, :, own_gain : own_gain + 5 * own_conv].reshape(tensor, layers, 5, own_conv)
+    taps = jnp.moveaxis(taps, 0, 2).reshape(layers, -1)
+    small = jnp.concatenate(
+        [
+            jnp.moveaxis(small[:, :, :own_gain], 0, 1).reshape(layers, rows_in),
+            jnp.pad(taps, ((0, 0), (0, rows_in - taps.shape[1]))),
+        ],
+        axis=0,
+    ).T
 
     def first_piece(layer):
         tile = jnp.concatenate(
             [
                 step_size_weight[layer],
-                jnp.zeros((rows_in, LANES - heads - bc_part), BF16),
-                coefficient_weight[layer].reshape(rows_in, bc_part),
+                small,
+                jnp.zeros((rows_in, LANES - heads - 2 * layers), BF16),
+                bc_rows[:, layer].reshape(rows_in, shared),
             ],
             axis=1,
         )
-        return jnp.concatenate([input_weight[layer, :, 1], tile], axis=1)
+        return [input_weight[layer, :, 1], tile]
 
     def second_piece(layer):
-        return jnp.concatenate([input_weight[layer, :, 0], output_weight[layer].T], axis=1)
-
-    def full_bc(first):
-        part = first[:, width + LANES - bc_part :].reshape(dp * context, rows_bc, shared)
-        every = gather_small(part, ("tensor",))
-        return jnp.moveaxis(every, 0, 1).reshape(model, shared)
-
-    small = jnp.concatenate(
-        [pre_gain, conv_bc.reshape(layers, -1), bias_bc], axis=1
-    )
-    small = gather_small(small, ("tensor", "context", "dp"))
-    own_gain, own_conv = pre_gain.shape[1], conv_bc.shape[2]
-    gains = jnp.moveaxis(small[:, :, :own_gain], 0, 1).reshape(layers, model).astype(F32)
-    conv_all = small[:, :, own_gain : own_gain + 4 * own_conv].reshape(-1, layers, 4, own_conv)
-    conv_all = jnp.moveaxis(conv_all, 0, 2).reshape(layers, 4, shared).astype(F32)
-    bias_all = jnp.moveaxis(small[:, :, own_gain + 4 * own_conv :], 0, 1)
-    bias_all = bias_all.reshape(layers, shared).astype(F32)
+        return [input_weight[layer, :, 0], output_weight[layer].T]
 
     edge_ids = shifted(seg_ids[:, -3:], "context", 1)
     ext_ids = jnp.concatenate([edge_ids, seg_ids], axis=1)
@@ -789,26 +1322,33 @@
 
     spread_table = (jnp.arange(LANES)[:, None] == jnp.arange(width)[None, :] // depth).astype(BF16)
 
-    first, second = [None] * layers, [None] * layers
-    gate_on = None
+    table = ring_pieces(jnp.concatenate(first_piece(0), axis=1))
+    first, tile_rows = placed(table, [total], width)
+    weights, before = [], table[min(1, dp - 1)][0][:16, :LANES]
     for layer in layer_range:
-        piece = first_piece(layer)
-        if gate_on is not None:
-            piece, gate_on = lax.optimization_barrier((piece, gate_on))
-        table = ring_pieces(piece)
-        (first[layer],) = placed(table, [width + LANES])
-        gate_on = table[-1][0]
-        piece, gate_on = lax.optimization_barrier((second_piece(layer), gate_on))
-        table = ring_pieces(piece)
-        second[layer] = placed(table, [width, width])
-        gate_on = table[-1][0]
+        front = first
+        if layer:
+            part = after(jnp.concatenate(first_piece(layer), axis=1), before)
+            front = lax.all_gather(part, ("dp", "context"), axis=0, tiled=True)
+            before = front[:8, :LANES]
+        part = after(jnp.concatenate(second_piece(layer), axis=1), before)
+        rest = lax.all_gather(part, ("dp", "context"), axis=0, tiled=True)
+        before = rest[:8, :LANES]
+        weights.append({"front": (front, 0), "gate": (rest, 0), "out": (rest, 1)})
+    small = tile_rows[heads : heads + 2 * layers]
+    gains = small[:layers]
+    taps = small[layers:].reshape(layers, dp * context, rows_in)[:, :, : 5 * tensor * own_conv]
+    taps = taps.reshape(layers, dp * context, 5, tensor * own_conv)
+    taps = jnp.moveaxis(taps, 1, 2).reshape(layers, 5, shared)
 
     consts = []
     for layer in layer_range:
         cw = jnp.concatenate(
             [
-                jnp.concatenate([conv_x[layer], conv_all[layer]], axis=1),
-                jnp.concatenate([bias_x[layer], bias_all[layer]])[None],
+                jnp.concatenate(
+                    [jnp.concatenate([conv_x[layer], bias_x[layer][None]], axis=0), taps[layer]],
+                    axis=1,
+                ),
                 jnp.zeros((3, conv), F32),
             ],
             axis=0,
@@ -831,124 +1371,220 @@
                 "gain": gate_gain[layer][None],
                 "exp": spread_table,
                 "red": spread_table.T,
-                "front": jnp.concatenate([first[layer], full_bc(first[layer])], axis=1),
-                "gate": second[layer][0],
-                "out": second[layer][1],
+                **weights[layer],
             }
         )
 
-    def chain(value, total, steps, kind):
-        carried = shifted(value.astype(kind), "context", steps)
+    def chain(value, total, steps):
+        carried = shifted(value, "context", steps)
         for _ in range(context - 2):
-            whole_value = value + carried.astype(F32) * total
-            carried = shifted(whole_value.astype(kind), "context", steps)
+            passed = value.astype(F32) + carried.astype(F32) * total
+            carried = shifted(passed.astype(value.dtype), "context", steps)
         return carried
 
     def through(growth):
         return jnp.repeat(growth[length - 1, :heads], depth)[None]
 
-    kept = [[None] * sequences for _ in layer_range]
+    places = jnp.arange(length // CHUNK, dtype=jnp.int32)
+    arrived, sending = rows_order(False), rows_order(True)
     streams = [own_rows(stream[s]).astype(F32) for s in seq_range]
-    normed = []
+    grads = [own_rows(cotangent[s]).astype(F32) for s in seq_range]
+    halo = shifted(stream[:, length - 16 :], "context", 1)
+    incoming = [(stream, halo, s) for s in seq_range]
+    work = [[{} for _ in seq_range] for _ in layer_range]
+    outputs = []
+    top = layers - 1
+    def step_project(layer, s):
+        k = work[layer][s]
+        k["stream"] = streams[s]
+        k["normed"], k["proj"], tail = project(
+            incoming[s],
+            None if layer else gains[0:1],
+            arrived if layer else places,
+            consts[layer]["front"],
+            width,
+            total,
+        )
+        k["rim"] = shifted(tail, "context", 1) if layer else tail
+
+    def step_scan(layer, s):
+        k = work[layer][s]
+        k["z"], k["y0"], k["states"], end, k["growth"] = scan_forward(
+            k["proj"], k["rim"], aux_all[s], seg_rows[s], consts[layer]
+        )
+        k["carried"] = chain(end, through(k["growth"]), 1)
+
+    def step_gate(layer, s):
+        k = work[layer][s]
+        k["gate"] = plain_product(k["normed"], consts[layer]["gate"], width)
+
+    def step_mix(layer, s):
+        k = work[layer][s]
+        k["y"], squares = mix_forward(
+            k["y0"], k["z"], k["growth"], k["carried"], k["gate"], consts[layer]
+        )
+        k["squares"] = from_others(squares, "tensor")
+
+    def step_out(layer, s):
+        k = work[layer][s]
+        kind = BF16 if layer == top else F32
+        sent, own = project_out(
+            k["y"], k["gate"], k["squares"], channels, kind, sending, consts[layer]
+        )
+        k["out"] = [own, flipped(sent, "tensor", 0)]
+
+    def step_pass(layer, s, name):
+        terms = work[layer][s][name]
+        terms.append(flipped(pass_on(*terms), "tensor", 1))
+
+    def step_norm(layer, s):
+        k = work[layer][s]
+        gain = None if layer == top else gains[layer + 1 : layer + 2]
+        streams[s], low = norm_forward(streams[s], k["out"], gain)
+        return gathered(low)
+
+    def step_grad(layer, s):
+        k = work[layer][s]
+        source = (cotangent, s) if layer == top else incoming[s]
+        k["grad"], dots, k["low"] = grad_scaled(
+            source, k["y"], k["gate"], places if layer == top else arrived, consts[layer]
+        )
+        k["dots"] = from_others(dots, "tensor")
+
+    def step_mix_back(layer, s):
+        k = work[layer][s]
+        k["scaled"], k["dgate"], k["dy"], k["acc"], dsin = mix_backward(
+            k["grad"], k["y"], k["gate"], k["z"], k["growth"], k["squares"], k["dots"],
+            channels, consts[layer],
+        )
+        k["dend"] = chain(dsin, through(k["growth"]), -1)
+
+    def step_scan_back(layer, s):
+        k = work[layer][s]
+        k["dproj"], k["wacc"], k["hacc"], k["tail"], drim = scan_backward(
+            k["dy"], k["z"], k["proj"], k["rim"], aux_all[s], seg_rows[s], k["states"],
+            k["carried"], k["growth"], k["dend"], consts[layer],
+        )
+        k["drim"] = shifted(drim, "context", -1)
+
+    def step_input_grad(layer, s):
+        k = work[layer][s]
+        sent, own, k["dproj"] = input_grad(
+            k["dproj"], k["dgate"], k["tail"], k["drim"], consts[layer]["front"],
+            consts[layer]["gate"], sending,
+        )
+        k["back"] = [own, flipped(sent, "tensor", 0)]
+
+    def step_norm_back(layer, s):
+        k = work[layer][s]
+        grads[s], low, k["dgain"] = norm_backward(
+            k["stream"], k["back"], grads[s], gains[layer : layer + 1]
+        )
+        return gathered(low)
+
+    def every(layer, name):
+        return [k[name] for k in work[layer]]
+
+    def step_second_grad(layer):
+        return weight_grad(
+            [
+                (every(layer, "normed"), every(layer, "dgate")),
+                (every(layer, "low"), every(layer, "scaled")),
+            ],
+            layer == 0,
+        )
+
+    def step_first_grad(layer):
+        return weight_grad([(every(layer, "normed"), every(layer, "dproj"))], layer == 0)
+
+    def scattered(value):
+        return lax.psum_scatter(
+            value[0], ("dp", "context"), scatter_dimension=0, tiled=True
+        ).astype(F32)
+
+    second_sums, first_sums = [None] * layers, [None] * layers
+    final = sequences - 1
     for s in seq_range:
-        wide = stream[s].astype(F32)
-        scale = lax.rsqrt(jnp.mean(wide * wide, axis=-1, keepdims=True) + eps)
-        normed.append((wide * scale * gains[0]).astype(BF16))
-    finals = []
+        step_project(0, s)
+        if s == 0:
+            step_scan(0, s)
     for layer in layer_range:
-        const = consts[layer]
-        nexts = []
+        if layer:
+            for s in seq_range:
+                step_project(layer, s)
+                step_scan(layer, s)
+            for s in seq_range:
+                step_gate(layer, s)
+                step_mix(layer, s)
+        else:
+            for s in seq_range:
+                step_gate(layer, s)
+                step_mix(layer, s)
+                if s < final:
+                    step_scan(layer, s + 1)
+                if layer < top:
+                    step_out(layer, s)
+                    step_pass(layer, s, "out")
+        if layer < top:
+            for s in seq_range:
+                incoming[s] = step_norm(layer, s)
+
+    def rest_of(layer):
+        incoming[final] = step_norm_back(layer, final)
+        first_sums[layer] = scattered(step_first_grad(layer))
+
+    for layer in reversed(layer_range):
         for s in seq_range:
-            proj = mm(normed[s], const["front"])
-            gate = mm(normed[s], const["gate"])
-            rim = shifted(
-                jnp.concatenate(
-                    [proj[length - 8 :, :width], proj[length - 8 :, width + LANES :]], axis=1
-                ).astype(BF16),
-                "context",
-                1,
+            step_grad(layer, s)
+            if s == 0 and layer < top:
+                rest_of(layer + 1)
+        for s in seq_range:
+            step_mix_back(layer, s)
+        grad = step_second_grad(layer)
+        if layer:
+            second_sums[layer] = scattered(grad)
+        steps = iter(()) if layer else ring_steps(grad)
+        for s in seq_range:
+            step_scan_back(layer, s)
+            if s == final:
+                for earlier in range(s):
+                    incoming[earlier] = step_norm_back(layer, earlier)
+            next(steps, None)
+            if layer == top:
+                step_out(layer, s)
+            elif layer == top - 1 and s == 0:
+                outputs.extend(step_norm(top, s) for s in seq_range)
+            step_input_grad(layer, s)
+            step_pass(layer, s, "back")
+            if layer == top:
+                step_pass(layer, s, "out")
+    next(steps, None)
+    grad = step_first_grad(0)
+    for value in steps:
+        second_sums[0] = value
+    steps = ring_steps(grad)
+    next(steps)
+    incoming[final] = step_norm_back(0, final)
+    next(steps)
+    layer_out = assembled(outputs, arrived)
+    for value in steps:
+        first_sums[0] = value
+    grad_stream = assembled(incoming, arrived)
+
+    out, small_local, small_shared = [], [], []
+    for layer in layer_range:
+        second_sum, first_sum = second_sums[layer], first_sums[layer]
+        out.append(
+            (
+                jnp.stack([second_sum[:, :width], first_sum[:, :width]], axis=1),
+                first_sum[:, width : width + heads],
+                scatter_places(first_sum[:, width + LANES :]),
+                second_sum[:, width:].T,
             )
-            z, y0, states, end, growth = scan_forward(proj, rim, aux_all[s], seg_rows[s], const)
-            carried = chain(end, through(growth), 1, FSTATE)
-            y, squares = mix_forward(y0, z, growth, carried, gate, const)
-            squares = summed_over(squares, ("tensor",))
-            kind = F32 if layer + 1 < layers else BF16
-            partial = project_out(y, gate, squares, channels, kind, const)
-            current = streams[s] + scatter_rows(partial)
-            kept[layer][s] = {
-                "normed": normed[s], "proj": proj, "gate": gate, "rim": rim, "z": z, "y": y,
-                "states": states, "growth": growth, "carried": carried, "squares": squares,
-                "stream": streams[s],
-            }
-            streams[s] = current
-            if layer + 1 < layers:
-                scale = lax.rsqrt(jnp.mean(current * current, axis=-1, keepdims=True) + eps)
-                nexts.append(gather_rows((current * scale * gains[layer + 1]).astype(BF16)))
-            else:
-                finals.append(gather_rows(current.astype(BF16)))
-        normed = nexts
-    layer_out = jnp.stack(finals)
-
-    grad_low = [cotangent[s] for s in seq_range]
-    grads = [own_rows(cotangent[s]).astype(F32) for s in seq_range]
-    out = [None] * layers
-    small_local, small_shared = [], []
-    for layer in reversed(layer_range):
-        const = consts[layer]
-        held = kept[layer]
-        nexts, back = [], []
-        gain_sum = 0.0
-        for s in seq_range:
-            k = held[s]
-            grad, dots = grad_scaled(grad_low[s], k["y"], k["gate"], const)
-            dots = summed_over(dots, ("tensor",))
-            scaled, dgate, dy, acc, dsin = mix_backward(
-                grad, k["y"], k["gate"], k["z"], k["growth"], k["squares"], dots, channels, const
-            )
-            dend = chain(dsin, through(k["growth"]), -1, BF16)
-            dproj, wacc, hacc, tail, drim = scan_backward(
-                dy, k["z"], k["proj"], k["rim"], aux_all[s], seg_rows[s], k["states"],
-                k["carried"], k["growth"], dend, const,
-            )
-            fixed = (tail + shifted(drim, "context", -1)).astype(BF16)
-            dproj = lax.dynamic_update_slice(dproj, fixed[:, :width], (length - 8, 0))
-            dproj = lax.dynamic_update_slice(dproj, fixed[:, width:], (length - 8, width + LANES))
-            partial = mm(dproj, const["front"], NT) + mm(dgate, const["gate"], NT)
-            total = scatter_rows(partial.astype(BF16))
-            current = k["stream"]
-            scale = lax.rsqrt(jnp.mean(current * current, axis=-1, keepdims=True) + eps)
-            unit = current * scale
-            gain_sum = gain_sum + jnp.sum(total * unit, axis=0)
-            pulled = total * gains[layer]
-            shift = jnp.mean(pulled * unit, axis=-1, keepdims=True)
-            grads[s] = grads[s] + scale * (pulled - unit * shift)
-            nexts.append(gather_rows(grads[s].astype(BF16)))
-            back.append((scaled, dgate, dproj, acc, wacc, hacc))
-
-        def over_tokens(left, right):
-            return sum(mm(a, b, TN) for a, b in zip(left, right))
-
-        normed_all = [k["normed"] for k in held]
-        front_grad = over_tokens(normed_all, [b[2] for b in back])
-        gate_grad = over_tokens(normed_all, [b[1] for b in back]).astype(BF16)
-        out_grad = over_tokens(grad_low, [b[0] for b in back]).astype(BF16)
-        second_sum = ring_scatter(
-            jnp.concatenate([gate_grad, out_grad], axis=1).reshape(dp * context, rows_in, -1)
-        )
-        bc_grad = front_grad[:, width + LANES :].reshape(dp * context, tensor, rows_bc * shared)
-        bc_grad = scatter_rows_of_tensor(bc_grad)
-        bc_grad = bc_grad.reshape(model, bc_part).astype(BF16)
-        first_blocks = jnp.concatenate(
-            [front_grad[:, : width + LANES - bc_part].astype(BF16), bc_grad], axis=1
-        )
-        first_sum = ring_scatter(first_blocks.reshape(dp * context, rows_in, -1))
-        out[layer] = (
-            jnp.stack([second_sum[:, :width], first_sum[:, :width]], axis=1),
-            first_sum[:, width : width + heads],
-            first_sum[:, width + LANES - bc_part :].reshape(rows_bc, shared),
-            second_sum[:, width:].T,
-        )
-        acc, wacc, hacc = (sum(b[i] for b in back) for i in (3, 4, 5))
+        )
+        acc, wacc, hacc, dgain = (
+            sum(every(layer, name)) for name in ("acc", "wacc", "hacc", "dgain")
+        )
         small_local.append(
             jnp.concatenate(
                 [
@@ -960,12 +1596,10 @@
                 ]
             )
         )
-        small_shared.append(jnp.concatenate([wacc[:5, width:].reshape(-1), gain_sum]))
-        grad_low = nexts
-    grad_stream = jnp.stack(grad_low)
-
-    shared_sum = summed_over(jnp.stack(small_shared[::-1]), ("tensor",))
-    local_sum = jnp.stack(small_local[::-1])
+        small_shared.append(jnp.concatenate([wacc[:5, width:].reshape(-1), dgain[0]]))
+
+    shared_sum = summed_over(jnp.stack(small_shared), ("tensor",))
+    local_sum = jnp.stack(small_local)
     cut = local_sum.shape[1]
     both = summed_over(
         jnp.concatenate([local_sum, shared_sum], axis=1), ("context", "dp")
@@ -997,18 +1631,6 @@
         local_sum[:, heads_at : heads_at + heads],
         local_sum[:, 5 * width : 6 * width],
     )
-
-
-def scatter_rows_of_tensor(value):
-    index = lax.axis_index("tensor")
-    blocks, _, n = value.shape
-    for bit in range(bits("tensor")):
-        mine = (index >> bit) & 1
-        value = value.reshape(blocks, -1, 2, n)
-        sent = lax.dynamic_index_in_dim(value, 1 - mine, 2, keepdims=False).astype(BF16)
-        kept = lax.dynamic_index_in_dim(value, mine, 2, keepdims=False).astype(F32)
-        value = kept + flipped(sent, "tensor", bit).astype(F32)
-    return value.reshape(blocks, n)
 
 
 def solution(mesh):

time: 1090 us -> 814 us (0.75)
  Pallas kernels: 196 us -> 348 us
  waiting for transfers between devices: 332 us -> 186 us
  other arithmetic: 108 us -> 21.2 us
  matrix products: 77.1 us -> 0 us
  local copies, waits for them, and re-layouts: 193 us -> 116 us
  starting transfers between devices: 166 us -> 113 us
  between operations: 5.21 us -> 17.5 us
    pallas_call x28 -> x69, Pallas kernels: 196 us -> 348 us  [call(): pl.pallas_call(without_tokens, cost_estimate=pl.CostEstimate(flops=int(co...]
    dot_general x28 -> x0, matrix products: 77.1 us -> none  [mm(): return lax.dot_general(a, b, dims, preferred_element_type=F32)]
    ppermute x17 -> x16, waiting for transfers between devices: 78.3 us -> 11.9 us  [shifted(): lax.ppermute(value, axis, [(source, source + steps) for source in range(l...]
    ppermute x56 -> x21, waiting for transfers between devices: 151 us -> 87.3 us  [ring(): lax.ppermute(value, axis, [(i, (i - 1) % count) for i in range(count)])]
    ppermute x56 -> x21, starting transfers between devices: 76.9 us -> 29.2 us  [ring(): lax.ppermute(value, axis, [(i, (i - 1) % count) for i in range(count)])]
    slice x26 -> x11, local copies, waits for them, and re-layouts: 31.4 us -> 7.41 us  [the longest x1 3.62 us: second_piece(): return [input_weight[layer, :, 0], output_weight[layer].T]]
    convert_element_type x29 -> x6, other arithmetic: 28.3 us -> 4.55 us  [the longest x2 2.26 us: scattered(): return lax.psum_scatter(value[0], ('dp', 'context'), scatter_dimension=0,...]
    unnamed x568 -> x519, local copies, waits for them, and re-layouts: 47.1 us -> 69.7 us
  transfers between devices with their start and end apart: 139 -> 117, of which waited for: 57 -> 31; matrix products, arithmetic and copies ran while one was open for 29% -> 8% of each run, Pallas kernels for 16% -> 41%
where the time goes in v2:
time: 814 us; the launch traced here: 801 us
  Pallas kernels  348 us (43%)
  waiting for transfers between devices  186 us (23%)
  local copies, waits for them, and re-layouts  116 us (14%)
  starting transfers between devices  113 us (14%)
  other arithmetic  21.2 us (3%)
  between operations  17.5 us (2%)
    pallas_call x69, Pallas kernels, call(): pl.pallas_call(without_tokens, cost_estimate=pl.CostEstimate(flops=int(co...  348 us
    ppermute x21, waiting for transfers between devices, ring(): lax.ppermute(value, axis, [(i, (i - 1) % count) for i in range(count)])  87.3 us
    ppermute x51, waiting for transfers between devices, flipped(): return lax.ppermute(value, axis, [(i, i ^ 1 << bit) for i in range(count)])  83.4 us
    unnamed x519, local copies, waits for them, and re-layouts  69.7 us
    ppermute x16, starting transfers between devices, shifted(): lax.ppermute(value, axis, [(source, source + steps) for source in range(l...  36.2 us
    ppermute x51, starting transfers between devices, flipped(): return lax.ppermute(value, axis, [(i, i ^ 1 << bit) for i in range(count)])  30.8 us
    ppermute x21, starting transfers between devices, ring(): lax.ppermute(value, axis, [(i, (i - 1) % count) for i in range(count)])  29.2 us
    ppermute x24, starting transfers between devices, from_others(): lax.ppermute(value, axis, [(i, i ^ step) for i in range(count)])  17.1 us
  transfers between devices with their start and end apart: 117, of which 31 were waited for; matrix products, arithmetic and copies ran while one was open for 8% of the time, Pallas kernels for 41%

profile of v2, /device:TPU:0, one launch (start us, length us, event | category | flops | bytes accessed | tf_op | source)
XLA Modules:
  0.0 801.3 jit_solution(7602229992616381996)
XLA Ops:
  35.3 19.0 %collective-permute-done.3.refs_0_.refs_3_ = bf16[192,1152]{1,0:T(8,128)(2,1)S(1)} collective-permute-done((bf16[192,1152]{1,0:T(8,128)(2,1)S(1)}, bf16[192,1152]{1,0:T(8,128)(2,1)S(1)}, u32[]{:S(2)}, u32[]{:S(2)}) %collective-permute-start.3) | collective-permute-done | bytes 442400 | tf_op jit(solution)/shard_map/ppermute | solution.py:95
  59.6 16.1 %collective-permute-done.5.refs_0_.refs_5_ = bf16[192,1152]{1,0:T(8,128)(2,1)S(1)} collective-permute-done((bf16[192,1152]{1,0:T(8,128)(2,1)S(1)}, bf16[192,1152]{1,0:T(8,128)(2,1)S(1)}, u32[]{:S(2)}, u32[]{:S(2)}) %collective-permute-start.5) | collective-permute-done | bytes 442400 | tf_op jit(solution)/shard_map/ppermute | solution.py:95
  89.1 16.5 %collective-permute-done.7.refs_7_ = bf16[192,1152]{1,0:T(8,128)(2,1)S(1)} collective-permute-done((bf16[192,1152]{1,0:T(8,128)(2,1)}, bf16[192,1152]{1,0:T(8,128)(2,1)S(1)}, u32[]{:S(2)}, u32[]{:S(2)}) %collective-permute-start.7) | collective-permute-done | bytes 442400 | tf_op jit(solution)/shard_map/ppermute | solution.py:95
  127.0 9.9 %shard_map.293 = (f32[512,1024]{1,0:T(8,128)}, f32[512,768]{1,0:T(8,128)S(1)}, f32[4,128,768]{2,1,0:T(8,128)S(1)}, f32[128,768]{1,0:T(8,128)S(1)}, f32[512,128]{1,0:T(8,128)S(1)}) custom-call(f32[512,1152]{1,0:T(8,128)} %copy-done.175, bf16[8,1024]{1,0:T(8,128)(2,1)S(1)} %get-tuple-element.154.refs_1_.refs_8_.refs_4_, f32[512,8]{1,0:T(8,128)S(1)} %copy-done.85, ...), custom_call_target="tpu_custom_call" | custom-call | flops 4750000128 | bytes 1024 | tf_op jit(solution)/shard_map/pallas_call | solution.py:61
  161.8 9.5 %shard_map.297 = (f32[512,1024]{1,0:T(8,128)}, f32[512,768]{1,0:T(8,128)S(1)}, f32[4,128,768]{2,1,0:T(8,128)S(1)}, f32[128,768]{1,0:T(8,128)S(1)}, f32[512,128]{1,0:T(8,128)S(1)}) custom-call(f32[512,1152]{1,0:T(8,128)} %copy-done.174, bf16[8,1024]{1,0:T(8,128)(2,1)S(1)} %get-tuple-element.160.refs_2_.refs_1_.refs_4_, f32[512,8]{1,0:T(8,128)S(1)} %copy-done.81, ...), custom_call_target="tpu_custom_call" | custom-call | flops 4750000128 | bytes 1024 | tf_op jit(solution)/shard_map/pallas_call | solution.py:61
  209.5 13.6 %collective-permute-done.16.refs_3_ = f32[128,1536]{1,0:T(8,128)S(1)} collective-permute-done((f32[128,1536]{1,0:T(8,128)}, f32[128,1536]{1,0:T(8,128)S(1)}, u32[]{:S(2)}, u32[]{:S(2)}) %collective-permute-start.16) | collective-permute-done | bytes 786464 | tf_op jit(solution)/shard_map/ppermute | solution.py:80
  228.1 10.3 %collective-permute-done.22.refs_2_ = bf16[128,1536]{1,0:T(8,128)(2,1)} collective-permute-done((bf16[128,1536]{1,0:T(8,128)(2,1)}, bf16[128,1536]{1,0:T(8,128)(2,1)}, u32[]{:S(2)}, u32[]{:S(2)}) %collective-permute-start.22) | collective-permute-done | bytes 393248 | tf_op jit(solution)/shard_map/ppermute | solution.py:80
  239.9 13.6 %collective-permute-done.25.refs_3_ = f32[128,1536]{1,0:T(8,128)S(1)} collective-permute-done((f32[128,1536]{1,0:T(8,128)}, f32[128,1536]{1,0:T(8,128)S(1)}, u32[]{:S(2)}, u32[]{:S(2)}) %collective-permute-start.25) | collective-permute-done | bytes 786464 | tf_op jit(solution)/shard_map/ppermute | solution.py:80
  273.1 9.7 %shard_map.307 = (f32[512,1024]{1,0:T(8,128)}, f32[512,768]{1,0:T(8,128)S(1)}, f32[4,128,768]{2,1,0:T(8,128)S(1)}, f32[128,768]{1,0:T(8,128)}, f32[512,128]{1,0:T(8,128)S(1)}) custom-call(f32[512,1152]{1,0:T(8,128)} %copy-done.177, bf16[8,1024]{1,0:T(8,128)(2,1)S(1)} %collective-permute-done.26.refs_1_.refs_4_, f32[512,8]{1,0:T(8,128)S(1)} %copy-done.86, ...), custom_call_target="tpu_custom_call" | custom-call | flops 4750000128 | bytes 1024 | tf_op jit(solution)/shard_map/pallas_call | solution.py:61
  299.5 9.7 %shard_map.309 = (f32[512,1024]{1,0:T(8,128)}, f32[512,768]{1,0:T(8,128)S(1)}, f32[4,128,768]{2,1,0:T(8,128)S(1)}, f32[128,768]{1,0:T(8,128)}, f32[512,128]{1,0:T(8,128)S(1)}) custom-call(f32[512,1152]{1,0:T(8,128)} %copy-done.176, bf16[8,1024]{1,0:T(8,128)(2,1)S(1)} %collective-permute-done.31.refs_1_.refs_4_, f32[512,8]{1,0:T(8,128)S(1)} %copy-done.82, ...), custom_call_target="tpu_custom_call" | custom-call | flops 4750000128 | bytes 1024 | tf_op jit(solution)/shard_map/pallas_call | solution.py:61
  371.2 10.5 %shard_map.318.refs_16_ = bf16[1536,1536]{1,0:T(8,128)(2,1)} custom-call(s32[2]{0:T(128)} %pad_add_fusion.1.refs_0_, bf16[512,1536]{1,0:T(8,128)(2,1)} %copy-done.31, bf16[512,1536]{1,0:T(8,128)(2,1)} %copy-done.33, bf16[2,512,1536]{2,1,0:T(8,128)(2,1)} %refs_4_.1, bf16[2,512,1536]{2,1,0:T(8,128)(2,1)} %refs_4_.1, bf16[512,768]{1,0:T(8,128)(2,1)} %copy-done.63, ...), custom_call_target="tpu_custom_call" | custom-call | flops 5000000000 | bytes 1024 | tf_op jit(solution)/shard_map/pallas_call | solution.py:61
  384.6 18.3 %shard_map.319 = (bf16[512,1152]{1,0:T(8,128)(2,1)S(1)}, f32[8,1024]{1,0:T(8,128)S(1)}, f32[8,128]{1,0:T(8,128)S(1)}, f32[16,1024]{1,0:T(8,128)S(1)}, f32[16,1024]{1,0:T(8,128)S(1)}) custom-call(f32[512,768]{1,0:T(8,128)S(1)} %copy-done.182, f32[512,1024]{1,0:T(8,128)} %get-tuple-element.181.refs_1_.refs_3_.refs_4_, f32[512,1152]{1,0:T(8,128)} %copy-done.177, ...), custom_call_target="tpu_custom_call" | custom-call | flops 8999999488 | bytes 1024 | tf_op jit(solution)/shard_map/pallas_call | solution.py:61
  410.7 8.5 %shard_map.321 = (bf16[2,128,1536]{2,1,0:T(8,128)(2,1)}, bf16[2,128,1536]{2,1,0:T(8,128)(2,1)S(1)}, bf16[512,1152]{1,0:T(8,128)(2,1)S(1)}) custom-call(s32[4]{0:T(128)S(1)} %copy-done.143, bf16[512,1152]{1,0:T(8,128)(2,1)S(1)} %get-tuple-element.212.refs_1_, bf16[512,768]{1,0:T(8,128)(2,1)S(1)} %copy-done.64, f32[16,1024]{1,0:T(8,128)S(1)} %get-tuple-element.213.refs_3_, ...), custom_call_target="tpu_custom_call" | custom-call | flops 3800000000 | bytes 1024 | tf_op jit(solution)/shard_map/pallas_call | solution.py:61
  430.0 18.4 %shard_map.324 = (bf16[512,1152]{1,0:T(8,128)(2,1)S(1)}, f32[8,1024]{1,0:T(8,128)S(1)}, f32[8,128]{1,0:T(8,128)S(1)}, f32[16,1024]{1,0:T(8,128)S(1)}, f32[16,1024]{1,0:T(8,128)S(1)}) custom-call(f32[512,768]{1,0:T(8,128)S(1)} %copy-done.179, f32[512,1024]{1,0:T(8,128)} %get-tuple-element.191.refs_1_.refs_3_.refs_4_, f32[512,1152]{1,0:T(8,128)} %copy-done.176, ...), custom_call_target="tpu_custom_call" | custom-call | flops 8999999488 | bytes 1024 | tf_op jit(solution)/shard_map/pallas_call | solution.py:61
  469.4 9.5 %collective-permute-done.52.refs_2_ = bf16[128,1536]{1,0:T(8,128)(2,1)S(1)} collective-permute-done((bf16[128,1536]{1,0:T(8,128)(2,1)S(1)}, bf16[128,1536]{1,0:T(8,128)(2,1)S(1)}, u32[]{:S(2)}, u32[]{:S(2)}) %collective-permute-start.52) | collective-permute-done | bytes 393248 | tf_op jit(solution)/shard_map/ppermute | solution.py:80
  496.4 8.5 %collective-permute-done.59.refs_2_ = bf16[128,1536]{1,0:T(8,128)(2,1)S(1)} collective-permute-done((bf16[128,1536]{1,0:T(8,128)(2,1)}, bf16[128,1536]{1,0:T(8,128)(2,1)S(1)}, u32[]{:S(2)}, u32[]{:S(2)}) %collective-permute-start.59) | collective-permute-done | bytes 393248 | tf_op jit(solution)/shard_map/ppermute | solution.py:80
  504.8 8.7 %shard_map.332.refs_9_ = bf16[1536,1152]{1,0:T(8,128)(2,1)} custom-call(s32[2]{0:T(128)} %pad_add_fusion.1.refs_0_, bf16[512,1536]{1,0:T(8,128)(2,1)} %copy-done.31, bf16[512,1536]{1,0:T(8,128)(2,1)} %copy-done.33, bf16[512,1152]{1,0:T(8,128)(2,1)} %copy-done.183, bf16[512,1152]{1,0:T(8,128)(2,1)} %copy-done.185, f32[8,1536]{1,0:T(8,128)} %copy-done.173), custom_call_target="tpu_custom_call" | custom-call | flops 5000000000 | bytes 1024 | tf_op jit(solution)/shard_map/pallas_call | solution.py:61
  540.4 11.8 %shard_map.336 = (bf16[4,192,1536]{2,1,0:T(8,128)(2,1)}, bf16[192,1536]{1,0:T(8,128)(2,1)}, bf16[192,1536]{1,0:T(8,128)(2,1)}, bf16[192,1536]{1,0:T(8,128)(2,1)}, bf16[192,1536]{1,0:T(8,128)(2,1)}) custom-call(s32[2]{0:T(128)} %pad_add_fusion.1.refs_0_, bf16[512,1536]{1,0:T(8,128)(2,1)} %copy-done.27, bf16[512,1536]{1,0:T(8,128)(2,1)} %copy-done.28, ...), custom_call_target="tpu_custom_call" | custom-call | flops 5000000000 | bytes 1024 | tf_op jit(solution)/shard_map/pallas_call | solution.py:61
  556.3 18.4 %shard_map.337 = (bf16[512,1152]{1,0:T(8,128)(2,1)S(1)}, f32[8,1024]{1,0:T(8,128)S(1)}, f32[8,128]{1,0:T(8,128)S(1)}, f32[16,1024]{1,0:T(8,128)S(1)}, f32[16,1024]{1,0:T(8,128)S(1)}) custom-call(f32[512,768]{1,0:T(8,128)S(1)} %get-tuple-element.249.refs_0_, f32[512,1024]{1,0:T(8,128)} %get-tuple-element.156.refs_1_.refs_3_.refs_4_, f32[512,1152]{1,0:T(8,128)} %copy-done.175, ...), custom_call_target="tpu_custom_call" | custom-call | flops 8999999488 | bytes 1024 | tf_op jit(solution)/shard_map/pallas_call | solution.py:61
  599.2 18.4 %shard_map.343 = (bf16[512,1152]{1,0:T(8,128)(2,1)S(1)}, f32[8,1024]{1,0:T(8,128)S(1)}, f32[8,128]{1,0:T(8,128)S(1)}, f32[16,1024]{1,0:T(8,128)S(1)}, f32[16,1024]{1,0:T(8,128)S(1)}) custom-call(f32[512,768]{1,0:T(8,128)S(1)} %get-tuple-element.258.refs_0_, f32[512,1024]{1,0:T(8,128)} %get-tuple-element.168.refs_1_.refs_3_.refs_4_, f32[512,1152]{1,0:T(8,128)} %copy-done.174, ...), custom_call_target="tpu_custom_call" | custom-call | flops 8999999488 | bytes 1024 | tf_op jit(solution)/shard_map/pallas_call | solution.py:61
  641.8 8.5 %collective-permute-done.84.refs_1_ = bf16[192,1536]{1,0:T(8,128)(2,1)} collective-permute-done((bf16[192,1536]{1,0:T(8,128)(2,1)}, bf16[192,1536]{1,0:T(8,128)(2,1)}, u32[]{:S(2)}, u32[]{:S(2)}) %collective-permute-start.84) | collective-permute-done | bytes 589856 | tf_op jit(solution)/shard_map/ppermute | solution.py:95
  654.8 10.1 %shard_map.349 = (bf16[4,192,1152]{2,1,0:T(8,128)(2,1)}, bf16[192,1152]{1,0:T(8,128)(2,1)}, bf16[192,1152]{1,0:T(8,128)(2,1)}, bf16[192,1152]{1,0:T(8,128)(2,1)}, bf16[192,1152]{1,0:T(8,128)(2,1)}) custom-call(s32[2]{0:T(128)} %pad_add_fusion.1.refs_0_, bf16[512,1536]{1,0:T(8,128)(2,1)} %copy-done.27, bf16[512,1536]{1,0:T(8,128)(2,1)} %copy-done.28, ...), custom_call_target="tpu_custom_call" | custom-call | flops 5000000000 | bytes 1024 | tf_op jit(solution)/shard_map/pallas_call | solution.py:61
  714.4 10.2 %collective-permute-done.110 = f32[2,7460]{1,0:T(2,128)S(1)} collective-permute-done((f32[2,7460]{1,0:T(2,128)S(1)}, f32[2,7460]{1,0:T(2,128)S(1)}, u32[]{:S(2)}, u32[]{:S(2)}) %collective-permute-start.110) | collective-permute-done | bytes 59712 | tf_op jit(solution)/shard_map/ppermute | solution.py:80
  755.3 17.8 %collective-permute-done.102.refs_2_ = bf16[192,1152]{1,0:T(8,128)(2,1)S(1)} collective-permute-done((bf16[192,1152]{1,0:T(8,128)(2,1)S(1)}, bf16[192,1152]{1,0:T(8,128)(2,1)S(1)}, u32[]{:S(2)}, u32[]{:S(2)}) %collective-permute-start.102) | collective-permute-done | bytes 442400 | tf_op jit(solution)/shard_map/ppermute | solution.py:95
  (968 shorter events, 478.4 us)
Async XLA Ops:
  7.2 145.2 %all-gather.4.cloned.1.call-start = ((), (), s32[]{:S(2)}) async-start(), calls=%async_computation.2 | async-start | bytes 5308416 | tf_op jit(solution)/shard_map/all_gather | solution.py:1335
  11.9 246.4 %all-gather.6.cloned.1.call-start = ((), (), s32[]{:S(2)}) async-start(), calls=%async_computation.3 | async-start | bytes 3981312 | tf_op jit(solution)/shard_map/all_gather | solution.py:1332
  21.7 295.0 %all-gather.8.cloned.1.call-start = ((), (), s32[]{:S(2)}) async-start(), calls=%async_computation.4 | async-start | bytes 5308416 | tf_op jit(solution)/shard_map/all_gather | solution.py:1335
  23.3 95.2 %collective-permute-start.9 = (bf16[2,16,1536]{2,1,0:T(8,128)(2,1)}, bf16[2,16,1536]{2,1,0:T(8,128)(2,1)S(1)}, u32[]{:S(2)}, u32[]{:S(2)}) collective-permute-start(bf16[2,16,1536]{2,1,0:T(8,128)(2,1)} %slice.295), channel_id=1, source_target_pairs={{0,4},{1,5},{2,6},{3,7},{8,12},{9,13},{10,14},{11,15},{16,20},{17,... | collective-permute-start | bytes 294920 | tf_op jit(solution)/shard_map/ppermute | solution.py:90
  27.0 32.3 %collective-permute-start.10 = (s32[2,3]{1,0:T(2,128)S(1)}, s32[2,3]{1,0:T(2,128)S(1)}, u32[]{:S(2)}, u32[]{:S(2)}) collective-permute-start(s32[2,3]{1,0:T(2,128)S(1)} %slice.296), channel_id=1, source_target_pairs={{0,4},{1,5},{2,6},{3,7},{8,12},{9,13},{10,14},{11,15},{16,20},{17,... | collective-permute-start | bytes 80 | tf_op jit(solution)/shard_map/ppermute | solution.py:90
  29.1 753.7 %reduce-scatter.3.cloned.1.call-start = ((), (), s32[]{:S(2)}) async-start(), calls=%async_computation.5 | async-start | bytes 5308416 | tf_op jit(solution)/shard_map/reduce_scatter | solution.py:1501
  76.5 29.0 %collective-permute-start.7 = (bf16[192,1152]{1,0:T(8,128)(2,1)}, bf16[192,1152]{1,0:T(8,128)(2,1)S(1)}, u32[]{:S(2)}, u32[]{:S(2)}) collective-permute-start(bf16[192,1152]{1,0:T(8,128)(2,1)} %shard_map.290.refs_9_), channel_id=1, source_target_pairs={{0,24},{8,0},{16,8},{24,16},{1,25},{9,1},{17,9},{25,17},{2,26},{10... | collective-permute-start | bytes 1327112 | tf_op jit(solution)/shard_map/ppermute | solution.py:95
  226.6 26.9 %collective-permute-start.25 = (f32[128,1536]{1,0:T(8,128)}, f32[128,1536]{1,0:T(8,128)S(1)}, u32[]{:S(2)}, u32[]{:S(2)}) collective-permute-start(f32[128,1536]{1,0:T(8,128)} %shard_map.303.refs_5_), channel_id=1, source_target_pairs={{0,2},{1,3},{2,0},{3,1},{4,6},{5,7},{6,4},{7,5},{8,10},{9,11},{10,... | collective-permute-start | bytes 2359304 | tf_op jit(solution)/shard_map/ppermute | solution.py:80
  228.1 30.1 %collective-permute-start.23 = (bf16[128,1536]{1,0:T(8,128)(2,1)}, bf16[128,1536]{1,0:T(8,128)(2,1)}, u32[]{:S(2)}, u32[]{:S(2)}) collective-permute-start(bf16[128,1536]{1,0:T(8,128)(2,1)} %get-tuple-element.176.refs_5_.refs_1_), channel_id=1, source_target_pairs={{0,1},{1,0},{2,3},{3,2},{4,5},{5,4},{6,7},{7,6},{8,9},{9,8},{10,11... | collective-permute-start | bytes 1179656 | tf_op jit(solution)/shard_map/ppermute | solution.py:80
  422.4 363.8 %reduce-scatter.5.cloned.1.call-start = ((), (), s32[]{:S(2)}) async-start(), calls=%async_computation.6 | async-start | bytes 3981312 | tf_op jit(solution)/shard_map/reduce_scatter | solution.py:1501
  424.7 25.8 %collective-permute-start.50 = (bf16[128,1536]{1,0:T(8,128)(2,1)S(1)}, bf16[128,1536]{1,0:T(8,128)(2,1)S(1)}, u32[]{:S(2)}, u32[]{:S(2)}) collective-permute-start(bf16[128,1536]{1,0:T(8,128)(2,1)S(1)} %shard_map.322.refs_2_), channel_id=1, source_target_pairs={{0,2},{1,3},{2,0},{3,1},{4,6},{5,7},{6,4},{7,5},{8,10},{9,11},{10,... | collective-permute-start | bytes 1179656 | tf_op jit(solution)/shard_map/ppermute | solution.py:80
  494.1 82.2 %collective-permute-start.49 = (bf16[128,1536]{1,0:T(8,128)(2,1)}, bf16[128,1536]{1,0:T(8,128)(2,1)}, u32[]{:S(2)}, u32[]{:S(2)}) collective-permute-start(bf16[128,1536]{1,0:T(8,128)(2,1)} %shard_map.323.refs_16_), channel_id=1, source_target_pairs={{0,2},{1,3},{2,0},{3,1},{4,6},{5,7},{6,4},{7,5},{8,10},{9,11},{10,... | collective-permute-start | bytes 1179656 | tf_op jit(solution)/shard_map/ppermute | solution.py:80
  494.6 28.4 %collective-permute-start.62 = (f32[8,512]{1,0:T(8,128)}, f32[8,512]{1,0:T(8,128)}, u32[]{:S(2)}, u32[]{:S(2)}) collective-permute-start(f32[8,512]{1,0:T(8,128)} %get-tuple-element.232.refs_6_.refs_12_), channel_id=1, source_target_pairs={{0,1},{1,0},{2,3},{3,2},{4,5},{5,4},{6,7},{7,6},{8,9},{9,8},{10,11... | collective-permute-start | bytes 49160 | tf_op jit(solution)/shard_map/ppermute | solution.py:232
  494.6 28.4 %collective-permute-start.63 = (f32[8,512]{1,0:T(8,128)}, f32[8,512]{1,0:T(8,128)}, u32[]{:S(2)}, u32[]{:S(2)}) collective-permute-start(f32[8,512]{1,0:T(8,128)} %get-tuple-element.232.refs_6_.refs_12_), channel_id=1, source_target_pairs={{0,2},{1,3},{2,0},{3,1},{4,6},{5,7},{6,4},{7,5},{8,10},{9,11},{10,... | collective-permute-start | bytes 49160 | tf_op jit(solution)/shard_map/ppermute | solution.py:232
  515.3 63.6 %collective-permute-start.73 = (bf16[128,1536]{1,0:T(8,128)(2,1)}, bf16[128,1536]{1,0:T(8,128)(2,1)S(1)}, u32[]{:S(2)}, u32[]{:S(2)}) collective-permute-start(bf16[128,1536]{1,0:T(8,128)(2,1)} %copy-done.204), channel_id=1, source_target_pairs={{0,2},{1,3},{2,0},{3,1},{4,6},{5,7},{6,4},{7,5},{8,10},{9,11},{10,... | collective-permute-start | bytes 1179656 | tf_op jit(solution)/shard_map/ppermute | solution.py:80
  531.0 24.2 %collective-permute-start.69 = (bf16[128,768]{1,0:T(8,128)(2,1)S(1)}, bf16[128,768]{1,0:T(8,128)(2,1)S(1)}, u32[]{:S(2)}, u32[]{:S(2)}) collective-permute-start(bf16[128,768]{1,0:T(8,128)(2,1)S(1)} %get-tuple-element.251), channel_id=1, source_target_pairs={{4,0},{5,1},{6,2},{7,3},{12,8},{13,9},{14,10},{15,11},{20,16},{21,... | collective-permute-start | bytes 589832 | tf_op jit(solution)/shard_map/ppermute | solution.py:90
  590.8 29.8 %collective-permute-start.81 = (bf16[192,1536]{1,0:T(8,128)(2,1)S(1)}, bf16[192,1536]{1,0:T(8,128)(2,1)S(1)}, u32[]{:S(2)}, u32[]{:S(2)}) collective-permute-start(bf16[192,1536]{1,0:T(8,128)(2,1)S(1)} %copy-done.252), channel_id=1, source_target_pairs={{0,4},{4,0},{1,5},{5,1},{2,6},{6,2},{3,7},{7,3},{8,12},{12,8},{9,1... | collective-permute-start | bytes 1769480 | tf_op jit(solution)/shard_map/ppermute | solution.py:95
  593.6 27.1 %collective-permute-start.82 = (bf16[192,1536]{1,0:T(8,128)(2,1)S(1)}, bf16[192,1536]{1,0:T(8,128)(2,1)S(1)}, u32[]{:S(2)}, u32[]{:S(2)}) collective-permute-start(bf16[192,1536]{1,0:T(8,128)(2,1)S(1)} %shard_map.338.refs_4_), channel_id=1, source_target_pairs={{0,24},{8,0},{16,8},{24,16},{1,25},{9,1},{17,9},{25,17},{2,26},{10... | collective-permute-start | bytes 1769480 | tf_op jit(solution)/shard_map/ppermute | solution.py:95
  593.9 25.0 %collective-permute-start.83 = (bf16[128,1536]{1,0:T(8,128)(2,1)S(1)}, bf16[128,1536]{1,0:T(8,128)(2,1)S(1)}, u32[]{:S(2)}, u32[]{:S(2)}) collective-permute-start(bf16[128,1536]{1,0:T(8,128)(2,1)S(1)} %shard_map.342.refs_16_), channel_id=1, source_target_pairs={{0,2},{1,3},{2,0},{3,1},{4,6},{5,7},{6,4},{7,5},{8,10},{9,11},{10,... | collective-permute-start | bytes 1179656 | tf_op jit(solution)/shard_map/ppermute | solution.py:80
  636.5 43.8 %collective-permute-start.89 = (bf16[192,1536]{1,0:T(8,128)(2,1)}, bf16[192,1536]{1,0:T(8,128)(2,1)S(1)}, u32[]{:S(2)}, u32[]{:S(2)}) collective-permute-start(bf16[192,1536]{1,0:T(8,128)(2,1)} %get-tuple-element.252.refs_16_), channel_id=1, source_target_pairs={{0,4},{4,0},{1,5},{5,1},{2,6},{6,2},{3,7},{7,3},{8,12},{12,8},{9,1... | collective-permute-start | bytes 1769480 | tf_op jit(solution)/shard_map/ppermute | solution.py:95
  641.0 47.0 %collective-permute-start.92 = (bf16[128,1536]{1,0:T(8,128)(2,1)}, bf16[128,1536]{1,0:T(8,128)(2,1)}, u32[]{:S(2)}, u32[]{:S(2)}) collective-permute-start(bf16[128,1536]{1,0:T(8,128)(2,1)} %shard_map.347.refs_3_), channel_id=1, source_target_pairs={{0,2},{1,3},{2,0},{3,1},{4,6},{5,7},{6,4},{7,5},{8,10},{9,11},{10,... | collective-permute-start | bytes 1179656 | tf_op jit(solution)/shard_map/ppermute | solution.py:80
  654.8 26.4 %collective-permute-start.90 = (bf16[192,1536]{1,0:T(8,128)(2,1)}, bf16[192,1536]{1,0:T(8,128)(2,1)S(1)}, u32[]{:S(2)}, u32[]{:S(2)}) collective-permute-start(bf16[192,1536]{1,0:T(8,128)(2,1)} %shard_map.348.refs_5_), channel_id=1, source_target_pairs={{0,24},{8,0},{16,8},{24,16},{1,25},{9,1},{17,9},{25,17},{2,26},{10... | collective-permute-start | bytes 1769480 | tf_op jit(solution)/shard_map/ppermute | solution.py:95
  747.4 26.0 %collective-permute-start.94 = (bf16[128,1536]{1,0:T(8,128)(2,1)}, bf16[128,1536]{1,0:T(8,128)(2,1)S(1)}, u32[]{:S(2)}, u32[]{:S(2)}) collective-permute-start(bf16[128,1536]{1,0:T(8,128)(2,1)} %get-tuple-element.280.refs_1_), channel_id=1, source_target_pairs={{0,1},{1,0},{2,3},{3,2},{4,5},{5,4},{6,7},{7,6},{8,9},{9,8},{10,11... | collective-permute-start | bytes 1179656 | tf_op jit(solution)/shard_map/ppermute | solution.py:80
  747.5 25.9 %collective-permute-start.95 = (bf16[128,1536]{1,0:T(8,128)(2,1)}, bf16[128,1536]{1,0:T(8,128)(2,1)S(1)}, u32[]{:S(2)}, u32[]{:S(2)}) collective-permute-start(bf16[128,1536]{1,0:T(8,128)(2,1)} %collective-permute-done.93.refs_2_), channel_id=1, source_target_pairs={{0,1},{1,0},{2,3},{3,2},{4,5},{5,4},{6,7},{7,6},{8,9},{9,8},{10,11... | collective-permute-start | bytes 1179656 | tf_op jit(solution)/shard_map/ppermute | solution.py:80
  (348 other events, 3938.3 us)
Sparse Core Ops, SparseCore 0:
  12.0 102.4 all-gather.3
  116.7 65.5 all-gather.5
  184.5 79.3 all-gather.7
  422.5 98.3 reduce-scatter.2
  675.8 102.0 reduce-scatter.4

commit v3 on v2

--- a/solution.py
+++ b/solution.py
@@ -18,8 +18,6 @@
 TN = (((0,), (0,)), ((), ()))
 NO_LINK = -1e30
 COST_SCALE = 0.5
-FWD_WIDE = True
-BWD_WIDE = True
 
 
 def mm(a, b, dims=NN):
@@ -135,15 +133,23 @@
     return lax.dynamic_slice_in_dim(value, lax.axis_index("tensor") * rows, rows, 0)
 
 
-def gathered(value):
-    pieces = [value]
-    for bit in reversed(range(bits("tensor"))):
-        pieces = pieces + [flipped(piece, "tensor", bit) for piece in pieces]
-    return pieces
-
-
 def relay_kernel(from_ref, to_ref):
     to_ref[...] = from_ref[...]
+
+
+def widen_kernel(from_ref, to_ref):
+    to_ref[...] = from_ref[...].astype(F32)
+
+
+def widened(value):
+    return kernel_call(
+        widen_kernel,
+        grid=(1,),
+        in_specs=[fixed_block(value.shape)],
+        out_specs=fixed_block(value.shape),
+        out_shape=jax.ShapeDtypeStruct(value.shape, F32),
+        compiler_params=params(),
+    )(value)
 
 
 def relayed(piece, *tokens):
@@ -158,17 +164,21 @@
     )(piece)
 
 
-def ring_pieces(piece):
-    table, arrived = [], piece
-    for k in range(lax.axis_size("dp")):
-        if k:
-            source = relayed(arrived, table[k - 2][-1]) if k > 1 else arrived
-            arrived = ring(source, "dp")
+def ring_pieces(table, piece):
+    def over_context(arrived):
         row = [arrived]
         for _ in range(lax.axis_size("context") - 1):
             row.append(ring(row[-1], "context"))
-        table.append(row)
-    return table
+        return row
+
+    arrived = piece
+    table.append(over_context(piece))
+    for k in range(1, lax.axis_size("dp")):
+        arrived = ring(arrived, "dp")
+        yield
+        arrived = relayed(arrived, table[k - 1][-1])
+        table.append(over_context(arrived))
+    yield
 
 
 def place_kernel(count, widths, tile_at, index_ref, *refs):
@@ -235,15 +245,137 @@
 
 
 def scatter_places(value):
-    index = lax.axis_index("tensor")
-    value = value.reshape(-1, value.shape[0] // lax.axis_size("tensor"), value.shape[1])
-    for bit in range(bits("tensor")):
-        mine = (index >> bit) & 1
-        value = value.reshape(-1, 2, *value.shape[1:])
-        sent = lax.dynamic_index_in_dim(value, 1 - mine, 1, keepdims=False)
-        kept = lax.dynamic_index_in_dim(value, mine, 1, keepdims=False)
-        value = kept + flipped(sent, "tensor", bit)
-    return value[0]
+    count, index = lax.axis_size("tensor"), lax.axis_index("tensor")
+    value = value.reshape(count, -1, value.shape[1])
+    total = lax.dynamic_index_in_dim(value, index, 0, keepdims=False)
+    for step in range(1, count):
+        sent = lax.dynamic_index_in_dim(value, index ^ step, 0, keepdims=False)
+        total = total + lax.ppermute(sent, "tensor", [(i, i ^ step) for i in range(count)])
+    return total
+
+
+def pack_kernel(layers, sequences, width, *refs):
+    inputs, (local_ref, shared_ref) = refs[:-2], refs[-2:]
+    local_ref[...] = jnp.zeros_like(local_ref)
+    shared_ref[...] = jnp.zeros_like(shared_ref)
+    for layer in range(layers):
+        mine = inputs[layer * sequences * 4 : (layer + 1) * sequences * 4]
+        taps, acc, small, gain = (sum(one[...] for one in mine[i::4]) for i in range(4))
+        local_ref[layer, 0:5, :width] = taps[0:5, :width]
+        local_ref[layer, 5:7, :width] = acc[0:2]
+        local_ref[layer, 0:2, width:] = small[0:2]
+        shared = taps.shape[1] - width
+        shared_ref[layer, 0:5, :shared] = taps[0:5, width:]
+        for i, (row, at) in enumerate(gain_places(gain.shape[1], shared)):
+            shared_ref[layer, row : row + 1, at : at + shared] = gain[
+                0:1, i * shared : (i + 1) * shared
+            ]
+
+
+def gain_places(model, shared):
+    places = [(5, 0), (6, 0), (7, 0)] + [(row, shared) for row in range(8)]
+    return places[: model // shared]
+
+
+def share_kernel(local_ref, *refs):
+    cut = local_ref.shape[2]
+    refs[-1][:, :, :cut] = local_ref[...]
+    refs[-1][:, :, cut:] = sum(one[...] for one in refs[:-1])
+
+
+def unpack_kernel(width, heads, shared, model, place_ref, a_ref, b_ref, red_ref, *outs):
+    taps_x, bias_x, dt_bias, rate, skip, gate_gain, taps_bc, bias_bc, pre_gain = outs
+    own_conv, own_gain = taps_bc.shape[2], pre_gain.shape[1]
+    cut = width + LANES
+    for layer in range(a_ref.shape[0]):
+        total = a_ref[layer] + b_ref[layer]
+        at = slice(layer, layer + 1)
+        taps_x[layer] = total[0:4, :width]
+        bias_x[at] = total[4:5, :width]
+        gate_gain[at] = total[5:6, :width]
+        dt_bias[at] = total[0:1, width : width + heads]
+        rate[at] = total[1:2, width : width + heads]
+        skip[at] = split_dot(total[:, :width], red_ref[...])[6:7, :heads]
+        part = total[:, cut : cut + shared]
+        part = pltpu.roll(part, shared - place_ref[0] * own_conv, axis=1)
+        taps_bc[layer] = part[0:4, :own_conv]
+        bias_bc[at] = part[4:5, :own_conv]
+        rows = [
+            total[row : row + 1, cut + col : cut + col + shared]
+            for row, col in gain_places(model, shared)
+        ]
+        gain = jnp.broadcast_to(jnp.concatenate(rows, axis=1), (8, model))
+        gain = pltpu.roll(gain, model - place_ref[0] * own_gain, axis=1)
+        pre_gain[at] = gain[0:1, :own_gain]
+
+
+def add_kernel(*refs):
+    refs[-1][...] = sum(one[...] for one in refs[:-1])
+
+
+def add_up(terms):
+    shape = terms[0].shape
+    return kernel_call(
+        add_kernel,
+        cost=1.0,
+        grid=(1,),
+        in_specs=[whole(shape)] * len(terms),
+        out_specs=whole(shape),
+        out_shape=jax.ShapeDtypeStruct(shape, terms[0].dtype),
+        compiler_params=params(),
+    )(*terms)
+
+
+def small_sums(work, width, heads, model, red):
+    layers, sequences = len(work), len(work[0])
+    inputs = [k[name] for ks in work for k in ks for name in ("wacc", "acc", "hacc", "dgain")]
+    shared = inputs[0].shape[1] - width
+    shapes = [(layers, 8, width + LANES), (layers, 8, 2 * shared)]
+    own, every = kernel_call(
+        functools.partial(pack_kernel, layers, sequences, width),
+        grid=(1,),
+        in_specs=[whole(one.shape) for one in inputs],
+        out_specs=[whole(shape) for shape in shapes],
+        out_shape=[jax.ShapeDtypeStruct(shape, F32) for shape in shapes],
+        compiler_params=params(),
+    )(*inputs)
+    parts = from_others(every, "tensor")
+    yield None
+    shape = (layers, 8, width + LANES + 2 * shared)
+    total = kernel_call(
+        share_kernel,
+        cost=1.0,
+        grid=(1,),
+        in_specs=[whole(one.shape) for one in (own, *parts)],
+        out_specs=whole(shape),
+        out_shape=jax.ShapeDtypeStruct(shape, F32),
+        compiler_params=params(),
+    )(own, *parts)
+    hops = [(axis, bit) for axis in ("context", "dp") for bit in range(bits(axis))]
+    for axis, bit in hops:
+        other = flipped(total, axis, bit)
+        yield None
+        if (axis, bit) != hops[-1]:
+            total = add_up([total, other])
+    devices = lax.axis_size("dp") * lax.axis_size("context") * lax.axis_size("tensor")
+    place = lax.axis_index("dp") * lax.axis_size("context") + lax.axis_index("context")
+    place = place * lax.axis_size("tensor") + lax.axis_index("tensor")
+    own_conv, own_gain = shared // devices, model // devices
+    shapes = [
+        (layers, 4, width), (layers, width), (layers, heads), (layers, heads), (layers, heads),
+        (layers, width), (layers, 4, own_conv), (layers, own_conv), (layers, own_gain),
+    ]
+    yield kernel_call(
+        functools.partial(unpack_kernel, width, heads, shared, model),
+        grid_spec=pltpu.PrefetchScalarGridSpec(
+            num_scalar_prefetch=1,
+            grid=(1,),
+            in_specs=[fixed_block(one.shape) for one in (total, other, red)],
+            out_specs=[fixed_block(one) for one in shapes],
+        ),
+        out_shape=[jax.ShapeDtypeStruct(one, F32) for one in shapes],
+        compiler_params=params(),
+    )(place.astype(jnp.int32)[None], total, other, red)
 
 
 def silu_parts(value):
@@ -268,12 +400,8 @@
     return mm(a_high, b_high, dims) + (mm(a_low, b_high, dims) + mm(a_high, b_low, dims))
 
 
-def fmm(a, b, dims=NN):
-    return wide_mm(a, b, dims) if FWD_WIDE else mm(a.astype(BF16), b.astype(BF16), dims)
-
-
-def bmm(a, b, dims=NN):
-    return wide_mm(a, b, dims) if BWD_WIDE else mm(a.astype(BF16), b.astype(BF16), dims)
+def low_mm(a, b, dims=NN):
+    return mm(a.astype(BF16), b.astype(BF16), dims)
 
 
 def iota(axis):
@@ -306,48 +434,42 @@
     return pl.BlockSpec(shape, lambda i, *_: (0,) * len(shape))
 
 
-def project_kernel(
-    norm, count, width, order_ref, *refs
-):
+def project_kernel(norm, count, width, order_ref, *refs):
     pieces, rest = refs[:count], refs[count:]
     if norm:
         gain_ref, halo_ref, rest = rest[0], rest[1], rest[2:]
-    w_refs, (normed_ref, proj_ref, rim_ref) = rest[:3], rest[3:]
+    w_ref, normed_ref, proj_ref, rim_ref, halo = rest
     step = pl.program_id(0)
-
-    def run(rows):
-        normed_ref[...] = rows
-        for j, w_ref in enumerate(w_refs):
-            size = w_ref.shape[1]
-            proj_ref[:, j * size : (j + 1) * size] = mm(rows, w_ref[...])
-
-    if norm:
-        wide = pieces[0][0].astype(F32)
-        run((wide * row_norm(wide) * gain_ref[...]).astype(BF16))
-
-        @pl.when(step == 0)
-        def _():
-            halo = halo_ref[0].astype(F32)
-            halo = (halo * row_norm(halo) * gain_ref[...]).astype(BF16)
-            row = jnp.concatenate([mm(halo, w_ref[...]) for w_ref in w_refs], axis=1)
-            rim_ref[:, :width] = row[8:, :width].astype(BF16)
-            rim_ref[:, width:] = row[8:, width + LANES :].astype(BF16)
-
-    else:
-        for m in range(count):
-
-            @pl.when(step == m)
-            def _(m=m):
-                run(pieces[m][...])
-
-    if norm:
-        return
-
-    @pl.when(order_ref[step] == pl.num_programs(0) - 1)
+    length, size = proj_ref.shape
+
+    @pl.when(step == 0)
     def _():
-        tail = proj_ref[CHUNK - 16 :].astype(BF16)
-        rim_ref[:, :width] = tail[8:, :width]
-        rim_ref[:, width:] = tail[8:, width + LANES :]
+        for m in range(length // CHUNK):
+            if norm:
+                wide = pieces[0][0, m * CHUNK : (m + 1) * CHUNK].astype(F32)
+                rows = (wide * row_norm(wide) * gain_ref[...]).astype(BF16)
+                normed_ref[m * CHUNK : (m + 1) * CHUNK] = rows
+            else:
+                place = pl.ds(pl.multiple_of(order_ref[m] * CHUNK, CHUNK), CHUNK)
+                normed_ref[place] = pieces[m][...]
+        if norm:
+            wide = halo_ref[0].astype(F32)
+            halo[...] = (wide * row_norm(wide) * gain_ref[...]).astype(BF16)
+        else:
+            halo[...] = normed_ref[length - 16 :]
+
+    weight = w_ref[...]
+    proj_ref[...] = mm(normed_ref[...], weight)
+    tail = mm(halo[...], weight)[8:].astype(BF16)
+    for i in range(width // size):
+
+        @pl.when(step == i)
+        def _(i=i):
+            rim_ref[:, i * size : (i + 1) * size] = tail
+
+    @pl.when(step == width // size)
+    def _():
+        rim_ref[:, width:] = tail[:, LANES:]
 
 
 def project(source, gain, order, front, width, total):
@@ -359,28 +481,28 @@
         model, length = stream.shape[2], stream.shape[1]
         inputs, count = [stream, gain, halo], 1
         specs = [
-            pl.BlockSpec((1, CHUNK, model), lambda i, order: (sequence, order[i], 0)),
+            pl.BlockSpec((1, length, model), lambda i, order: (sequence, 0, 0)),
             fixed_block((1, model)),
             pl.BlockSpec((1, 16, model), lambda i, order: (sequence, 0, 0)),
         ]
     else:
-        model, count = source[0].shape[1], len(source)
+        model, count = source[0][0].shape[1], len(source)
         length = count * CHUNK
-        inputs = list(source)
-        specs = [fixed_block((CHUNK, model))] * count
+        inputs, specs = [one for one, _ in source], piece_specs(source, CHUNK)
     conv = total - LANES
     return kernel_call(
         functools.partial(project_kernel, norm, count, width),
-        cost=6.5,
+        cost=5.0,
         grid_spec=pltpu.PrefetchScalarGridSpec(
             num_scalar_prefetch=1,
-            grid=(length // CHUNK,),
-            in_specs=specs + [columns(weights, at + j, third) for j in range(3)],
+            grid=(3,),
+            in_specs=specs + [pl.BlockSpec((model, third), lambda i, order: (0, at + i))],
             out_specs=[
-                pl.BlockSpec((CHUNK, model), lambda i, order: (order[i], 0)),
-                pl.BlockSpec((CHUNK, total), lambda i, order: (order[i], 0)),
+                fixed_block((length, model)),
+                pl.BlockSpec((length, third), lambda i, order: (0, i)),
                 fixed_block((8, conv)),
             ],
+            scratch_shapes=[pltpu.VMEM((16, model), BF16)],
         ),
         out_shape=[
             jax.ShapeDtypeStruct((length, model), BF16),
@@ -388,7 +510,7 @@
             jax.ShapeDtypeStruct((8, conv), BF16),
         ],
         compiler_params=params(),
-    )(order, *inputs, weights, weights, weights)
+    )(order, *inputs, weights)
 
 
 def plain_kernel(a_ref, w_ref, out_ref):
@@ -398,27 +520,56 @@
 def plain_product(a, weight, width):
     weights, at = weight
     length, model = a.shape
+    half = width // 2
     return kernel_call(
         plain_kernel,
-        cost=3.7,
-        grid=(length // CHUNK,),
-        in_specs=[row_spec(model), columns(weights, at, width)],
-        out_specs=row_spec(width),
+        cost=3.0,
+        grid=(2,),
+        in_specs=[
+            fixed_block((length, model)),
+            pl.BlockSpec((model, half), lambda i: (0, 2 * at + i)),
+        ],
+        out_specs=pl.BlockSpec((length, half), lambda i: (0, i)),
         out_shape=jax.ShapeDtypeStruct((length, width), F32),
         compiler_params=params(),
     )(a, weights)
 
 
-def norm_forward_kernel(stream_ref, keep_ref, first_ref, second_ref, gain_ref, new_ref, low_ref):
+def rows_of(ref):
+    return (ref[...] if len(ref.shape) == 2 else ref[0]).astype(F32)
+
+
+def norm_forward_kernel(place_ref, stream_ref, keep_ref, first_ref, second_ref, *refs):
     total = keep_ref[0].astype(F32) + first_ref[0].astype(F32) + second_ref[...].astype(F32)
-    new = stream_ref[...] + total
-    new_ref[...] = new
-    low_ref[...] = (new * row_norm(new) * gain_ref[...]).astype(BF16)
-
-
-def last_forward_kernel(stream_ref, keep_ref, first_ref, second_ref, low_ref):
-    total = keep_ref[0].astype(F32) + first_ref[0].astype(F32) + second_ref[...].astype(F32)
-    low_ref[...] = (stream_ref[...] + total).astype(BF16)
+    new = rows_of(stream_ref) + total
+    if len(refs) == 1:
+        refs[0][...] = new.astype(BF16)
+    else:
+        gain_ref, new_ref, low_ref = refs
+        new_ref[...] = new
+        low_ref[...] = (new * row_norm(new) * gain_ref[...]).astype(BF16)
+
+
+def join_kernel(own_ref, other_ref, out_ref):
+    rows = own_ref.shape[0]
+    out_ref[:rows] = own_ref[...]
+    out_ref[rows:] = other_ref[...]
+
+
+def joined_rows(own, other):
+    rows, model = own.shape
+    return kernel_call(
+        join_kernel,
+        grid=(1,),
+        in_specs=[fixed_block((rows, model))] * 2,
+        out_specs=fixed_block((2 * rows, model)),
+        out_shape=jax.ShapeDtypeStruct((2 * rows, model), own.dtype),
+        compiler_params=params(),
+    )(own, other)
+
+
+def piece_specs(pieces, rows):
+    return [pl.BlockSpec((rows, one.shape[1]), lambda i, *_, at=at: (at, 0)) for one, at in pieces]
 
 
 def pass_on_kernel(keep_ref, first_ref, out_ref):
@@ -439,45 +590,44 @@
     )(kept, first)
 
 
+def rows_spec(one, rows):
+    if isinstance(one, tuple):
+        array, s = one
+        return array, pl.BlockSpec((1, rows, array.shape[2]), lambda i, place: (s, place[0], 0))
+    return one, fixed_block(one.shape)
+
+
 def term_specs(rows, model):
-    return [
-        fixed_block((rows, model)),
-        fixed_block((1, rows, model)),
-        fixed_block((1, rows, model)),
-        fixed_block((rows, model)),
-    ]
-
-
-def norm_forward(stream, terms, gain):
-    rows, model = stream.shape
-    kept, first, second = terms
-    if gain is None:
-        return stream, kernel_call(
-            last_forward_kernel,
-            grid=(1,),
-            in_specs=term_specs(rows, model),
-            out_specs=fixed_block((rows, model)),
-            out_shape=jax.ShapeDtypeStruct((rows, model), BF16),
-            compiler_params=params(),
-        )(stream, kept, first, second)
+    part = fixed_block((1, rows, model))
+    return [part, part, fixed_block((rows, model))]
+
+
+def norm_forward(stream, terms, gain, place):
+    rows, model = terms[2].shape
+    stream, spec = rows_spec(stream, rows)
+    low = jax.ShapeDtypeStruct((rows, model), BF16)
+    last = gain is None
     return kernel_call(
         norm_forward_kernel,
-        grid=(1,),
-        in_specs=term_specs(rows, model) + [fixed_block((1, model))],
-        out_specs=[fixed_block((rows, model))] * 2,
-        out_shape=[
-            jax.ShapeDtypeStruct((rows, model), F32),
-            jax.ShapeDtypeStruct((rows, model), BF16),
-        ],
-        compiler_params=params(),
-    )(stream, kept, first, second, gain)
+        grid_spec=pltpu.PrefetchScalarGridSpec(
+            num_scalar_prefetch=1,
+            grid=(1,),
+            in_specs=[spec]
+            + term_specs(rows, model)
+            + ([] if last else [fixed_block((1, model))]),
+            out_specs=[fixed_block((rows, model))] * (1 if last else 2),
+        ),
+        out_shape=[low] if last else [jax.ShapeDtypeStruct((rows, model), F32), low],
+        compiler_params=params(),
+    )(place, stream, *terms, *([] if last else [gain]))
 
 
 def norm_backward_kernel(
-    stream_ref, keep_ref, first_ref, second_ref, grad_ref, gain_ref, new_ref, low_ref, dgain_ref
+    place_ref, stream_ref, keep_ref, first_ref, second_ref, grad_ref, gain_ref, new_ref, low_ref,
+    dgain_ref,
 ):
     total = keep_ref[0].astype(F32) + first_ref[0].astype(F32) + second_ref[...].astype(F32)
-    current = stream_ref[...]
+    current = rows_of(stream_ref)
     scale = row_norm(current)
     unit = current * scale
     dgain_ref[...] = jnp.broadcast_to(
@@ -485,25 +635,32 @@
     )
     pulled = total * gain_ref[...]
     shift = jnp.mean(pulled * unit, axis=-1, keepdims=True)
-    new = grad_ref[...] + scale * (pulled - unit * shift)
+    new = rows_of(grad_ref) + scale * (pulled - unit * shift)
     new_ref[...] = new
     low_ref[...] = new.astype(BF16)
 
 
-def norm_backward(stream, terms, grad, gain):
-    rows, model = stream.shape
+def norm_backward(stream, terms, grad, gain, place):
+    rows, model = terms[2].shape
+    stream, stream_spec = rows_spec(stream, rows)
+    grad, grad_spec = rows_spec(grad, rows)
     return kernel_call(
         norm_backward_kernel,
-        grid=(1,),
-        in_specs=term_specs(rows, model) + [fixed_block((rows, model)), fixed_block((1, model))],
-        out_specs=[fixed_block((rows, model))] * 2 + [fixed_block((8, model))],
+        grid_spec=pltpu.PrefetchScalarGridSpec(
+            num_scalar_prefetch=1,
+            grid=(1,),
+            in_specs=[stream_spec]
+            + term_specs(rows, model)
+            + [grad_spec, fixed_block((1, model))],
+            out_specs=[fixed_block((rows, model))] * 2 + [fixed_block((8, model))],
+        ),
         out_shape=[
             jax.ShapeDtypeStruct((rows, model), F32),
             jax.ShapeDtypeStruct((rows, model), BF16),
             jax.ShapeDtypeStruct((8, model), F32),
         ],
         compiler_params=params(),
-    )(stream, *terms, grad, gain)
+    )(place, stream, *terms, grad, gain)
 
 
 def assemble_kernel(count, order_ref, *refs):
@@ -516,7 +673,7 @@
 
 
 def assembled(groups, order):
-    each, (rows, model) = len(groups[0]), groups[0][0].shape
+    each, (rows, model) = len(groups[0]), groups[0][0][0].shape
     pieces = [piece for group in groups for piece in group]
     count = len(pieces)
     return kernel_call(
@@ -525,14 +682,14 @@
         grid_spec=pltpu.PrefetchScalarGridSpec(
             num_scalar_prefetch=1,
             grid=(count,),
-            in_specs=[fixed_block((rows, model))] * count,
+            in_specs=piece_specs(pieces, rows),
             out_specs=pl.BlockSpec(
                 (1, rows, model), lambda i, order: (i // each, order[i % each], 0)
             ),
         ),
         out_shape=jax.ShapeDtypeStruct((len(groups), each * rows, model), BF16),
         compiler_params=params(),
-    )(order, *pieces)
+    )(order, *[one for one, _ in pieces])
 
 
 def input_grad_kernel(parts, width, order_ref, dproj_ref, dgate_ref, tail_ref, rim_ref, *refs):
@@ -720,10 +877,11 @@
 
 
 def scan_forward_kernel(
-    heads, width, p_ref, rim_ref, aux_ref, segr_ref, cw_ref, hp_ref, skip_ref, exp_ref,
+    heads, width, p_ref, rim_ref, marks_ref, cw_ref, hp_ref, skip_ref, exp_ref,
     z_ref, y_ref, st_ref, end_ref, gr_ref, vbuf, state, offset,
 ):
     chunk = pl.program_id(0)
+    aux = column_of(marks_ref[...])
 
     @pl.when(chunk == 0)
     def _():
@@ -739,7 +897,7 @@
     vbuf[8:, width:] = rounded(p_ref[:, width + LANES :])
     z = cw_ref[4:5] + cw_ref[3:4] * vbuf[8:]
     for k in range(3):
-        z = z + cw_ref[k : k + 1] * vbuf[5 + k : 5 + k + CHUNK] * aux_ref[:, k : k + 1]
+        z = z + cw_ref[k : k + 1] * vbuf[5 + k : 5 + k + CHUNK] * aux[:, k : k + 1]
     z_ref[...] = z
     act = z * jax.nn.sigmoid(z)
     x = act[:, :width]
@@ -753,10 +911,10 @@
         (iota(0) >= iota(1)).astype(F32), decay, NN, precision=HIGH, preferred_element_type=F32
     )
     cum_t = cum.T
-    seg_col = aux_ref[:, 5:6]
-    link = jnp.where((seg_col == segr_ref[0]) & (iota(0) >= iota(1)), 0.0, NO_LINK)
-    scores = fmm(c_val, b_val, NT)
-    growth = jnp.exp(cum) * aux_ref[:, 3:4]
+    seg_col = aux[:, 5:6]
+    link = jnp.where((seg_col == marks_ref[5:6]) & (iota(0) >= iota(1)), 0.0, NO_LINK)
+    scores = wide_mm(c_val, b_val, NT)
+    growth = jnp.exp(cum) * aux[:, 3:4]
     last = cum[CHUNK - 1 : CHUNK]
     weight = jnp.exp(last - cum) * (seg_col == seg_col[CHUNK - 1 : CHUNK]).astype(F32)
     wide = split_dot(jnp.concatenate([step, growth, weight], axis=0), exp_ref[...])
@@ -770,15 +928,15 @@
             spread = cum[:, head : head + 1] - cum_t[head : head + 1, :]
             mats.append(jnp.exp(spread + link) * scores)
         tile = xd[:, pair * LANES : (pair + 1) * LANES]
-        pieces.append(fmm(jnp.concatenate(mats, axis=1), head_halves(tile, lower)))
+        pieces.append(wide_mm(jnp.concatenate(mats, axis=1), head_halves(tile, lower)))
     held = state[...]
     st_ref[0] = held
-    carried = fmm(c_val, held) * growth_e
+    carried = wide_mm(c_val, held) * growth_e
     y_ref[...] = jnp.concatenate(pieces, axis=1) + carried + skip_ref[...] * x
-    new = held * growth_e[CHUNK - 1 : CHUNK] + fmm(b_val, xd * weight_e, TN)
+    new = held * growth_e[CHUNK - 1 : CHUNK] + wide_mm(b_val, xd * weight_e, TN)
     state[...] = new
     end_ref[...] = new
-    gr_ref[...] = jnp.exp(offset[...] + cum) * aux_ref[:, 4:5]
+    gr_ref[...] = jnp.exp(offset[...] + cum) * aux[:, 4:5]
     offset[...] = offset[...] + last
 
 
@@ -792,7 +950,7 @@
     return pl.BlockSpec(shape, lambda i: (0,) * len(shape))
 
 
-def scan_forward(proj, rim, aux, seg_rows, consts):
+def scan_forward(proj, rim, marks, consts):
     length, total = proj.shape
     heads, width = consts["heads"], consts["width"]
     chunks, conv = length // CHUNK, total - LANES
@@ -803,8 +961,7 @@
         in_specs=[
             row_spec(total),
             whole((8, conv)),
-            row_spec(8),
-            pl.BlockSpec((1, 1, CHUNK), lambda i: (i, 0, 0)),
+            pl.BlockSpec((8, CHUNK), lambda i: (0, i)),
             whole((8, conv)),
             whole((8, LANES)),
             whole((1, width)),
@@ -830,12 +987,12 @@
             pltpu.VMEM((1, LANES), F32),
         ],
         compiler_params=params(),
-    )(proj, rim, aux, seg_rows, consts["cw"], consts["hp"], consts["skip"], consts["exp"])
+    )(proj, rim, marks, consts["cw"], consts["hp"], consts["skip"], consts["exp"])
 
 
 def mix_forward_kernel(y0_ref, zc_ref, gr_ref, sin_ref, gate_ref, exp_ref, y_ref, sq_ref):
     c_val = zc_ref[...] * jax.nn.sigmoid(zc_ref[...])
-    carried = fmm(c_val, sin_ref[...].astype(F32))
+    carried = wide_mm(c_val, sin_ref[...].astype(F32))
     y = y0_ref[...] + carried * split_dot(gr_ref[...], exp_ref[...])
     y_ref[...] = y
     gate = gate_ref[...]
@@ -877,7 +1034,7 @@
         for m in range(parts):
             source = pl.ds(pl.multiple_of(order_ref[m] * CHUNK, CHUNK), CHUNK)
             square = sum(one[:, source] for one in squares)
-            scale = lax.rsqrt(column_of(square)[:, 0:1] / channels + eps)
+            scale = lax.rsqrt(column_of(square)[:, 1:2] / channels + eps)
             gate = gate_ref[source]
             gated = y_ref[source] * (gate * jax.nn.sigmoid(gate))
             rows[m * CHUNK : (m + 1) * CHUNK] = (gated * scale * gain_ref[...]).astype(BF16)
@@ -918,32 +1075,50 @@
 def grad_scaled_kernel(count, order_ref, *refs):
     pieces, rest = refs[:count], refs[count:]
     w_ref, y_ref, gate_ref, gain_ref, gs_ref, dot_ref = rest[:6]
+    sums = rest[-1]
+    step = pl.program_id(0)
+    length = gs_ref.shape[0]
+    if count > 1:
+
+        @pl.when(step == 0)
+        def _():
+            for m in range(count):
+                place = pl.ds(pl.multiple_of(order_ref[m] * CHUNK, CHUNK), CHUNK)
+                rest[6][place] = pieces[m][...]
+
+        rows = rest[6][...]
+    else:
+        rows = pieces[0][0]
+    grad = mm(rows, w_ref[...])
+    gs_ref[...] = grad
     gate = gate_ref[...]
     gated = y_ref[...] * (gate * jax.nn.sigmoid(gate))
-
-    def run(rows):
-        grad = mm(rows, w_ref[...])
-        gs_ref[...] = grad
-        product = jnp.sum(grad * gain_ref[...] * gated, axis=1, keepdims=True)
-        dot_ref[...] = jnp.broadcast_to(product, (CHUNK, CHUNK)).T[:8]
-
-    if count == 1:
-        run(pieces[0][0])
-    else:
-        for m in range(count):
-
-            @pl.when(pl.program_id(0) == m)
-            def _(m=m):
-                rest[6][...] = pieces[m][...]
-                run(pieces[m][...])
+    product = jnp.sum(grad * gain_ref[...] * gated, axis=1, keepdims=True)
+    square = jnp.sum(gated * gated, axis=1, keepdims=True)
+    lane = lax.broadcasted_iota(jnp.int32, (length, LANES), 1)
+    part = jnp.where(lane == 0, product, square)
+
+    @pl.when(step == 0)
+    def _():
+        sums[...] = part
+
+    @pl.when(step > 0)
+    def _():
+        sums[...] += part
+
+    @pl.when(step == pl.num_programs(0) - 1)
+    def _():
+        for m in range(length // CHUNK):
+            at = slice(m * CHUNK, (m + 1) * CHUNK)
+            dot_ref[:, at] = sums[at].T[:8]
 
 
 def grad_scaled(source, y, gate, order, consts):
     length, width = y.shape
     weights, at = consts["out"]
-    model = weights.shape[0]
-    row = pl.BlockSpec((CHUNK, width), lambda i, order: (order[i], 0))
-    out_specs = [row, pl.BlockSpec((8, CHUNK), lambda i, order: (0, order[i]))]
+    model, half = weights.shape[0], width // 2
+    part = pl.BlockSpec((length, half), lambda i, order: (0, i))
+    out_specs = [part, fixed_block((8, length))]
     out_shape = [
         jax.ShapeDtypeStruct((length, width), F32),
         jax.ShapeDtypeStruct((8, length), F32),
@@ -951,20 +1126,27 @@
     if len(source) == 2:
         stream, sequence = source
         inputs, count = [stream], 1
-        specs = [pl.BlockSpec((1, CHUNK, model), lambda i, order: (sequence, order[i], 0))]
+        specs = [pl.BlockSpec((1, length, model), lambda i, order: (sequence, 0, 0))]
     else:
-        inputs, count = list(source), len(source)
-        specs = [fixed_block((CHUNK, model))] * count
-        out_specs.append(pl.BlockSpec((CHUNK, model), lambda i, order: (order[i], 0)))
+        inputs, count = [one for one, _ in source], len(source)
+        specs = piece_specs(source, CHUNK)
+        out_specs.append(fixed_block((length, model)))
         out_shape.append(jax.ShapeDtypeStruct((length, model), BF16))
     out = kernel_call(
         functools.partial(grad_scaled_kernel, count),
-        cost=5.5,
+        cost=4.5,
         grid_spec=pltpu.PrefetchScalarGridSpec(
             num_scalar_prefetch=1,
-            grid=(length // CHUNK,),
-            in_specs=specs + [columns(weights, at, width), row, row, fixed_block((1, width))],
+            grid=(2,),
+            in_specs=specs
+            + [
+                pl.BlockSpec((model, half), lambda i, order: (0, 2 * at + i)),
+                part,
+                part,
+                pl.BlockSpec((1, half), lambda i, order: (0, i)),
+            ],
             out_specs=out_specs,
+            scratch_shapes=[pltpu.VMEM((length, LANES), F32)],
         ),
         out_shape=out_shape,
         compiler_params=params(),
@@ -975,7 +1157,7 @@
 def mix_backward_kernel(
     channels, shares, gs_ref, y_ref, gate_ref, zx_ref, zc_ref, gr_ref, gain_ref, exp_ref, *refs
 ):
-    squares, dots, refs = refs[:shares], refs[shares : 2 * shares], refs[2 * shares :]
+    shared, refs = refs[:shares], refs[shares:]
     scaled_ref, dgate_ref, dy_ref, acc_ref, dsin_ref, dsin = refs
     at = pl.program_id(0)
 
@@ -984,13 +1166,9 @@
         acc_ref[...] = jnp.zeros_like(acc_ref)
         dsin[...] = jnp.zeros_like(dsin)
 
-    stats = column_of(
-        jnp.concatenate(
-            [sum(one[...] for one in squares), sum(one[...] for one in dots)], axis=0
-        )
-    )
-    scale = lax.rsqrt(stats[:, 0:1] / channels + eps)
-    pull = scale * scale * scale * stats[:, 8:9] / channels
+    stats = column_of(sum(one[...] for one in shared))
+    scale = lax.rsqrt(stats[:, 1:2] / channels + eps)
+    pull = scale * scale * scale * stats[:, 0:1] / channels
     grad, y, gate = gs_ref[...], y_ref[...], gate_ref[...]
     silu, sig = silu_parts(gate)
     gated = y * silu
@@ -1011,12 +1189,12 @@
         dsin_ref[...] = dsin[...].astype(BF16)
 
 
-def mix_backward(grad, y, gate, z, growth, squares, dots, channels, consts):
+def mix_backward(grad, y, gate, z, growth, stats, channels, consts):
     length, width = y.shape
     last = z.shape[1] // LANES - 1
     stat = pl.BlockSpec((8, CHUNK), lambda i: (0, i))
     return kernel_call(
-        functools.partial(mix_backward_kernel, float(channels), len(squares)),
+        functools.partial(mix_backward_kernel, float(channels), len(stats)),
         cost=5.0,
         grid=(length // CHUNK,),
         in_specs=[
@@ -1029,7 +1207,7 @@
             whole((1, width)),
             whole((LANES, width)),
         ]
-        + [stat] * (2 * len(squares)),
+        + [stat] * len(stats),
         out_specs=[
             row_spec(width),
             row_spec(width),
@@ -1046,16 +1224,17 @@
         ],
         scratch_shapes=[pltpu.VMEM((LANES, width), F32)],
         compiler_params=params(),
-    )(grad, y, gate, z, z, growth, consts["gain"], consts["exp"], *squares, *dots)
+    )(grad, y, gate, z, z, growth, consts["gain"], consts["exp"], *stats)
 
 
 def scan_backward_kernel(
-    heads, width, chunks, dy_ref, z_ref, p_ref, before_ref, rim_ref, aux_ref, segr_ref, cw_ref,
+    heads, width, chunks, dy_ref, z_ref, p_ref, before_ref, rim_ref, marks_ref, cw_ref,
     hp_ref, skip_ref, exp_ref, red_ref, st_ref, sin_ref, grprev_ref, dend_ref,
     dproj_ref, wacc_ref, hacc_ref, tail_ref, drim_ref, vbuf, zbuf, dstate,
 ):
     step_at = pl.program_id(0)
     chunk = chunks - 1 - step_at
+    aux = column_of(marks_ref[...])
 
     @pl.when(step_at == 0)
     def _():
@@ -1089,9 +1268,9 @@
         (iota(0) >= iota(1)).astype(F32), decay, NN, precision=HIGH, preferred_element_type=F32
     )
     cum_t = cum.T
-    seg_col = aux_ref[:, 5:6]
-    link = jnp.where((seg_col == segr_ref[0]) & (iota(0) <= iota(1)), 0.0, NO_LINK)
-    growth = jnp.exp(cum) * aux_ref[:, 3:4]
+    seg_col = aux[:, 5:6]
+    link = jnp.where((seg_col == marks_ref[5:6]) & (iota(0) <= iota(1)), 0.0, NO_LINK)
+    growth = jnp.exp(cum) * aux[:, 3:4]
     last = cum[CHUNK - 1 : CHUNK]
     weight = jnp.exp(last - cum) * (seg_col == seg_col[CHUNK - 1 : CHUNK]).astype(F32)
     reach = jnp.where(chunk == 0, 1.0, grprev_ref[7:8])
@@ -1105,9 +1284,9 @@
     after = dstate[...]
     xd = x * step_e
     dy = dy_ref[...]
-    scores = bmm(b_val, c_val, NT)
-    carried = bmm(c_val, held) * growth_e
-    fed = bmm(b_val, after) * weight_e
+    scores = wide_mm(b_val, c_val, NT)
+    carried = low_mm(c_val, held) * growth_e
+    fed = low_mm(b_val, after) * weight_e
     dy_grown = dy * growth_e
     lower = lane < LANES // 2
     dscores = jnp.zeros((CHUNK, CHUNK), F32)
@@ -1115,7 +1294,7 @@
     rows, pieces = [], []
     for pair in range(heads // 2):
         at = slice(pair * LANES, (pair + 1) * LANES)
-        products = bmm(head_halves(xd[:, at], lower), dy[:, at], NT)
+        products = wide_mm(head_halves(xd[:, at], lower), dy[:, at], NT)
         mats = []
         for side, head in enumerate((2 * pair, 2 * pair + 1)):
             spread = cum_t[head : head + 1, :] - cum[:, head : head + 1]
@@ -1127,7 +1306,7 @@
             rows.append(jnp.sum(energy, axis=0, keepdims=True))
             into = jnp.where(lane == head, jnp.sum(energy, axis=1, keepdims=True), into)
             mats.append(mat)
-        pieces.append(bmm(jnp.concatenate(mats, axis=1), head_halves(dy[:, at], lower)))
+        pieces.append(low_mm(jnp.concatenate(mats, axis=1), head_halves(dy[:, at], lower)))
     dxd = jnp.concatenate(pieces, axis=1) + fed
     kept = jnp.sum(after * held, axis=0, keepdims=True) * growth_e[CHUNK - 1 : CHUNK]
     sums = split_dot(
@@ -1154,14 +1333,14 @@
     dx = dxd * step_e + skip_ref[...] * dy
     db = wide_mm(dscores, c_val) + wide_mm(xd * weight_e, after, NT)
     dc = wide_mm(dscores, b_val, TN) + wide_mm(dy_grown, held, NT)
-    dstate[...] = after * growth_e[CHUNK - 1 : CHUNK] + bmm(c_val, dy_grown, TN)
+    dstate[...] = after * growth_e[CHUNK - 1 : CHUNK] + wide_mm(c_val, dy_grown, TN)
 
     dz = jnp.concatenate([dx, db, dc], axis=1) * slope
     wacc_ref[3:4] += jnp.sum(dz * vbuf[8:], axis=0, keepdims=True)
     wacc_ref[4:5] += jnp.sum(dz, axis=0, keepdims=True)
     dv = cw_ref[3:4] * dz
     for k in range(3):
-        masked = dz * aux_ref[:, k : k + 1]
+        masked = dz * aux[:, k : k + 1]
         wacc_ref[k : k + 1] += jnp.sum(
             masked * vbuf[5 + k : 5 + k + CHUNK], axis=0, keepdims=True
         )
@@ -1187,7 +1366,7 @@
         zbuf[k, 8 + CHUNK :] = zbuf[k, 8:16]
 
 
-def scan_backward(dy, z, proj, rim, aux, seg_rows, states, carried, growth, dend, consts):
+def scan_backward(dy, z, proj, rim, marks, states, carried, growth, dend, consts):
     length, total = proj.shape
     heads, width = consts["heads"], consts["width"]
     chunks, conv = length // CHUNK, total - LANES
@@ -1211,8 +1390,7 @@
             back(total),
             previous(total),
             whole((8, conv)),
-            back(8),
-            pl.BlockSpec((1, 1, CHUNK), lambda i: (chunks - 1 - i, 0, 0)),
+            pl.BlockSpec((8, CHUNK), lambda i: (0, chunks - 1 - i)),
             whole((8, conv)),
             whole((8, LANES)),
             whole((1, width)),
@@ -1244,7 +1422,7 @@
         ],
         compiler_params=params(),
     )(
-        dy, z, proj, proj, rim, aux, seg_rows, consts["cw"], consts["hp"], consts["skip"],
+        dy, z, proj, proj, rim, marks, consts["cw"], consts["hp"], consts["skip"],
         consts["exp"], consts["red"], states, carried, growth, dend,
     )
 
@@ -1316,25 +1494,38 @@
     aux_all = jnp.stack(
         [ext_ids[:, k : k + length] == seg_ids for k in range(3)]
         + [seg_ids == prior, seg_ids == edge_ids[:, 2:3], seg_ids, seg_ids, seg_ids],
-        axis=2,
+        axis=1,
     ).astype(F32)
-    seg_rows = seg_ids.astype(F32).reshape(sequences, length // CHUNK, 1, CHUNK)
 
     spread_table = (jnp.arange(LANES)[:, None] == jnp.arange(width)[None, :] // depth).astype(BF16)
 
-    table = ring_pieces(jnp.concatenate(first_piece(0), axis=1))
+    def joined(*parts):
+        return jnp.concatenate([one for part in parts for one in part], axis=1)
+
+    third = total // 3
+    upper_piece = joined(second_piece(1), first_piece(1))
+    table, second_table = [], []
+    halo = shifted(stream[:, length - 16 :], "context", 1)
+    precede(halo, edge_ids)
+    for _ in ring_pieces(table, joined(first_piece(0))):
+        pass
+    second_ring = ring_pieces(second_table, relayed(joined(second_piece(0))))
+    next(second_ring)
+    places = jnp.arange(length // CHUNK, dtype=jnp.int32)
+    arrived, sending = rows_order(False), rows_order(True)
+    own_place = lax.axis_index("tensor").astype(jnp.int32)[None]
+    precede(aux_all, spread_table, spread_table.T, arrived, sending)
     first, tile_rows = placed(table, [total], width)
-    weights, before = [], table[min(1, dp - 1)][0][:16, :LANES]
-    for layer in layer_range:
-        front = first
-        if layer:
-            part = after(jnp.concatenate(first_piece(layer), axis=1), before)
-            front = lax.all_gather(part, ("dp", "context"), axis=0, tiled=True)
-            before = front[:8, :LANES]
-        part = after(jnp.concatenate(second_piece(layer), axis=1), before)
-        rest = lax.all_gather(part, ("dp", "context"), axis=0, tiled=True)
-        before = rest[:8, :LANES]
-        weights.append({"front": (front, 0), "gate": (rest, 0), "out": (rest, 1)})
+
+    def every_row(part):
+        return lax.all_gather(part, ("dp", "context"), axis=0, tiled=True)
+
+    weights = [
+        {"front": (first, 0)},
+        {},
+    ]
+    streams = [(stream, s) for s in seq_range]
+    grads = [(cotangent, s) for s in seq_range]
     small = tile_rows[heads : heads + 2 * layers]
     gains = small[:layers]
     taps = small[layers:].reshape(layers, dp * context, rows_in)[:, :, : 5 * tensor * own_conv]
@@ -1385,11 +1576,9 @@
     def through(growth):
         return jnp.repeat(growth[length - 1, :heads], depth)[None]
 
-    places = jnp.arange(length // CHUNK, dtype=jnp.int32)
-    arrived, sending = rows_order(False), rows_order(True)
-    streams = [own_rows(stream[s]).astype(F32) for s in seq_range]
-    grads = [own_rows(cotangent[s]).astype(F32) for s in seq_range]
-    halo = shifted(stream[:, length - 16 :], "context", 1)
+    for const in consts:
+        precede(const["cw"], const["hp"], const["skip"], const["gain"])
+    precede(gains)
     incoming = [(stream, halo, s) for s in seq_range]
     work = [[{} for _ in seq_range] for _ in layer_range]
     outputs = []
@@ -1410,7 +1599,7 @@
     def step_scan(layer, s):
         k = work[layer][s]
         k["z"], k["y0"], k["states"], end, k["growth"] = scan_forward(
-            k["proj"], k["rim"], aux_all[s], seg_rows[s], consts[layer]
+            k["proj"], k["rim"], aux_all[s], consts[layer]
         )
         k["carried"] = chain(end, through(k["growth"]), 1)
 
@@ -1423,13 +1612,15 @@
         k["y"], squares = mix_forward(
             k["y0"], k["z"], k["growth"], k["carried"], k["gate"], consts[layer]
         )
-        k["squares"] = from_others(squares, "tensor")
+        if layer < top:
+            k["squares"] = from_others(squares, "tensor")
 
     def step_out(layer, s):
         k = work[layer][s]
         kind = BF16 if layer == top else F32
         sent, own = project_out(
-            k["y"], k["gate"], k["squares"], channels, kind, sending, consts[layer]
+            k["y"], k["gate"], k["squares" if layer < top else "stats"], channels, kind, sending,
+            consts[layer],
         )
         k["out"] = [own, flipped(sent, "tensor", 0)]
 
@@ -1440,8 +1631,14 @@
     def step_norm(layer, s):
         k = work[layer][s]
         gain = None if layer == top else gains[layer + 1 : layer + 2]
-        streams[s], low = norm_forward(streams[s], k["out"], gain)
-        return gathered(low)
+        *new, low = norm_forward(streams[s], k["out"], gain, own_place)
+        streams[s] = new[0] if new else None
+        k["rows"] = [low, flipped(low, "tensor", 1)]
+
+    def step_join(layer, s, name):
+        own, other = work[layer][s][name]
+        across = flipped(joined_rows(own, other), "tensor", 0)
+        return [(own, 0), (other, 0), (across, 0), (across, 1)]
 
     def step_grad(layer, s):
         k = work[layer][s]
@@ -1449,20 +1646,19 @@
         k["grad"], dots, k["low"] = grad_scaled(
             source, k["y"], k["gate"], places if layer == top else arrived, consts[layer]
         )
-        k["dots"] = from_others(dots, "tensor")
+        k["stats"] = from_others(dots, "tensor")
 
     def step_mix_back(layer, s):
         k = work[layer][s]
         k["scaled"], k["dgate"], k["dy"], k["acc"], dsin = mix_backward(
-            k["grad"], k["y"], k["gate"], k["z"], k["growth"], k["squares"], k["dots"],
-            channels, consts[layer],
+            k["grad"], k["y"], k["gate"], k["z"], k["growth"], k["stats"], channels, consts[layer],
         )
         k["dend"] = chain(dsin, through(k["growth"]), -1)
 
     def step_scan_back(layer, s):
         k = work[layer][s]
         k["dproj"], k["wacc"], k["hacc"], k["tail"], drim = scan_backward(
-            k["dy"], k["z"], k["proj"], k["rim"], aux_all[s], seg_rows[s], k["states"],
+            k["dy"], k["z"], k["proj"], k["rim"], aux_all[s], k["states"],
             k["carried"], k["growth"], k["dend"], consts[layer],
         )
         k["drim"] = shifted(drim, "context", -1)
@@ -1478,9 +1674,9 @@
     def step_norm_back(layer, s):
         k = work[layer][s]
         grads[s], low, k["dgain"] = norm_backward(
-            k["stream"], k["back"], grads[s], gains[layer : layer + 1]
-        )
-        return gathered(low)
+            k["stream"], k["back"], grads[s], gains[layer : layer + 1], own_place
+        )
+        k["grad_low"] = [low, flipped(low, "tensor", 1)]
 
     def every(layer, name):
         return [k[name] for k in work[layer]]
@@ -1498,80 +1694,117 @@
         return weight_grad([(every(layer, "normed"), every(layer, "dproj"))], layer == 0)
 
     def scattered(value):
-        return lax.psum_scatter(
-            value[0], ("dp", "context"), scatter_dimension=0, tiled=True
-        ).astype(F32)
+        return lax.psum_scatter(value, ("dp", "context"), scatter_dimension=0, tiled=True)
 
     second_sums, first_sums = [None] * layers, [None] * layers
-    final = sequences - 1
+    project_0, scan_0, gate_0, mix_0, out_0, grad_0, mixed_0, scanned_0, input_0 = (
+        functools.partial(step, 0)
+        for step in (
+            step_project, step_scan, step_gate, step_mix, step_out, step_grad, step_mix_back,
+            step_scan_back, step_input_grad,
+        )
+    )
+    project_1, scan_1, gate_1, mix_1, out_1, grad_1, mixed_1, scanned_1, input_1 = (
+        functools.partial(step, 1)
+        for step in (
+            step_project, step_scan, step_gate, step_mix, step_out, step_grad, step_mix_back,
+            step_scan_back, step_input_grad,
+        )
+    )
+
+    project_0(0)
+    next(second_ring)
+    scan_0(0)
+    next(second_ring)
+    project_0(1)
+    next(second_ring, None)
+    upper = every_row(relayed(upper_piece))
+    consts[1].update(front=(upper, 2 * width // third), gate=(upper, 0), out=(upper, 1))
+    scan_0(1)
+    precede(work[0][0]["carried"])
+    (second,) = placed(second_table, [2 * width])
+    consts[0].update(gate=(second, 0), out=(second, 1))
+    gate_0(0)
+    mix_0(0)
+    gate_0(1)
+    mix_0(1)
+    out_0(0)
+    step_pass(0, 0, "out")
+    out_0(1)
+    step_pass(0, 1, "out")
+    step_norm(0, 0)
+    step_norm(0, 1)
+    incoming[0] = step_join(0, 0, "rows")
+    project_1(0)
+    incoming[1] = step_join(0, 1, "rows")
+    project_1(1)
+    scan_1(0)
+    scan_1(1)
+    gate_1(0)
+    mix_1(0)
+    gate_1(1)
+    mix_1(1)
+    grad_1(0)
+    grad_1(1)
+    mixed_1(0)
+    mixed_1(1)
+    second_sums[1] = scattered(step_second_grad(1)[0])
+    scanned_1(0)
+    out_1(0)
+    input_1(0)
+    step_pass(1, 0, "back")
+    scanned_1(1)
+    step_norm_back(1, 0)
+    out_1(1)
+    input_1(1)
+    incoming[0] = step_join(1, 0, "grad_low")
+    grad_0(0)
+    step_pass(1, 1, "back")
+    first_grad = step_first_grad(1)
+    mixed_0(0)
+    step_norm_back(1, 1)
+    precede(second_sums[1])
+    step_pass(1, 0, "out")
+    step_pass(1, 1, "out")
+    first_sums[1] = scattered(first_grad[0])
+    scanned_0(0)
+    incoming[1] = step_join(1, 1, "grad_low")
+    grad_0(1)
+    input_0(0)
+    mixed_0(1)
+    second_steps = ring_steps(step_second_grad(0))
+    step_pass(0, 0, "back")
+    scanned_0(1)
+    next(second_steps)
+    step_norm_back(0, 0)
     for s in seq_range:
-        step_project(0, s)
-        if s == 0:
-            step_scan(0, s)
-    for layer in layer_range:
-        if layer:
-            for s in seq_range:
-                step_project(layer, s)
-                step_scan(layer, s)
-            for s in seq_range:
-                step_gate(layer, s)
-                step_mix(layer, s)
-        else:
-            for s in seq_range:
-                step_gate(layer, s)
-                step_mix(layer, s)
-                if s < final:
-                    step_scan(layer, s + 1)
-                if layer < top:
-                    step_out(layer, s)
-                    step_pass(layer, s, "out")
-        if layer < top:
-            for s in seq_range:
-                incoming[s] = step_norm(layer, s)
-
-    def rest_of(layer):
-        incoming[final] = step_norm_back(layer, final)
-        first_sums[layer] = scattered(step_first_grad(layer))
-
-    for layer in reversed(layer_range):
-        for s in seq_range:
-            step_grad(layer, s)
-            if s == 0 and layer < top:
-                rest_of(layer + 1)
-        for s in seq_range:
-            step_mix_back(layer, s)
-        grad = step_second_grad(layer)
-        if layer:
-            second_sums[layer] = scattered(grad)
-        steps = iter(()) if layer else ring_steps(grad)
-        for s in seq_range:
-            step_scan_back(layer, s)
-            if s == final:
-                for earlier in range(s):
-                    incoming[earlier] = step_norm_back(layer, earlier)
-            next(steps, None)
-            if layer == top:
-                step_out(layer, s)
-            elif layer == top - 1 and s == 0:
-                outputs.extend(step_norm(top, s) for s in seq_range)
-            step_input_grad(layer, s)
-            step_pass(layer, s, "back")
-            if layer == top:
-                step_pass(layer, s, "out")
-    next(steps, None)
-    grad = step_first_grad(0)
-    for value in steps:
-        second_sums[0] = value
-    steps = ring_steps(grad)
-    next(steps)
-    incoming[final] = step_norm_back(0, final)
-    next(steps)
+        step_norm(1, s)
+    input_0(1)
+    next(second_steps)
+    step_pass(0, 1, "back")
+    precede(first_sums[1])
+    first_steps = ring_steps(step_first_grad(0))
+    next(second_steps)
+    step_norm_back(0, 1)
+    small_steps = small_sums(work, width, heads, model, consts[0]["red"])
+    next(small_steps)
+    next(first_steps)
+    outputs.extend(step_join(1, s, "rows") for s in seq_range)
     layer_out = assembled(outputs, arrived)
-    for value in steps:
-        first_sums[0] = value
+    next(first_steps)
+    next(small_steps)
+    second_sums[0] = next(second_steps)
+    second_sums[1], first_sums[1] = widened(second_sums[1]), widened(first_sums[1])
+    incoming[0] = step_join(0, 0, "grad_low")
+    next(first_steps)
+    next(small_steps)
+    incoming[1] = step_join(0, 1, "grad_low")
     grad_stream = assembled(incoming, arrived)
-
-    out, small_local, small_shared = [], [], []
+    first_sums[0] = next(first_steps)
+    for value in small_steps:
+        small_out = value
+
+    out = []
     for layer in layer_range:
         second_sum, first_sum = second_sums[layer], first_sums[layer]
         out.append(
@@ -1582,54 +1815,25 @@
                 second_sum[:, width:].T,
             )
         )
-        acc, wacc, hacc, dgain = (
-            sum(every(layer, name)) for name in ("acc", "wacc", "hacc", "dgain")
-        )
-        small_local.append(
-            jnp.concatenate(
-                [
-                    wacc[:5, :width].reshape(-1),
-                    acc[0],
-                    acc[1].reshape(heads, depth).sum(axis=1),
-                    hacc[0, :heads],
-                    hacc[1, :heads],
-                ]
-            )
-        )
-        small_shared.append(jnp.concatenate([wacc[:5, width:].reshape(-1), dgain[0]]))
-
-    shared_sum = summed_over(jnp.stack(small_shared), ("tensor",))
-    local_sum = jnp.stack(small_local)
-    cut = local_sum.shape[1]
-    both = summed_over(
-        jnp.concatenate([local_sum, shared_sum], axis=1), ("context", "dp")
+    taps_x, sum_bias_x, dt_sum, rate_sum, skip_sum, gate_sum, taps_bc, sum_bias_bc, gain_sum = (
+        small_out
     )
-    local_sum, shared_sum = both[:, :cut], both[:, cut:]
-    place = (lax.axis_index("dp") * context + lax.axis_index("context")) * tensor
-    place = place + lax.axis_index("tensor")
-    taps = shared_sum[:, : 5 * shared].reshape(layers, 5, shared)
-    taps = lax.dynamic_slice_in_dim(taps, place * own_conv, own_conv, 2)
-    grad_gain = lax.dynamic_slice_in_dim(
-        shared_sum[:, 5 * shared :], place * own_gain, own_gain, 1
-    )
-    taps_x = local_sum[:, : 5 * width].reshape(layers, 5, width)
-    heads_at = 6 * width
     return (
         layer_out,
         grad_stream,
         jnp.stack([o[0] for o in out]),
         jnp.stack([o[1] for o in out]),
         jnp.stack([o[2] for o in out]),
-        grad_gain,
-        taps[:, :4],
-        taps[:, 4],
+        gain_sum,
+        taps_bc,
+        sum_bias_bc,
         jnp.stack([o[3] for o in out]),
-        taps_x[:, :4],
-        taps_x[:, 4],
-        local_sum[:, heads_at + heads : heads_at + 2 * heads],
-        local_sum[:, heads_at + 2 * heads : heads_at + 3 * heads],
-        local_sum[:, heads_at : heads_at + heads],
-        local_sum[:, 5 * width : 6 * width],
+        taps_x,
+        sum_bias_x,
+        dt_sum,
+        rate_sum,
+        skip_sum,
+        gate_sum,
     )
 
 

time: 814 us -> 771 us (0.947)
  local copies, waits for them, and re-layouts: 116 us -> 95.3 us
  waiting for transfers between devices: 186 us -> 173 us
  other arithmetic: 21.2 us -> 11.7 us
    ppermute x21 -> x28, waiting for transfers between devices: 87.3 us -> 58.1 us  [ring(): lax.ppermute(value, axis, [(i, (i - 1) % count) for i in range(count)])]
    ppermute x21 -> x28, starting transfers between devices: 29.2 us -> 47.7 us  [ring(): lax.ppermute(value, axis, [(i, (i - 1) % count) for i in range(count)])]
    ppermute x51 -> x37, waiting for transfers between devices: 83.4 us -> 68.6 us  [flipped(): return lax.ppermute(value, axis, [(i, i ^ 1 << bit) for i in range(count)])]
    ppermute x16, waiting for transfers between devices: 11.9 us -> 24.2 us  [shifted(): lax.ppermute(value, axis, [(source, source + steps) for source in range(l...]
    another operation x7, local copies, waits for them, and re-layouts: 10.8 us -> 0.09 us  [local(): jnp.stack([ext_ids[:, k:k + length] == seg_ids for k in range(3)] + [seg_...]
    all_gather x3 -> x1, waiting for transfers between devices: 0.01 us -> 10.2 us  [every_row(): return lax.all_gather(part, ('dp', 'context'), axis=0, tiled=True)]
    slice x19 -> x2, local copies, waits for them, and re-layouts: 15.5 us -> 5.3 us  [the longest x1 4.42 us: first_piece(): return [input_weight[layer, :, 1], tile]]
    ppermute x51 -> x37, starting transfers between devices: 30.8 us -> 21.7 us  [flipped(): return lax.ppermute(value, axis, [(i, i ^ 1 << bit) for i in range(count)])]
  transfers between devices with their start and end apart: 117 -> 111, of which waited for: 31 -> 38; matrix products, arithmetic and copies ran while one was open for 8% -> 4% of each run, Pallas kernels for 41% -> 42%
where the time goes in v3:
time: 771 us; the launch traced here: 759 us
  Pallas kernels  346 us (45%)
  waiting for transfers between devices  173 us (22%)
  starting transfers between devices  116 us (15%)
  local copies, waits for them, and re-layouts  95.3 us (12%)
  between operations  17.3 us (2%)
  other arithmetic  11.7 us (2%)
    pallas_call x91, Pallas kernels, call(): pl.pallas_call(without_tokens, cost_estimate=pl.CostEstimate(flops=int(co...  346 us
    unnamed x504, local copies, waits for them, and re-layouts  75.8 us
    ppermute x37, waiting for transfers between devices, flipped(): return lax.ppermute(value, axis, [(i, i ^ 1 << bit) for i in range(count)])  68.6 us
    ppermute x28, waiting for transfers between devices, ring(): lax.ppermute(value, axis, [(i, (i - 1) % count) for i in range(count)])  58.1 us
    ppermute x28, starting transfers between devices, ring(): lax.ppermute(value, axis, [(i, (i - 1) % count) for i in range(count)])  47.7 us
    ppermute x16, starting transfers between devices, shifted(): lax.ppermute(value, axis, [(source, source + steps) for source in range(l...  28.3 us
    ppermute x16, waiting for transfers between devices, shifted(): lax.ppermute(value, axis, [(source, source + steps) for source in range(l...  24.2 us
    ppermute x37, starting transfers between devices, flipped(): return lax.ppermute(value, axis, [(i, i ^ 1 << bit) for i in range(count)])  21.7 us
  transfers between devices with their start and end apart: 111, of which 38 were waited for; matrix products, arithmetic and copies ran while one was open for 4% of the time, Pallas kernels for 42%

profile of v3, /device:TPU:0, one launch (start us, length us, event | category | flops | bytes accessed | tf_op | source)
XLA Modules:
  0.0 758.6 jit_solution(8842645994345315439)
XLA Ops:
  35.0 7.7 %collective-permute-done.2.refs_3_.refs_2_ = bf16[192,1152]{1,0:T(8,128)(2,1)S(1)} collective-permute-done((bf16[192,1152]{1,0:T(8,128)(2,1)S(1)}, bf16[192,1152]{1,0:T(8,128)(2,1)S(1)}, u32[]{:S(2)}, u32[]{:S(2)}) %collective-permute-start.2) | collective-permute-done | bytes 442400 | tf_op jit(solution)/shard_map/ppermute | solution.py:93
  105.5 9.3 %shard_map.296 = (f32[512,1024]{1,0:T(8,128)}, f32[512,768]{1,0:T(8,128)S(1)}, f32[4,128,768]{2,1,0:T(8,128)S(1)}, f32[128,768]{1,0:T(8,128)S(1)}, f32[512,128]{1,0:T(8,128)S(1)}) custom-call(f32[512,1152]{1,0:T(8,128)} %copy-done.196, bf16[8,1024]{1,0:T(8,128)(2,1)S(1)} %get-tuple-element.165.refs_1_.refs_4_, ...), custom_call_target="tpu_custom_call" | custom-call | flops 4750000128 | bytes 1024 | tf_op jit(solution)/shard_map/pallas_call | solution.py:59
  148.8 9.4 %shard_map.301 = (f32[512,1024]{1,0:T(8,128)}, f32[512,768]{1,0:T(8,128)S(1)}, f32[4,128,768]{2,1,0:T(8,128)S(1)}, f32[128,768]{1,0:T(8,128)S(1)}, f32[512,128]{1,0:T(8,128)S(1)}) custom-call(f32[512,1152]{1,0:T(8,128)} %copy-done.197, bf16[8,1024]{1,0:T(8,128)(2,1)S(1)} %copy-done.211, f32[8,512]{1,0:T(8,128)S(1)} %copy-done.103, f32[8,1024]{1,0:T(8,128)S(1)} %copy-done.92, ...), custom_call_target="tpu_custom_call" | custom-call | flops 4750000128 | bytes 1024 | tf_op jit(solution)/shard_map/pallas_call | solution.py:59
  209.2 16.7 %collective-permute-done.24.refs_4_ = f32[128,1536]{1,0:T(8,128)S(1)} collective-permute-done((f32[128,1536]{1,0:T(8,128)S(1)}, f32[128,1536]{1,0:T(8,128)S(1)}, u32[]{:S(2)}, u32[]{:S(2)}) %collective-permute-start.24) | collective-permute-done | bytes 786464 | tf_op jit(solution)/shard_map/ppermute | solution.py:78
  227.8 15.0 %collective-permute-done.30.refs_4_ = f32[128,1536]{1,0:T(8,128)S(1)} collective-permute-done((f32[128,1536]{1,0:T(8,128)S(1)}, f32[128,1536]{1,0:T(8,128)S(1)}, u32[]{:S(2)}, u32[]{:S(2)}) %collective-permute-start.30) | collective-permute-done | bytes 786464 | tf_op jit(solution)/shard_map/ppermute | solution.py:78
  253.3 10.2 %all-gather.2.cloned.1.call-done.refs_5_.refs_1_.refs_2_.refs_4_.refs_6_.refs_7_.refs_8_ = bf16[1536,2688]{1,0:T(8,128)(2,1)} async-done(((bf16[192,2688]{1,0:T(8,128)(2,1)}), bf16[1536,2688]{1,0:T(8,128)(2,1)}) %all-gather.2.cloned.1.call-update) | async-done | bytes 8257552 | tf_op jit(solution)/shard_map/all_gather | solution.py:1521
  285.0 9.2 %shard_map.317 = (f32[512,1024]{1,0:T(8,128)S(1)}, f32[512,768]{1,0:T(8,128)S(1)}, f32[4,128,768]{2,1,0:T(8,128)S(1)}, f32[128,768]{1,0:T(8,128)S(1)}, f32[512,128]{1,0:T(8,128)S(1)}) custom-call(f32[512,1152]{1,0:T(8,128)} %get-tuple-element.189.refs_0_.refs_2_.refs_3_, bf16[8,1024]{1,0:T(8,128)(2,1)S(1)} %collective-permute-done.32.refs_1_.refs_4_, ...), custom_call_target="tpu_custom_call" | custom-call | flops 4750000128 | bytes 1024 | tf_op jit(solution)/shard_map/pallas_call | solution.py:59
  298.1 9.2 %shard_map.318 = (f32[512,1024]{1,0:T(8,128)}, f32[512,768]{1,0:T(8,128)S(1)}, f32[4,128,768]{2,1,0:T(8,128)S(1)}, f32[128,768]{1,0:T(8,128)S(1)}, f32[512,128]{1,0:T(8,128)S(1)}) custom-call(f32[512,1152]{1,0:T(8,128)} %get-tuple-element.197.refs_0_.refs_2_.refs_3_, bf16[8,1024]{1,0:T(8,128)(2,1)S(1)} %collective-permute-done.36.refs_1_.refs_4_, ...), custom_call_target="tpu_custom_call" | custom-call | flops 4750000128 | bytes 1024 | tf_op jit(solution)/shard_map/pallas_call | solution.py:59
  353.5 10.3 %shard_map.327.refs_15_ = bf16[1536,1536]{1,0:T(8,128)(2,1)} custom-call(s32[2]{0:T(128)} %pad_add_fusion.1.refs_0_, bf16[512,1536]{1,0:T(8,128)(2,1)} %copy-done.25, bf16[512,1536]{1,0:T(8,128)(2,1)} %copy-done.26, bf16[2,512,1536]{2,1,0:T(8,128)(2,1)} %refs_5_.3, bf16[2,512,1536]{2,1,0:T(8,128)(2,1)} %refs_5_.3, bf16[512,768]{1,0:T(8,128)(2,1)} %copy-done.64, ...), custom_call_target="tpu_custom_call" | custom-call | flops 5000000000 | bytes 1024 | tf_op jit(solution)/shard_map/pallas_call | solution.py:59
  365.6 9.5 %collective-permute-done.41.refs_14_ = bf16[128,768]{1,0:T(8,128)(2,1)S(1)} collective-permute-done((bf16[128,768]{1,0:T(8,128)(2,1)S(1)}, bf16[128,768]{1,0:T(8,128)(2,1)S(1)}, u32[]{:S(2)}, u32[]{:S(2)}) %collective-permute-start.41) | collective-permute-done | bytes 196640 | tf_op jit(solution)/shard_map/ppermute | solution.py:88
  377.9 16.9 %shard_map.328 = (bf16[512,1152]{1,0:T(8,128)(2,1)S(1)}, f32[8,1024]{1,0:T(8,128)S(1)}, f32[8,128]{1,0:T(8,128)S(1)}, f32[16,1024]{1,0:T(8,128)S(1)}, f32[16,1024]{1,0:T(8,128)S(1)}) custom-call(f32[512,768]{1,0:T(8,128)S(1)} %copy-done.135, f32[512,1024]{1,0:T(8,128)} %copy-done.7, f32[512,1152]{1,0:T(8,128)} %get-tuple-element.189.refs_0_.refs_2_.refs_3_, ...), custom_call_target="tpu_custom_call" | custom-call | flops 8999999488 | bytes 1024 | tf_op jit(solution)/shard_map/pallas_call | solution.py:59
  402.8 7.6 %shard_map.330 = (bf16[2,128,1536]{2,1,0:T(8,128)(2,1)S(1)}, bf16[2,128,1536]{2,1,0:T(8,128)(2,1)S(1)}, bf16[512,1152]{1,0:T(8,128)(2,1)S(1)}) custom-call(s32[4]{0:T(128)S(1)} %copy-done.98, bf16[512,1152]{1,0:T(8,128)(2,1)S(1)} %get-tuple-element.227.refs_1_, bf16[512,768]{1,0:T(8,128)(2,1)S(1)} %copy-done.65, f32[16,1024]{1,0:T(8,128)S(1)} %get-tuple-element.228.refs_3_, ...), custom_call_target="tpu_custom_call" | custom-call | flops 3800000000 | bytes 1024 | tf_op jit(solution)/shard_map/pallas_call | solution.py:59
  422.8 16.8 %shard_map.332 = (bf16[512,1152]{1,0:T(8,128)(2,1)S(1)}, f32[8,1024]{1,0:T(8,128)S(1)}, f32[8,128]{1,0:T(8,128)S(1)}, f32[16,1024]{1,0:T(8,128)S(1)}, f32[16,1024]{1,0:T(8,128)S(1)}) custom-call(f32[512,768]{1,0:T(8,128)S(1)} %copy-done.128, f32[512,1024]{1,0:T(8,128)} %get-tuple-element.201.refs_1_.refs_3_.refs_4_, ...), custom_call_target="tpu_custom_call" | custom-call | flops 8999999488 | bytes 1024 | tf_op jit(solution)/shard_map/pallas_call | solution.py:59
  452.0 7.6 %shard_map.335 = (bf16[2,128,1536]{2,1,0:T(8,128)(2,1)S(1)}, bf16[2,128,1536]{2,1,0:T(8,128)(2,1)S(1)}, bf16[512,1152]{1,0:T(8,128)(2,1)S(1)}) custom-call(s32[4]{0:T(128)S(1)} %copy-done.98, bf16[512,1152]{1,0:T(8,128)(2,1)S(1)} %get-tuple-element.232.refs_1_, bf16[512,768]{1,0:T(8,128)(2,1)S(1)} %copy-done.63, f32[16,1024]{1,0:T(8,128)S(1)} %get-tuple-element.233.refs_3_, ...), custom_call_target="tpu_custom_call" | custom-call | flops 3800000000 | bytes 1024 | tf_op jit(solution)/shard_map/pallas_call | solution.py:59
  469.4 8.7 %shard_map.339.refs_12_ = bf16[1536,1152]{1,0:T(8,128)(2,1)} custom-call(s32[2]{0:T(128)} %pad_add_fusion.1.refs_0_, bf16[512,1536]{1,0:T(8,128)(2,1)} %copy-done.25, bf16[512,1536]{1,0:T(8,128)(2,1)} %copy-done.26, bf16[512,1152]{1,0:T(8,128)(2,1)} %copy-done.137, bf16[512,1152]{1,0:T(8,128)(2,1)} %copy-done.139, bf16[128,1536]{1,0:T(8,128)(2,1)} %shard_map.338.refs_5_), custom_call_target="tpu_custom_call" | custom-call | flops 5000000000 | bytes 1024 | tf_op jit(solution)/shard_map/pallas_call | solution.py:59
  481.8 8.7 %collective-permute-done.56.refs_10_ = f32[8,512]{1,0:T(8,128)S(1)} collective-permute-done((f32[8,512]{1,0:T(8,128)S(1)}, f32[8,512]{1,0:T(8,128)S(1)}, u32[]{:S(2)}, u32[]{:S(2)}) %collective-permute-start.56) | collective-permute-done | bytes 16416 | tf_op jit(solution)/shard_map/ppermute | solution.py:242
  509.2 17.1 %shard_map.344 = (bf16[512,1152]{1,0:T(8,128)(2,1)S(1)}, f32[8,1024]{1,0:T(8,128)S(1)}, f32[8,128]{1,0:T(8,128)S(1)}, f32[16,1024]{1,0:T(8,128)S(1)}, f32[16,1024]{1,0:T(8,128)S(1)}) custom-call(f32[512,768]{1,0:T(8,128)S(1)} %copy-done.131, f32[512,1024]{1,0:T(8,128)} %get-tuple-element.167.refs_1_.refs_3_.refs_4_, f32[512,1152]{1,0:T(8,128)} %copy-done.196, ...), custom_call_target="tpu_custom_call" | custom-call | flops 8999999488 | bytes 1024 | tf_op jit(solution)/shard_map/pallas_call | solution.py:59
  535.1 7.7 %shard_map.347 = (bf16[2,128,1536]{2,1,0:T(8,128)(2,1)S(1)}, bf16[2,128,1536]{2,1,0:T(8,128)(2,1)S(1)}, bf16[512,1152]{1,0:T(8,128)(2,1)S(1)}) custom-call(s32[4]{0:T(128)S(1)} %copy-done.98, bf16[512,1152]{1,0:T(8,128)(2,1)S(1)} %get-tuple-element.251.refs_1_, bf16[512,768]{1,0:T(8,128)(2,1)S(1)} %get-tuple-element.252.refs_2_.refs_5_, ...), custom_call_target="tpu_custom_call" | custom-call | flops 3800000000 | bytes 1024 | tf_op jit(solution)/shard_map/pallas_call | solution.py:59
  558.4 11.7 %shard_map.349 = (bf16[4,192,1536]{2,1,0:T(8,128)(2,1)}, bf16[192,1536]{1,0:T(8,128)(2,1)}, bf16[192,1536]{1,0:T(8,128)(2,1)}, bf16[192,1536]{1,0:T(8,128)(2,1)}, bf16[192,1536]{1,0:T(8,128)(2,1)}) custom-call(s32[2]{0:T(128)} %pad_add_fusion.1.refs_0_, bf16[512,1536]{1,0:T(8,128)(2,1)} %copy-done.21, bf16[512,1536]{1,0:T(8,128)(2,1)} %copy-done.24, ...), custom_call_target="tpu_custom_call" | custom-call | flops 5000000000 | bytes 1024 | tf_op jit(solution)/shard_map/pallas_call | solution.py:59
  575.4 17.1 %shard_map.351 = (bf16[512,1152]{1,0:T(8,128)(2,1)S(1)}, f32[8,1024]{1,0:T(8,128)S(1)}, f32[8,128]{1,0:T(8,128)S(1)}, f32[16,1024]{1,0:T(8,128)S(1)}, f32[16,1024]{1,0:T(8,128)S(1)}) custom-call(f32[512,768]{1,0:T(8,128)S(1)} %copy-done.133, f32[512,1024]{1,0:T(8,128)} %get-tuple-element.177.refs_1_.refs_3_.refs_4_, f32[512,1152]{1,0:T(8,128)} %copy-done.197, ...), custom_call_target="tpu_custom_call" | custom-call | flops 8999999488 | bytes 1024 | tf_op jit(solution)/shard_map/pallas_call | solution.py:59
  604.1 7.6 %shard_map.356 = (bf16[2,128,1536]{2,1,0:T(8,128)(2,1)S(1)}, bf16[2,128,1536]{2,1,0:T(8,128)(2,1)S(1)}, bf16[512,1152]{1,0:T(8,128)(2,1)S(1)}) custom-call(s32[4]{0:T(128)S(1)} %copy-done.98, bf16[512,1152]{1,0:T(8,128)(2,1)S(1)} %get-tuple-element.277.refs_1_, bf16[512,768]{1,0:T(8,128)(2,1)S(1)} %copy-done.42, f32[16,1024]{1,0:T(8,128)S(1)} %get-tuple-element.278.refs_3_, ...), custom_call_target="tpu_custom_call" | custom-call | flops 3800000000 | bytes 1024 | tf_op jit(solution)/shard_map/pallas_call | solution.py:59
  615.6 14.0 %collective-permute-done.75.refs_1_ = bf16[192,1536]{1,0:T(8,128)(2,1)S(1)} collective-permute-done((bf16[192,1536]{1,0:T(8,128)(2,1)S(1)}, bf16[192,1536]{1,0:T(8,128)(2,1)S(1)}, u32[]{:S(2)}, u32[]{:S(2)}) %collective-permute-start.75) | collective-permute-done | bytes 589856 | tf_op jit(solution)/shard_map/ppermute | solution.py:93
  635.6 10.1 %shard_map.359 = (bf16[4,192,1152]{2,1,0:T(8,128)(2,1)}, bf16[192,1152]{1,0:T(8,128)(2,1)}, bf16[192,1152]{1,0:T(8,128)(2,1)}, bf16[192,1152]{1,0:T(8,128)(2,1)}, bf16[192,1152]{1,0:T(8,128)(2,1)}) custom-call(s32[2]{0:T(128)} %pad_add_fusion.1.refs_0_, bf16[512,1536]{1,0:T(8,128)(2,1)} %copy-done.21, bf16[512,1536]{1,0:T(8,128)(2,1)} %copy-done.24, ...), custom_call_target="tpu_custom_call" | custom-call | flops 5000000000 | bytes 1024 | tf_op jit(solution)/shard_map/pallas_call | solution.py:59
  678.4 12.7 %collective-permute-done.90.refs_1_ = bf16[192,1152]{1,0:T(8,128)(2,1)} collective-permute-done((bf16[192,1152]{1,0:T(8,128)(2,1)}, bf16[192,1152]{1,0:T(8,128)(2,1)}, u32[]{:S(2)}, u32[]{:S(2)}) %collective-permute-start.90) | collective-permute-done | bytes 442400 | tf_op jit(solution)/shard_map/ppermute | solution.py:93
  (895 shorter events, 470.7 us)
Async XLA Ops:
  7.2 256.4 %all-gather.2.cloned.1.call-start = ((), (), s32[]{:S(2)}) async-start(), calls=%async_computation.2 | async-start | bytes 9289728 | tf_op jit(solution)/shard_map/all_gather | solution.py:1521
  10.9 24.0 %collective-permute-start.4 = (bf16[2,16,1536]{2,1,0:T(8,128)(2,1)S(1)}, bf16[2,16,1536]{2,1,0:T(8,128)(2,1)S(1)}, u32[]{:S(2)}, u32[]{:S(2)}) collective-permute-start(bf16[2,16,1536]{2,1,0:T(8,128)(2,1)S(1)} %slice.182), channel_id=1, source_target_pairs={{0,4},{1,5},{2,6},{3,7},{8,12},{9,13},{10,14},{11,15},{16,20},{17,... | collective-permute-start | bytes 294920 | tf_op jit(solution)/shard_map/ppermute | solution.py:88
  71.6 26.1 %collective-permute-start.11 = (bf16[192,1536]{1,0:T(8,128)(2,1)S(1)}, bf16[192,1536]{1,0:T(8,128)(2,1)}, u32[]{:S(2)}, u32[]{:S(2)}) collective-permute-start(bf16[192,1536]{1,0:T(8,128)(2,1)S(1)} %shard_map.292.refs_9_.refs_1_), channel_id=1, source_target_pairs={{0,24},{8,0},{16,8},{24,16},{1,25},{9,1},{17,9},{25,17},{2,26},{10... | collective-permute-start | bytes 1769480 | tf_op jit(solution)/shard_map/ppermute | solution.py:93
  139.7 362.5 %reduce-scatter.3.cloned.1.call-start = ((), (), s32[]{:S(2)}) async-start(), calls=%async_computation.3 | async-start | bytes 5308416 | tf_op jit(solution)/shard_map/reduce_scatter | solution.py:1697
  139.7 28.3 %collective-permute-start.18 = (bf16[192,1536]{1,0:T(8,128)(2,1)}, bf16[192,1536]{1,0:T(8,128)(2,1)S(1)}, u32[]{:S(2)}, u32[]{:S(2)}) collective-permute-start(bf16[192,1536]{1,0:T(8,128)(2,1)} %copy-done.76), channel_id=1, source_target_pairs={{0,4},{4,0},{1,5},{5,1},{2,6},{6,2},{3,7},{7,3},{8,12},{12,8},{9,1... | collective-permute-start | bytes 1769480 | tf_op jit(solution)/shard_map/ppermute | solution.py:93
  140.8 27.2 %collective-permute-start.13 = (f32[128,768]{1,0:T(8,128)}, f32[128,768]{1,0:T(8,128)S(1)}, u32[]{:S(2)}, u32[]{:S(2)}) collective-permute-start(f32[128,768]{1,0:T(8,128)} %copy-done.183), channel_id=1, source_target_pairs={{0,4},{1,5},{2,6},{3,7},{8,12},{9,13},{10,14},{11,15},{16,20},{17,... | collective-permute-start | bytes 1179656 | tf_op jit(solution)/shard_map/ppermute | solution.py:88
  159.4 25.1 %collective-permute-start.22 = (f32[128,768]{1,0:T(8,128)S(1)}, f32[128,768]{1,0:T(8,128)S(1)}, u32[]{:S(2)}, u32[]{:S(2)}) collective-permute-start(f32[128,768]{1,0:T(8,128)S(1)} %get-tuple-element.178), channel_id=1, source_target_pairs={{0,4},{1,5},{2,6},{3,7},{8,12},{9,13},{10,14},{11,15},{16,20},{17,... | collective-permute-start | bytes 1179656 | tf_op jit(solution)/shard_map/ppermute | solution.py:88
  208.6 34.1 %collective-permute-start.30 = (f32[128,1536]{1,0:T(8,128)S(1)}, f32[128,1536]{1,0:T(8,128)S(1)}, u32[]{:S(2)}, u32[]{:S(2)}) collective-permute-start(f32[128,1536]{1,0:T(8,128)S(1)} %shard_map.310.refs_6_), channel_id=1, source_target_pairs={{0,2},{1,3},{2,0},{3,1},{4,6},{5,7},{6,4},{7,5},{8,10},{9,11},{10,... | collective-permute-start | bytes 2359304 | tf_op jit(solution)/shard_map/ppermute | solution.py:78
  227.2 23.1 %collective-permute-start.29 = (bf16[128,1536]{1,0:T(8,128)(2,1)S(1)}, bf16[128,1536]{1,0:T(8,128)(2,1)S(1)}, u32[]{:S(2)}, u32[]{:S(2)}) collective-permute-start(bf16[128,1536]{1,0:T(8,128)(2,1)S(1)} %get-tuple-element.187.refs_6_.refs_0_.refs_1_), channel_id=1, source_target_pairs={{0,2},{1,3},{2,0},{3,1},{4,6},{5,7},{6,4},{7,5},{8,10},{9,11},{10,... | collective-permute-start | bytes 1179656 | tf_op jit(solution)/shard_map/ppermute | solution.py:78
  363.8 271.7 %reduce-scatter.5.cloned.1.call-start = ((), (), s32[]{:S(2)}) async-start(), calls=%async_computation.4 | async-start | bytes 3981312 | tf_op jit(solution)/shard_map/reduce_scatter | solution.py:1697
  413.8 27.2 %collective-permute-start.50 = (bf16[128,1536]{1,0:T(8,128)(2,1)S(1)}, bf16[128,1536]{1,0:T(8,128)(2,1)S(1)}, u32[]{:S(2)}, u32[]{:S(2)}) collective-permute-start(bf16[128,1536]{1,0:T(8,128)(2,1)S(1)} %shard_map.331.refs_15_), channel_id=1, source_target_pairs={{0,2},{1,3},{2,0},{3,1},{4,6},{5,7},{6,4},{7,5},{8,10},{9,11},{10,... | collective-permute-start | bytes 1179656 | tf_op jit(solution)/shard_map/ppermute | solution.py:78
  478.0 23.2 %collective-permute-start.45 = (bf16[2,128,1536]{2,1,0:T(8,128)(2,1)}, bf16[2,128,1536]{2,1,0:T(8,128)(2,1)S(1)}, u32[]{:S(2)}, u32[]{:S(2)}) collective-permute-start(bf16[2,128,1536]{2,1,0:T(8,128)(2,1)} %get-tuple-element.222.refs_9_), channel_id=1, source_target_pairs={{0,1},{1,0},{2,3},{3,2},{4,5},{5,4},{6,7},{7,6},{8,9},{9,8},{10,11... | collective-permute-start | bytes 2359304 | tf_op jit(solution)/shard_map/ppermute | solution.py:78
  478.2 28.7 %collective-permute-start.60 = (bf16[2,128,1536]{2,1,0:T(8,128)(2,1)}, bf16[2,128,1536]{2,1,0:T(8,128)(2,1)}, u32[]{:S(2)}, u32[]{:S(2)}) collective-permute-start(bf16[2,128,1536]{2,1,0:T(8,128)(2,1)} %get-tuple-element.237.refs_9_), channel_id=1, source_target_pairs={{0,1},{1,0},{2,3},{3,2},{4,5},{5,4},{6,7},{7,6},{8,9},{9,8},{10,11... | collective-permute-start | bytes 2359304 | tf_op jit(solution)/shard_map/ppermute | solution.py:78
  500.6 25.7 %collective-permute-start.62 = (bf16[128,1536]{1,0:T(8,128)(2,1)S(1)}, bf16[128,1536]{1,0:T(8,128)(2,1)S(1)}, u32[]{:S(2)}, u32[]{:S(2)}) collective-permute-start(bf16[128,1536]{1,0:T(8,128)(2,1)S(1)} %get-tuple-element.255.refs_0_.refs_1_), channel_id=1, source_target_pairs={{0,2},{1,3},{2,0},{3,1},{4,6},{5,7},{6,4},{7,5},{8,10},{9,11},{10,... | collective-permute-start | bytes 1179656 | tf_op jit(solution)/shard_map/ppermute | solution.py:78
  542.8 30.6 %collective-permute-start.64 = (bf16[2,128,1536]{2,1,0:T(8,128)(2,1)S(1)}, bf16[2,128,1536]{2,1,0:T(8,128)(2,1)S(1)}, u32[]{:S(2)}, u32[]{:S(2)}) collective-permute-start(bf16[2,128,1536]{2,1,0:T(8,128)(2,1)S(1)} %get-tuple-element.259.refs_12_), channel_id=1, source_target_pairs={{0,1},{1,0},{2,3},{3,2},{4,5},{5,4},{6,7},{7,6},{8,9},{9,8},{10,11... | collective-permute-start | bytes 2359304 | tf_op jit(solution)/shard_map/ppermute | solution.py:78
  545.0 54.7 %collective-permute-start.58 = (bf16[128,1536]{1,0:T(8,128)(2,1)}, bf16[128,1536]{1,0:T(8,128)(2,1)S(1)}, u32[]{:S(2)}, u32[]{:S(2)}) collective-permute-start(bf16[128,1536]{1,0:T(8,128)(2,1)} %shard_map.342.refs_2_), channel_id=1, source_target_pairs={{0,2},{1,3},{2,0},{3,1},{4,6},{5,7},{6,4},{7,5},{8,10},{9,11},{10,... | collective-permute-start | bytes 1179656 | tf_op jit(solution)/shard_map/ppermute | solution.py:78
  546.4 55.8 %collective-permute-start.73 = (bf16[128,1536]{1,0:T(8,128)(2,1)}, bf16[128,1536]{1,0:T(8,128)(2,1)}, u32[]{:S(2)}, u32[]{:S(2)}) collective-permute-start(bf16[128,1536]{1,0:T(8,128)(2,1)} %shard_map.343.refs_15_), channel_id=1, source_target_pairs={{0,2},{1,3},{2,0},{3,1},{4,6},{5,7},{6,4},{7,5},{8,10},{9,11},{10,... | collective-permute-start | bytes 1179656 | tf_op jit(solution)/shard_map/ppermute | solution.py:78
  570.1 24.7 %collective-permute-start.69 = (bf16[192,1536]{1,0:T(8,128)(2,1)}, bf16[192,1536]{1,0:T(8,128)(2,1)S(1)}, u32[]{:S(2)}, u32[]{:S(2)}) collective-permute-start(bf16[192,1536]{1,0:T(8,128)(2,1)} %get-tuple-element.270), channel_id=1, source_target_pairs={{0,4},{4,0},{1,5},{5,1},{2,6},{6,2},{3,7},{7,3},{8,12},{12,8},{9,1... | collective-permute-start | bytes 1769480 | tf_op jit(solution)/shard_map/ppermute | solution.py:93
  615.5 32.1 %collective-permute-start.79 = (bf16[192,1536]{1,0:T(8,128)(2,1)}, bf16[192,1536]{1,0:T(8,128)(2,1)S(1)}, u32[]{:S(2)}, u32[]{:S(2)}) collective-permute-start(bf16[192,1536]{1,0:T(8,128)(2,1)} %get-tuple-element.289), channel_id=1, source_target_pairs={{0,4},{4,0},{1,5},{5,1},{2,6},{6,2},{3,7},{7,3},{8,12},{12,8},{9,1... | collective-permute-start | bytes 1769480 | tf_op jit(solution)/shard_map/ppermute | solution.py:93
  665.5 32.8 %collective-permute-start.85 = (bf16[192,1536]{1,0:T(8,128)(2,1)}, bf16[192,1536]{1,0:T(8,128)(2,1)}, u32[]{:S(2)}, u32[]{:S(2)}) collective-permute-start(bf16[192,1536]{1,0:T(8,128)(2,1)} %get-tuple-element.267.refs_2_), channel_id=1, source_target_pairs={{0,4},{4,0},{1,5},{5,1},{2,6},{6,2},{3,7},{7,3},{8,12},{12,8},{9,1... | collective-permute-start | bytes 1769480 | tf_op jit(solution)/shard_map/ppermute | solution.py:93
  667.0 32.1 %collective-permute-start.86 = (bf16[192,1536]{1,0:T(8,128)(2,1)S(1)}, bf16[192,1536]{1,0:T(8,128)(2,1)}, u32[]{:S(2)}, u32[]{:S(2)}) collective-permute-start(bf16[192,1536]{1,0:T(8,128)(2,1)S(1)} %shard_map.360.refs_7_), channel_id=1, source_target_pairs={{0,24},{8,0},{16,8},{24,16},{1,25},{9,1},{17,9},{25,17},{2,26},{10... | collective-permute-start | bytes 1769480 | tf_op jit(solution)/shard_map/ppermute | solution.py:93
  667.3 23.7 %collective-permute-start.90 = (bf16[192,1152]{1,0:T(8,128)(2,1)}, bf16[192,1152]{1,0:T(8,128)(2,1)}, u32[]{:S(2)}, u32[]{:S(2)}) collective-permute-start(bf16[192,1152]{1,0:T(8,128)(2,1)} %get-tuple-element.297), channel_id=1, source_target_pairs={{0,4},{4,0},{1,5},{5,1},{2,6},{6,2},{3,7},{7,3},{8,12},{12,8},{9,1... | collective-permute-start | bytes 1327112 | tf_op jit(solution)/shard_map/ppermute | solution.py:93
  668.7 23.8 %collective-permute-start.91 = (bf16[192,1152]{1,0:T(8,128)(2,1)}, bf16[192,1152]{1,0:T(8,128)(2,1)}, u32[]{:S(2)}, u32[]{:S(2)}) collective-permute-start(bf16[192,1152]{1,0:T(8,128)(2,1)} %shard_map.363.refs_2_), channel_id=1, source_target_pairs={{0,24},{8,0},{16,8},{24,16},{1,25},{9,1},{17,9},{25,17},{2,26},{10... | collective-permute-start | bytes 1327112 | tf_op jit(solution)/shard_map/ppermute | solution.py:93
  669.0 24.9 %collective-permute-start.87 = (f32[2,8,512]{2,1,0:T(8,128)S(1)}, f32[2,8,512]{2,1,0:T(8,128)S(1)}, u32[]{:S(2)}, u32[]{:S(2)}) collective-permute-start(f32[2,8,512]{2,1,0:T(8,128)S(1)} %copy-done.191), channel_id=1, source_target_pairs={{0,1},{1,0},{2,3},{3,2},{4,5},{5,4},{6,7},{7,6},{8,9},{9,8},{10,11... | collective-permute-start | bytes 98312 | tf_op jit(solution)/shard_map/ppermute | solution.py:242
  (335 other events, 2969.3 us)
Sparse Core Ops, SparseCore 0:
  139.8 123.7 all-gather.1
  364.0 94.6 reduce-scatter.2
  478.2 81.2 reduce-scatter.4

commit v4 on v3

--- a/solution.py
+++ b/solution.py
@@ -1716,10 +1716,10 @@
     next(second_ring)
     scan_0(0)
     next(second_ring)
+    upper = every_row(relayed(upper_piece))
+    consts[1].update(front=(upper, 2 * width // third), gate=(upper, 0), out=(upper, 1))
     project_0(1)
     next(second_ring, None)
-    upper = every_row(relayed(upper_piece))
-    consts[1].update(front=(upper, 2 * width // third), gate=(upper, 0), out=(upper, 1))
     scan_0(1)
     precede(work[0][0]["carried"])
     (second,) = placed(second_table, [2 * width])
@@ -1731,26 +1731,28 @@
     out_0(0)
     step_pass(0, 0, "out")
     out_0(1)
+    step_norm(0, 0)
     step_pass(0, 1, "out")
-    step_norm(0, 0)
-    step_norm(0, 1)
     incoming[0] = step_join(0, 0, "rows")
     project_1(0)
+    step_norm(0, 1)
     incoming[1] = step_join(0, 1, "rows")
+    scan_1(0)
     project_1(1)
-    scan_1(0)
+    gate_1(0)
     scan_1(1)
-    gate_1(0)
     mix_1(0)
     gate_1(1)
+    grad_1(0)
     mix_1(1)
-    grad_1(0)
     grad_1(1)
     mixed_1(0)
     mixed_1(1)
+    precede(work[1][0]["dend"])
     second_sums[1] = scattered(step_second_grad(1)[0])
     scanned_1(0)
     out_1(0)
+    precede(work[1][1]["dend"])
     input_1(0)
     step_pass(1, 0, "back")
     scanned_1(1)
@@ -1758,49 +1760,51 @@
     out_1(1)
     input_1(1)
     incoming[0] = step_join(1, 0, "grad_low")
+    step_pass(1, 1, "back")
     grad_0(0)
-    step_pass(1, 1, "back")
+    step_pass(1, 0, "out")
+    step_pass(1, 1, "out")
+    precede(*work[0][0]["stats"])
     first_grad = step_first_grad(1)
     mixed_0(0)
     step_norm_back(1, 1)
     precede(second_sums[1])
-    step_pass(1, 0, "out")
-    step_pass(1, 1, "out")
     first_sums[1] = scattered(first_grad[0])
     scanned_0(0)
+    for s in seq_range:
+        step_norm(1, s)
     incoming[1] = step_join(1, 1, "grad_low")
     grad_0(1)
     input_0(0)
     mixed_0(1)
     second_steps = ring_steps(step_second_grad(0))
     step_pass(0, 0, "back")
+    precede(first_sums[1])
     scanned_0(1)
+    outputs.extend(step_join(1, s, "rows") for s in seq_range)
     next(second_steps)
     step_norm_back(0, 0)
-    for s in seq_range:
-        step_norm(1, s)
     input_0(1)
+    first_steps = ring_steps(step_first_grad(0))
+    step_pass(0, 1, "back")
     next(second_steps)
-    step_pass(0, 1, "back")
-    precede(first_sums[1])
-    first_steps = ring_steps(step_first_grad(0))
-    next(second_steps)
+    incoming[0] = step_join(0, 0, "grad_low")
+    next(first_steps)
+    layer_out = assembled(outputs, arrived)
     step_norm_back(0, 1)
     small_steps = small_sums(work, width, heads, model, consts[0]["red"])
     next(small_steps)
     next(first_steps)
-    outputs.extend(step_join(1, s, "rows") for s in seq_range)
-    layer_out = assembled(outputs, arrived)
+    next(small_steps)
+    next(second_steps)
+    second_sums[1], first_sums[1] = widened(second_sums[1]), widened(first_sums[1])
+    incoming[1] = step_join(0, 1, "grad_low")
     next(first_steps)
     next(small_steps)
-    second_sums[0] = next(second_steps)
-    second_sums[1], first_sums[1] = widened(second_sums[1]), widened(first_sums[1])
-    incoming[0] = step_join(0, 0, "grad_low")
-    next(first_steps)
-    next(small_steps)
-    incoming[1] = step_join(0, 1, "grad_low")
     grad_stream = assembled(incoming, arrived)
     first_sums[0] = next(first_steps)
+    next(small_steps)
+    second_sums[0] = next(second_steps)
     for value in small_steps:
         small_out = value
 

time: 771 us -> 753 us (0.977)
  waiting for transfers between devices: 173 us -> 130 us
  Pallas kernels: 346 us -> 359 us
  starting transfers between devices: 116 us -> 129 us
    ppermute x16, waiting for transfers between devices: 24.2 us -> 6.42 us  [shifted(): lax.ppermute(value, axis, [(source, source + steps) for source in range(l...]
    pallas_call x91, Pallas kernels: 346 us -> 359 us  [call(): pl.pallas_call(without_tokens, cost_estimate=pl.CostEstimate(flops=int(co...]
    ppermute x28, waiting for transfers between devices: 58.1 us -> 48.8 us  [ring(): lax.ppermute(value, axis, [(i, (i - 1) % count) for i in range(count)])]
    ppermute x28, starting transfers between devices: 47.7 us -> 56.9 us  [ring(): lax.ppermute(value, axis, [(i, (i - 1) % count) for i in range(count)])]
    ppermute x21, waiting for transfers between devices: 11.7 us -> 3.28 us  [from_others(): lax.ppermute(value, axis, [(i, i ^ step) for i in range(count)])]
    unnamed x504 -> x574, local copies, waits for them, and re-layouts: 75.8 us -> 71.9 us
  transfers between devices with their start and end apart: 111 -> 111, of which waited for: 38 -> 36; matrix products, arithmetic and copies ran while one was open for 4% -> 5% of each run, Pallas kernels for 42% -> 46%
where the time goes in v4:
time: 753 us; the launch traced here: 740 us
  Pallas kernels  359 us (48%)
  waiting for transfers between devices  130 us (17%)
  starting transfers between devices  129 us (17%)
  local copies, waits for them, and re-layouts  94.6 us (13%)
  between operations  17.5 us (2%)
  other arithmetic  10.7 us (1%)
    pallas_call x91, Pallas kernels, call(): pl.pallas_call(without_tokens, cost_estimate=pl.CostEstimate(flops=int(co...  359 us
    unnamed x574, local copies, waits for them, and re-layouts  71.9 us
    ppermute x37, waiting for transfers between devices, flipped(): return lax.ppermute(value, axis, [(i, i ^ 1 << bit) for i in range(count)])  62.6 us
    ppermute x28, starting transfers between devices, ring(): lax.ppermute(value, axis, [(i, (i - 1) % count) for i in range(count)])  56.9 us
    ppermute x28, waiting for transfers between devices, ring(): lax.ppermute(value, axis, [(i, (i - 1) % count) for i in range(count)])  48.8 us
    ppermute x16, starting transfers between devices, shifted(): lax.ppermute(value, axis, [(source, source + steps) for source in range(l...  32 us
    ppermute x37, starting transfers between devices, flipped(): return lax.ppermute(value, axis, [(i, i ^ 1 << bit) for i in range(count)])  23.5 us
  transfers between devices with their start and end apart: 111, of which 36 were waited for; matrix products, arithmetic and copies ran while one was open for 5% of the time, Pallas kernels for 46%

profile of v4, /device:TPU:0, one launch (start us, length us, event | category | flops | bytes accessed | tf_op | source)
XLA Modules:
  0.0 740.3 jit_solution(8473239293342098737)
XLA Ops:
  34.7 7.6 %collective-permute-done.2.refs_3_.refs_2_ = bf16[192,1152]{1,0:T(8,128)(2,1)S(1)} collective-permute-done((bf16[192,1152]{1,0:T(8,128)(2,1)S(1)}, bf16[192,1152]{1,0:T(8,128)(2,1)S(1)}, u32[]{:S(2)}, u32[]{:S(2)}) %collective-permute-start.2) | collective-permute-done | bytes 442400 | tf_op jit(solution)/shard_map/ppermute | solution.py:93
  109.2 9.3 %shard_map.296 = (f32[512,1024]{1,0:T(8,128)}, f32[512,768]{1,0:T(8,128)S(1)}, f32[4,128,768]{2,1,0:T(8,128)S(1)}, f32[128,768]{1,0:T(8,128)S(1)}, f32[512,128]{1,0:T(8,128)S(1)}) custom-call(f32[512,1152]{1,0:T(8,128)} %copy-done.232, bf16[8,1024]{1,0:T(8,128)(2,1)S(1)} %get-tuple-element.165.refs_1_.refs_4_, ...), custom_call_target="tpu_custom_call" | custom-call | flops 4750000128 | bytes 1024 | tf_op jit(solution)/shard_map/pallas_call | solution.py:59
  125.0 6.8 shard_map.299
  133.2 14.1 %collective-permute-done.16.refs_2_.refs_6_ = bf16[192,1536]{1,0:T(8,128)(2,1)S(1)} collective-permute-done((bf16[192,1536]{1,0:T(8,128)(2,1)}, bf16[192,1536]{1,0:T(8,128)(2,1)S(1)}, u32[]{:S(2)}, u32[]{:S(2)}) %collective-permute-start.16) | collective-permute-done | bytes 589856 | tf_op jit(solution)/shard_map/ppermute | solution.py:93
  152.9 9.4 %shard_map.301 = (f32[512,1024]{1,0:T(8,128)}, f32[512,768]{1,0:T(8,128)S(1)}, f32[4,128,768]{2,1,0:T(8,128)S(1)}, f32[128,768]{1,0:T(8,128)S(1)}, f32[512,128]{1,0:T(8,128)S(1)}) custom-call(f32[512,1152]{1,0:T(8,128)} %copy-done.231, bf16[8,1024]{1,0:T(8,128)(2,1)S(1)} %get-tuple-element.171.refs_1_.refs_4_, ...), custom_call_target="tpu_custom_call" | custom-call | flops 4750000128 | bytes 1024 | tf_op jit(solution)/shard_map/pallas_call | solution.py:59
  204.9 18.9 %collective-permute-done.24.refs_4_ = f32[128,1536]{1,0:T(8,128)S(1)} collective-permute-done((f32[128,1536]{1,0:T(8,128)S(1)}, f32[128,1536]{1,0:T(8,128)S(1)}, u32[]{:S(2)}, u32[]{:S(2)}) %collective-permute-start.24) | collective-permute-done | bytes 786464 | tf_op jit(solution)/shard_map/ppermute | solution.py:78
  227.7 8.7 %collective-permute-done.28.refs_1_.refs_2_ = bf16[128,1536]{1,0:T(8,128)(2,1)S(1)} collective-permute-done((bf16[128,1536]{1,0:T(8,128)(2,1)S(1)}, bf16[128,1536]{1,0:T(8,128)(2,1)S(1)}, u32[]{:S(2)}, u32[]{:S(2)}) %collective-permute-start.28) | collective-permute-done | bytes 393248 | tf_op jit(solution)/shard_map/ppermute | solution.py:78
  240.3 7.7 %all-gather.2.cloned.1.call-done.refs_5_.refs_1_.refs_2_.refs_4_.refs_6_.refs_7_.refs_8_ = bf16[1536,2688]{1,0:T(8,128)(2,1)} async-done(((bf16[192,2688]{1,0:T(8,128)(2,1)}), bf16[1536,2688]{1,0:T(8,128)(2,1)}) %all-gather.2.cloned.1.call-update) | async-done | bytes 8257552 | tf_op jit(solution)/shard_map/all_gather | solution.py:1521
  263.2 9.0 %collective-permute-done.33.refs_1_.refs_2_ = bf16[128,1536]{1,0:T(8,128)(2,1)S(1)} collective-permute-done((bf16[128,1536]{1,0:T(8,128)(2,1)S(1)}, bf16[128,1536]{1,0:T(8,128)(2,1)S(1)}, u32[]{:S(2)}, u32[]{:S(2)}) %collective-permute-start.33) | collective-permute-done | bytes 393248 | tf_op jit(solution)/shard_map/ppermute | solution.py:78
  276.6 9.2 %shard_map.316 = (f32[512,1024]{1,0:T(8,128)}, f32[512,768]{1,0:T(8,128)S(1)}, f32[4,128,768]{2,1,0:T(8,128)S(1)}, f32[128,768]{1,0:T(8,128)S(1)}, f32[512,128]{1,0:T(8,128)S(1)}) custom-call(f32[512,1152]{1,0:T(8,128)} %get-tuple-element.188.refs_0_.refs_2_.refs_3_, bf16[8,1024]{1,0:T(8,128)(2,1)S(1)} %collective-permute-done.31.refs_1_.refs_4_, ...), custom_call_target="tpu_custom_call" | custom-call | flops 4750000128 | bytes 1024 | tf_op jit(solution)/shard_map/pallas_call | solution.py:59
  302.0 9.7 %shard_map.319 = (f32[512,1024]{1,0:T(8,128)}, f32[512,768]{1,0:T(8,128)S(1)}, f32[4,128,768]{2,1,0:T(8,128)S(1)}, f32[128,768]{1,0:T(8,128)S(1)}, f32[512,128]{1,0:T(8,128)S(1)}) custom-call(f32[512,1152]{1,0:T(8,128)} %copy-done.151, bf16[8,1024]{1,0:T(8,128)(2,1)S(1)} %collective-permute-done.36.refs_1_.refs_4_, f32[8,512]{1,0:T(8,128)S(1)} %copy-done.122, ...), custom_call_target="tpu_custom_call" | custom-call | flops 4750000128 | bytes 1024 | tf_op jit(solution)/shard_map/pallas_call | solution.py:59
  358.4 10.3 %shard_map.327.refs_15_ = bf16[1536,1536]{1,0:T(8,128)(2,1)} custom-call(s32[2]{0:T(128)} %pad_add_fusion.1.refs_0_, bf16[512,1536]{1,0:T(8,128)(2,1)} %copy-done.28, bf16[512,1536]{1,0:T(8,128)(2,1)} %copy-done.29, bf16[2,512,1536]{2,1,0:T(8,128)(2,1)} %refs_5_.3, bf16[2,512,1536]{2,1,0:T(8,128)(2,1)} %refs_5_.3, bf16[512,768]{1,0:T(8,128)(2,1)} %copy-done.63, ...), custom_call_target="tpu_custom_call" | custom-call | flops 5000000000 | bytes 1024 | tf_op jit(solution)/shard_map/pallas_call | solution.py:59
  373.4 17.2 %shard_map.328 = (bf16[512,1152]{1,0:T(8,128)(2,1)S(1)}, f32[8,1024]{1,0:T(8,128)S(1)}, f32[8,128]{1,0:T(8,128)S(1)}, f32[16,1024]{1,0:T(8,128)S(1)}, f32[16,1024]{1,0:T(8,128)S(1)}) custom-call(f32[512,768]{1,0:T(8,128)S(1)} %copy-done.157, f32[512,1024]{1,0:T(8,128)} %get-tuple-element.192.refs_1_.refs_3_.refs_4_, ...), custom_call_target="tpu_custom_call" | custom-call | flops 8999999488 | bytes 1024 | tf_op jit(solution)/shard_map/pallas_call | solution.py:59
  398.2 7.7 %shard_map.330 = (bf16[2,128,1536]{2,1,0:T(8,128)(2,1)S(1)}, bf16[2,128,1536]{2,1,0:T(8,128)(2,1)S(1)}, bf16[512,1152]{1,0:T(8,128)(2,1)S(1)}) custom-call(s32[4]{0:T(128)S(1)} %copy-done.107, bf16[512,1152]{1,0:T(8,128)(2,1)S(1)} %get-tuple-element.223.refs_1_, bf16[512,768]{1,0:T(8,128)(2,1)S(1)} %copy-done.64, f32[16,1024]{1,0:T(8,128)S(1)} %get-tuple-element.224.refs_3_, ...), custom_call_target="tpu_custom_call" | custom-call | flops 3800000000 | bytes 1024 | tf_op jit(solution)/shard_map/pallas_call | solution.py:59
  410.9 16.9 %shard_map.332 = (bf16[512,1152]{1,0:T(8,128)(2,1)S(1)}, f32[8,1024]{1,0:T(8,128)S(1)}, f32[8,128]{1,0:T(8,128)S(1)}, f32[16,1024]{1,0:T(8,128)S(1)}, f32[16,1024]{1,0:T(8,128)S(1)}) custom-call(f32[512,768]{1,0:T(8,128)S(1)} %get-tuple-element.229.refs_0_, f32[512,1024]{1,0:T(8,128)} %get-tuple-element.205.refs_1_.refs_3_.refs_4_, f32[512,1152]{1,0:T(8,128)} %copy-done.151, ...), custom_call_target="tpu_custom_call" | custom-call | flops 8999999488 | bytes 1024 | tf_op jit(solution)/shard_map/pallas_call | solution.py:59
  438.2 7.7 %shard_map.335 = (bf16[2,128,1536]{2,1,0:T(8,128)(2,1)S(1)}, bf16[2,128,1536]{2,1,0:T(8,128)(2,1)S(1)}, bf16[512,1152]{1,0:T(8,128)(2,1)S(1)}) custom-call(s32[4]{0:T(128)S(1)} %copy-done.107, bf16[512,1152]{1,0:T(8,128)(2,1)S(1)} %get-tuple-element.233.refs_1_, bf16[512,768]{1,0:T(8,128)(2,1)S(1)} %copy-done.62, f32[16,1024]{1,0:T(8,128)S(1)} %get-tuple-element.234.refs_3_, ...), custom_call_target="tpu_custom_call" | custom-call | flops 3800000000 | bytes 1024 | tf_op jit(solution)/shard_map/pallas_call | solution.py:59
  460.3 8.7 %shard_map.341.refs_12_ = bf16[1536,1152]{1,0:T(8,128)(2,1)} custom-call(s32[2]{0:T(128)} %pad_add_fusion.1.refs_0_, bf16[512,1536]{1,0:T(8,128)(2,1)} %copy-done.28, bf16[512,1536]{1,0:T(8,128)(2,1)} %copy-done.29, bf16[512,1152]{1,0:T(8,128)(2,1)} %copy-done.159, bf16[512,1152]{1,0:T(8,128)(2,1)} %copy-done.160, bf16[128,1536]{1,0:T(8,128)(2,1)} %shard_map.340.refs_5_, ...), custom_call_target="tpu_custom_call" | custom-call | flops 5000000000 | bytes 1024 | tf_op jit(solution)/shard_map/pallas_call | solution.py:59
  493.8 17.3 %shard_map.344 = (bf16[512,1152]{1,0:T(8,128)(2,1)S(1)}, f32[8,1024]{1,0:T(8,128)S(1)}, f32[8,128]{1,0:T(8,128)S(1)}, f32[16,1024]{1,0:T(8,128)S(1)}, f32[16,1024]{1,0:T(8,128)S(1)}) custom-call(f32[512,768]{1,0:T(8,128)S(1)} %copy-done.155, f32[512,1024]{1,0:T(8,128)} %get-tuple-element.167.refs_1_.refs_3_.refs_4_, f32[512,1152]{1,0:T(8,128)} %copy-done.232, ...), custom_call_target="tpu_custom_call" | custom-call | flops 8999999488 | bytes 1024 | tf_op jit(solution)/shard_map/pallas_call | solution.py:59
  526.2 7.6 %shard_map.349 = (bf16[2,128,1536]{2,1,0:T(8,128)(2,1)S(1)}, bf16[2,128,1536]{2,1,0:T(8,128)(2,1)S(1)}, bf16[512,1152]{1,0:T(8,128)(2,1)S(1)}) custom-call(s32[4]{0:T(128)S(1)} %copy-done.108, bf16[512,1152]{1,0:T(8,128)(2,1)S(1)} %get-tuple-element.255.refs_1_, bf16[512,768]{1,0:T(8,128)(2,1)S(1)} %get-tuple-element.256.refs_2_.refs_5_, ...), custom_call_target="tpu_custom_call" | custom-call | flops 3800000000 | bytes 1024 | tf_op jit(solution)/shard_map/pallas_call | solution.py:59
  548.5 11.7 %shard_map.351 = (bf16[4,192,1536]{2,1,0:T(8,128)(2,1)}, bf16[192,1536]{1,0:T(8,128)(2,1)}, bf16[192,1536]{1,0:T(8,128)(2,1)}, bf16[192,1536]{1,0:T(8,128)(2,1)}, bf16[192,1536]{1,0:T(8,128)(2,1)}) custom-call(s32[2]{0:T(128)} %pad_add_fusion.1.refs_0_, bf16[512,1536]{1,0:T(8,128)(2,1)} %copy-done.23, bf16[512,1536]{1,0:T(8,128)(2,1)} %copy-done.27, ...), custom_call_target="tpu_custom_call" | custom-call | flops 5000000000 | bytes 1024 | tf_op jit(solution)/shard_map/pallas_call | solution.py:59
  568.4 16.9 %shard_map.353 = (bf16[512,1152]{1,0:T(8,128)(2,1)S(1)}, f32[8,1024]{1,0:T(8,128)S(1)}, f32[8,128]{1,0:T(8,128)S(1)}, f32[16,1024]{1,0:T(8,128)S(1)}, f32[16,1024]{1,0:T(8,128)S(1)}) custom-call(f32[512,768]{1,0:T(8,128)S(1)} %get-tuple-element.260.refs_0_, f32[512,1024]{1,0:T(8,128)} %get-tuple-element.177.refs_1_.refs_3_.refs_4_, f32[512,1152]{1,0:T(8,128)} %copy-done.231, ...), custom_call_target="tpu_custom_call" | custom-call | flops 8999999488 | bytes 1024 | tf_op jit(solution)/shard_map/pallas_call | solution.py:59
  596.3 8.2 %shard_map.358 = (bf16[2,128,1536]{2,1,0:T(8,128)(2,1)}, bf16[2,128,1536]{2,1,0:T(8,128)(2,1)S(1)}, bf16[512,1152]{1,0:T(8,128)(2,1)S(1)}) custom-call(s32[4]{0:T(128)S(1)} %copy-done.108, bf16[512,1152]{1,0:T(8,128)(2,1)S(1)} %get-tuple-element.273.refs_1_, bf16[512,768]{1,0:T(8,128)(2,1)S(1)} %copy-done.40, f32[16,1024]{1,0:T(8,128)S(1)} %get-tuple-element.274.refs_3_, ...), custom_call_target="tpu_custom_call" | custom-call | flops 3800000000 | bytes 1024 | tf_op jit(solution)/shard_map/pallas_call | solution.py:59
  610.8 10.0 %shard_map.359 = (bf16[4,192,1152]{2,1,0:T(8,128)(2,1)}, bf16[192,1152]{1,0:T(8,128)(2,1)}, bf16[192,1152]{1,0:T(8,128)(2,1)}, bf16[192,1152]{1,0:T(8,128)(2,1)}, bf16[192,1152]{1,0:T(8,128)(2,1)}) custom-call(s32[2]{0:T(128)} %pad_add_fusion.1.refs_0_, bf16[512,1536]{1,0:T(8,128)(2,1)} %copy-done.23, bf16[512,1536]{1,0:T(8,128)(2,1)} %copy-done.27, ...), custom_call_target="tpu_custom_call" | custom-call | flops 5000000000 | bytes 1024 | tf_op jit(solution)/shard_map/pallas_call | solution.py:59
  708.2 7.6 %collective-permute-done.98.refs_1_ = f32[2,8,1408]{2,1,0:T(8,128)S(1)} collective-permute-done((f32[2,8,1408]{2,1,0:T(8,128)S(1)}, f32[2,8,1408]{2,1,0:T(8,128)S(1)}, u32[]{:S(2)}, u32[]{:S(2)}) %collective-permute-start.98) | collective-permute-done | bytes 90144 | tf_op jit(solution)/shard_map/ppermute | solution.py:78
  (965 shorter events, 464.4 us)
Async XLA Ops:
  7.2 240.8 %all-gather.2.cloned.1.call-start = ((), (), s32[]{:S(2)}) async-start(), calls=%async_computation.2 | async-start | bytes 9289728 | tf_op jit(solution)/shard_map/all_gather | solution.py:1521
  10.9 23.8 %collective-permute-start.4 = (bf16[2,16,1536]{2,1,0:T(8,128)(2,1)S(1)}, bf16[2,16,1536]{2,1,0:T(8,128)(2,1)S(1)}, u32[]{:S(2)}, u32[]{:S(2)}) collective-permute-start(bf16[2,16,1536]{2,1,0:T(8,128)(2,1)S(1)} %slice.182), channel_id=1, source_target_pairs={{0,4},{1,5},{2,6},{3,7},{8,12},{9,13},{10,14},{11,15},{16,20},{17,... | collective-permute-start | bytes 294920 | tf_op jit(solution)/shard_map/ppermute | solution.py:88
  71.3 27.4 %collective-permute-start.11 = (bf16[192,1536]{1,0:T(8,128)(2,1)S(1)}, bf16[192,1536]{1,0:T(8,128)(2,1)}, u32[]{:S(2)}, u32[]{:S(2)}) collective-permute-start(bf16[192,1536]{1,0:T(8,128)(2,1)S(1)} %shard_map.292.refs_9_.refs_1_), channel_id=1, source_target_pairs={{0,24},{8,0},{16,8},{24,16},{1,25},{9,1},{17,9},{25,17},{2,26},{10... | collective-permute-start | bytes 1769480 | tf_op jit(solution)/shard_map/ppermute | solution.py:93
  124.0 364.8 %reduce-scatter.3.cloned.1.call-start = ((), (), s32[]{:S(2)}) async-start(), calls=%async_computation.3 | async-start | bytes 5308416 | tf_op jit(solution)/shard_map/reduce_scatter | solution.py:1697
  124.0 23.3 %collective-permute-start.16 = (bf16[192,1536]{1,0:T(8,128)(2,1)}, bf16[192,1536]{1,0:T(8,128)(2,1)S(1)}, u32[]{:S(2)}, u32[]{:S(2)}) collective-permute-start(bf16[192,1536]{1,0:T(8,128)(2,1)} %copy-done.69), channel_id=1, source_target_pairs={{0,4},{4,0},{1,5},{5,1},{2,6},{6,2},{3,7},{7,3},{8,12},{12,8},{9,1... | collective-permute-start | bytes 1769480 | tf_op jit(solution)/shard_map/ppermute | solution.py:93
  287.0 27.6 %collective-permute-start.34 = (f32[128,768]{1,0:T(8,128)S(1)}, f32[128,768]{1,0:T(8,128)S(1)}, u32[]{:S(2)}, u32[]{:S(2)}) collective-permute-start(f32[128,768]{1,0:T(8,128)S(1)} %get-tuple-element.194), channel_id=1, source_target_pairs={{0,4},{1,5},{2,6},{3,7},{8,12},{9,13},{10,14},{11,15},{16,20},{17,... | collective-permute-start | bytes 1179656 | tf_op jit(solution)/shard_map/ppermute | solution.py:88
  368.9 197.6 %reduce-scatter.5.cloned.1.call-start = ((), (), s32[]{:S(2)}) async-start(), calls=%async_computation.4 | async-start | bytes 3981312 | tf_op jit(solution)/shard_map/reduce_scatter | solution.py:1697
  368.9 29.3 %collective-permute-start.47 = (bf16[128,768]{1,0:T(8,128)(2,1)S(1)}, bf16[128,768]{1,0:T(8,128)(2,1)S(1)}, u32[]{:S(2)}, u32[]{:S(2)}) collective-permute-start(bf16[128,768]{1,0:T(8,128)(2,1)S(1)} %get-tuple-element.226), channel_id=1, source_target_pairs={{4,0},{5,1},{6,2},{7,3},{12,8},{13,9},{14,10},{15,11},{20,16},{21,... | collective-permute-start | bytes 589832 | tf_op jit(solution)/shard_map/ppermute | solution.py:88
  478.3 32.8 %collective-permute-start.54 = (bf16[128,1536]{1,0:T(8,128)(2,1)}, bf16[128,1536]{1,0:T(8,128)(2,1)}, u32[]{:S(2)}, u32[]{:S(2)}) collective-permute-start(bf16[128,1536]{1,0:T(8,128)(2,1)} %shard_map.339.refs_2_), channel_id=1, source_target_pairs={{0,2},{1,3},{2,0},{3,1},{4,6},{5,7},{6,4},{7,5},{8,10},{9,11},{10,... | collective-permute-start | bytes 1179656 | tf_op jit(solution)/shard_map/ppermute | solution.py:78
  479.3 34.0 %collective-permute-start.63 = (bf16[128,1536]{1,0:T(8,128)(2,1)}, bf16[128,1536]{1,0:T(8,128)(2,1)}, u32[]{:S(2)}, u32[]{:S(2)}) collective-permute-start(bf16[128,1536]{1,0:T(8,128)(2,1)} %shard_map.340.refs_5_), channel_id=1, source_target_pairs={{0,2},{1,3},{2,0},{3,1},{4,6},{5,7},{6,4},{7,5},{8,10},{9,11},{10,... | collective-permute-start | bytes 1179656 | tf_op jit(solution)/shard_map/ppermute | solution.py:78
  483.9 31.3 %collective-permute-start.62 = (bf16[128,1536]{1,0:T(8,128)(2,1)S(1)}, bf16[128,1536]{1,0:T(8,128)(2,1)}, u32[]{:S(2)}, u32[]{:S(2)}) collective-permute-start(bf16[128,1536]{1,0:T(8,128)(2,1)S(1)} %get-tuple-element.252.refs_0_.refs_1_), channel_id=1, source_target_pairs={{0,2},{1,3},{2,0},{3,1},{4,6},{5,7},{6,4},{7,5},{8,10},{9,11},{10,... | collective-permute-start | bytes 1179656 | tf_op jit(solution)/shard_map/ppermute | solution.py:78
  533.9 29.3 %collective-permute-start.70 = (bf16[2,128,1536]{2,1,0:T(8,128)(2,1)S(1)}, bf16[2,128,1536]{2,1,0:T(8,128)(2,1)S(1)}, u32[]{:S(2)}, u32[]{:S(2)}) collective-permute-start(bf16[2,128,1536]{2,1,0:T(8,128)(2,1)S(1)} %get-tuple-element.259.refs_12_), channel_id=1, source_target_pairs={{0,1},{1,0},{2,3},{3,2},{4,5},{5,4},{6,7},{7,6},{8,9},{9,8},{10,11... | collective-permute-start | bytes 2359304 | tf_op jit(solution)/shard_map/ppermute | solution.py:78
  536.0 50.7 %collective-permute-start.61 = (bf16[128,1536]{1,0:T(8,128)(2,1)}, bf16[128,1536]{1,0:T(8,128)(2,1)}, u32[]{:S(2)}, u32[]{:S(2)}) collective-permute-start(bf16[128,1536]{1,0:T(8,128)(2,1)} %shard_map.345.refs_5_.refs_0_.refs_1_), channel_id=1, source_target_pairs={{0,2},{1,3},{2,0},{3,1},{4,6},{5,7},{6,4},{7,5},{8,10},{9,11},{10,... | collective-permute-start | bytes 1179656 | tf_op jit(solution)/shard_map/ppermute | solution.py:78
  537.4 52.6 %collective-permute-start.72 = (bf16[128,1536]{1,0:T(8,128)(2,1)}, bf16[128,1536]{1,0:T(8,128)(2,1)}, u32[]{:S(2)}, u32[]{:S(2)}) collective-permute-start(bf16[128,1536]{1,0:T(8,128)(2,1)} %shard_map.346.refs_2_.refs_0_.refs_5_), channel_id=1, source_target_pairs={{0,2},{1,3},{2,0},{3,1},{4,6},{5,7},{6,4},{7,5},{8,10},{9,11},{10,... | collective-permute-start | bytes 1179656 | tf_op jit(solution)/shard_map/ppermute | solution.py:78
  560.2 31.1 %collective-permute-start.76 = (bf16[192,1536]{1,0:T(8,128)(2,1)}, bf16[192,1536]{1,0:T(8,128)(2,1)}, u32[]{:S(2)}, u32[]{:S(2)}) collective-permute-start(bf16[192,1536]{1,0:T(8,128)(2,1)} %get-tuple-element.278), channel_id=1, source_target_pairs={{0,4},{4,0},{1,5},{5,1},{2,6},{6,2},{3,7},{7,3},{8,12},{12,8},{9,1... | collective-permute-start | bytes 1769480 | tf_op jit(solution)/shard_map/ppermute | solution.py:93
  563.2 46.2 %collective-permute-start.79 = (bf16[192,1536]{1,0:T(8,128)(2,1)}, bf16[192,1536]{1,0:T(8,128)(2,1)}, u32[]{:S(2)}, u32[]{:S(2)}) collective-permute-start(bf16[192,1536]{1,0:T(8,128)(2,1)} %get-tuple-element.285), channel_id=1, source_target_pairs={{0,4},{4,0},{1,5},{5,1},{2,6},{6,2},{3,7},{7,3},{8,12},{12,8},{9,1... | collective-permute-start | bytes 1769480 | tf_op jit(solution)/shard_map/ppermute | solution.py:93
  565.9 27.3 %collective-permute-start.75 = (bf16[128,1536]{1,0:T(8,128)(2,1)}, bf16[128,1536]{1,0:T(8,128)(2,1)}, u32[]{:S(2)}, u32[]{:S(2)}) collective-permute-start(bf16[128,1536]{1,0:T(8,128)(2,1)} %shard_map.352.refs_15_), channel_id=1, source_target_pairs={{0,2},{1,3},{2,0},{3,1},{4,6},{5,7},{6,4},{7,5},{8,10},{9,11},{10,... | collective-permute-start | bytes 1179656 | tf_op jit(solution)/shard_map/ppermute | solution.py:78
  605.6 32.1 %collective-permute-start.71 = (bf16[256,1536]{1,0:T(8,128)(2,1)}, bf16[256,1536]{1,0:T(8,128)(2,1)S(1)}, u32[]{:S(2)}, u32[]{:S(2)}) collective-permute-start(bf16[256,1536]{1,0:T(8,128)(2,1)} %shard_map.354.refs_2_), channel_id=1, source_target_pairs={{0,1},{1,0},{2,3},{3,2},{4,5},{5,4},{6,7},{7,6},{8,9},{9,8},{10,11... | collective-permute-start | bytes 2359304 | tf_op jit(solution)/shard_map/ppermute | solution.py:78
  606.1 33.1 %collective-permute-start.73 = (bf16[256,1536]{1,0:T(8,128)(2,1)S(1)}, bf16[256,1536]{1,0:T(8,128)(2,1)S(1)}, u32[]{:S(2)}, u32[]{:S(2)}) collective-permute-start(bf16[256,1536]{1,0:T(8,128)(2,1)S(1)} %shard_map.355.refs_2_), channel_id=1, source_target_pairs={{0,1},{1,0},{2,3},{3,2},{4,5},{5,4},{6,7},{7,6},{8,9},{9,8},{10,11... | collective-permute-start | bytes 2359304 | tf_op jit(solution)/shard_map/ppermute | solution.py:78
  625.4 38.5 %collective-permute-start.85 = (bf16[192,1536]{1,0:T(8,128)(2,1)}, bf16[192,1536]{1,0:T(8,128)(2,1)}, u32[]{:S(2)}, u32[]{:S(2)}) collective-permute-start(bf16[192,1536]{1,0:T(8,128)(2,1)} %get-tuple-element.290), channel_id=1, source_target_pairs={{0,4},{4,0},{1,5},{5,1},{2,6},{6,2},{3,7},{7,3},{8,12},{12,8},{9,1... | collective-permute-start | bytes 1769480 | tf_op jit(solution)/shard_map/ppermute | solution.py:93
  634.7 32.4 %collective-permute-start.86 = (bf16[192,1536]{1,0:T(8,128)(2,1)}, bf16[192,1536]{1,0:T(8,128)(2,1)}, u32[]{:S(2)}, u32[]{:S(2)}) collective-permute-start(bf16[192,1536]{1,0:T(8,128)(2,1)} %shard_map.361.refs_2_), channel_id=1, source_target_pairs={{0,24},{8,0},{16,8},{24,16},{1,25},{9,1},{17,9},{25,17},{2,26},{10... | collective-permute-start | bytes 1769480 | tf_op jit(solution)/shard_map/ppermute | solution.py:93
  662.0 35.7 %collective-permute-start.82 = (bf16[256,1536]{1,0:T(8,128)(2,1)}, bf16[256,1536]{1,0:T(8,128)(2,1)}, u32[]{:S(2)}, u32[]{:S(2)}) collective-permute-start(bf16[256,1536]{1,0:T(8,128)(2,1)} %shard_map.362.refs_2_), channel_id=1, source_target_pairs={{0,1},{1,0},{2,3},{3,2},{4,5},{5,4},{6,7},{7,6},{8,9},{9,8},{10,11... | collective-permute-start | bytes 2359304 | tf_op jit(solution)/shard_map/ppermute | solution.py:78
  674.6 27.4 %collective-permute-start.92 = (bf16[256,1536]{1,0:T(8,128)(2,1)}, bf16[256,1536]{1,0:T(8,128)(2,1)}, u32[]{:S(2)}, u32[]{:S(2)}) collective-permute-start(bf16[256,1536]{1,0:T(8,128)(2,1)} %shard_map.372.refs_3_), channel_id=1, source_target_pairs={{0,1},{1,0},{2,3},{3,2},{4,5},{5,4},{6,7},{7,6},{8,9},{9,8},{10,11... | collective-permute-start | bytes 2359304 | tf_op jit(solution)/shard_map/ppermute | solution.py:78
  682.6 24.7 %collective-permute-start.99 = (bf16[192,1152]{1,0:T(8,128)(2,1)S(1)}, bf16[192,1152]{1,0:T(8,128)(2,1)S(1)}, u32[]{:S(2)}, u32[]{:S(2)}) collective-permute-start(bf16[192,1152]{1,0:T(8,128)(2,1)S(1)} %copy-done.188), channel_id=1, source_target_pairs={{0,4},{4,0},{1,5},{5,1},{2,6},{6,2},{3,7},{7,3},{8,12},{12,8},{9,1... | collective-permute-start | bytes 1327112 | tf_op jit(solution)/shard_map/ppermute | solution.py:93
  (370 other events, 3272.9 us)
Sparse Core Ops, SparseCore 0:
  124.1 123.8 all-gather.1
  369.0 95.4 reduce-scatter.2
  469.2 82.1 reduce-scatter.4

commit v5 on v4

--- a/solution.py
+++ b/solution.py
@@ -853,7 +853,7 @@
     )(own, *terms)
 
 
-def ring_steps(blocks):
+def ring_steps(blocks, whole_first=False):
     dp, context = lax.axis_size("dp"), lax.axis_size("context")
     own, others = blocks[0], blocks[1:]
     places = list(range(1, dp)) + [0]
@@ -866,6 +866,8 @@
                 part = (side.astype(F32) + part.astype(F32)).astype(BF16)
             side = ring(part, "context")
         sides.append([] if side is None else [side])
+    if whole_first:
+        precede(*sides[-1])
     passed = []
     for k, side in zip(places, sides):
         value = ring_add(own, k, side + passed, BF16 if k else F32)
@@ -1777,7 +1779,7 @@
     grad_0(1)
     input_0(0)
     mixed_0(1)
-    second_steps = ring_steps(step_second_grad(0))
+    second_steps = ring_steps(step_second_grad(0), True)
     step_pass(0, 0, "back")
     precede(first_sums[1])
     scanned_0(1)
@@ -1785,26 +1787,26 @@
     next(second_steps)
     step_norm_back(0, 0)
     input_0(1)
+    next(second_steps)
     first_steps = ring_steps(step_first_grad(0))
     step_pass(0, 1, "back")
     next(second_steps)
     incoming[0] = step_join(0, 0, "grad_low")
     next(first_steps)
+    second_sums[0] = next(second_steps)
     layer_out = assembled(outputs, arrived)
     step_norm_back(0, 1)
     small_steps = small_sums(work, width, heads, model, consts[0]["red"])
     next(small_steps)
     next(first_steps)
     next(small_steps)
-    next(second_steps)
     second_sums[1], first_sums[1] = widened(second_sums[1]), widened(first_sums[1])
     incoming[1] = step_join(0, 1, "grad_low")
+    next(small_steps)
     next(first_steps)
-    next(small_steps)
     grad_stream = assembled(incoming, arrived)
     first_sums[0] = next(first_steps)
     next(small_steps)
-    second_sums[0] = next(second_steps)
     for value in small_steps:
         small_out = value
 

time: 753 us -> 738 us (0.980)
  local copies, waits for them, and re-layouts: 94.6 us -> 84.9 us
    unnamed x574 -> x552, local copies, waits for them, and re-layouts: 71.9 us -> 64.8 us
  transfers between devices with their start and end apart: 111 -> 111, of which waited for: 36 -> 39; matrix products, arithmetic and copies ran while one was open for 5% -> 5% of each run, Pallas kernels for 46% -> 46%
where the time goes in v5:
time: 738 us; the launch traced here: 726 us
  Pallas kernels  352 us (48%)
  waiting for transfers between devices  131 us (18%)
  starting transfers between devices  129 us (17%)
  local copies, waits for them, and re-layouts  84.9 us (12%)
  between operations  17.6 us (2%)
  other arithmetic  10.6 us (1%)
    pallas_call x91, Pallas kernels, call(): pl.pallas_call(without_tokens, cost_estimate=pl.CostEstimate(flops=int(co...  352 us
    unnamed x552, local copies, waits for them, and re-layouts  64.8 us
    ppermute x37, waiting for transfers between devices, flipped(): return lax.ppermute(value, axis, [(i, i ^ 1 << bit) for i in range(count)])  64.4 us
    ppermute x28, starting transfers between devices, ring(): lax.ppermute(value, axis, [(i, (i - 1) % count) for i in range(count)])  58.3 us
    ppermute x28, waiting for transfers between devices, ring(): lax.ppermute(value, axis, [(i, (i - 1) % count) for i in range(count)])  45.4 us
    ppermute x16, starting transfers between devices, shifted(): lax.ppermute(value, axis, [(source, source + steps) for source in range(l...  32 us
    ppermute x37, starting transfers between devices, flipped(): return lax.ppermute(value, axis, [(i, i ^ 1 << bit) for i in range(count)])  21.4 us
  transfers between devices with their start and end apart: 111, of which 39 were waited for; matrix products, arithmetic and copies ran while one was open for 5% of the time, Pallas kernels for 46%

profile of v5, /device:TPU:0, one launch (start us, length us, event | category | flops | bytes accessed | tf_op | source)
XLA Modules:
  0.0 725.8 jit_solution(13412891609927810909)
XLA Ops:
  34.7 7.6 %collective-permute-done.2.refs_3_.refs_2_ = bf16[192,1152]{1,0:T(8,128)(2,1)S(1)} collective-permute-done((bf16[192,1152]{1,0:T(8,128)(2,1)S(1)}, bf16[192,1152]{1,0:T(8,128)(2,1)S(1)}, u32[]{:S(2)}, u32[]{:S(2)}) %collective-permute-start.2) | collective-permute-done | bytes 442400 | tf_op jit(solution)/shard_map/ppermute | solution.py:93
  109.2 9.3 %shard_map.296 = (f32[512,1024]{1,0:T(8,128)}, f32[512,768]{1,0:T(8,128)S(1)}, f32[4,128,768]{2,1,0:T(8,128)S(1)}, f32[128,768]{1,0:T(8,128)S(1)}, f32[512,128]{1,0:T(8,128)S(1)}) custom-call(f32[512,1152]{1,0:T(8,128)} %copy-done.225, bf16[8,1024]{1,0:T(8,128)(2,1)S(1)} %get-tuple-element.165.refs_1_.refs_4_, ...), custom_call_target="tpu_custom_call" | custom-call | flops 4750000128 | bytes 1024 | tf_op jit(solution)/shard_map/pallas_call | solution.py:59
  125.1 6.8 shard_map.299
  133.3 14.1 %collective-permute-done.16.refs_2_.refs_6_ = bf16[192,1536]{1,0:T(8,128)(2,1)S(1)} collective-permute-done((bf16[192,1536]{1,0:T(8,128)(2,1)}, bf16[192,1536]{1,0:T(8,128)(2,1)S(1)}, u32[]{:S(2)}, u32[]{:S(2)}) %collective-permute-start.16) | collective-permute-done | bytes 589856 | tf_op jit(solution)/shard_map/ppermute | solution.py:93
  153.0 9.4 %shard_map.301 = (f32[512,1024]{1,0:T(8,128)}, f32[512,768]{1,0:T(8,128)S(1)}, f32[4,128,768]{2,1,0:T(8,128)S(1)}, f32[128,768]{1,0:T(8,128)S(1)}, f32[512,128]{1,0:T(8,128)S(1)}) custom-call(f32[512,1152]{1,0:T(8,128)} %copy-done.224, bf16[8,1024]{1,0:T(8,128)(2,1)S(1)} %get-tuple-element.171.refs_1_.refs_4_, ...), custom_call_target="tpu_custom_call" | custom-call | flops 4750000128 | bytes 1024 | tf_op jit(solution)/shard_map/pallas_call | solution.py:59
  205.0 18.9 %collective-permute-done.24.refs_4_ = f32[128,1536]{1,0:T(8,128)S(1)} collective-permute-done((f32[128,1536]{1,0:T(8,128)S(1)}, f32[128,1536]{1,0:T(8,128)S(1)}, u32[]{:S(2)}, u32[]{:S(2)}) %collective-permute-start.24) | collective-permute-done | bytes 786464 | tf_op jit(solution)/shard_map/ppermute | solution.py:78
  227.8 8.7 %collective-permute-done.28.refs_1_.refs_2_ = bf16[128,1536]{1,0:T(8,128)(2,1)S(1)} collective-permute-done((bf16[128,1536]{1,0:T(8,128)(2,1)S(1)}, bf16[128,1536]{1,0:T(8,128)(2,1)S(1)}, u32[]{:S(2)}, u32[]{:S(2)}) %collective-permute-start.28) | collective-permute-done | bytes 393248 | tf_op jit(solution)/shard_map/ppermute | solution.py:78
  240.4 7.6 %all-gather.2.cloned.1.call-done.refs_5_.refs_1_.refs_2_.refs_4_.refs_6_.refs_7_.refs_8_ = bf16[1536,2688]{1,0:T(8,128)(2,1)} async-done(((bf16[192,2688]{1,0:T(8,128)(2,1)}), bf16[1536,2688]{1,0:T(8,128)(2,1)}) %all-gather.2.cloned.1.call-update) | async-done | bytes 8257552 | tf_op jit(solution)/shard_map/all_gather | solution.py:1523
  263.3 9.0 %collective-permute-done.33.refs_1_.refs_2_ = bf16[128,1536]{1,0:T(8,128)(2,1)S(1)} collective-permute-done((bf16[128,1536]{1,0:T(8,128)(2,1)S(1)}, bf16[128,1536]{1,0:T(8,128)(2,1)S(1)}, u32[]{:S(2)}, u32[]{:S(2)}) %collective-permute-start.33) | collective-permute-done | bytes 393248 | tf_op jit(solution)/shard_map/ppermute | solution.py:78
  276.7 9.2 %shard_map.316 = (f32[512,1024]{1,0:T(8,128)}, f32[512,768]{1,0:T(8,128)S(1)}, f32[4,128,768]{2,1,0:T(8,128)S(1)}, f32[128,768]{1,0:T(8,128)S(1)}, f32[512,128]{1,0:T(8,128)S(1)}) custom-call(f32[512,1152]{1,0:T(8,128)} %get-tuple-element.188.refs_0_.refs_2_.refs_3_, bf16[8,1024]{1,0:T(8,128)(2,1)S(1)} %collective-permute-done.31.refs_1_.refs_4_, ...), custom_call_target="tpu_custom_call" | custom-call | flops 4750000128 | bytes 1024 | tf_op jit(solution)/shard_map/pallas_call | solution.py:59
  302.1 9.7 %shard_map.319 = (f32[512,1024]{1,0:T(8,128)}, f32[512,768]{1,0:T(8,128)S(1)}, f32[4,128,768]{2,1,0:T(8,128)S(1)}, f32[128,768]{1,0:T(8,128)S(1)}, f32[512,128]{1,0:T(8,128)S(1)}) custom-call(f32[512,1152]{1,0:T(8,128)} %copy-done.152, bf16[8,1024]{1,0:T(8,128)(2,1)S(1)} %collective-permute-done.36.refs_1_.refs_4_, f32[8,512]{1,0:T(8,128)S(1)} %copy-done.123, ...), custom_call_target="tpu_custom_call" | custom-call | flops 4750000128 | bytes 1024 | tf_op jit(solution)/shard_map/pallas_call | solution.py:59
  358.6 10.3 %shard_map.327.refs_15_ = bf16[1536,1536]{1,0:T(8,128)(2,1)} custom-call(s32[2]{0:T(128)} %pad_add_fusion.1.refs_0_, bf16[512,1536]{1,0:T(8,128)(2,1)} %copy-done.27, bf16[512,1536]{1,0:T(8,128)(2,1)} %copy-done.28, bf16[2,512,1536]{2,1,0:T(8,128)(2,1)} %refs_5_.3, bf16[2,512,1536]{2,1,0:T(8,128)(2,1)} %refs_5_.3, bf16[512,768]{1,0:T(8,128)(2,1)} %copy-done.66, ...), custom_call_target="tpu_custom_call" | custom-call | flops 5000000000 | bytes 1024 | tf_op jit(solution)/shard_map/pallas_call | solution.py:59
  373.6 17.2 %shard_map.328 = (bf16[512,1152]{1,0:T(8,128)(2,1)S(1)}, f32[8,1024]{1,0:T(8,128)S(1)}, f32[8,128]{1,0:T(8,128)S(1)}, f32[16,1024]{1,0:T(8,128)S(1)}, f32[16,1024]{1,0:T(8,128)S(1)}) custom-call(f32[512,768]{1,0:T(8,128)S(1)} %copy-done.160, f32[512,1024]{1,0:T(8,128)} %get-tuple-element.192.refs_1_.refs_3_.refs_4_, ...), custom_call_target="tpu_custom_call" | custom-call | flops 8999999488 | bytes 1024 | tf_op jit(solution)/shard_map/pallas_call | solution.py:59
  398.3 7.7 %shard_map.330 = (bf16[2,128,1536]{2,1,0:T(8,128)(2,1)S(1)}, bf16[2,128,1536]{2,1,0:T(8,128)(2,1)S(1)}, bf16[512,1152]{1,0:T(8,128)(2,1)S(1)}) custom-call(s32[4]{0:T(128)S(1)} %copy-done.108, bf16[512,1152]{1,0:T(8,128)(2,1)S(1)} %get-tuple-element.223.refs_1_, bf16[512,768]{1,0:T(8,128)(2,1)S(1)} %copy-done.67, f32[16,1024]{1,0:T(8,128)S(1)} %get-tuple-element.224.refs_3_, ...), custom_call_target="tpu_custom_call" | custom-call | flops 3800000000 | bytes 1024 | tf_op jit(solution)/shard_map/pallas_call | solution.py:59
  411.1 16.9 %shard_map.332 = (bf16[512,1152]{1,0:T(8,128)(2,1)S(1)}, f32[8,1024]{1,0:T(8,128)S(1)}, f32[8,128]{1,0:T(8,128)S(1)}, f32[16,1024]{1,0:T(8,128)S(1)}, f32[16,1024]{1,0:T(8,128)S(1)}) custom-call(f32[512,768]{1,0:T(8,128)S(1)} %get-tuple-element.229.refs_0_, f32[512,1024]{1,0:T(8,128)} %get-tuple-element.205.refs_1_.refs_3_.refs_4_, f32[512,1152]{1,0:T(8,128)} %copy-done.152, ...), custom_call_target="tpu_custom_call" | custom-call | flops 8999999488 | bytes 1024 | tf_op jit(solution)/shard_map/pallas_call | solution.py:59
  438.3 7.6 %shard_map.335 = (bf16[2,128,1536]{2,1,0:T(8,128)(2,1)S(1)}, bf16[2,128,1536]{2,1,0:T(8,128)(2,1)S(1)}, bf16[512,1152]{1,0:T(8,128)(2,1)S(1)}) custom-call(s32[4]{0:T(128)S(1)} %copy-done.108, bf16[512,1152]{1,0:T(8,128)(2,1)S(1)} %get-tuple-element.233.refs_1_, bf16[512,768]{1,0:T(8,128)(2,1)S(1)} %copy-done.65, f32[16,1024]{1,0:T(8,128)S(1)} %get-tuple-element.234.refs_3_, ...), custom_call_target="tpu_custom_call" | custom-call | flops 3800000000 | bytes 1024 | tf_op jit(solution)/shard_map/pallas_call | solution.py:59
  460.6 8.7 %shard_map.341.refs_12_ = bf16[1536,1152]{1,0:T(8,128)(2,1)} custom-call(s32[2]{0:T(128)} %pad_add_fusion.1.refs_0_, bf16[512,1536]{1,0:T(8,128)(2,1)} %copy-done.27, bf16[512,1536]{1,0:T(8,128)(2,1)} %copy-done.28, bf16[512,1152]{1,0:T(8,128)(2,1)} %copy-done.162, bf16[512,1152]{1,0:T(8,128)(2,1)} %copy-done.163, bf16[128,1536]{1,0:T(8,128)(2,1)} %shard_map.340.refs_5_, ...), custom_call_target="tpu_custom_call" | custom-call | flops 5000000000 | bytes 1024 | tf_op jit(solution)/shard_map/pallas_call | solution.py:59
  493.9 17.3 %shard_map.344 = (bf16[512,1152]{1,0:T(8,128)(2,1)S(1)}, f32[8,1024]{1,0:T(8,128)S(1)}, f32[8,128]{1,0:T(8,128)S(1)}, f32[16,1024]{1,0:T(8,128)S(1)}, f32[16,1024]{1,0:T(8,128)S(1)}) custom-call(f32[512,768]{1,0:T(8,128)S(1)} %copy-done.158, f32[512,1024]{1,0:T(8,128)} %get-tuple-element.167.refs_1_.refs_3_.refs_4_, f32[512,1152]{1,0:T(8,128)} %copy-done.225, ...), custom_call_target="tpu_custom_call" | custom-call | flops 8999999488 | bytes 1024 | tf_op jit(solution)/shard_map/pallas_call | solution.py:59
  526.3 7.6 %shard_map.349 = (bf16[2,128,1536]{2,1,0:T(8,128)(2,1)S(1)}, bf16[2,128,1536]{2,1,0:T(8,128)(2,1)S(1)}, bf16[512,1152]{1,0:T(8,128)(2,1)S(1)}) custom-call(s32[4]{0:T(128)S(1)} %copy-done.109, bf16[512,1152]{1,0:T(8,128)(2,1)S(1)} %get-tuple-element.255.refs_1_, bf16[512,768]{1,0:T(8,128)(2,1)S(1)} %get-tuple-element.256.refs_2_.refs_5_, ...), custom_call_target="tpu_custom_call" | custom-call | flops 3800000000 | bytes 1024 | tf_op jit(solution)/shard_map/pallas_call | solution.py:59
  549.7 11.7 %shard_map.351 = (bf16[4,192,1536]{2,1,0:T(8,128)(2,1)}, bf16[192,1536]{1,0:T(8,128)(2,1)}, bf16[192,1536]{1,0:T(8,128)(2,1)}, bf16[192,1536]{1,0:T(8,128)(2,1)}, bf16[192,1536]{1,0:T(8,128)(2,1)}) custom-call(s32[2]{0:T(128)} %pad_add_fusion.1.refs_0_, bf16[512,1536]{1,0:T(8,128)(2,1)} %copy-done.22, bf16[512,1536]{1,0:T(8,128)(2,1)} %copy-done.26, ...), custom_call_target="tpu_custom_call" | custom-call | flops 5000000000 | bytes 1024 | tf_op jit(solution)/shard_map/pallas_call | solution.py:59
  569.6 17.2 %shard_map.353 = (bf16[512,1152]{1,0:T(8,128)(2,1)S(1)}, f32[8,1024]{1,0:T(8,128)S(1)}, f32[8,128]{1,0:T(8,128)S(1)}, f32[16,1024]{1,0:T(8,128)S(1)}, f32[16,1024]{1,0:T(8,128)S(1)}) custom-call(f32[512,768]{1,0:T(8,128)S(1)} %copy-done.156, f32[512,1024]{1,0:T(8,128)} %get-tuple-element.177.refs_1_.refs_3_.refs_4_, f32[512,1152]{1,0:T(8,128)} %copy-done.224, ...), custom_call_target="tpu_custom_call" | custom-call | flops 8999999488 | bytes 1024 | tf_op jit(solution)/shard_map/pallas_call | solution.py:59
  604.6 7.6 %shard_map.358 = (bf16[2,128,1536]{2,1,0:T(8,128)(2,1)S(1)}, bf16[2,128,1536]{2,1,0:T(8,128)(2,1)S(1)}, bf16[512,1152]{1,0:T(8,128)(2,1)S(1)}) custom-call(s32[4]{0:T(128)S(1)} %copy-done.109, bf16[512,1152]{1,0:T(8,128)(2,1)S(1)} %get-tuple-element.276.refs_1_, bf16[512,768]{1,0:T(8,128)(2,1)S(1)} %copy-done.39, f32[16,1024]{1,0:T(8,128)S(1)} %get-tuple-element.277.refs_3_, ...), custom_call_target="tpu_custom_call" | custom-call | flops 3800000000 | bytes 1024 | tf_op jit(solution)/shard_map/pallas_call | solution.py:59
  617.5 10.0 %shard_map.360 = (bf16[4,192,1152]{2,1,0:T(8,128)(2,1)}, bf16[192,1152]{1,0:T(8,128)(2,1)}, bf16[192,1152]{1,0:T(8,128)(2,1)}, bf16[192,1152]{1,0:T(8,128)(2,1)}, bf16[192,1152]{1,0:T(8,128)(2,1)}) custom-call(s32[2]{0:T(128)} %pad_add_fusion.1.refs_0_, bf16[512,1536]{1,0:T(8,128)(2,1)} %copy-done.22, bf16[512,1536]{1,0:T(8,128)(2,1)} %copy-done.26, ...), custom_call_target="tpu_custom_call" | custom-call | flops 5000000000 | bytes 1024 | tf_op jit(solution)/shard_map/pallas_call | solution.py:59
  638.0 8.3 %collective-permute-done.85.refs_1_.refs_2_ = bf16[128,1536]{1,0:T(8,128)(2,1)} collective-permute-done((bf16[128,1536]{1,0:T(8,128)(2,1)}, bf16[128,1536]{1,0:T(8,128)(2,1)}, u32[]{:S(2)}, u32[]{:S(2)}) %collective-permute-start.85) | collective-permute-done | bytes 393248 | tf_op jit(solution)/shard_map/ppermute | solution.py:78
  (943 shorter events, 449.7 us)
Async XLA Ops:
  7.2 240.9 %all-gather.2.cloned.1.call-start = ((), (), s32[]{:S(2)}) async-start(), calls=%async_computation.2 | async-start | bytes 9289728 | tf_op jit(solution)/shard_map/all_gather | solution.py:1523
  10.9 23.8 %collective-permute-start.4 = (bf16[2,16,1536]{2,1,0:T(8,128)(2,1)S(1)}, bf16[2,16,1536]{2,1,0:T(8,128)(2,1)S(1)}, u32[]{:S(2)}, u32[]{:S(2)}) collective-permute-start(bf16[2,16,1536]{2,1,0:T(8,128)(2,1)S(1)} %slice.182), channel_id=1, source_target_pairs={{0,4},{1,5},{2,6},{3,7},{8,12},{9,13},{10,14},{11,15},{16,20},{17,... | collective-permute-start | bytes 294920 | tf_op jit(solution)/shard_map/ppermute | solution.py:88
  71.3 27.4 %collective-permute-start.11 = (bf16[192,1536]{1,0:T(8,128)(2,1)S(1)}, bf16[192,1536]{1,0:T(8,128)(2,1)}, u32[]{:S(2)}, u32[]{:S(2)}) collective-permute-start(bf16[192,1536]{1,0:T(8,128)(2,1)S(1)} %shard_map.292.refs_9_.refs_1_), channel_id=1, source_target_pairs={{0,24},{8,0},{16,8},{24,16},{1,25},{9,1},{17,9},{25,17},{2,26},{10... | collective-permute-start | bytes 1769480 | tf_op jit(solution)/shard_map/ppermute | solution.py:93
  75.6 23.1 %collective-permute-start.12 = (bf16[192,1536]{1,0:T(8,128)(2,1)S(1)}, bf16[192,1536]{1,0:T(8,128)(2,1)S(1)}, u32[]{:S(2)}, u32[]{:S(2)}) collective-permute-start(bf16[192,1536]{1,0:T(8,128)(2,1)S(1)} %shard_map.292.refs_9_.refs_1_), channel_id=1, source_target_pairs={{0,4},{4,0},{1,5},{5,1},{2,6},{6,2},{3,7},{7,3},{8,12},{12,8},{9,1... | collective-permute-start | bytes 1769480 | tf_op jit(solution)/shard_map/ppermute | solution.py:93
  124.1 364.9 %reduce-scatter.3.cloned.1.call-start = ((), (), s32[]{:S(2)}) async-start(), calls=%async_computation.3 | async-start | bytes 5308416 | tf_op jit(solution)/shard_map/reduce_scatter | solution.py:1699
  124.1 23.3 %collective-permute-start.16 = (bf16[192,1536]{1,0:T(8,128)(2,1)}, bf16[192,1536]{1,0:T(8,128)(2,1)S(1)}, u32[]{:S(2)}, u32[]{:S(2)}) collective-permute-start(bf16[192,1536]{1,0:T(8,128)(2,1)} %copy-done.72), channel_id=1, source_target_pairs={{0,4},{4,0},{1,5},{5,1},{2,6},{6,2},{3,7},{7,3},{8,12},{12,8},{9,1... | collective-permute-start | bytes 1769480 | tf_op jit(solution)/shard_map/ppermute | solution.py:93
  203.8 23.0 %collective-permute-start.29 = (f32[2,128,1536]{2,1,0:T(8,128)S(1)}, f32[2,128,1536]{2,1,0:T(8,128)S(1)}, u32[]{:S(2)}, u32[]{:S(2)}) collective-permute-start(f32[2,128,1536]{2,1,0:T(8,128)S(1)} %get-tuple-element.184.refs_6_), channel_id=1, source_target_pairs={{0,1},{1,0},{2,3},{3,2},{4,5},{5,4},{6,7},{7,6},{8,9},{9,8},{10,11... | collective-permute-start | bytes 4718600 | tf_op jit(solution)/shard_map/ppermute | solution.py:78
  287.1 27.6 %collective-permute-start.34 = (f32[128,768]{1,0:T(8,128)S(1)}, f32[128,768]{1,0:T(8,128)S(1)}, u32[]{:S(2)}, u32[]{:S(2)}) collective-permute-start(f32[128,768]{1,0:T(8,128)S(1)} %get-tuple-element.194), channel_id=1, source_target_pairs={{0,4},{1,5},{2,6},{3,7},{8,12},{9,13},{10,14},{11,15},{16,20},{17,... | collective-permute-start | bytes 1179656 | tf_op jit(solution)/shard_map/ppermute | solution.py:88
  369.0 198.2 %reduce-scatter.5.cloned.1.call-start = ((), (), s32[]{:S(2)}) async-start(), calls=%async_computation.4 | async-start | bytes 3981312 | tf_op jit(solution)/shard_map/reduce_scatter | solution.py:1699
  369.0 29.3 %collective-permute-start.47 = (bf16[128,768]{1,0:T(8,128)(2,1)S(1)}, bf16[128,768]{1,0:T(8,128)(2,1)S(1)}, u32[]{:S(2)}, u32[]{:S(2)}) collective-permute-start(bf16[128,768]{1,0:T(8,128)(2,1)S(1)} %get-tuple-element.226), channel_id=1, source_target_pairs={{4,0},{5,1},{6,2},{7,3},{12,8},{13,9},{14,10},{15,11},{20,16},{21,... | collective-permute-start | bytes 589832 | tf_op jit(solution)/shard_map/ppermute | solution.py:88
  478.4 32.8 %collective-permute-start.54 = (bf16[128,1536]{1,0:T(8,128)(2,1)}, bf16[128,1536]{1,0:T(8,128)(2,1)}, u32[]{:S(2)}, u32[]{:S(2)}) collective-permute-start(bf16[128,1536]{1,0:T(8,128)(2,1)} %shard_map.339.refs_2_), channel_id=1, source_target_pairs={{0,2},{1,3},{2,0},{3,1},{4,6},{5,7},{6,4},{7,5},{8,10},{9,11},{10,... | collective-permute-start | bytes 1179656 | tf_op jit(solution)/shard_map/ppermute | solution.py:78
  479.6 33.8 %collective-permute-start.63 = (bf16[128,1536]{1,0:T(8,128)(2,1)}, bf16[128,1536]{1,0:T(8,128)(2,1)}, u32[]{:S(2)}, u32[]{:S(2)}) collective-permute-start(bf16[128,1536]{1,0:T(8,128)(2,1)} %shard_map.340.refs_5_), channel_id=1, source_target_pairs={{0,2},{1,3},{2,0},{3,1},{4,6},{5,7},{6,4},{7,5},{8,10},{9,11},{10,... | collective-permute-start | bytes 1179656 | tf_op jit(solution)/shard_map/ppermute | solution.py:78
  484.3 31.1 %collective-permute-start.62 = (bf16[128,1536]{1,0:T(8,128)(2,1)S(1)}, bf16[128,1536]{1,0:T(8,128)(2,1)}, u32[]{:S(2)}, u32[]{:S(2)}) collective-permute-start(bf16[128,1536]{1,0:T(8,128)(2,1)S(1)} %get-tuple-element.252.refs_0_.refs_1_), channel_id=1, source_target_pairs={{0,2},{1,3},{2,0},{3,1},{4,6},{5,7},{6,4},{7,5},{8,10},{9,11},{10,... | collective-permute-start | bytes 1179656 | tf_op jit(solution)/shard_map/ppermute | solution.py:78
  534.0 30.4 %collective-permute-start.70 = (bf16[2,128,1536]{2,1,0:T(8,128)(2,1)S(1)}, bf16[2,128,1536]{2,1,0:T(8,128)(2,1)S(1)}, u32[]{:S(2)}, u32[]{:S(2)}) collective-permute-start(bf16[2,128,1536]{2,1,0:T(8,128)(2,1)S(1)} %get-tuple-element.259.refs_12_), channel_id=1, source_target_pairs={{0,1},{1,0},{2,3},{3,2},{4,5},{5,4},{6,7},{7,6},{8,9},{9,8},{10,11... | collective-permute-start | bytes 2359304 | tf_op jit(solution)/shard_map/ppermute | solution.py:78
  536.1 51.4 %collective-permute-start.61 = (bf16[128,1536]{1,0:T(8,128)(2,1)}, bf16[128,1536]{1,0:T(8,128)(2,1)}, u32[]{:S(2)}, u32[]{:S(2)}) collective-permute-start(bf16[128,1536]{1,0:T(8,128)(2,1)} %shard_map.345.refs_5_.refs_0_.refs_1_), channel_id=1, source_target_pairs={{0,2},{1,3},{2,0},{3,1},{4,6},{5,7},{6,4},{7,5},{8,10},{9,11},{10,... | collective-permute-start | bytes 1179656 | tf_op jit(solution)/shard_map/ppermute | solution.py:78
  537.5 53.9 %collective-permute-start.72 = (bf16[128,1536]{1,0:T(8,128)(2,1)}, bf16[128,1536]{1,0:T(8,128)(2,1)}, u32[]{:S(2)}, u32[]{:S(2)}) collective-permute-start(bf16[128,1536]{1,0:T(8,128)(2,1)} %shard_map.346.refs_2_.refs_0_.refs_5_), channel_id=1, source_target_pairs={{0,2},{1,3},{2,0},{3,1},{4,6},{5,7},{6,4},{7,5},{8,10},{9,11},{10,... | collective-permute-start | bytes 1179656 | tf_op jit(solution)/shard_map/ppermute | solution.py:78
  561.4 32.2 %collective-permute-start.74 = (bf16[192,1536]{1,0:T(8,128)(2,1)}, bf16[192,1536]{1,0:T(8,128)(2,1)S(1)}, u32[]{:S(2)}, u32[]{:S(2)}) collective-permute-start(bf16[192,1536]{1,0:T(8,128)(2,1)} %get-tuple-element.270.refs_2_), channel_id=1, source_target_pairs={{0,4},{4,0},{1,5},{5,1},{2,6},{6,2},{3,7},{7,3},{8,12},{12,8},{9,1... | collective-permute-start | bytes 1769480 | tf_op jit(solution)/shard_map/ppermute | solution.py:93
  564.4 29.2 %collective-permute-start.77 = (bf16[192,1536]{1,0:T(8,128)(2,1)}, bf16[192,1536]{1,0:T(8,128)(2,1)}, u32[]{:S(2)}, u32[]{:S(2)}) collective-permute-start(bf16[192,1536]{1,0:T(8,128)(2,1)} %get-tuple-element.275), channel_id=1, source_target_pairs={{0,4},{4,0},{1,5},{5,1},{2,6},{6,2},{3,7},{7,3},{8,12},{12,8},{9,1... | collective-permute-start | bytes 1769480 | tf_op jit(solution)/shard_map/ppermute | solution.py:93
  566.6 33.0 %collective-permute-start.80 = (bf16[128,1536]{1,0:T(8,128)(2,1)}, bf16[128,1536]{1,0:T(8,128)(2,1)}, u32[]{:S(2)}, u32[]{:S(2)}) collective-permute-start(bf16[128,1536]{1,0:T(8,128)(2,1)} %shard_map.352.refs_15_), channel_id=1, source_target_pairs={{0,2},{1,3},{2,0},{3,1},{4,6},{5,7},{6,4},{7,5},{8,10},{9,11},{10,... | collective-permute-start | bytes 1179656 | tf_op jit(solution)/shard_map/ppermute | solution.py:78
  587.5 26.4 %collective-permute-start.76 = (bf16[192,1536]{1,0:T(8,128)(2,1)S(1)}, bf16[192,1536]{1,0:T(8,128)(2,1)S(1)}, u32[]{:S(2)}, u32[]{:S(2)}) collective-permute-start(bf16[192,1536]{1,0:T(8,128)(2,1)S(1)} %copy-done.270), channel_id=1, source_target_pairs={{0,4},{4,0},{1,5},{5,1},{2,6},{6,2},{3,7},{7,3},{8,12},{12,8},{9,1... | collective-permute-start | bytes 1769480 | tf_op jit(solution)/shard_map/ppermute | solution.py:93
  617.0 35.6 %collective-permute-start.71 = (bf16[256,1536]{1,0:T(8,128)(2,1)}, bf16[256,1536]{1,0:T(8,128)(2,1)}, u32[]{:S(2)}, u32[]{:S(2)}) collective-permute-start(bf16[256,1536]{1,0:T(8,128)(2,1)} %shard_map.354.refs_2_), channel_id=1, source_target_pairs={{0,1},{1,0},{2,3},{3,2},{4,5},{5,4},{6,7},{7,6},{8,9},{9,8},{10,11... | collective-permute-start | bytes 2359304 | tf_op jit(solution)/shard_map/ppermute | solution.py:78
  617.2 35.4 %collective-permute-start.73 = (bf16[256,1536]{1,0:T(8,128)(2,1)}, bf16[256,1536]{1,0:T(8,128)(2,1)}, u32[]{:S(2)}, u32[]{:S(2)}) collective-permute-start(bf16[256,1536]{1,0:T(8,128)(2,1)} %shard_map.355.refs_2_), channel_id=1, source_target_pairs={{0,1},{1,0},{2,3},{3,2},{4,5},{5,4},{6,7},{7,6},{8,9},{9,8},{10,11... | collective-permute-start | bytes 2359304 | tf_op jit(solution)/shard_map/ppermute | solution.py:78
  651.7 34.1 %collective-permute-start.95 = (bf16[192,1152]{1,0:T(8,128)(2,1)}, bf16[192,1152]{1,0:T(8,128)(2,1)}, u32[]{:S(2)}, u32[]{:S(2)}) collective-permute-start(bf16[192,1152]{1,0:T(8,128)(2,1)} %get-tuple-element.299), channel_id=1, source_target_pairs={{0,4},{4,0},{1,5},{5,1},{2,6},{6,2},{3,7},{7,3},{8,12},{12,8},{9,1... | collective-permute-start | bytes 1327112 | tf_op jit(solution)/shard_map/ppermute | solution.py:93
  652.5 40.9 %collective-permute-start.86 = (bf16[256,1536]{1,0:T(8,128)(2,1)}, bf16[256,1536]{1,0:T(8,128)(2,1)S(1)}, u32[]{:S(2)}, u32[]{:S(2)}) collective-permute-start(bf16[256,1536]{1,0:T(8,128)(2,1)} %shard_map.363.refs_2_), channel_id=1, source_target_pairs={{0,1},{1,0},{2,3},{3,2},{4,5},{5,4},{6,7},{7,6},{8,9},{9,8},{10,11... | collective-permute-start | bytes 2359304 | tf_op jit(solution)/shard_map/ppermute | solution.py:78
  (359 other events, 3166.8 us)
Sparse Core Ops, SparseCore 0:
  124.2 123.8 all-gather.1
  369.1 95.2 reduce-scatter.2
  469.5 82.0 reduce-scatter.4

commit v6 on v5

--- a/solution.py
+++ b/solution.py
@@ -1738,8 +1738,8 @@
     incoming[0] = step_join(0, 0, "rows")
     project_1(0)
     step_norm(0, 1)
+    scan_1(0)
     incoming[1] = step_join(0, 1, "rows")
-    scan_1(0)
     project_1(1)
     gate_1(0)
     scan_1(1)

time: 738 us -> 725 us (0.982)
  waiting for transfers between devices: 131 us -> 120 us
    ppermute x37, waiting for transfers between devices: 64.4 us -> 55.2 us  [flipped(): return lax.ppermute(value, axis, [(i, i ^ 1 << bit) for i in range(count)])]
    unnamed x552 -> x550, local copies, waits for them, and re-layouts: 64.8 us -> 64.1 us
  transfers between devices with their start and end apart: 111 -> 111, of which waited for: 39 -> 37; matrix products, arithmetic and copies ran while one was open for 5% -> 5% of each run, Pallas kernels for 46% -> 47%
where the time goes in v6:
time: 725 us; the launch traced here: 713 us
  Pallas kernels  353 us (49%)
  starting transfers between devices  128 us (18%)
  waiting for transfers between devices  120 us (17%)
  local copies, waits for them, and re-layouts  84.3 us (12%)
  between operations  17.7 us (2%)
  other arithmetic  10.7 us (1%)
    pallas_call x91, Pallas kernels, call(): pl.pallas_call(without_tokens, cost_estimate=pl.CostEstimate(flops=int(co...  353 us
    unnamed x550, local copies, waits for them, and re-layouts  64.1 us
    ppermute x28, starting transfers between devices, ring(): lax.ppermute(value, axis, [(i, (i - 1) % count) for i in range(count)])  58.3 us
    ppermute x37, waiting for transfers between devices, flipped(): return lax.ppermute(value, axis, [(i, i ^ 1 << bit) for i in range(count)])  55.2 us
    ppermute x28, waiting for transfers between devices, ring(): lax.ppermute(value, axis, [(i, (i - 1) % count) for i in range(count)])  45.4 us
    ppermute x16, starting transfers between devices, shifted(): lax.ppermute(value, axis, [(source, source + steps) for source in range(l...  29.2 us
    ppermute x37, starting transfers between devices, flipped(): return lax.ppermute(value, axis, [(i, i ^ 1 << bit) for i in range(count)])  22.8 us
  transfers between devices with their start and end apart: 111, of which 37 were waited for; matrix products, arithmetic and copies ran while one was open for 5% of the time, Pallas kernels for 47%

profile of v6, /device:TPU:0, one launch (start us, length us, event | category | flops | bytes accessed | tf_op | source)
XLA Modules:
  0.0 713.3 jit_solution(17923725230687804866)
XLA Ops:
  34.7 7.6 %collective-permute-done.2.refs_3_.refs_2_ = bf16[192,1152]{1,0:T(8,128)(2,1)S(1)} collective-permute-done((bf16[192,1152]{1,0:T(8,128)(2,1)S(1)}, bf16[192,1152]{1,0:T(8,128)(2,1)S(1)}, u32[]{:S(2)}, u32[]{:S(2)}) %collective-permute-start.2) | collective-permute-done | bytes 442400 | tf_op jit(solution)/shard_map/ppermute | solution.py:93
  109.3 9.3 %shard_map.296 = (f32[512,1024]{1,0:T(8,128)}, f32[512,768]{1,0:T(8,128)S(1)}, f32[4,128,768]{2,1,0:T(8,128)S(1)}, f32[128,768]{1,0:T(8,128)S(1)}, f32[512,128]{1,0:T(8,128)S(1)}) custom-call(f32[512,1152]{1,0:T(8,128)} %copy-done.224, bf16[8,1024]{1,0:T(8,128)(2,1)S(1)} %get-tuple-element.165.refs_1_.refs_4_, ...), custom_call_target="tpu_custom_call" | custom-call | flops 4750000128 | bytes 1024 | tf_op jit(solution)/shard_map/pallas_call | solution.py:59
  125.1 6.8 shard_map.299
  133.3 14.1 %collective-permute-done.16.refs_2_.refs_6_ = bf16[192,1536]{1,0:T(8,128)(2,1)S(1)} collective-permute-done((bf16[192,1536]{1,0:T(8,128)(2,1)}, bf16[192,1536]{1,0:T(8,128)(2,1)S(1)}, u32[]{:S(2)}, u32[]{:S(2)}) %collective-permute-start.16) | collective-permute-done | bytes 589856 | tf_op jit(solution)/shard_map/ppermute | solution.py:93
  153.0 9.4 %shard_map.301 = (f32[512,1024]{1,0:T(8,128)}, f32[512,768]{1,0:T(8,128)S(1)}, f32[4,128,768]{2,1,0:T(8,128)S(1)}, f32[128,768]{1,0:T(8,128)S(1)}, f32[512,128]{1,0:T(8,128)S(1)}) custom-call(f32[512,1152]{1,0:T(8,128)} %copy-done.223, bf16[8,1024]{1,0:T(8,128)(2,1)S(1)} %get-tuple-element.171.refs_1_.refs_4_, ...), custom_call_target="tpu_custom_call" | custom-call | flops 4750000128 | bytes 1024 | tf_op jit(solution)/shard_map/pallas_call | solution.py:59
  205.0 18.9 %collective-permute-done.24.refs_4_ = f32[128,1536]{1,0:T(8,128)S(1)} collective-permute-done((f32[128,1536]{1,0:T(8,128)S(1)}, f32[128,1536]{1,0:T(8,128)S(1)}, u32[]{:S(2)}, u32[]{:S(2)}) %collective-permute-start.24) | collective-permute-done | bytes 786464 | tf_op jit(solution)/shard_map/ppermute | solution.py:78
  227.8 8.7 %collective-permute-done.28.refs_1_.refs_2_ = bf16[128,1536]{1,0:T(8,128)(2,1)S(1)} collective-permute-done((bf16[128,1536]{1,0:T(8,128)(2,1)S(1)}, bf16[128,1536]{1,0:T(8,128)(2,1)S(1)}, u32[]{:S(2)}, u32[]{:S(2)}) %collective-permute-start.28) | collective-permute-done | bytes 393248 | tf_op jit(solution)/shard_map/ppermute | solution.py:78
  240.5 7.6 %all-gather.2.cloned.1.call-done.refs_5_.refs_1_.refs_2_.refs_4_.refs_6_.refs_7_.refs_8_ = bf16[1536,2688]{1,0:T(8,128)(2,1)} async-done(((bf16[192,2688]{1,0:T(8,128)(2,1)}), bf16[1536,2688]{1,0:T(8,128)(2,1)}) %all-gather.2.cloned.1.call-update) | async-done | bytes 8257552 | tf_op jit(solution)/shard_map/all_gather | solution.py:1523
  266.2 9.2 %shard_map.315 = (f32[512,1024]{1,0:T(8,128)}, f32[512,768]{1,0:T(8,128)S(1)}, f32[4,128,768]{2,1,0:T(8,128)S(1)}, f32[128,768]{1,0:T(8,128)S(1)}, f32[512,128]{1,0:T(8,128)S(1)}) custom-call(f32[512,1152]{1,0:T(8,128)} %get-tuple-element.188.refs_0_.refs_2_.refs_3_, bf16[8,1024]{1,0:T(8,128)(2,1)S(1)} %collective-permute-done.31.refs_1_.refs_4_, ...), custom_call_target="tpu_custom_call" | custom-call | flops 4750000128 | bytes 1024 | tf_op jit(solution)/shard_map/pallas_call | solution.py:59
  279.4 6.7 shard_map.317
  290.8 9.7 %shard_map.319 = (f32[512,1024]{1,0:T(8,128)}, f32[512,768]{1,0:T(8,128)S(1)}, f32[4,128,768]{2,1,0:T(8,128)S(1)}, f32[128,768]{1,0:T(8,128)S(1)}, f32[512,128]{1,0:T(8,128)S(1)}) custom-call(f32[512,1152]{1,0:T(8,128)} %get-tuple-element.197.refs_0_.refs_2_.refs_3_, bf16[8,1024]{1,0:T(8,128)(2,1)S(1)} %collective-permute-done.36.refs_1_.refs_4_, ...), custom_call_target="tpu_custom_call" | custom-call | flops 4750000128 | bytes 1024 | tf_op jit(solution)/shard_map/pallas_call | solution.py:59
  346.2 10.3 %shard_map.327.refs_15_ = bf16[1536,1536]{1,0:T(8,128)(2,1)} custom-call(s32[2]{0:T(128)} %pad_add_fusion.1.refs_0_, bf16[512,1536]{1,0:T(8,128)(2,1)} %copy-done.27, bf16[512,1536]{1,0:T(8,128)(2,1)} %copy-done.28, bf16[2,512,1536]{2,1,0:T(8,128)(2,1)} %refs_5_.3, bf16[2,512,1536]{2,1,0:T(8,128)(2,1)} %refs_5_.3, bf16[512,768]{1,0:T(8,128)(2,1)} %copy-done.64, ...), custom_call_target="tpu_custom_call" | custom-call | flops 5000000000 | bytes 1024 | tf_op jit(solution)/shard_map/pallas_call | solution.py:59
  361.2 17.2 %shard_map.328 = (bf16[512,1152]{1,0:T(8,128)(2,1)S(1)}, f32[8,1024]{1,0:T(8,128)S(1)}, f32[8,128]{1,0:T(8,128)S(1)}, f32[16,1024]{1,0:T(8,128)S(1)}, f32[16,1024]{1,0:T(8,128)S(1)}) custom-call(f32[512,768]{1,0:T(8,128)S(1)} %copy-done.159, f32[512,1024]{1,0:T(8,128)} %get-tuple-element.192.refs_1_.refs_3_.refs_4_, ...), custom_call_target="tpu_custom_call" | custom-call | flops 8999999488 | bytes 1024 | tf_op jit(solution)/shard_map/pallas_call | solution.py:59
  386.0 7.7 %shard_map.330 = (bf16[2,128,1536]{2,1,0:T(8,128)(2,1)S(1)}, bf16[2,128,1536]{2,1,0:T(8,128)(2,1)S(1)}, bf16[512,1152]{1,0:T(8,128)(2,1)S(1)}) custom-call(s32[4]{0:T(128)S(1)} %copy-done.108, bf16[512,1152]{1,0:T(8,128)(2,1)S(1)} %get-tuple-element.223.refs_1_, bf16[512,768]{1,0:T(8,128)(2,1)S(1)} %copy-done.65, f32[16,1024]{1,0:T(8,128)S(1)} %get-tuple-element.224.refs_3_, ...), custom_call_target="tpu_custom_call" | custom-call | flops 3800000000 | bytes 1024 | tf_op jit(solution)/shard_map/pallas_call | solution.py:59
  398.8 16.9 %shard_map.332 = (bf16[512,1152]{1,0:T(8,128)(2,1)S(1)}, f32[8,1024]{1,0:T(8,128)S(1)}, f32[8,128]{1,0:T(8,128)S(1)}, f32[16,1024]{1,0:T(8,128)S(1)}, f32[16,1024]{1,0:T(8,128)S(1)}) custom-call(f32[512,768]{1,0:T(8,128)S(1)} %get-tuple-element.229.refs_0_, f32[512,1024]{1,0:T(8,128)} %get-tuple-element.205.refs_1_.refs_3_.refs_4_, ...), custom_call_target="tpu_custom_call" | custom-call | flops 8999999488 | bytes 1024 | tf_op jit(solution)/shard_map/pallas_call | solution.py:59
  426.5 7.6 %shard_map.335 = (bf16[2,128,1536]{2,1,0:T(8,128)(2,1)S(1)}, bf16[2,128,1536]{2,1,0:T(8,128)(2,1)S(1)}, bf16[512,1152]{1,0:T(8,128)(2,1)S(1)}) custom-call(s32[4]{0:T(128)S(1)} %copy-done.108, bf16[512,1152]{1,0:T(8,128)(2,1)S(1)} %get-tuple-element.233.refs_1_, bf16[512,768]{1,0:T(8,128)(2,1)S(1)} %copy-done.63, f32[16,1024]{1,0:T(8,128)S(1)} %get-tuple-element.234.refs_3_, ...), custom_call_target="tpu_custom_call" | custom-call | flops 3800000000 | bytes 1024 | tf_op jit(solution)/shard_map/pallas_call | solution.py:59
  448.5 8.7 %shard_map.341.refs_12_ = bf16[1536,1152]{1,0:T(8,128)(2,1)} custom-call(s32[2]{0:T(128)} %pad_add_fusion.1.refs_0_, bf16[512,1536]{1,0:T(8,128)(2,1)} %copy-done.27, bf16[512,1536]{1,0:T(8,128)(2,1)} %copy-done.28, bf16[512,1152]{1,0:T(8,128)(2,1)} %copy-done.161, bf16[512,1152]{1,0:T(8,128)(2,1)} %copy-done.162, bf16[128,1536]{1,0:T(8,128)(2,1)} %shard_map.340.refs_5_, ...), custom_call_target="tpu_custom_call" | custom-call | flops 5000000000 | bytes 1024 | tf_op jit(solution)/shard_map/pallas_call | solution.py:59
  481.4 17.4 %shard_map.344 = (bf16[512,1152]{1,0:T(8,128)(2,1)S(1)}, f32[8,1024]{1,0:T(8,128)S(1)}, f32[8,128]{1,0:T(8,128)S(1)}, f32[16,1024]{1,0:T(8,128)S(1)}, f32[16,1024]{1,0:T(8,128)S(1)}) custom-call(f32[512,768]{1,0:T(8,128)S(1)} %copy-done.157, f32[512,1024]{1,0:T(8,128)} %get-tuple-element.167.refs_1_.refs_3_.refs_4_, f32[512,1152]{1,0:T(8,128)} %copy-done.224, ...), custom_call_target="tpu_custom_call" | custom-call | flops 8999999488 | bytes 1024 | tf_op jit(solution)/shard_map/pallas_call | solution.py:59
  513.8 7.6 %shard_map.349 = (bf16[2,128,1536]{2,1,0:T(8,128)(2,1)S(1)}, bf16[2,128,1536]{2,1,0:T(8,128)(2,1)S(1)}, bf16[512,1152]{1,0:T(8,128)(2,1)S(1)}) custom-call(s32[4]{0:T(128)S(1)} %copy-done.109, bf16[512,1152]{1,0:T(8,128)(2,1)S(1)} %get-tuple-element.255.refs_1_, bf16[512,768]{1,0:T(8,128)(2,1)S(1)} %get-tuple-element.256.refs_2_.refs_5_, ...), custom_call_target="tpu_custom_call" | custom-call | flops 3800000000 | bytes 1024 | tf_op jit(solution)/shard_map/pallas_call | solution.py:59
  537.1 11.7 %shard_map.351 = (bf16[4,192,1536]{2,1,0:T(8,128)(2,1)}, bf16[192,1536]{1,0:T(8,128)(2,1)}, bf16[192,1536]{1,0:T(8,128)(2,1)}, bf16[192,1536]{1,0:T(8,128)(2,1)}, bf16[192,1536]{1,0:T(8,128)(2,1)}) custom-call(s32[2]{0:T(128)} %pad_add_fusion.1.refs_0_, bf16[512,1536]{1,0:T(8,128)(2,1)} %copy-done.22, bf16[512,1536]{1,0:T(8,128)(2,1)} %copy-done.26, ...), custom_call_target="tpu_custom_call" | custom-call | flops 5000000000 | bytes 1024 | tf_op jit(solution)/shard_map/pallas_call | solution.py:59
  557.1 17.2 %shard_map.353 = (bf16[512,1152]{1,0:T(8,128)(2,1)S(1)}, f32[8,1024]{1,0:T(8,128)S(1)}, f32[8,128]{1,0:T(8,128)S(1)}, f32[16,1024]{1,0:T(8,128)S(1)}, f32[16,1024]{1,0:T(8,128)S(1)}) custom-call(f32[512,768]{1,0:T(8,128)S(1)} %copy-done.155, f32[512,1024]{1,0:T(8,128)} %get-tuple-element.177.refs_1_.refs_3_.refs_4_, f32[512,1152]{1,0:T(8,128)} %copy-done.223, ...), custom_call_target="tpu_custom_call" | custom-call | flops 8999999488 | bytes 1024 | tf_op jit(solution)/shard_map/pallas_call | solution.py:59
  592.1 7.6 %shard_map.358 = (bf16[2,128,1536]{2,1,0:T(8,128)(2,1)S(1)}, bf16[2,128,1536]{2,1,0:T(8,128)(2,1)S(1)}, bf16[512,1152]{1,0:T(8,128)(2,1)S(1)}) custom-call(s32[4]{0:T(128)S(1)} %copy-done.109, bf16[512,1152]{1,0:T(8,128)(2,1)S(1)} %get-tuple-element.276.refs_1_, bf16[512,768]{1,0:T(8,128)(2,1)S(1)} %copy-done.37, f32[16,1024]{1,0:T(8,128)S(1)} %get-tuple-element.277.refs_3_, ...), custom_call_target="tpu_custom_call" | custom-call | flops 3800000000 | bytes 1024 | tf_op jit(solution)/shard_map/pallas_call | solution.py:59
  605.0 10.0 %shard_map.360 = (bf16[4,192,1152]{2,1,0:T(8,128)(2,1)}, bf16[192,1152]{1,0:T(8,128)(2,1)}, bf16[192,1152]{1,0:T(8,128)(2,1)}, bf16[192,1152]{1,0:T(8,128)(2,1)}, bf16[192,1152]{1,0:T(8,128)(2,1)}) custom-call(s32[2]{0:T(128)} %pad_add_fusion.1.refs_0_, bf16[512,1536]{1,0:T(8,128)(2,1)} %copy-done.22, bf16[512,1536]{1,0:T(8,128)(2,1)} %copy-done.26, ...), custom_call_target="tpu_custom_call" | custom-call | flops 5000000000 | bytes 1024 | tf_op jit(solution)/shard_map/pallas_call | solution.py:59
  625.5 8.3 %collective-permute-done.85.refs_1_.refs_2_ = bf16[128,1536]{1,0:T(8,128)(2,1)} collective-permute-done((bf16[128,1536]{1,0:T(8,128)(2,1)}, bf16[128,1536]{1,0:T(8,128)(2,1)}, u32[]{:S(2)}, u32[]{:S(2)}) %collective-permute-start.85) | collective-permute-done | bytes 393248 | tf_op jit(solution)/shard_map/ppermute | solution.py:78
  (941 shorter events, 439.4 us)
Async XLA Ops:
  7.2 240.9 %all-gather.2.cloned.1.call-start = ((), (), s32[]{:S(2)}) async-start(), calls=%async_computation.2 | async-start | bytes 9289728 | tf_op jit(solution)/shard_map/all_gather | solution.py:1523
  10.9 23.8 %collective-permute-start.4 = (bf16[2,16,1536]{2,1,0:T(8,128)(2,1)S(1)}, bf16[2,16,1536]{2,1,0:T(8,128)(2,1)S(1)}, u32[]{:S(2)}, u32[]{:S(2)}) collective-permute-start(bf16[2,16,1536]{2,1,0:T(8,128)(2,1)S(1)} %slice.182), channel_id=1, source_target_pairs={{0,4},{1,5},{2,6},{3,7},{8,12},{9,13},{10,14},{11,15},{16,20},{17,... | collective-permute-start | bytes 294920 | tf_op jit(solution)/shard_map/ppermute | solution.py:88
  71.3 27.5 %collective-permute-start.11 = (bf16[192,1536]{1,0:T(8,128)(2,1)S(1)}, bf16[192,1536]{1,0:T(8,128)(2,1)}, u32[]{:S(2)}, u32[]{:S(2)}) collective-permute-start(bf16[192,1536]{1,0:T(8,128)(2,1)S(1)} %shard_map.292.refs_9_.refs_1_), channel_id=1, source_target_pairs={{0,24},{8,0},{16,8},{24,16},{1,25},{9,1},{17,9},{25,17},{2,26},{10... | collective-permute-start | bytes 1769480 | tf_op jit(solution)/shard_map/ppermute | solution.py:93
  75.6 23.1 %collective-permute-start.12 = (bf16[192,1536]{1,0:T(8,128)(2,1)S(1)}, bf16[192,1536]{1,0:T(8,128)(2,1)S(1)}, u32[]{:S(2)}, u32[]{:S(2)}) collective-permute-start(bf16[192,1536]{1,0:T(8,128)(2,1)S(1)} %shard_map.292.refs_9_.refs_1_), channel_id=1, source_target_pairs={{0,4},{4,0},{1,5},{5,1},{2,6},{6,2},{3,7},{7,3},{8,12},{12,8},{9,1... | collective-permute-start | bytes 1769480 | tf_op jit(solution)/shard_map/ppermute | solution.py:93
  124.1 352.3 %reduce-scatter.3.cloned.1.call-start = ((), (), s32[]{:S(2)}) async-start(), calls=%async_computation.3 | async-start | bytes 5308416 | tf_op jit(solution)/shard_map/reduce_scatter | solution.py:1699
  124.1 23.3 %collective-permute-start.16 = (bf16[192,1536]{1,0:T(8,128)(2,1)}, bf16[192,1536]{1,0:T(8,128)(2,1)S(1)}, u32[]{:S(2)}, u32[]{:S(2)}) collective-permute-start(bf16[192,1536]{1,0:T(8,128)(2,1)} %copy-done.70), channel_id=1, source_target_pairs={{0,4},{4,0},{1,5},{5,1},{2,6},{6,2},{3,7},{7,3},{8,12},{12,8},{9,1... | collective-permute-start | bytes 1769480 | tf_op jit(solution)/shard_map/ppermute | solution.py:93
  238.2 24.0 %collective-permute-start.32 = (f32[128,1536]{1,0:T(8,128)}, f32[128,1536]{1,0:T(8,128)}, u32[]{:S(2)}, u32[]{:S(2)}) collective-permute-start(f32[128,1536]{1,0:T(8,128)} %shard_map.311.refs_2_), channel_id=1, source_target_pairs={{0,2},{1,3},{2,0},{3,1},{4,6},{5,7},{6,4},{7,5},{8,10},{9,11},{10,... | collective-permute-start | bytes 2359304 | tf_op jit(solution)/shard_map/ppermute | solution.py:78
  277.3 25.1 %collective-permute-start.33 = (f32[128,768]{1,0:T(8,128)S(1)}, f32[128,768]{1,0:T(8,128)S(1)}, u32[]{:S(2)}, u32[]{:S(2)}) collective-permute-start(f32[128,768]{1,0:T(8,128)S(1)} %get-tuple-element.194), channel_id=1, source_target_pairs={{0,4},{1,5},{2,6},{3,7},{8,12},{9,13},{10,14},{11,15},{16,20},{17,... | collective-permute-start | bytes 1179656 | tf_op jit(solution)/shard_map/ppermute | solution.py:88
  356.6 198.0 %reduce-scatter.5.cloned.1.call-start = ((), (), s32[]{:S(2)}) async-start(), calls=%async_computation.4 | async-start | bytes 3981312 | tf_op jit(solution)/shard_map/reduce_scatter | solution.py:1699
  356.7 29.3 %collective-permute-start.47 = (bf16[128,768]{1,0:T(8,128)(2,1)S(1)}, bf16[128,768]{1,0:T(8,128)(2,1)S(1)}, u32[]{:S(2)}, u32[]{:S(2)}) collective-permute-start(bf16[128,768]{1,0:T(8,128)(2,1)S(1)} %get-tuple-element.226), channel_id=1, source_target_pairs={{4,0},{5,1},{6,2},{7,3},{12,8},{13,9},{14,10},{15,11},{20,16},{21,... | collective-permute-start | bytes 589832 | tf_op jit(solution)/shard_map/ppermute | solution.py:88
  466.6 32.2 %collective-permute-start.54 = (bf16[128,1536]{1,0:T(8,128)(2,1)}, bf16[128,1536]{1,0:T(8,128)(2,1)}, u32[]{:S(2)}, u32[]{:S(2)}) collective-permute-start(bf16[128,1536]{1,0:T(8,128)(2,1)} %shard_map.339.refs_2_), channel_id=1, source_target_pairs={{0,2},{1,3},{2,0},{3,1},{4,6},{5,7},{6,4},{7,5},{8,10},{9,11},{10,... | collective-permute-start | bytes 1179656 | tf_op jit(solution)/shard_map/ppermute | solution.py:78
  467.5 33.5 %collective-permute-start.63 = (bf16[128,1536]{1,0:T(8,128)(2,1)}, bf16[128,1536]{1,0:T(8,128)(2,1)}, u32[]{:S(2)}, u32[]{:S(2)}) collective-permute-start(bf16[128,1536]{1,0:T(8,128)(2,1)} %shard_map.340.refs_5_), channel_id=1, source_target_pairs={{0,2},{1,3},{2,0},{3,1},{4,6},{5,7},{6,4},{7,5},{8,10},{9,11},{10,... | collective-permute-start | bytes 1179656 | tf_op jit(solution)/shard_map/ppermute | solution.py:78
  472.1 30.8 %collective-permute-start.62 = (bf16[128,1536]{1,0:T(8,128)(2,1)S(1)}, bf16[128,1536]{1,0:T(8,128)(2,1)}, u32[]{:S(2)}, u32[]{:S(2)}) collective-permute-start(bf16[128,1536]{1,0:T(8,128)(2,1)S(1)} %get-tuple-element.252.refs_0_.refs_1_), channel_id=1, source_target_pairs={{0,2},{1,3},{2,0},{3,1},{4,6},{5,7},{6,4},{7,5},{8,10},{9,11},{10,... | collective-permute-start | bytes 1179656 | tf_op jit(solution)/shard_map/ppermute | solution.py:78
  521.5 30.3 %collective-permute-start.70 = (bf16[2,128,1536]{2,1,0:T(8,128)(2,1)S(1)}, bf16[2,128,1536]{2,1,0:T(8,128)(2,1)S(1)}, u32[]{:S(2)}, u32[]{:S(2)}) collective-permute-start(bf16[2,128,1536]{2,1,0:T(8,128)(2,1)S(1)} %get-tuple-element.259.refs_12_), channel_id=1, source_target_pairs={{0,1},{1,0},{2,3},{3,2},{4,5},{5,4},{6,7},{7,6},{8,9},{9,8},{10,11... | collective-permute-start | bytes 2359304 | tf_op jit(solution)/shard_map/ppermute | solution.py:78
  523.5 51.5 %collective-permute-start.61 = (bf16[128,1536]{1,0:T(8,128)(2,1)}, bf16[128,1536]{1,0:T(8,128)(2,1)}, u32[]{:S(2)}, u32[]{:S(2)}) collective-permute-start(bf16[128,1536]{1,0:T(8,128)(2,1)} %shard_map.345.refs_5_.refs_0_.refs_1_), channel_id=1, source_target_pairs={{0,2},{1,3},{2,0},{3,1},{4,6},{5,7},{6,4},{7,5},{8,10},{9,11},{10,... | collective-permute-start | bytes 1179656 | tf_op jit(solution)/shard_map/ppermute | solution.py:78
  524.9 53.9 %collective-permute-start.72 = (bf16[128,1536]{1,0:T(8,128)(2,1)}, bf16[128,1536]{1,0:T(8,128)(2,1)}, u32[]{:S(2)}, u32[]{:S(2)}) collective-permute-start(bf16[128,1536]{1,0:T(8,128)(2,1)} %shard_map.346.refs_2_.refs_0_.refs_5_), channel_id=1, source_target_pairs={{0,2},{1,3},{2,0},{3,1},{4,6},{5,7},{6,4},{7,5},{8,10},{9,11},{10,... | collective-permute-start | bytes 1179656 | tf_op jit(solution)/shard_map/ppermute | solution.py:78
  548.8 32.3 %collective-permute-start.74 = (bf16[192,1536]{1,0:T(8,128)(2,1)}, bf16[192,1536]{1,0:T(8,128)(2,1)S(1)}, u32[]{:S(2)}, u32[]{:S(2)}) collective-permute-start(bf16[192,1536]{1,0:T(8,128)(2,1)} %get-tuple-element.270.refs_2_), channel_id=1, source_target_pairs={{0,4},{4,0},{1,5},{5,1},{2,6},{6,2},{3,7},{7,3},{8,12},{12,8},{9,1... | collective-permute-start | bytes 1769480 | tf_op jit(solution)/shard_map/ppermute | solution.py:93
  551.8 29.3 %collective-permute-start.77 = (bf16[192,1536]{1,0:T(8,128)(2,1)}, bf16[192,1536]{1,0:T(8,128)(2,1)}, u32[]{:S(2)}, u32[]{:S(2)}) collective-permute-start(bf16[192,1536]{1,0:T(8,128)(2,1)} %get-tuple-element.275), channel_id=1, source_target_pairs={{0,4},{4,0},{1,5},{5,1},{2,6},{6,2},{3,7},{7,3},{8,12},{12,8},{9,1... | collective-permute-start | bytes 1769480 | tf_op jit(solution)/shard_map/ppermute | solution.py:93
  554.0 33.1 %collective-permute-start.80 = (bf16[128,1536]{1,0:T(8,128)(2,1)}, bf16[128,1536]{1,0:T(8,128)(2,1)}, u32[]{:S(2)}, u32[]{:S(2)}) collective-permute-start(bf16[128,1536]{1,0:T(8,128)(2,1)} %shard_map.352.refs_15_), channel_id=1, source_target_pairs={{0,2},{1,3},{2,0},{3,1},{4,6},{5,7},{6,4},{7,5},{8,10},{9,11},{10,... | collective-permute-start | bytes 1179656 | tf_op jit(solution)/shard_map/ppermute | solution.py:78
  575.0 26.4 %collective-permute-start.76 = (bf16[192,1536]{1,0:T(8,128)(2,1)S(1)}, bf16[192,1536]{1,0:T(8,128)(2,1)S(1)}, u32[]{:S(2)}, u32[]{:S(2)}) collective-permute-start(bf16[192,1536]{1,0:T(8,128)(2,1)S(1)} %copy-done.269), channel_id=1, source_target_pairs={{0,4},{4,0},{1,5},{5,1},{2,6},{6,2},{3,7},{7,3},{8,12},{12,8},{9,1... | collective-permute-start | bytes 1769480 | tf_op jit(solution)/shard_map/ppermute | solution.py:93
  604.4 35.6 %collective-permute-start.71 = (bf16[256,1536]{1,0:T(8,128)(2,1)}, bf16[256,1536]{1,0:T(8,128)(2,1)}, u32[]{:S(2)}, u32[]{:S(2)}) collective-permute-start(bf16[256,1536]{1,0:T(8,128)(2,1)} %shard_map.354.refs_2_), channel_id=1, source_target_pairs={{0,1},{1,0},{2,3},{3,2},{4,5},{5,4},{6,7},{7,6},{8,9},{9,8},{10,11... | collective-permute-start | bytes 2359304 | tf_op jit(solution)/shard_map/ppermute | solution.py:78
  604.7 35.5 %collective-permute-start.73 = (bf16[256,1536]{1,0:T(8,128)(2,1)}, bf16[256,1536]{1,0:T(8,128)(2,1)}, u32[]{:S(2)}, u32[]{:S(2)}) collective-permute-start(bf16[256,1536]{1,0:T(8,128)(2,1)} %shard_map.355.refs_2_), channel_id=1, source_target_pairs={{0,1},{1,0},{2,3},{3,2},{4,5},{5,4},{6,7},{7,6},{8,9},{9,8},{10,11... | collective-permute-start | bytes 2359304 | tf_op jit(solution)/shard_map/ppermute | solution.py:78
  639.1 34.1 %collective-permute-start.95 = (bf16[192,1152]{1,0:T(8,128)(2,1)}, bf16[192,1152]{1,0:T(8,128)(2,1)}, u32[]{:S(2)}, u32[]{:S(2)}) collective-permute-start(bf16[192,1152]{1,0:T(8,128)(2,1)} %get-tuple-element.299), channel_id=1, source_target_pairs={{0,4},{4,0},{1,5},{5,1},{2,6},{6,2},{3,7},{7,3},{8,12},{12,8},{9,1... | collective-permute-start | bytes 1327112 | tf_op jit(solution)/shard_map/ppermute | solution.py:93
  640.0 40.9 %collective-permute-start.86 = (bf16[256,1536]{1,0:T(8,128)(2,1)}, bf16[256,1536]{1,0:T(8,128)(2,1)S(1)}, u32[]{:S(2)}, u32[]{:S(2)}) collective-permute-start(bf16[256,1536]{1,0:T(8,128)(2,1)} %shard_map.363.refs_2_), channel_id=1, source_target_pairs={{0,1},{1,0},{2,3},{3,2},{4,5},{5,4},{6,7},{7,6},{8,9},{9,8},{10,11... | collective-permute-start | bytes 2359304 | tf_op jit(solution)/shard_map/ppermute | solution.py:78
  (358 other events, 3098.9 us)
Sparse Core Ops, SparseCore 0:
  124.2 123.8 all-gather.1
  356.7 95.1 reduce-scatter.2
  457.4 81.6 reduce-scatter.4
